TPU v7x, 32 devices: a whole 2x2x4 slice. The times are simulated.
32 devices in a mesh: wide: 8 (over z, x), narrow: 4 (over y, core).
Axes of the slice: x: 2, y: 2, z: 4, core: 2. Of those that a mesh axis runs over, the one named last changes fastest.
Arguments:
- tokens: bfloat16 [1024, 1024], P('wide'), may hold values from -6 to 6
- cotangent: bfloat16 [1024, 1024], P('wide'), may hold values from -6 to 6
- expert_ids: int32 [1024, 1], P('wide'), may hold values from 0 to 1; in each aligned block of 128 rows (0 to 127, 128 to 255, ...) at most 128 rows name the same one
- route_prob: float32 [1024], P('wide'), may hold values from 0.2 to 1
- gate_weight: bfloat16 [2048, 2816], P('wide', 'narrow'), may hold values from -0.1875 to 0.1875
- up_weight: bfloat16 [2048, 2816], P('wide', 'narrow'), may hold values from -0.1875 to 0.1875
- down_weight: bfloat16 [2048, 2816], P('wide', 'narrow'), may hold values from -0.109375 to 0.109375
Outputs:
- output: bfloat16 [1024, 1024], P('wide', 'narrow')
- tokens_grad: bfloat16 [1024, 1024], P('wide', 'narrow')
- prob_grad: float32 [1024], P('wide')
- gate_grad: float32 [2048, 2816], P('wide', 'narrow')
- up_grad: float32 [2048, 2816], P('wide', 'narrow')
- down_grad: float32 [2048, 2816], P('wide', 'narrow')
Inputs may be any that keep to these rules, and one draw needn't show every extreme that they name: `expert_ids`: among the 128 tokens of one index of wide, no expert is chosen by more than 128 tokens, and in some such groups one expert is chosen by exactly 128.
All inputs are finite; a program needn't handle non-finite values.
Results may differ from a plain program's by a relative error of at most 0.01.
Values may be sent and summed in bfloat16 or wider, within the bound.
No kernel may reach another device: no remote copies, remote signals or barrier semaphores. Data moves between devices by JAX's collectives and lax.ppermute only.
A program may use at most 64 MiB of HBM per device.

v0:
```python
import jax
import jax.numpy as jnp
from jax import lax
from jax.sharding import PartitionSpec as P


def partner_2(x, axis, apart):
    return lax.ppermute(x, axis, [(i, i ^ 1 << apart) for i in range(lax.axis_size(axis))])


def transpose_dot(left, right):
    return lax.dot_general(
        left, right, (((1,), (1,)), ((), ())), preferred_element_type=jnp.float32
    )


def rows_dot(left, right):
    return lax.dot_general(
        left, right, (((0,), (0,)), ((), ())), preferred_element_type=jnp.float32
    )


def columns(array, first, count):
    return lax.dynamic_slice_in_dim(array, first, count, 1)


def shards(tokens, cotangent, expert_ids, route_prob, gate_weight, up_weight, down_weight):
    wide_count = lax.axis_size("wide")
    expert_count = wide_count // 4
    tok_rows, feature_width = tokens.shape
    hidden_width = gate_weight.shape[1]
    capacity = min(4 * tok_rows // expert_count, tok_rows)
    slot_count = capacity // 4
    total_rows = wide_count * slot_count
    block_rows = min(128, total_rows)
    member_index = lax.axis_index("wide") % 4
    low_bit = member_index % 2
    high_bit = member_index // 2
    chosen = expert_ids[:, 0]
    onehot = (chosen[:, None] == jnp.arange(expert_count, dtype=jnp.int32)[None, :]).astype(
        jnp.int32
    )
    token_rank = jnp.sum((jnp.cumsum(onehot, axis=0) - onehot) * onehot, axis=1)
    target = 4 * chosen + (token_rank + member_index) % 4
    slot_place = target * slot_count + token_rank // 4
    source = (
        jnp.full((total_rows,), tok_rows, jnp.int32)
        .at[slot_place]
        .set(jnp.arange(tok_rows, dtype=jnp.int32))
    )
    sent_counts = jnp.sum(
        (target[:, None] == jnp.arange(wide_count, dtype=jnp.int32)[None, :]).astype(jnp.int32),
        axis=0,
    )
    scaled = (route_prob[:, None] * cotangent.astype(jnp.float32)).astype(jnp.bfloat16)
    blank_row = jnp.zeros((1, feature_width), jnp.bfloat16)
    send_tokens = jnp.concatenate([tokens, blank_row], 0)[source]
    send_scaled = jnp.concatenate([scaled, blank_row], 0)[source]
    got_tokens, got_scaled, got_counts = (
        lax.all_to_all(send_tokens, "wide", split_axis=0, concat_axis=0, tiled=True),
        lax.all_to_all(send_scaled, "wide", split_axis=0, concat_axis=0, tiled=True),
        lax.all_to_all(
            sent_counts[:, None].astype(jnp.bfloat16),
            "wide",
            split_axis=0,
            concat_axis=0,
            tiled=True,
        ),
    )
    live_mask = (
        jnp.arange(slot_count, dtype=jnp.int32)[None, :] < got_counts.astype(jnp.int32)
    ).reshape(total_rows)
    live_rows = live_mask.astype(jnp.int32)
    filled = jnp.sum(live_rows)
    position = jnp.where(
        live_mask, jnp.cumsum(live_rows) - 1, filled + jnp.cumsum(1 - live_rows) - 1
    )
    packed_order = (
        jnp.zeros((total_rows,), jnp.int32)
        .at[position]
        .set(jnp.arange(total_rows, dtype=jnp.int32))
    )
    packed_tokens = got_tokens[packed_order]
    packed_scaled = got_scaled[packed_order]
    stacked = jnp.stack([gate_weight, up_weight, down_weight])
    partner = partner_2(stacked, "wide", 0)
    stacked = jnp.where(
        low_bit == 0, jnp.concatenate([stacked, partner], 1), jnp.concatenate([partner, stacked], 1)
    )
    partner = partner_2(stacked, "wide", 1)
    stacked = jnp.where(
        high_bit == 0,
        jnp.concatenate([stacked, partner], 1),
        jnp.concatenate([partner, stacked], 1),
    )
    gate_full = stacked[0]
    up_full = stacked[1]
    down_full = stacked[2]

    def block_step(block_index, state_tuple):
        row_start = block_index * block_rows
        rows_in = lax.dynamic_slice_in_dim(packed_tokens, row_start, block_rows, 0)
        rows_cot = lax.dynamic_slice_in_dim(packed_scaled, row_start, block_rows, 0)
        gate_val = jnp.dot(rows_in, gate_full, preferred_element_type=jnp.float32)
        up_val = jnp.dot(rows_in, up_full, preferred_element_type=jnp.float32)
        gate_sigma = jax.nn.sigmoid(gate_val)
        active = gate_val * gate_sigma
        hidden = (active * up_val).astype(jnp.bfloat16)
        out_part = transpose_dot(hidden, down_full)
        d_hidden = jnp.dot(rows_cot, down_full, preferred_element_type=jnp.float32)
        d_gate = (d_hidden * up_val * gate_sigma * (1.0 + gate_val * (1.0 - gate_sigma))).astype(
            jnp.bfloat16
        )
        d_up = (d_hidden * active).astype(jnp.bfloat16)
        in_part = transpose_dot(d_gate, gate_full) + transpose_dot(d_up, up_full)
        out_buffer = lax.dynamic_update_slice_in_dim(state_tuple[0], out_part, row_start, 0)
        in_buffer = lax.dynamic_update_slice_in_dim(state_tuple[1], in_part, row_start, 0)
        grad_state = tuple(
            (
                lax.dynamic_update_slice_in_dim(buffer_arr, value_arr, row_start, 0)
                for buffer_arr, value_arr in zip(state_tuple[2:], (d_gate, d_up, hidden))
            )
        )
        return (out_buffer, in_buffer) + grad_state

    zero_rows = jnp.zeros((total_rows, feature_width), jnp.float32)
    empty_rows = jnp.zeros((total_rows, hidden_width), jnp.bfloat16)
    count_blocks = (filled + block_rows - 1) // block_rows
    results = lax.fori_loop(
        0, count_blocks, block_step, (zero_rows, zero_rows, empty_rows, empty_rows, empty_rows)
    )
    out_received = results[0][position]
    in_received = results[1][position]
    ffn_sum, grad_sum = (
        lax.psum_scatter(
            out_received.astype(jnp.bfloat16), "narrow", scatter_dimension=1, tiled=True
        ).astype(jnp.float32),
        lax.psum_scatter(
            in_received.astype(jnp.bfloat16), "narrow", scatter_dimension=1, tiled=True
        ).astype(jnp.float32),
    )
    back_out, back_in = (
        lax.all_to_all(
            ffn_sum.astype(jnp.bfloat16), "wide", split_axis=0, concat_axis=0, tiled=True
        ),
        lax.all_to_all(
            grad_sum.astype(jnp.bfloat16), "wide", split_axis=0, concat_axis=0, tiled=True
        ),
    )
    ffn_tokens = back_out[slot_place]
    grad_tokens = back_in[slot_place]
    narrow_width = feature_width // lax.axis_size("narrow")
    cot_columns = columns(cotangent, lax.axis_index("narrow") * narrow_width, narrow_width).astype(
        jnp.float32
    )
    ffn_values = ffn_tokens.astype(jnp.float32)
    output = (route_prob[:, None] * ffn_values).astype(jnp.bfloat16)
    prob_grad = lax.psum(jnp.sum(ffn_values * cot_columns, axis=1), "narrow")
    half_width = feature_width // 2
    fourth = feature_width // 4
    full_grads = jnp.stack(
        [
            rows_dot(packed_tokens, results[2]),
            rows_dot(packed_tokens, results[3]),
            rows_dot(packed_scaled, results[4]),
        ]
    )
    kept = lax.dynamic_slice_in_dim(full_grads, high_bit * half_width, half_width, 1)
    kept = kept + partner_2(
        lax.dynamic_slice_in_dim(full_grads, (1 - high_bit) * half_width, half_width, 1).astype(
            jnp.bfloat16
        ),
        "wide",
        1,
    ).astype(jnp.float32)
    final = lax.dynamic_slice_in_dim(kept, low_bit * fourth, fourth, 1)
    final = final + partner_2(
        lax.dynamic_slice_in_dim(kept, (1 - low_bit) * fourth, fourth, 1).astype(jnp.bfloat16),
        "wide",
        0,
    ).astype(jnp.float32)
    gate_grad = final[0]
    up_grad = final[1]
    down_grad = final[2]
    return (output, grad_tokens, prob_grad, gate_grad, up_grad, down_grad)


def solution(mesh):
    in_specs = (
        P("wide", None),
        P("wide", None),
        P("wide", None),
        P("wide"),
        P("wide", "narrow"),
        P("wide", "narrow"),
        P("wide", "narrow"),
    )
    out_specs = (
        P("wide", "narrow"),
        P("wide", "narrow"),
        P("wide"),
        P("wide", "narrow"),
        P("wide", "narrow"),
        P("wide", "narrow"),
    )
    return jax.shard_map(shards, mesh=mesh, in_specs=in_specs, out_specs=out_specs, check_vma=False)
```

profile of v0, /device:TPU:0, one launch (start us, length us, event | category | flops | bytes accessed | tf_op | source)
XLA Modules:
  0.0 249.9 jit_solution(8436774551074140840)
XLA Ops:
  8.6 3.0 %collective-permute-start = (bf16[3,256,704]{1,2,0:T(8,128)(2,1)S(1)}, bf16[3,256,704]{1,2,0:T(8,128)(2,1)}, u32[]{:S(2)}, u32[]{:S(2)}) collective-permute-start(bf16[3,256,704]{1,2,0:T(8,128)(2,1)S(1)} %pad_maximum_fusion.1), channel_id=1, source_target_pairs={{0,4},{4,0},{8,12},{12,8},{16,20},{20,16},{24,28},{28,24},{1,5},{5... | collective-permute-start | bytes 3244040 | tf_op jit(solution)/shard_map/ppermute | solution.py:8
  12.9 4.9 %all-to-all-start = ((bf16[8,1,1]{2,1,0:T(2,128)(2,1)}), bf16[8,1,1]{2,1,0:T(2,128)(2,1)S(1)}, u32[]{:S(2)}, u32[]{:S(2)}) async-start(bf16[8,1,1]{2,1,0:T(2,128)(2,1)} %copy.27), calls=%async_computation | async-start | bytes 8192 | tf_op jit(solution)/shard_map/all_to_all | solution.py:62
  18.8 16.8 %collective-permute-done = bf16[3,256,704]{1,2,0:T(8,128)(2,1)} collective-permute-done((bf16[3,256,704]{1,2,0:T(8,128)(2,1)S(1)}, bf16[3,256,704]{1,2,0:T(8,128)(2,1)}, u32[]{:S(2)}, u32[]{:S(2)}) %collective-permute-start) | collective-permute-done | bytes 1081376 | tf_op jit(solution)/shard_map/ppermute | solution.py:8
  35.6 2.3 maximum_select_fusion.1
  40.0 2.0 gather_fusion
  42.0 4.8 %all-to-all-start.1 = ((bf16[8,32,1024]{2,1,0:T(8,128)(2,1)}), bf16[8,32,1024]{2,1,0:T(8,128)(2,1)S(1)}, u32[]{:S(2)}, u32[]{:S(2)}) async-start(bf16[8,32,1024]{2,1,0:T(8,128)(2,1)} %bitcast.5), calls=%async_computation.1 | async-start | bytes 1048576 | tf_op jit(solution)/shard_map/all_to_all | solution.py:60
  46.9 2.0 gather_fusion.2
  51.9 45.0 %all-to-all-done.1 = bf16[8,32,1024]{2,1,0:T(8,128)(2,1)S(1)} async-done(((bf16[8,32,1024]{2,1,0:T(8,128)(2,1)}), bf16[8,32,1024]{2,1,0:T(8,128)(2,1)S(1)}, u32[]{:S(2)}, u32[]{:S(2)}) %all-to-all-start.1) | async-done | bytes 524320 | tf_op jit(solution)/shard_map/all_to_all | solution.py:60
  96.8 3.6 %all-to-all-start.2 = ((bf16[8,32,1024]{2,1,0:T(8,128)(2,1)}), bf16[8,32,1024]{2,1,0:T(8,128)(2,1)S(1)}, u32[]{:S(2)}, u32[]{:S(2)}) async-start(bf16[8,32,1024]{2,1,0:T(8,128)(2,1)} %bitcast.89), calls=%async_computation.2 | async-start | bytes 1048576 | tf_op jit(solution)/shard_map/all_to_all | solution.py:61
  104.6 7.7 %all-to-all-done.2 = bf16[8,32,1024]{2,1,0:T(8,128)(2,1)S(1)} async-done(((bf16[8,32,1024]{2,1,0:T(8,128)(2,1)}), bf16[8,32,1024]{2,1,0:T(8,128)(2,1)S(1)}, u32[]{:S(2)}, u32[]{:S(2)}) %all-to-all-start.2) | async-done | bytes 524320 | tf_op jit(solution)/shard_map/all_to_all | solution.py:61
  112.3 2.0 gather_fusion.3
  114.3 3.0 %maximum_select_fusion = bf16[3,1024,704]{1,2,0:T(8,128)(2,1)S(1)} fusion(bf16[3,512,704]{1,2,0:T(8,128)(2,1)} %collective-permute-done.1, bf16[3,512,704]{1,2,0:T(8,128)(2,1)S(1)} %maximum_select_fusion.1, pred[]{:T(512)S(6)} %eq.49), kind=kLoop, calls=%fused_computation.31 | loop fusion | flops 19464192 | bytes 8650753 | tf_op jit(solution)/shard_map/jit(_where)/select_n | solution.py:91
  117.3 2.1 slice_bitcast_fusion
  121.8 2.6 %copy.30 = bf16[1024,704]{1,0:T(8,128)(2,1)} copy(bf16[1024,704]{0,1:T(8,128)(2,1)} %get-tuple-element.152) | data formatting | bytes 2883584 | tf_op jit(solution)/shard_map/while | solution.py:129
  127.7 13.0 %while.18 = (s32[]{:T(128)}, bf16[256,1024]{1,0:T(8,128)(2,1)}, bf16[256,1024]{1,0:T(8,128)(2,1)}, bf16[256,704]{0,1:T(8,128)(2,1)S(1)}, bf16[256,704]{0,1:T(8,1...) while((s32[]{:T(128)}, bf16[256,1024]{1,0:T(8,128)(2,1)}, ...), condition=%wide.region_11.12_spmd, body=%wide.region_10.11_spmd.sunk | while | flops 1108779008 | bytes 39241228 | solution.py:129
  146.0 2.1 copy-done.9
  152.2 37.4 %collective-permute-done.2 = bf16[3,512,704]{1,2,0:T(8,128)(2,1)} collective-permute-done((bf16[3,512,704]{1,2,0:T(8,128)(2,1)S(1)}, bf16[3,512,704]{1,2,0:T(8,128)(2,1)}, u32[]{:S(2)}, u32[]{:S(2)}) %collective-permute-start.2) | collective-permute-done | bytes 2162720 | tf_op jit(solution)/shard_map/ppermute | solution.py:8
  189.6 3.6 %convert_add_fusion = f32[3,512,704]{1,2,0:T(8,128)S(1)} fusion(bf16[3,512,704]{1,2,0:T(8,128)(2,1)} %collective-permute-done.2, f32[3,1024,704]{1,2,0:T(8,128)} %copy-done.9, s32[]{:T(128)S(6)} %select_n.137), kind=kLoop, calls=%fused_computation.32 | loop fusion | flops 2162688 | bytes 10813444 | tf_op jit(solution)/shard_map/add | solution.py:169
  193.2 2.0 copy-done.10
  197.2 3.4 %all-to-all-start.3 = ((bf16[8,32,256]{2,1,0:T(8,128)(2,1)}), bf16[8,32,256]{2,1,0:T(8,128)(2,1)S(1)}, u32[]{:S(2)}, u32[]{:S(2)}) async-start(bf16[8,32,256]{2,1,0:T(8,128)(2,1)} %bitcast.97), calls=%async_computation.4 | async-start | bytes 262144 | tf_op jit(solution)/shard_map/all_to_all | solution.py:143
  200.6 17.6 %all-to-all-done.3 = bf16[8,32,256]{2,1,0:T(8,128)(2,1)S(1)} async-done(((bf16[8,32,256]{2,1,0:T(8,128)(2,1)}), bf16[8,32,256]{2,1,0:T(8,128)(2,1)S(1)}, u32[]{:S(2)}, u32[]{:S(2)}) %all-to-all-start.3) | async-done | bytes 131104 | tf_op jit(solution)/shard_map/all_to_all | solution.py:143
  218.2 5.0 %all-to-all-start.4 = ((bf16[8,32,256]{2,1,0:T(8,128)(2,1)}), bf16[8,32,256]{2,1,0:T(8,128)(2,1)S(1)}, u32[]{:S(2)}, u32[]{:S(2)}) async-start(bf16[8,32,256]{2,1,0:T(8,128)(2,1)} %bitcast.96), calls=%async_computation.6 | async-start | bytes 262144 | tf_op jit(solution)/shard_map/all_to_all | solution.py:146
  224.1 6.5 %all-to-all-done.4 = bf16[8,32,256]{2,1,0:T(8,128)(2,1)S(1)} async-done(((bf16[8,32,256]{2,1,0:T(8,128)(2,1)}), bf16[8,32,256]{2,1,0:T(8,128)(2,1)S(1)}, u32[]{:S(2)}, u32[]{:S(2)}) %all-to-all-start.4) | async-done | bytes 131104 | tf_op jit(solution)/shard_map/all_to_all | solution.py:146
  233.7 6.1 %psum.7 = f32[128]{0:T(128)} all-reduce(f32[128]{0:T(128)S(1)} %get-tuple-element.158), channel_id=1, replica_groups=mesh['wide'=8,'narrow'=4] {'narrow'}, use_global_device_ids=true, to_apply=%region_15.16 | all-reduce | flops 128 | bytes 1024 | tf_op jit(solution)/shard_map/psum | solution.py:158
  (152 shorter events, 49.1 us)
Async XLA Ops:
  7.2 28.4 %copy-start.17 = (bf16[256,704]{0,1:T(8,128)(2,1)S(1)}, bf16[256,704]{0,1:T(8,128)(2,1)}, u32[]{:S(2)}) copy-start(bf16[256,704]{0,1:T(8,128)(2,1)} %param.15) | copy-start | bytes 1081348
  7.2 28.4 %copy-start.18 = (bf16[256,704]{0,1:T(8,128)(2,1)S(1)}, bf16[256,704]{0,1:T(8,128)(2,1)}, u32[]{:S(2)}) copy-start(bf16[256,704]{0,1:T(8,128)(2,1)} %param.14) | copy-start | bytes 1081348
  7.2 4.4 %copy-start.21 = (s32[128,1]{0,1:T(1,128)S(1)}, s32[128,1]{0,1:T(1,128)}, u32[]{:S(2)}) copy-start(s32[128,1]{0,1:T(1,128)} %param.11) | copy-start | bytes 1540
  8.6 27.0 %collective-permute-start = (bf16[3,256,704]{1,2,0:T(8,128)(2,1)S(1)}, bf16[3,256,704]{1,2,0:T(8,128)(2,1)}, u32[]{:S(2)}, u32[]{:S(2)}) collective-permute-start(bf16[3,256,704]{1,2,0:T(8,128)(2,1)S(1)} %pad_maximum_fusion.1), channel_id=1, source_target_pairs={{0,4},{4,0},{8,12},{12,8},{16,20},{20,16},{24,28},{28,24},{1,5},{5... | collective-permute-start | bytes 3244040 | tf_op jit(solution)/shard_map/ppermute | solution.py:8
  12.9 29.1 %all-to-all-start = ((bf16[8,1,1]{2,1,0:T(2,128)(2,1)}), bf16[8,1,1]{2,1,0:T(2,128)(2,1)S(1)}, u32[]{:S(2)}, u32[]{:S(2)}) async-start(bf16[8,1,1]{2,1,0:T(2,128)(2,1)} %copy.27), calls=%async_computation | async-start | bytes 8192 | tf_op jit(solution)/shard_map/all_to_all | solution.py:62
  18.7 21.2 %copy-start.20 = (bf16[128,1024]{1,0:T(8,128)(2,1)S(1)}, bf16[128,1024]{1,0:T(8,128)(2,1)}, u32[]{:S(2)}) copy-start(bf16[128,1024]{1,0:T(8,128)(2,1)} %param.9) | copy-start | bytes 786436
  38.0 76.3 %collective-permute-start.1 = (bf16[3,512,704]{1,2,0:T(8,128)(2,1)S(1)}, bf16[3,512,704]{1,2,0:T(8,128)(2,1)}, u32[]{:S(2)}, u32[]{:S(2)}) collective-permute-start(bf16[3,512,704]{1,2,0:T(8,128)(2,1)S(1)} %maximum_select_fusion.1), channel_id=1, source_target_pairs={{0,8},{4,12},{8,0},{12,4},{16,24},{20,28},{24,16},{28,20},{1,9},{5... | collective-permute-start | bytes 6488072 | tf_op jit(solution)/shard_map/ppermute | solution.py:8
  40.0 6.8 %copy-start.19 = (bf16[128,1024]{1,0:T(8,128)(2,1)S(1)}, bf16[128,1024]{1,0:T(8,128)(2,1)}, u32[]{:S(2)}) copy-start(bf16[128,1024]{1,0:T(8,128)(2,1)} %param.10) | copy-start | bytes 786436
  40.0 6.8 %copy-start.22 = (f32[128]{0:T(128)S(1)}, f32[128]{0:T(128)}, u32[]{:S(2)}) copy-start(f32[128]{0:T(128)} %param.12) | copy-start | bytes 1540
  42.0 54.9 %all-to-all-start.1 = ((bf16[8,32,1024]{2,1,0:T(8,128)(2,1)}), bf16[8,32,1024]{2,1,0:T(8,128)(2,1)S(1)}, u32[]{:S(2)}, u32[]{:S(2)}) async-start(bf16[8,32,1024]{2,1,0:T(8,128)(2,1)} %bitcast.5), calls=%async_computation.1 | async-start | bytes 1048576 | tf_op jit(solution)/shard_map/all_to_all | solution.py:60
  96.8 15.5 %all-to-all-start.2 = ((bf16[8,32,1024]{2,1,0:T(8,128)(2,1)}), bf16[8,32,1024]{2,1,0:T(8,128)(2,1)S(1)}, u32[]{:S(2)}, u32[]{:S(2)}) async-start(bf16[8,32,1024]{2,1,0:T(8,128)(2,1)} %bitcast.89), calls=%async_computation.2 | async-start | bytes 1048576 | tf_op jit(solution)/shard_map/all_to_all | solution.py:61
  100.4 96.8 %reduce-scatter.3.cloned.1.call-start = ((), (), s32[]{:S(2)}) async-start(), calls=%async_computation.7 | async-start | bytes 655360 | tf_op jit(solution)/shard_map/reduce_scatter | solution.py:135
  127.7 2.6 %copy-start.11 = (bf16[256,1024]{1,0:T(8,128)(2,1)S(1)}, bf16[256,1024]{1,0:T(8,128)(2,1)}, u32[]{:S(2)}) copy-start(bf16[256,1024]{1,0:T(8,128)(2,1)} %get-tuple-element.291) | copy-start | bytes 1572868 | tf_op jit(solution)/shard_map/while
  127.7 2.6 %copy-start.12 = (bf16[256,704]{0,1:T(8,128)(2,1)S(1)}, bf16[256,704]{0,1:T(8,128)(2,1)}, u32[]{:S(2)}) copy-start(bf16[256,704]{0,1:T(8,128)(2,1)} %get-tuple-element.268) | copy-start | bytes 1081348 | tf_op jit(solution)/shard_map/while
  127.7 2.6 %copy-start.15 = (bf16[256,704]{0,1:T(8,128)(2,1)S(1)}, bf16[256,704]{0,1:T(8,128)(2,1)}, u32[]{:S(2)}) copy-start(bf16[256,704]{0,1:T(8,128)(2,1)} %get-tuple-element.269) | copy-start | bytes 1081348 | tf_op jit(solution)/shard_map/while
  134.2 2.6 %copy-start.12 = (bf16[256,704]{0,1:T(8,128)(2,1)S(1)}, bf16[256,704]{0,1:T(8,128)(2,1)}, u32[]{:S(2)}) copy-start(bf16[256,704]{0,1:T(8,128)(2,1)} %get-tuple-element.268) | copy-start | bytes 1081348 | tf_op jit(solution)/shard_map/while
  134.2 2.6 %copy-start.15 = (bf16[256,704]{0,1:T(8,128)(2,1)S(1)}, bf16[256,704]{0,1:T(8,128)(2,1)}, u32[]{:S(2)}) copy-start(bf16[256,704]{0,1:T(8,128)(2,1)} %get-tuple-element.269) | copy-start | bytes 1081348 | tf_op jit(solution)/shard_map/while
  144.8 3.3 %copy-start.9 = (f32[3,1024,704]{1,2,0:T(8,128)}, f32[3,1024,704]{1,2,0:T(8,128)S(1)}, u32[]{:S(2)}) copy-start(f32[3,1024,704]{1,2,0:T(8,128)S(1)} %pad_maximum_fusion) | copy-start | bytes 25952260
  144.8 3.3 %copy-start.3 = (bf16[256,1024]{1,0:T(8,128)(2,1)S(1)}, bf16[256,1024]{1,0:T(8,128)(2,1)}, u32[]{:S(2)}) copy-start(bf16[256,1024]{1,0:T(8,128)(2,1)} %get-tuple-element.73) | copy-start | bytes 1572868
  145.2 44.4 %collective-permute-start.2 = (bf16[3,512,704]{1,2,0:T(8,128)(2,1)S(1)}, bf16[3,512,704]{1,2,0:T(8,128)(2,1)}, u32[]{:S(2)}, u32[]{:S(2)}) collective-permute-start(bf16[3,512,704]{1,2,0:T(8,128)(2,1)S(1)} %dynamic-slice_convert_fusion), channel_id=1, source_target_pairs={{0,8},{4,12},{8,0},{12,4},{16,24},{20,28},{24,16},{28,20},{1,9},{5... | collective-permute-start | bytes 6488072 | tf_op jit(solution)/shard_map/ppermute | solution.py:8
  150.1 50.5 %reduce-scatter.5.cloned.1.call-start = ((), (), s32[]{:S(2)}) async-start(), calls=%async_computation.8 | async-start | bytes 655360 | tf_op jit(solution)/shard_map/reduce_scatter | solution.py:138
  195.4 44.4 %collective-permute-start.3 = (bf16[3,256,704]{1,2,0:T(8,128)(2,1)S(1)}, bf16[3,256,704]{1,2,0:T(8,128)(2,1)S(1)}, u32[]{:S(2)}, u32[]{:S(2)}) collective-permute-start(bf16[3,256,704]{1,2,0:T(8,128)(2,1)S(1)} %dynamic-slice_convert_fusion.1), channel_id=1, source_target_pairs={{0,4},{4,0},{8,12},{12,8},{16,20},{20,16},{24,28},{28,24},{1,5},{5... | collective-permute-start | bytes 3244040 | tf_op jit(solution)/shard_map/ppermute | solution.py:8
  197.2 21.0 %all-to-all-start.3 = ((bf16[8,32,256]{2,1,0:T(8,128)(2,1)}), bf16[8,32,256]{2,1,0:T(8,128)(2,1)S(1)}, u32[]{:S(2)}, u32[]{:S(2)}) async-start(bf16[8,32,256]{2,1,0:T(8,128)(2,1)} %bitcast.97), calls=%async_computation.4 | async-start | bytes 262144 | tf_op jit(solution)/shard_map/all_to_all | solution.py:143
  218.2 12.4 %all-to-all-start.4 = ((bf16[8,32,256]{2,1,0:T(8,128)(2,1)}), bf16[8,32,256]{2,1,0:T(8,128)(2,1)S(1)}, u32[]{:S(2)}, u32[]{:S(2)}) async-start(bf16[8,32,256]{2,1,0:T(8,128)(2,1)} %bitcast.96), calls=%async_computation.6 | async-start | bytes 262144 | tf_op jit(solution)/shard_map/all_to_all | solution.py:146
  (21 other events, 34.0 us)
Sparse Core Ops, SparseCore 0:
  150.2 19.8 reduce-scatter.2
  173.4 21.6 reduce-scatter.4
where the time goes:
time: 251 us; the launch traced here: 250 us
  waiting for transfers between devices  131 us (52%)
  local copies, waits for them, and re-layouts  36 us (14%)
  starting transfers between devices  29.3 us (12%)
  other arithmetic  18.3 us (7%)
  between operations  15 us (6%)
  matrix products  13.8 us (5%)
  blocking collectives  6.13 us (2%)
    ppermute x4, waiting for transfers between devices, partner_2(): lax.ppermute(x, axis, [(i, i ^ 1 << apart) for i in range(lax.axis_size(a...  54.3 us
    all_to_all x1, waiting for transfers between devices, shards(): lax.all_to_all(send_tokens, 'wide', split_axis=0, concat_axis=0, tiled=True)  45 us
    all_to_all x1, waiting for transfers between devices, shards(): lax.all_to_all(ffn_sum.astype(jnp.bfloat16), 'wide', split_axis=0, concat...  17.6 us
    all_to_all x1, waiting for transfers between devices, shards(): lax.all_to_all(send_scaled, 'wide', split_axis=0, concat_axis=0, tiled=True)  7.68 us
    ppermute x4, starting transfers between devices, partner_2(): lax.ppermute(x, axis, [(i, i ^ 1 << apart) for i in range(lax.axis_size(a...  7.58 us
    all_to_all x1, waiting for transfers between devices, shards(): lax.all_to_all(grad_sum.astype(jnp.bfloat16), 'wide', split_axis=0, conca...  6.49 us
    psum x1, blocking collectives, shards(): prob_grad = lax.psum(jnp.sum(ffn_values * cot_columns, axis=1), 'narrow')  6.13 us
    all_to_all x1, starting transfers between devices, shards(): lax.all_to_all(grad_sum.astype(jnp.bfloat16), 'wide', split_axis=0, conca...  5.04 us
  transfers between devices with their start and end apart: 11, of which 6 were waited for; matrix products, arithmetic and copies ran while one was open for 12% of the time, Pallas kernels for 0%

commit v1 on v0

v1 whole, which is shorter than its diff:
```python
import functools

import jax
import jax.numpy as jnp
from jax import lax
from jax.experimental import pallas as pl
from jax.experimental.pallas import tpu as pltpu
from jax.sharding import PartitionSpec as P

VMEM = pl.BlockSpec(memory_space=pltpu.VMEM)
PARAMS = pltpu.CompilerParams(vmem_limit_bytes=48 * 1024 * 1024)


def partner(x, axis, mask):
    return lax.ppermute(x, axis, [(i, i ^ mask) for i in range(lax.axis_size(axis))])


def dot_nn(left, right):
    return lax.dot_general(
        left, right, (((1,), (0,)), ((), ())), preferred_element_type=jnp.float32
    )


def dot_nt(left, right):
    return lax.dot_general(
        left, right, (((1,), (1,)), ((), ())), preferred_element_type=jnp.float32
    )


def at_quarter(index, width):
    return pl.ds(pl.multiple_of(index * width, width), width)


def halves_kernel(gate, up, down, keep, give):
    half = keep.shape[1]
    x_bit = lax.axis_index("wide") % 2
    keep_rows = pl.ds(pl.multiple_of(x_bit * half, 16), half)
    give_rows = pl.ds(pl.multiple_of((1 - x_bit) * half, 16), half)
    for i, ref in enumerate((gate, up, down)):
        keep[i] = ref[keep_rows, :]
        give[i] = ref[give_rows, :]


def split_halves(gate, up, down):
    hidden, width = gate.shape
    shape = jax.ShapeDtypeStruct((3, hidden // 2, width), jnp.bfloat16)
    return pl.pallas_call(
        halves_kernel,
        out_shape=(shape, shape),
        in_specs=[VMEM] * 3,
        out_specs=[VMEM] * 2,
        compiler_params=PARAMS,
    )(gate, up, down)


def route_kernel(tokens, cotangent, ids, prob, own, same, other):
    rows, features = tokens.shape
    width = same.shape[2]
    mine = lax.axis_index("wide") // 4
    column = at_quarter(lax.axis_index("narrow"), width)
    chosen = jnp.transpose(jnp.broadcast_to(ids[...], (128, rows)).astype(jnp.float32))[:, :1]
    weight = jnp.transpose(jnp.broadcast_to(prob[...], (128, rows)))[:, :1]
    is_mine = chosen == mine.astype(jnp.float32)
    here = jnp.where(is_mine, 1.0, 0.0)
    for i, ref in enumerate((tokens, cotangent)):
        factor = here if i == 0 else here * weight
        own[i] = (ref[...].astype(jnp.float32) * factor).astype(jnp.bfloat16)
        part = ref[:, column].astype(jnp.float32)
        if i == 1:
            part = part * weight
        same[i] = (part * here).astype(jnp.bfloat16)
        other[i] = (part * (1.0 - here)).astype(jnp.bfloat16)


def route_rows(tokens, cotangent, ids, prob, width):
    rows, features = tokens.shape
    return pl.pallas_call(
        route_kernel,
        out_shape=(
            jax.ShapeDtypeStruct((2, rows, features), jnp.bfloat16),
            jax.ShapeDtypeStruct((2, rows, width), jnp.bfloat16),
            jax.ShapeDtypeStruct((2, rows, width), jnp.bfloat16),
        ),
        in_specs=[VMEM] * 4,
        out_specs=[VMEM] * 3,
        compiler_params=PARAMS,
    )(tokens, cotangent, ids, prob)


def forward_kernel(has_own, *refs):
    own = refs[0] if has_own else None
    pieces, weights = refs[has_own : has_own + 4], refs[has_own + 4 : has_own + 8]
    kept, sent, grads, x_all, s_all, w_all = refs[has_own + 8 :]
    blocks, _, slots, width = pieces[0].shape
    member = lax.axis_index("wide") % 4
    place = lax.axis_index("narrow")
    for k, ref in enumerate(weights):
        column = at_quarter(member ^ k, width)
        for i in range(3):
            w_all[i, :, column] = ref[i]
    first = 0
    if has_own:
        x_all[:slots, :] = own[0]
        s_all[:slots, :] = own[1]
        first = slots
    for mask, ref in enumerate(pieces):
        column = at_quarter(place ^ mask, width)
        for block in range(blocks):
            rows = slice(first + block * slots, first + (block + 1) * slots)
            x_all[rows, column] = ref[block, 0]
            s_all[rows, column] = ref[block, 1]
    total = x_all.shape[0]
    tile = min(256, total)

    @pl.loop(0, total // tile)
    def _(step):
        rows = pl.ds(pl.multiple_of(step * tile, tile), tile)
        x_tile, s_tile = x_all[rows, :], s_all[rows, :]
        gate = dot_nt(w_all[0], x_tile)
        up = dot_nt(w_all[1], x_tile)
        d_hidden = dot_nt(w_all[2], s_tile)
        sigma = jax.nn.sigmoid(gate)
        active = gate * sigma
        hidden = (active * up).astype(jnp.bfloat16)
        d_gate = (d_hidden * up * sigma * (1.0 + gate * (1.0 - sigma))).astype(jnp.bfloat16)
        d_up = (d_hidden * active).astype(jnp.bfloat16)
        grads[0, :, rows] = d_gate
        grads[1, :, rows] = d_up
        grads[2, :, rows] = hidden
        hidden_t, d_gate_t, d_up_t = hidden.T, d_gate.T, d_up.T
        for mask in range(4):
            column = at_quarter(place ^ mask, width)
            out_part = dot_nn(hidden_t, w_all[2, :, column])
            in_part = dot_nn(d_gate_t, w_all[0, :, column]) + dot_nn(d_up_t, w_all[1, :, column])
            target = sent if mask % 2 else kept
            target[mask // 2, 0, rows, :] = out_part.astype(target.dtype)
            target[mask // 2, 1, rows, :] = in_part.astype(target.dtype)


def forward(own, pieces, weights):
    blocks, _, slots, width = pieces[0].shape
    half = weights[0].shape[1]
    has_own = own is not None
    total = (blocks + has_own) * slots
    features = 4 * width
    return pl.pallas_call(
        functools.partial(forward_kernel, int(has_own)),
        out_shape=(
            jax.ShapeDtypeStruct((2, 2, total, width), jnp.float32),
            jax.ShapeDtypeStruct((2, 2, total, width), jnp.bfloat16),
            jax.ShapeDtypeStruct((3, half, total), jnp.bfloat16),
            jax.ShapeDtypeStruct((total, features), jnp.bfloat16),
            jax.ShapeDtypeStruct((total, features), jnp.bfloat16),
        ),
        in_specs=[VMEM] * (8 + has_own),
        out_specs=[VMEM] * 5,
        scratch_shapes=[pltpu.VMEM((3, half, features), jnp.bfloat16)],
        compiler_params=PARAMS,
    )(*([own] if has_own else []), *pieces, *weights)


def grads_kernel(grads, x_all, s_all, *outs):
    half, total = grads.shape[1:]
    width = outs[0].shape[2]
    member = lax.axis_index("wide") % 4
    left = grads[0:2].reshape(2 * half, total)
    for k in (1, 2, 3, 0):
        column = at_quarter(member ^ k, width)
        both = dot_nn(left, x_all[:, column])
        outs[k][0] = both[:half].astype(outs[k].dtype)
        outs[k][1] = both[half:].astype(outs[k].dtype)
        outs[k][2] = dot_nn(grads[2], s_all[:, column]).astype(outs[k].dtype)


def weight_grads(grads, x_all, s_all):
    half = grads.shape[1]
    width = x_all.shape[1] // 4
    return pl.pallas_call(
        grads_kernel,
        out_shape=tuple(
            jax.ShapeDtypeStruct((3, half, width), jnp.bfloat16 if k else jnp.float32)
            for k in range(4)
        ),
        in_specs=[VMEM] * 3,
        out_specs=[VMEM] * 4,
        compiler_params=PARAMS,
    )(grads, x_all, s_all)


def join_kernel(own, got_x, got_z, got_d, *outs):
    half = own.shape[1]
    x_bit = lax.axis_index("wide") % 2
    keep_rows = pl.ds(pl.multiple_of(x_bit * half, 16), half)
    give_rows = pl.ds(pl.multiple_of((1 - x_bit) * half, 16), half)
    for i, ref in enumerate(outs):
        ref[keep_rows, :] = own[i] + got_z[i].astype(jnp.float32)
        ref[give_rows, :] = got_x[i].astype(jnp.float32) + got_d[i].astype(jnp.float32)


def join_grads(own, got_x, got_z, got_d):
    _, half, width = own.shape
    shape = jax.ShapeDtypeStruct((2 * half, width), jnp.float32)
    return pl.pallas_call(
        join_kernel,
        out_shape=(shape,) * 3,
        in_specs=[VMEM] * 4,
        out_specs=[VMEM] * 3,
        compiler_params=PARAMS,
    )(own, got_x, got_z, got_d)


def shards(tokens, cotangent, expert_ids, route_prob, gate_weight, up_weight, down_weight):
    wide_count = lax.axis_size("wide")
    narrow_count = lax.axis_size("narrow")
    expert_count = wide_count // 4
    tok_rows, features = tokens.shape
    width = features // narrow_count
    slots = min(4 * tok_rows // expert_count, tok_rows)
    direct = expert_count == 2 and slots == tok_rows
    place = lax.axis_index("narrow")
    masks = (1, 4, 5)
    groups = [
        [4 * e + 2 * b + a for e in range(expert_count) for a in range(2)] for b in range(2)
    ]

    if direct:
        own, same, other = route_rows(
            tokens, cotangent, expert_ids.T, route_prob[None, :], width
        )
        mine = jnp.stack(
            [partner(part, "wide", mask) for mask, part in zip(masks, (same, other, other))]
        )
    else:
        own = None
        chosen = expert_ids[:, 0]
        onehot = (chosen[:, None] == jnp.arange(expert_count, dtype=jnp.int32)[None, :]).astype(
            jnp.int32
        )
        rank = jnp.sum((jnp.cumsum(onehot, axis=0) - onehot) * onehot, axis=1)
        slot_place = chosen * slots + rank
        source = (
            jnp.full((expert_count * slots,), tok_rows, jnp.int32)
            .at[slot_place]
            .set(jnp.arange(tok_rows, dtype=jnp.int32))
        )
        scaled = (route_prob[:, None] * cotangent.astype(jnp.float32)).astype(jnp.bfloat16)
        both = jnp.stack([tokens, scaled])
        both = lax.dynamic_slice_in_dim(both, place * width, width, 2)
        both = jnp.concatenate([both, jnp.zeros((2, 1, width), jnp.bfloat16)], 1)
        routed = both[:, source].reshape(2, expert_count, slots, width).transpose(1, 0, 2, 3)
        routed = jnp.repeat(routed, 2, axis=0)
        mine = lax.all_to_all(
            routed, "wide", split_axis=0, concat_axis=0, axis_index_groups=groups, tiled=True
        )

    keep, give = split_halves(gate_weight.T, up_weight.T, down_weight.T)
    weights = (
        keep,
        partner(give, "wide", 1),
        partner(keep, "wide", 2),
        partner(give, "wide", 3),
    )
    across = partner(mine, "narrow", 2)
    pieces = (mine, partner(mine, "narrow", 1), across, partner(across, "narrow", 1))
    kept, sent, grads, x_all, s_all = forward(own, pieces, weights)

    got = partner(sent, "narrow", 1)
    grad_own, grad_x, grad_z, grad_d = weight_grads(grads, x_all, s_all)
    got_x = partner(grad_x, "wide", 1)
    got_z = partner(grad_z, "wide", 2)
    got_d = partner(grad_d, "wide", 3)

    across = partner((kept[1] + got[1].astype(jnp.float32)).astype(jnp.bfloat16), "narrow", 2)
    result = kept[0] + got[0].astype(jnp.float32) + across.astype(jnp.float32)
    if direct:
        total = result[:, :slots]
        for k, mask in enumerate(masks):
            rows = result[:, (k + 1) * slots : (k + 2) * slots].astype(jnp.bfloat16)
            total = total + partner(rows, "wide", mask).astype(jnp.float32)
    else:
        parts = result.astype(jnp.bfloat16).reshape(2, 2 * expert_count, slots, width)
        back = lax.all_to_all(
            parts, "wide", split_axis=1, concat_axis=1, axis_index_groups=groups, tiled=True
        )
        back = back.reshape(2, expert_count, 2, slots, width).astype(jnp.float32).sum(2)
        total = back.reshape(2, expert_count * slots, width)[:, slot_place]
    ffn = total[0].astype(jnp.bfloat16).astype(jnp.float32)
    tokens_grad = total[1].astype(jnp.bfloat16)
    output = (route_prob[:, None] * ffn).astype(jnp.bfloat16)
    cot_columns = lax.dynamic_slice_in_dim(cotangent, place * width, width, 1)
    prob_grad = lax.psum(jnp.sum(ffn * cot_columns.astype(jnp.float32), axis=1), "narrow")
    gate_grad, up_grad, down_grad = join_grads(grad_own, got_x, got_z, got_d)
    return (output, tokens_grad, prob_grad, gate_grad.T, up_grad.T, down_grad.T)


def solution(mesh):
    in_specs = (
        P("wide", None),
        P("wide", None),
        P("wide", None),
        P("wide"),
        P("wide", "narrow"),
        P("wide", "narrow"),
        P("wide", "narrow"),
    )
    out_specs = (
        P("wide", "narrow"),
        P("wide", "narrow"),
        P("wide"),
        P("wide", "narrow"),
        P("wide", "narrow"),
        P("wide", "narrow"),
    )
    return jax.shard_map(shards, mesh=mesh, in_specs=in_specs, out_specs=out_specs, check_vma=False)
```

time: 251 us -> 110 us (0.44)
  waiting for transfers between devices: 131 us -> 56.2 us
  local copies, waits for them, and re-layouts: 36 us -> 9.99 us
  between operations: 15 us -> 0.7 us
  matrix products: 13.8 us -> 0 us
  other arithmetic: 18.3 us -> 5.23 us
  Pallas kernels: 0 us -> 9.41 us
  starting transfers between devices: 29.3 us -> 22.1 us
    all_to_all x5 -> x0, waiting for transfers between devices: 76.7 us -> none  [the longest x1 45 us: shards(): lax.all_to_all(send_tokens, 'wide', split_axis=0, concat_axis=0, tiled=True)]
    all_to_all x5 -> x0, starting transfers between devices: 21.6 us -> none  [the longest x1 5.04 us: shards(): lax.all_to_all(grad_sum.astype(jnp.bfloat16), 'wide', split_axis=0, conca...]
    ppermute x4 -> x17, starting transfers between devices: 7.58 us -> 22.1 us  [partner(): lax.ppermute(x, axis, [(i, i ^ mask) for i in range(lax.axis_size(axis))])]
    gather x8 -> x0, local copies, waits for them, and re-layouts: 14.1 us -> none  [the longest x1 1.96 us: shards(): packed_scaled = got_scaled[packed_order]]
    dot_general x15 -> x0, matrix products: 13.8 us -> none  [the longest x6 3.94 us: transpose_dot(): lax.dot_general(left, right, (((1,), (1,)), ((), ())), preferred_element_...]
    pallas_call x0 -> x5, Pallas kernels: none -> 9.41 us  [the longest x1 5.78 us: forward(): pl.pallas_call(functools.partial(forward_kernel, int(has_own)), out_shape...]
    while x47 -> x0, local copies, waits for them, and re-layouts: 6.72 us -> none  [the longest x3 4.96 us: shards(): lax.fori_loop(0, count_blocks, block_step, (zero_rows, zero_rows, empty_r...]
    add x2 -> x0, other arithmetic: 5.45 us -> none  [the longest x1 3.61 us: shards(): kept + partner_2(lax.dynamic_slice_in_dim(full_grads, (1 - high_bit) * ha...]
  transfers between devices with their start and end apart: 11 -> 17, of which waited for: 6 -> 11; matrix products, arithmetic and copies ran while one was open for 12% -> 2% of each run, Pallas kernels for 0% -> 3%
where the time goes in v1:
time: 110 us
  waiting for transfers between devices  56.2 us (51%)
  starting transfers between devices  22.1 us (20%)
  local copies, waits for them, and re-layouts  9.99 us (9%)
  Pallas kernels  9.41 us (9%)
  blocking collectives  6.13 us (6%)
  other arithmetic  5.23 us (5%)
    ppermute x17, waiting for transfers between devices, partner(): lax.ppermute(x, axis, [(i, i ^ mask) for i in range(lax.axis_size(axis))])  56.2 us
    ppermute x17, starting transfers between devices, partner(): lax.ppermute(x, axis, [(i, i ^ mask) for i in range(lax.axis_size(axis))])  22.1 us
    unnamed x24, local copies, waits for them, and re-layouts  8.62 us
    psum x1, blocking collectives, shards(): lax.psum(jnp.sum(ffn * cot_columns.astype(jnp.float32), axis=1), 'narrow')  6.13 us
    pallas_call x1, Pallas kernels, forward(): pl.pallas_call(functools.partial(forward_kernel, int(has_own)), out_shape...  5.78 us
    another operation x2, other arithmetic  2.26 us
  transfers between devices with their start and end apart: 17, of which 11 were waited for; matrix products, arithmetic and copies ran while one was open for 2% of the time, Pallas kernels for 3%

profile of v1, /device:TPU:0, one launch (start us, length us, event | category | flops | bytes accessed | tf_op | source)
XLA Modules:
  0.0 109.7 jit_solution(6363485267326724779)
XLA Ops:
  4.1 4.1 %collective-permute-start.1 = (bf16[2,128,256]{2,1,0:T(8,128)(2,1)S(1)}, bf16[2,128,256]{2,1,0:T(8,128)(2,1)S(1)}, u32[]{:S(2)}, u32[]{:S(2)}) collective-permute-start(bf16[2,128,256]{2,1,0:T(8,128)(2,1)S(1)} %get-tuple-element.25), channel_id=1, source_target_pairs={{0,16},{4,20},{8,24},{12,28},{16,0},{20,4},{24,8},{28,12},{1,17},{... | collective-permute-start | bytes 393224 | tf_op jit(solution)/shard_map/ppermute | solution.py:15
  8.2 1.3 %collective-permute-start.2 = (bf16[2,128,256]{2,1,0:T(8,128)(2,1)S(1)}, bf16[2,128,256]{2,1,0:T(8,128)(2,1)S(1)}, u32[]{:S(2)}, u32[]{:S(2)}) collective-permute-start(bf16[2,128,256]{2,1,0:T(8,128)(2,1)S(1)} %get-tuple-element.25), channel_id=1, source_target_pairs={{0,20},{4,16},{8,28},{12,24},{16,4},{20,0},{24,12},{28,8},{1,21},{... | collective-permute-start | bytes 393224 | tf_op jit(solution)/shard_map/ppermute | solution.py:15
  9.8 8.4 %collective-permute-done.1 = bf16[2,128,256]{2,1,0:T(8,128)(2,1)S(1)} collective-permute-done((bf16[2,128,256]{2,1,0:T(8,128)(2,1)S(1)}, bf16[2,128,256]{2,1,0:T(8,128)(2,1)S(1)}, u32[]{:S(2)}, u32[]{:S(2)}) %collective-permute-start.1) | collective-permute-done | bytes 131104 | tf_op jit(solution)/shard_map/ppermute | solution.py:15
  18.2 3.0 %collective-permute-done.2 = bf16[2,128,256]{2,1,0:T(8,128)(2,1)S(1)} collective-permute-done((bf16[2,128,256]{2,1,0:T(8,128)(2,1)S(1)}, bf16[2,128,256]{2,1,0:T(8,128)(2,1)S(1)}, u32[]{:S(2)}, u32[]{:S(2)}) %collective-permute-start.2) | collective-permute-done | bytes 131104 | tf_op jit(solution)/shard_map/ppermute | solution.py:15
  21.2 1.6 %collective-permute-start.4 = (bf16[3,2,128,256]{3,2,1,0:T(8,128)(2,1)S(1)}, bf16[3,2,128,256]{3,2,1,0:T(8,128)(2,1)S(1)}, u32[]{:S(2)}, u32[]{:S(2)}) collective-permute-start(bf16[3,2,128,256]{3,2,1,0:T(8,128)(2,1)S(1)} %pad_maximum_fusion.refs_1_), channel_id=1, source_target_pairs={{0,2},{1,3},{2,0},{3,1},{4,6},{5,7},{6,4},{7,5},{8,10},{9,11},{10,... | collective-permute-start | bytes 1179656 | tf_op jit(solution)/shard_map/ppermute | solution.py:15
  27.1 2.3 %collective-permute-start.8 = (bf16[3,352,256]{2,1,0:T(8,128)(2,1)S(1)}, bf16[3,352,256]{2,1,0:T(8,128)(2,1)S(1)}, u32[]{:S(2)}, u32[]{:S(2)}) collective-permute-start(bf16[3,352,256]{2,1,0:T(8,128)(2,1)S(1)} %get-tuple-element.27), channel_id=1, source_target_pairs={{0,12},{4,8},{8,4},{12,0},{16,28},{20,24},{24,20},{28,16},{1,13},{... | collective-permute-start | bytes 1622024 | tf_op jit(solution)/shard_map/ppermute | solution.py:15
  29.3 1.9 %collective-permute-done.4.refs_3_ = bf16[3,2,128,256]{3,2,1,0:T(8,128)(2,1)S(1)} collective-permute-done((bf16[3,2,128,256]{3,2,1,0:T(8,128)(2,1)S(1)}, bf16[3,2,128,256]{3,2,1,0:T(8,128)(2,1)S(1)}, u32[]{:S(2)}, u32[]{:S(2)}) %collective-permute-start.4) | collective-permute-done | bytes 393248 | tf_op jit(solution)/shard_map/ppermute | solution.py:15
  31.3 8.9 %collective-permute-done.6.refs_6_ = bf16[3,352,256]{2,1,0:T(8,128)(2,1)S(1)} collective-permute-done((bf16[3,352,256]{2,1,0:T(8,128)(2,1)S(1)}, bf16[3,352,256]{2,1,0:T(8,128)(2,1)S(1)}, u32[]{:S(2)}, u32[]{:S(2)}) %collective-permute-start.6) | collective-permute-done | bytes 540704 | tf_op jit(solution)/shard_map/ppermute | solution.py:15
  40.2 1.4 %collective-permute-done.7.refs_7_ = bf16[3,352,256]{2,1,0:T(8,128)(2,1)S(1)} collective-permute-done((bf16[3,352,256]{2,1,0:T(8,128)(2,1)S(1)}, bf16[3,352,256]{2,1,0:T(8,128)(2,1)S(1)}, u32[]{:S(2)}, u32[]{:S(2)}) %collective-permute-start.7) | collective-permute-done | bytes 540704 | tf_op jit(solution)/shard_map/ppermute | solution.py:15
  41.6 9.9 %collective-permute-done.8.refs_8_ = bf16[3,352,256]{2,1,0:T(8,128)(2,1)S(1)} collective-permute-done((bf16[3,352,256]{2,1,0:T(8,128)(2,1)S(1)}, bf16[3,352,256]{2,1,0:T(8,128)(2,1)S(1)}, u32[]{:S(2)}, u32[]{:S(2)}) %collective-permute-start.8) | collective-permute-done | bytes 540704 | tf_op jit(solution)/shard_map/ppermute | solution.py:15
  51.5 5.8 %shard_map.120 = (f32[2,2,512,256]{3,2,1,0:T(8,128)}, bf16[2,2,512,256]{3,2,1,0:T(8,128)(2,1)S(1)}, bf16[3,352,512]{2,1,0:T(8,128)(2,1)}, bf16[512,1024]{1,0:T(8,128)(2,1)}, bf16[512,1024]{1,0:T(8,128)(2,1)}) custom-call(bf16[2,128,1024]{2,1,0:T(8,128)(2,1)S(1)} %get-tuple-element.23.refs_0_, bf16[3,2,128,256]{3,2,1,0:T(8,128)(2,1)S(1)} %pad_maximum_fusion.refs_1_, ...), custom_call_target="tpu_custom_call" | custom-call | tf_op jit(solution)/shard_map/pallas_call | solution.py:146
  57.3 2.7 %collective-permute-done.9 = bf16[2,2,512,256]{3,2,1,0:T(8,128)(2,1)S(1)} collective-permute-done((bf16[2,2,512,256]{3,2,1,0:T(8,128)(2,1)S(1)}, bf16[2,2,512,256]{3,2,1,0:T(8,128)(2,1)S(1)}, u32[]{:S(2)}, u32[]{:S(2)}) %collective-permute-start.9) | collective-permute-done | bytes 1048608 | tf_op jit(solution)/shard_map/ppermute | solution.py:15
  60.0 1.3 %fusion = bf16[2,512,256]{2,1,0:T(8,128)(2,1)S(1)} fusion(f32[2,2,512,256]{3,2,1,0:T(8,128)} %get-tuple-element.28, bf16[2,2,512,256]{3,2,1,0:T(8,128)(2,1)S(1)} %collective-permute-done.9), kind=kLoop, calls=%fused_computation.2 | loop fusion | flops 786432 | bytes 2097152 | tf_op jit(solution)/shard_map/convert_element_type | solution.py:273
  61.9 1.2 %copy-done.1 = bf16[512,1024]{1,0:T(8,128)(2,1)S(1)} copy-done((bf16[512,1024]{1,0:T(8,128)(2,1)S(1)}, bf16[512,1024]{1,0:T(8,128)(2,1)}, u32[]{:S(2)}) %copy-start.1) | copy-done | bytes 1048600
  64.3 1.8 %shard_map.121 = (f32[3,352,256]{2,1,0:T(8,128)S(1)}, bf16[3,352,256]{2,1,0:T(8,128)(2,1)S(1)}, bf16[3,352,256]{2,1,0:T(8,128)(2,1)}, bf16[3,352,256]{2,1,0:T(8,128)(2,1)S(1)}) custom-call(bf16[3,352,512]{2,1,0:T(8,128)(2,1)S(1)} %copy-done, bf16[512,1024]{1,0:T(8,128)(2,1)S(1)} %copy-done.1, bf16[512,1024]{1,0:T(8,128)(2,1)S(1)} %copy-done.2), custom_call_target="tpu_custom_call" | custom-call | tf_op jit(solution)/shard_map/pallas_call | solution.py:178
  66.9 1.5 %collective-permute-start.15 = (bf16[3,352,256]{2,1,0:T(8,128)(2,1)}, bf16[3,352,256]{2,1,0:T(8,128)(2,1)S(1)}, u32[]{:S(2)}, u32[]{:S(2)}) collective-permute-start(bf16[3,352,256]{2,1,0:T(8,128)(2,1)} %get-tuple-element.35), channel_id=1, source_target_pairs={{0,8},{4,12},{8,0},{12,4},{16,24},{20,28},{24,16},{28,20},{1,9},{5... | collective-permute-start | bytes 1622024 | tf_op jit(solution)/shard_map/ppermute | solution.py:15
  69.6 5.7 %collective-permute-done.10 = bf16[2,512,256]{2,1,0:T(8,128)(2,1)S(1)} collective-permute-done((bf16[2,512,256]{2,1,0:T(8,128)(2,1)S(1)}, bf16[2,512,256]{2,1,0:T(8,128)(2,1)S(1)}, u32[]{:S(2)}, u32[]{:S(2)}) %collective-permute-start.10) | collective-permute-done | bytes 524320 | tf_op jit(solution)/shard_map/ppermute | solution.py:15
  77.7 3.3 %collective-permute-start.12 = (bf16[2,128,256]{2,1,0:T(8,128)(2,1)}, bf16[2,128,256]{2,1,0:T(8,128)(2,1)}, u32[]{:S(2)}, u32[]{:S(2)}) collective-permute-start(bf16[2,128,256]{2,1,0:T(8,128)(2,1)} %get-tuple-element.44), channel_id=1, source_target_pairs={{0,16},{4,20},{8,24},{12,28},{16,0},{20,4},{24,8},{28,12},{1,17},{... | collective-permute-start | bytes 393224 | tf_op jit(solution)/shard_map/ppermute | solution.py:15
  81.7 3.4 %collective-permute-start.13 = (bf16[2,128,256]{2,1,0:T(8,128)(2,1)S(1)}, bf16[2,128,256]{2,1,0:T(8,128)(2,1)}, u32[]{:S(2)}, u32[]{:S(2)}) collective-permute-start(bf16[2,128,256]{2,1,0:T(8,128)(2,1)S(1)} %get-tuple-element.43), channel_id=1, source_target_pairs={{0,20},{4,16},{8,28},{12,24},{16,4},{20,0},{24,12},{28,8},{1,21},{... | collective-permute-start | bytes 393224 | tf_op jit(solution)/shard_map/ppermute | solution.py:15
  85.2 1.4 %collective-permute-done.15.got_z = bf16[3,352,256]{2,1,0:T(8,128)(2,1)S(1)} collective-permute-done((bf16[3,352,256]{2,1,0:T(8,128)(2,1)}, bf16[3,352,256]{2,1,0:T(8,128)(2,1)S(1)}, u32[]{:S(2)}, u32[]{:S(2)}) %collective-permute-start.15) | collective-permute-done | bytes 540704 | tf_op jit(solution)/shard_map/ppermute | solution.py:15
  86.6 12.2 %collective-permute-done.16.got_d = bf16[3,352,256]{2,1,0:T(8,128)(2,1)S(1)} collective-permute-done((bf16[3,352,256]{2,1,0:T(8,128)(2,1)S(1)}, bf16[3,352,256]{2,1,0:T(8,128)(2,1)S(1)}, u32[]{:S(2)}, u32[]{:S(2)}) %collective-permute-start.16) | collective-permute-done | bytes 540704 | tf_op jit(solution)/shard_map/ppermute | solution.py:15
  98.8 1.5 %shard_map.122 = (f32[704,256]{1,0:T(8,128)}, f32[704,256]{1,0:T(8,128)}, f32[704,256]{1,0:T(8,128)}) custom-call(f32[3,352,256]{2,1,0:T(8,128)S(1)} %get-tuple-element.33.own, bf16[3,352,256]{2,1,0:T(8,128)(2,1)S(1)} %collective-permute-done.14.got_x, bf16[3,352,256]{2,1,0:T(8,128)(2,1)S(1)} %collective-permute-done.15.got_z, ...), custom_call_target="tpu_custom_call" | custom-call | tf_op jit(solution)/shard_map/pallas_call | solution.py:203
  102.0 1.6 %fusion.5 = (f32[128]{0:T(128)S(1)}, bf16[128,256]{1,0:T(8,128)(2,1)}) fusion(bf16[128,1024]{1,0:T(8,128)(2,1)} %cotangent.1, s32[]{:T(128)S(6)} %select_n.3, bf16[2,128,256]{2,1,0:T(8,128)(2,1)S(1)} %fusion.3, f32[128]{0:T(128)S(1)} %copy-done.9), kind=kLoop, calls=%fused_computation.11 | loop fusion | flops 196480 | bytes 197636 | tf_op jit(solution)/shard_map/reduce_sum | solution.py:291
  103.6 6.1 %psum.7 = f32[128]{0:T(128)} all-reduce(f32[128]{0:T(128)S(1)} %get-tuple-element.45), channel_id=1, replica_groups=mesh['wide'=8,'narrow'=4] {'narrow'}, use_global_device_ids=true, to_apply=%region_1.0 | all-reduce | flops 128 | bytes 1024 | tf_op jit(solution)/shard_map/psum | solution.py:291
  (47 shorter events, 16.7 us)
Async XLA Ops:
  4.1 14.0 %collective-permute-start.1 = (bf16[2,128,256]{2,1,0:T(8,128)(2,1)S(1)}, bf16[2,128,256]{2,1,0:T(8,128)(2,1)S(1)}, u32[]{:S(2)}, u32[]{:S(2)}) collective-permute-start(bf16[2,128,256]{2,1,0:T(8,128)(2,1)S(1)} %get-tuple-element.25), channel_id=1, source_target_pairs={{0,16},{4,20},{8,24},{12,28},{16,0},{20,4},{24,8},{28,12},{1,17},{... | collective-permute-start | bytes 393224 | tf_op jit(solution)/shard_map/ppermute | solution.py:15
  8.2 12.9 %collective-permute-start.2 = (bf16[2,128,256]{2,1,0:T(8,128)(2,1)S(1)}, bf16[2,128,256]{2,1,0:T(8,128)(2,1)S(1)}, u32[]{:S(2)}, u32[]{:S(2)}) collective-permute-start(bf16[2,128,256]{2,1,0:T(8,128)(2,1)S(1)} %get-tuple-element.25), channel_id=1, source_target_pairs={{0,20},{4,16},{8,28},{12,24},{16,4},{20,0},{24,12},{28,8},{1,21},{... | collective-permute-start | bytes 393224 | tf_op jit(solution)/shard_map/ppermute | solution.py:15
  9.5 11.6 %collective-permute-start = (bf16[2,128,256]{2,1,0:T(8,128)(2,1)S(1)}, bf16[2,128,256]{2,1,0:T(8,128)(2,1)S(1)}, u32[]{:S(2)}, u32[]{:S(2)}) collective-permute-start(bf16[2,128,256]{2,1,0:T(8,128)(2,1)S(1)} %get-tuple-element.24), channel_id=1, source_target_pairs={{0,4},{4,0},{8,12},{12,8},{16,20},{20,16},{24,28},{28,24},{1,5},{5... | collective-permute-start | bytes 393224 | tf_op jit(solution)/shard_map/ppermute | solution.py:15
  21.2 10.1 %collective-permute-start.4 = (bf16[3,2,128,256]{3,2,1,0:T(8,128)(2,1)S(1)}, bf16[3,2,128,256]{3,2,1,0:T(8,128)(2,1)S(1)}, u32[]{:S(2)}, u32[]{:S(2)}) collective-permute-start(bf16[3,2,128,256]{3,2,1,0:T(8,128)(2,1)S(1)} %pad_maximum_fusion.refs_1_), channel_id=1, source_target_pairs={{0,2},{1,3},{2,0},{3,1},{4,6},{5,7},{6,4},{7,5},{8,10},{9,11},{10,... | collective-permute-start | bytes 1179656 | tf_op jit(solution)/shard_map/ppermute | solution.py:15
  23.7 1.0 copy-start.5
  24.7 1.0 copy-start.6
  25.8 14.4 %collective-permute-start.6 = (bf16[3,352,256]{2,1,0:T(8,128)(2,1)S(1)}, bf16[3,352,256]{2,1,0:T(8,128)(2,1)S(1)}, u32[]{:S(2)}, u32[]{:S(2)}) collective-permute-start(bf16[3,352,256]{2,1,0:T(8,128)(2,1)S(1)} %get-tuple-element.27), channel_id=1, source_target_pairs={{0,4},{4,0},{8,12},{12,8},{16,20},{20,16},{24,28},{28,24},{1,5},{5... | collective-permute-start | bytes 1622024 | tf_op jit(solution)/shard_map/ppermute | solution.py:15
  26.4 15.2 %collective-permute-start.7 = (bf16[3,352,256]{2,1,0:T(8,128)(2,1)S(1)}, bf16[3,352,256]{2,1,0:T(8,128)(2,1)S(1)}, u32[]{:S(2)}, u32[]{:S(2)}) collective-permute-start(bf16[3,352,256]{2,1,0:T(8,128)(2,1)S(1)} %get-tuple-element.26.refs_5_), channel_id=1, source_target_pairs={{0,8},{4,12},{8,0},{12,4},{16,24},{20,28},{24,16},{28,20},{1,9},{5... | collective-permute-start | bytes 1622024 | tf_op jit(solution)/shard_map/ppermute | solution.py:15
  27.1 24.4 %collective-permute-start.8 = (bf16[3,352,256]{2,1,0:T(8,128)(2,1)S(1)}, bf16[3,352,256]{2,1,0:T(8,128)(2,1)S(1)}, u32[]{:S(2)}, u32[]{:S(2)}) collective-permute-start(bf16[3,352,256]{2,1,0:T(8,128)(2,1)S(1)} %get-tuple-element.27), channel_id=1, source_target_pairs={{0,12},{4,8},{8,4},{12,0},{16,28},{20,24},{24,20},{28,16},{1,13},{... | collective-permute-start | bytes 1622024 | tf_op jit(solution)/shard_map/ppermute | solution.py:15
  29.3 1.9 %collective-permute-start.3 = (bf16[3,2,128,256]{3,2,1,0:T(8,128)(2,1)S(1)}, bf16[3,2,128,256]{3,2,1,0:T(8,128)(2,1)S(1)}, u32[]{:S(2)}, u32[]{:S(2)}) collective-permute-start(bf16[3,2,128,256]{3,2,1,0:T(8,128)(2,1)S(1)} %pad_maximum_fusion.refs_1_), channel_id=1, source_target_pairs={{0,1},{1,0},{2,3},{3,2},{4,5},{5,4},{6,7},{7,6},{8,9},{9,8},{10,11... | collective-permute-start | bytes 1179656 | tf_op jit(solution)/shard_map/ppermute | solution.py:15
  31.2 20.3 %collective-permute-start.5 = (bf16[3,2,128,256]{3,2,1,0:T(8,128)(2,1)S(1)}, bf16[3,2,128,256]{3,2,1,0:T(8,128)(2,1)S(1)}, u32[]{:S(2)}, u32[]{:S(2)}) collective-permute-start(bf16[3,2,128,256]{3,2,1,0:T(8,128)(2,1)S(1)} %collective-permute-done.4.refs_3_), channel_id=1, source_target_pairs={{0,1},{1,0},{2,3},{3,2},{4,5},{5,4},{6,7},{7,6},{8,9},{9,8},{10,11... | collective-permute-start | bytes 1179656 | tf_op jit(solution)/shard_map/ppermute | solution.py:15
  57.3 4.6 %copy-start = (bf16[3,352,512]{2,1,0:T(8,128)(2,1)S(1)}, bf16[3,352,512]{2,1,0:T(8,128)(2,1)}, u32[]{:S(2)}) copy-start(bf16[3,352,512]{2,1,0:T(8,128)(2,1)} %get-tuple-element.30.grads) | copy-start | bytes 3244036
  57.3 2.7 %collective-permute-start.9 = (bf16[2,2,512,256]{3,2,1,0:T(8,128)(2,1)S(1)}, bf16[2,2,512,256]{3,2,1,0:T(8,128)(2,1)S(1)}, u32[]{:S(2)}, u32[]{:S(2)}) collective-permute-start(bf16[2,2,512,256]{3,2,1,0:T(8,128)(2,1)S(1)} %get-tuple-element.29), channel_id=1, source_target_pairs={{0,1},{1,0},{2,3},{3,2},{4,5},{5,4},{6,7},{7,6},{8,9},{9,8},{10,11... | collective-permute-start | bytes 3145736 | tf_op jit(solution)/shard_map/ppermute | solution.py:15
  61.3 14.0 %collective-permute-start.10 = (bf16[2,512,256]{2,1,0:T(8,128)(2,1)S(1)}, bf16[2,512,256]{2,1,0:T(8,128)(2,1)S(1)}, u32[]{:S(2)}, u32[]{:S(2)}) collective-permute-start(bf16[2,512,256]{2,1,0:T(8,128)(2,1)S(1)} %fusion), channel_id=1, source_target_pairs={{0,2},{1,3},{2,0},{3,1},{4,6},{5,7},{6,4},{7,5},{8,10},{9,11},{10,... | collective-permute-start | bytes 1572872 | tf_op jit(solution)/shard_map/ppermute | solution.py:15
  61.9 1.2 %copy-start.1 = (bf16[512,1024]{1,0:T(8,128)(2,1)S(1)}, bf16[512,1024]{1,0:T(8,128)(2,1)}, u32[]{:S(2)}) copy-start(bf16[512,1024]{1,0:T(8,128)(2,1)} %get-tuple-element.31.x_all) | copy-start | bytes 3145732
  63.1 1.2 %copy-start.2 = (bf16[512,1024]{1,0:T(8,128)(2,1)S(1)}, bf16[512,1024]{1,0:T(8,128)(2,1)}, u32[]{:S(2)}) copy-start(bf16[512,1024]{1,0:T(8,128)(2,1)} %get-tuple-element.32.s_all) | copy-start | bytes 3145732
  64.3 11.0 %copy-start.11 = (f32[2,2,512,256]{3,2,1,0:T(8,128)S(1)}, f32[2,2,512,256]{3,2,1,0:T(8,128)}, u32[]{:S(2)}) copy-start(f32[2,2,512,256]{3,2,1,0:T(8,128)} %get-tuple-element.28) | copy-start | bytes 6291460
  66.1 15.6 %collective-permute-start.14 = (bf16[3,352,256]{2,1,0:T(8,128)(2,1)S(1)}, bf16[3,352,256]{2,1,0:T(8,128)(2,1)S(1)}, u32[]{:S(2)}, u32[]{:S(2)}) collective-permute-start(bf16[3,352,256]{2,1,0:T(8,128)(2,1)S(1)} %get-tuple-element.34), channel_id=1, source_target_pairs={{0,4},{4,0},{8,12},{12,8},{16,20},{20,16},{24,28},{28,24},{1,5},{5... | collective-permute-start | bytes 1622024 | tf_op jit(solution)/shard_map/ppermute | solution.py:15
  66.9 19.6 %collective-permute-start.15 = (bf16[3,352,256]{2,1,0:T(8,128)(2,1)}, bf16[3,352,256]{2,1,0:T(8,128)(2,1)S(1)}, u32[]{:S(2)}, u32[]{:S(2)}) collective-permute-start(bf16[3,352,256]{2,1,0:T(8,128)(2,1)} %get-tuple-element.35), channel_id=1, source_target_pairs={{0,8},{4,12},{8,0},{12,4},{16,24},{20,28},{24,16},{28,20},{1,9},{5... | collective-permute-start | bytes 1622024 | tf_op jit(solution)/shard_map/ppermute | solution.py:15
  68.4 30.3 %collective-permute-start.16 = (bf16[3,352,256]{2,1,0:T(8,128)(2,1)S(1)}, bf16[3,352,256]{2,1,0:T(8,128)(2,1)S(1)}, u32[]{:S(2)}, u32[]{:S(2)}) collective-permute-start(bf16[3,352,256]{2,1,0:T(8,128)(2,1)S(1)} %get-tuple-element.36), channel_id=1, source_target_pairs={{0,12},{4,8},{8,4},{12,0},{16,28},{20,24},{24,20},{28,16},{1,13},{... | collective-permute-start | bytes 1622024 | tf_op jit(solution)/shard_map/ppermute | solution.py:15
  76.5 25.5 %copy-start.9 = (f32[128]{0:T(128)S(1)}, f32[128]{0:T(128)}, u32[]{:S(2)}) copy-start(f32[128]{0:T(128)} %param.10) | copy-start | bytes 1540
  77.2 23.0 %collective-permute-start.11 = (bf16[2,128,256]{2,1,0:T(8,128)(2,1)}, bf16[2,128,256]{2,1,0:T(8,128)(2,1)S(1)}, u32[]{:S(2)}, u32[]{:S(2)}) collective-permute-start(bf16[2,128,256]{2,1,0:T(8,128)(2,1)} %get-tuple-element.42), channel_id=1, source_target_pairs={{0,4},{4,0},{8,12},{12,8},{16,20},{20,16},{24,28},{28,24},{1,5},{5... | collective-permute-start | bytes 393224 | tf_op jit(solution)/shard_map/ppermute | solution.py:15
  77.7 22.5 %collective-permute-start.12 = (bf16[2,128,256]{2,1,0:T(8,128)(2,1)}, bf16[2,128,256]{2,1,0:T(8,128)(2,1)}, u32[]{:S(2)}, u32[]{:S(2)}) collective-permute-start(bf16[2,128,256]{2,1,0:T(8,128)(2,1)} %get-tuple-element.44), channel_id=1, source_target_pairs={{0,16},{4,20},{8,24},{12,28},{16,0},{20,4},{24,8},{28,12},{1,17},{... | collective-permute-start | bytes 393224 | tf_op jit(solution)/shard_map/ppermute | solution.py:15
  81.7 18.5 %collective-permute-start.13 = (bf16[2,128,256]{2,1,0:T(8,128)(2,1)S(1)}, bf16[2,128,256]{2,1,0:T(8,128)(2,1)}, u32[]{:S(2)}, u32[]{:S(2)}) collective-permute-start(bf16[2,128,256]{2,1,0:T(8,128)(2,1)S(1)} %get-tuple-element.43), channel_id=1, source_target_pairs={{0,20},{4,16},{8,28},{12,24},{16,4},{20,0},{24,12},{28,8},{1,21},{... | collective-permute-start | bytes 393224 | tf_op jit(solution)/shard_map/ppermute | solution.py:15
  (5 other events, 4.2 us)

commit v2 on v1

v2 whole, which is shorter than its diff:
```python
import functools

import jax
import jax.numpy as jnp
from jax import lax
from jax.experimental import pallas as pl
from jax.experimental.pallas import tpu as pltpu
from jax.sharding import PartitionSpec as P

VMEM = pl.BlockSpec(memory_space=pltpu.VMEM)
HBM = pl.BlockSpec(memory_space=pltpu.HBM)
PARAMS = pltpu.CompilerParams(vmem_limit_bytes=32 * 1024 * 1024)
PROLOGUE_PARAMS = pltpu.CompilerParams(vmem_limit_bytes=61 * 1024 * 1024)


def partner(x, axis, mask):
    return lax.ppermute(x, axis, [(i, i ^ mask) for i in range(lax.axis_size(axis))])


def dot_nn(left, right):
    return lax.dot_general(
        left, right, (((1,), (0,)), ((), ())), preferred_element_type=jnp.float32
    )


def dot_nt(left, right):
    return lax.dot_general(
        left, right, (((1,), (1,)), ((), ())), preferred_element_type=jnp.float32
    )


def at_quarter(index, width):
    return pl.ds(pl.multiple_of(index * width, width), width)


def prologue_kernel(routed, gate, up, down, *refs):
    if routed:
        tokens, cotangent, ids, prob, keep, give, own, same, other = refs[:9]
        held, ids_row, prob_row, sems = refs[9:]
        parts = ((tokens, held.at[0]), (cotangent, held.at[1]), (ids, ids_row), (prob, prob_row))
    else:
        keep, give, sems = refs
        parts = ()
    half = keep.shape[1]
    x_bit = lax.axis_index("wide") % 2
    keep_rows = pl.ds(pl.multiple_of(x_bit * half, 16), half)
    give_rows = pl.ds(pl.multiple_of((1 - x_bit) * half, 16), half)
    for i, ref in enumerate((gate, up, down)):
        parts += ((ref.at[keep_rows, :], keep.at[i]), (ref.at[give_rows, :], give.at[i]))
    copies = [pltpu.make_async_copy(src, dst, sems.at[i]) for i, (src, dst) in enumerate(parts)]
    for copy in copies:
        copy.start()
    if routed:
        for copy in copies[:4]:
            copy.wait()
        rows = held.shape[1]
        width = same.shape[2]
        mine = lax.axis_index("wide") // 4
        column = at_quarter(lax.axis_index("narrow"), width)
        chosen = jnp.broadcast_to(ids_row[...], (128, rows)).astype(jnp.float32).T[:, :1]
        weight = jnp.broadcast_to(prob_row[...], (128, rows)).T[:, :1]
        here = jnp.where(chosen == mine.astype(jnp.float32), 1.0, 0.0)
        for i in range(2):
            factor = weight if i else jnp.ones_like(weight)
            own[i] = (held[i].astype(jnp.float32) * (factor * here)).astype(jnp.bfloat16)
            part = held[i, :, column].astype(jnp.float32)
            same[i] = (part * (factor * here)).astype(jnp.bfloat16)
            other[i] = (part * (factor * (1.0 - here))).astype(jnp.bfloat16)
    for copy in copies[len(copies) - 6 :]:
        copy.wait()


def prologue(weights, token_args, width):
    hidden, quarter = weights[0].shape
    half = jax.ShapeDtypeStruct((3, hidden // 2, quarter), jnp.bfloat16)
    outs, scratch = (half, half), []
    if token_args:
        rows, features = token_args[0].shape
        part = jax.ShapeDtypeStruct((2, rows, width), jnp.bfloat16)
        outs += (jax.ShapeDtypeStruct((2, rows, features), jnp.bfloat16), part, part)
        scratch = [
            pltpu.VMEM((2, rows, features), jnp.bfloat16),
            pltpu.VMEM((1, rows), jnp.int32),
            pltpu.VMEM((1, rows), jnp.float32),
        ]
    return pl.pallas_call(
        functools.partial(prologue_kernel, bool(token_args)),
        out_shape=outs,
        in_specs=[HBM] * (3 + len(token_args)),
        out_specs=[VMEM] * len(outs),
        scratch_shapes=scratch + [pltpu.SemaphoreType.DMA((10,))],
        compiler_params=PROLOGUE_PARAMS,
    )(*weights, *token_args)


def gather_kernel(has_own, *refs):
    own = refs[0] if has_own else None
    pieces, weights = refs[has_own : has_own + 4], refs[has_own + 4 : has_own + 7]
    x_all, s_all, w_all, part = refs[has_own + 7 :]
    blocks, _, slots, width = pieces[0].shape
    member = lax.axis_index("wide") % 4
    place = lax.axis_index("narrow")
    for k, ref in enumerate(weights):
        column = at_quarter(member ^ k, width)
        for i in range(3):
            w_all[i, :, column] = ref[i]
    first = 0
    if has_own:
        x_all[:slots, :] = own[0]
        s_all[:slots, :] = own[1]
        first = slots
    for mask, ref in enumerate(pieces):
        column = at_quarter(place ^ mask, width)
        for block in range(blocks):
            rows = slice(first + block * slots, first + (block + 1) * slots)
            x_all[rows, column] = ref[block, 0]
            s_all[rows, column] = ref[block, 1]
    total = x_all.shape[0]
    tile = min(256, total)

    @pl.loop(0, total // tile)
    def _(step):
        rows = pl.ds(pl.multiple_of(step * tile, tile), tile)
        for i in range(3):
            held = s_all if i == 2 else x_all
            sums = None
            for k in range(3):
                column = at_quarter(member ^ k, width)
                term = dot_nt(w_all[i, :, column], held[rows, column])
                sums = term if sums is None else sums + term
            part[i, :, rows] = sums


def gather_parts(own, pieces, weights):
    blocks, _, slots, width = pieces[0].shape
    half = weights[0].shape[1]
    has_own = own is not None
    total = (blocks + has_own) * slots
    features = 4 * width
    return pl.pallas_call(
        functools.partial(gather_kernel, int(has_own)),
        out_shape=(
            jax.ShapeDtypeStruct((total, features), jnp.bfloat16),
            jax.ShapeDtypeStruct((total, features), jnp.bfloat16),
            jax.ShapeDtypeStruct((3, half, features), jnp.bfloat16),
            jax.ShapeDtypeStruct((3, half, total), jnp.float32),
        ),
        in_specs=[VMEM] * (7 + has_own),
        out_specs=[VMEM] * 4,
        compiler_params=PARAMS,
        cost_estimate=pl.CostEstimate(
            flops=6 * 2 * half * 3 * width * total, bytes_accessed=0, transcendentals=0
        ),
    )(*([own] if has_own else []), *pieces, *weights)


def main_kernel(x_all, s_all, w_part, part, last, kept, sent, own, to_x, to_z, to_d, grads, w_all):
    outs = (own, to_x, to_z, to_d)
    half, width = last.shape[1:]
    member = lax.axis_index("wide") % 4
    place = lax.axis_index("narrow")
    last_column = at_quarter(member ^ 3, width)
    w_all[...] = w_part[...]
    for i in range(3):
        w_all[i, :, last_column] = last[i]
    total = x_all.shape[0]
    tile = min(256, total)

    @pl.loop(0, total // tile)
    def _(step):
        rows = pl.ds(pl.multiple_of(step * tile, tile), tile)
        x_tile, s_tile = x_all[rows, last_column], s_all[rows, last_column]
        gate = part[0, :, rows] + dot_nt(last[0], x_tile)
        up = part[1, :, rows] + dot_nt(last[1], x_tile)
        d_hidden = part[2, :, rows] + dot_nt(last[2], s_tile)
        sigma = jax.nn.sigmoid(gate)
        active = gate * sigma
        hidden = (active * up).astype(jnp.bfloat16)
        d_gate = (d_hidden * up * sigma * (1.0 + gate * (1.0 - sigma))).astype(jnp.bfloat16)
        d_up = (d_hidden * active).astype(jnp.bfloat16)
        grads[0, :, rows] = d_gate
        grads[1, :, rows] = d_up
        grads[2, :, rows] = hidden
        hidden_t, d_gate_t, d_up_t = hidden.T, d_gate.T, d_up.T
        for mask in range(4):
            column = at_quarter(place ^ mask, width)
            out_part = dot_nn(hidden_t, w_all[2, :, column])
            in_part = dot_nn(d_gate_t, w_all[0, :, column]) + dot_nn(d_up_t, w_all[1, :, column])
            target = sent if mask % 2 else kept
            target[mask // 2, 0, rows, :] = out_part.astype(target.dtype)
            target[mask // 2, 1, rows, :] = in_part.astype(target.dtype)

    left = grads[0:2].reshape(2 * half, total)
    for k in (3, 2, 1, 0):
        column = at_quarter(member ^ k, width)
        both = dot_nn(left, x_all[:, column])
        outs[k][0] = both[:half].astype(outs[k].dtype)
        outs[k][1] = both[half:].astype(outs[k].dtype)
        outs[k][2] = dot_nn(grads[2], s_all[:, column]).astype(outs[k].dtype)


def main(x_all, s_all, w_part, part, last):
    total, features = x_all.shape
    _, half, width = last.shape
    return pl.pallas_call(
        main_kernel,
        out_shape=(
            jax.ShapeDtypeStruct((2, 2, total, width), jnp.float32),
            jax.ShapeDtypeStruct((2, 2, total, width), jnp.bfloat16),
        )
        + tuple(
            jax.ShapeDtypeStruct((3, half, width), jnp.bfloat16 if k > 1 else jnp.float32)
            for k in range(4)
        ),
        in_specs=[VMEM] * 5,
        out_specs=[VMEM] * 6,
        scratch_shapes=[
            pltpu.VMEM((3, half, total), jnp.bfloat16),
            pltpu.VMEM((3, half, features), jnp.bfloat16),
        ],
        compiler_params=PARAMS,
        cost_estimate=pl.CostEstimate(
            flops=12 * 2 * half * features * total, bytes_accessed=0, transcendentals=0
        ),
    )(x_all, s_all, w_part, part, last)


def join_kernel(own, got_x, got_z, *outs):
    half = own.shape[1]
    x_bit = lax.axis_index("wide") % 2
    keep_rows = pl.ds(pl.multiple_of(x_bit * half, 16), half)
    give_rows = pl.ds(pl.multiple_of((1 - x_bit) * half, 16), half)
    for i, ref in enumerate(outs):
        ref[keep_rows, :] = own[i] + got_z[i].astype(jnp.float32)
        ref[give_rows, :] = got_x[i].astype(jnp.float32)


def join_grads(own, got_x, got_z):
    _, half, width = own.shape
    shape = jax.ShapeDtypeStruct((2 * half, width), jnp.float32)
    return pl.pallas_call(
        join_kernel,
        out_shape=(shape,) * 3,
        in_specs=[VMEM] * 3,
        out_specs=[VMEM] * 3,
        compiler_params=PARAMS,
    )(own, got_x, got_z)


def shards(tokens, cotangent, expert_ids, route_prob, gate_weight, up_weight, down_weight):
    wide_count = lax.axis_size("wide")
    narrow_count = lax.axis_size("narrow")
    expert_count = wide_count // 4
    tok_rows, features = tokens.shape
    width = features // narrow_count
    slots = min(4 * tok_rows // expert_count, tok_rows)
    direct = expert_count == 2 and slots == tok_rows
    place = lax.axis_index("narrow")
    masks = (1, 4, 5)
    groups = [
        [4 * e + 2 * b + a for e in range(expert_count) for a in range(2)] for b in range(2)
    ]

    weights = (gate_weight.T, up_weight.T, down_weight.T)
    if direct:
        keep, give, own, same, other = prologue(
            weights, (tokens, cotangent, expert_ids.T, route_prob[None, :]), width
        )
        mine = jnp.stack(
            [partner(part, "wide", mask) for mask, part in zip(masks, (same, other, other))]
        )
    else:
        own = None
        keep, give = prologue(weights, (), width)
        chosen = expert_ids[:, 0]
        onehot = (chosen[:, None] == jnp.arange(expert_count, dtype=jnp.int32)[None, :]).astype(
            jnp.int32
        )
        rank = jnp.sum((jnp.cumsum(onehot, axis=0) - onehot) * onehot, axis=1)
        slot_place = chosen * slots + rank
        source = (
            jnp.full((expert_count * slots,), tok_rows, jnp.int32)
            .at[slot_place]
            .set(jnp.arange(tok_rows, dtype=jnp.int32))
        )
        scaled = (route_prob[:, None] * cotangent.astype(jnp.float32)).astype(jnp.bfloat16)
        both = jnp.stack([tokens, scaled])
        both = lax.dynamic_slice_in_dim(both, place * width, width, 2)
        both = jnp.concatenate([both, jnp.zeros((2, 1, width), jnp.bfloat16)], 1)
        routed = both[:, source].reshape(2, expert_count, slots, width).transpose(1, 0, 2, 3)
        routed = jnp.repeat(routed, 2, axis=0)
        mine = lax.all_to_all(
            routed, "wide", split_axis=0, concat_axis=0, axis_index_groups=groups, tiled=True
        )

    from_x = partner(give, "wide", 1)
    from_z = partner(keep, "wide", 2)
    from_d = partner(from_x, "wide", 2)
    across = partner(mine, "narrow", 2)
    pieces = (mine, partner(mine, "narrow", 1), across, partner(across, "narrow", 1))
    held = gather_parts(own, pieces, (keep, from_x, from_z))
    kept, sent, grad_own, grad_x, grad_z, grad_d = main(*held, from_d)

    got = partner(sent, "narrow", 1)
    got_d = partner(grad_d, "wide", 2)
    grad_x = (grad_x + got_d.astype(jnp.float32)).astype(jnp.bfloat16)
    grad_x, grad_z = lax.optimization_barrier((grad_x, grad_z))
    got_x = partner(grad_x, "wide", 1)
    got_z = partner(grad_z, "wide", 2)

    across = partner((kept[1] + got[1].astype(jnp.float32)).astype(jnp.bfloat16), "narrow", 2)
    result = kept[0] + got[0].astype(jnp.float32) + across.astype(jnp.float32)
    if direct:
        total = result[:, :slots]
        for k, mask in enumerate(masks):
            rows = result[:, (k + 1) * slots : (k + 2) * slots].astype(jnp.bfloat16)
            total = total + partner(rows, "wide", mask).astype(jnp.float32)
    else:
        parts = result.astype(jnp.bfloat16).reshape(2, 2 * expert_count, slots, width)
        back = lax.all_to_all(
            parts, "wide", split_axis=1, concat_axis=1, axis_index_groups=groups, tiled=True
        )
        back = back.reshape(2, expert_count, 2, slots, width).astype(jnp.float32).sum(2)
        total = back.reshape(2, expert_count * slots, width)[:, slot_place]
    ffn = total[0].astype(jnp.bfloat16).astype(jnp.float32)
    tokens_grad = total[1].astype(jnp.bfloat16)
    output = (route_prob[:, None] * ffn).astype(jnp.bfloat16)
    cot_columns = lax.dynamic_slice_in_dim(cotangent, place * width, width, 1)
    prob_grad = lax.psum(jnp.sum(ffn * cot_columns.astype(jnp.float32), axis=1), "narrow")
    gate_grad, up_grad, down_grad = join_grads(grad_own, got_x, got_z)
    return (output, tokens_grad, prob_grad, gate_grad.T, up_grad.T, down_grad.T)


def solution(mesh):
    in_specs = (
        P("wide", None),
        P("wide", None),
        P("wide", None),
        P("wide"),
        P("wide", "narrow"),
        P("wide", "narrow"),
        P("wide", "narrow"),
    )
    out_specs = (
        P("wide", "narrow"),
        P("wide", "narrow"),
        P("wide"),
        P("wide", "narrow"),
        P("wide", "narrow"),
        P("wide", "narrow"),
    )
    return jax.shard_map(shards, mesh=mesh, in_specs=in_specs, out_specs=out_specs, check_vma=False)
```

time: 110 us -> 97.5 us (0.89)
  local copies, waits for them, and re-layouts: 9.99 us -> 3.45 us
  starting transfers between devices: 22.1 us -> 18.6 us
  waiting for transfers between devices: 56.2 us -> 53.6 us
  other arithmetic: 5.23 us -> 4.11 us
    unnamed x24 -> x6, local copies, waits for them, and re-layouts: 8.62 us -> 2.09 us
    ppermute x17, starting transfers between devices: 22.1 us -> 18.6 us  [partner(): lax.ppermute(x, axis, [(i, i ^ mask) for i in range(lax.axis_size(axis))])]
    ppermute x17, waiting for transfers between devices: 56.2 us -> 53.6 us  [partner(): lax.ppermute(x, axis, [(i, i ^ mask) for i in range(lax.axis_size(axis))])]
    convert_element_type x1, other arithmetic: 1.34 us -> 0.12 us  [shards(): (kept[1] + got[1].astype(jnp.float32)).astype(jnp.bfloat16)]
    pallas_call x5 -> x4, Pallas kernels: 9.41 us -> 10.5 us  [the longest x1 4.59 us: main(): pl.pallas_call(main_kernel, out_shape=(jax.ShapeDtypeStruct((2, 2, total,...]
  transfers between devices with their start and end apart: 17 -> 17, of which waited for: 11 -> 9; matrix products, arithmetic and copies ran while one was open for 2% -> 2% of each run, Pallas kernels for 3% -> 3%
where the time goes in v2:
time: 97.5 us; the launch traced here: 97.2 us
  waiting for transfers between devices  53.6 us (55%)
  starting transfers between devices  18.6 us (19%)
  Pallas kernels  10.5 us (11%)
  blocking collectives  6.13 us (6%)
  other arithmetic  4.11 us (4%)
  local copies, waits for them, and re-layouts  3.45 us (4%)
    ppermute x17, waiting for transfers between devices, partner(): lax.ppermute(x, axis, [(i, i ^ mask) for i in range(lax.axis_size(axis))])  53.6 us
    ppermute x17, starting transfers between devices, partner(): lax.ppermute(x, axis, [(i, i ^ mask) for i in range(lax.axis_size(axis))])  18.6 us
    psum x1, blocking collectives, shards(): lax.psum(jnp.sum(ffn * cot_columns.astype(jnp.float32), axis=1), 'narrow')  6.13 us
    pallas_call x1, Pallas kernels, main(): pl.pallas_call(main_kernel, out_shape=(jax.ShapeDtypeStruct((2, 2, total,...  4.59 us
    pallas_call x1, Pallas kernels, prologue(): pl.pallas_call(functools.partial(prologue_kernel, bool(token_args)), out_...  2.7 us
    another operation x2, other arithmetic  2.26 us
    unnamed x6, local copies, waits for them, and re-layouts  2.09 us
  transfers between devices with their start and end apart: 17, of which 9 were waited for; matrix products, arithmetic and copies ran while one was open for 2% of the time, Pallas kernels for 3%

profile of v2, /device:TPU:0, one launch (start us, length us, event | category | flops | bytes accessed | tf_op | source)
XLA Modules:
  0.0 97.2 jit_solution(1944331980815947413)
XLA Ops:
  0.6 2.7 %shard_map.118 = (bf16[3,352,256]{2,1,0:T(8,128)(2,1)}, bf16[3,352,256]{2,1,0:T(8,128)(2,1)}, bf16[2,128,1024]{2,1,0:T(8,128)(2,1)}, bf16[2,128,256]{2,1,0:T(8,128)(2,1)}, bf16[2,128,256]{2,1,0:T(8,128)(2,1)}) custom-call(bf16[704,256]{1,0:T(8,128)(2,1)} %bitcast.25, bf16[704,256]{1,0:T(8,128)(2,1)} %bitcast.26, bf16[704,256]{1,0:T(8,128)(2,1)} %bitcast.27, ...), custom_call_target="tpu_custom_call" | custom-call | tf_op jit(solution)/shard_map/pallas_call | solution.py:86
  3.3 4.1 %collective-permute-start.1 = (bf16[2,128,256]{2,1,0:T(8,128)(2,1)}, bf16[2,128,256]{2,1,0:T(8,128)(2,1)S(1)}, u32[]{:S(2)}, u32[]{:S(2)}) collective-permute-start(bf16[2,128,256]{2,1,0:T(8,128)(2,1)} %get-tuple-element.28), channel_id=1, source_target_pairs={{0,16},{4,20},{8,24},{12,28},{16,0},{20,4},{24,8},{28,12},{1,17},{... | collective-permute-start | bytes 393224 | tf_op jit(solution)/shard_map/ppermute | solution.py:17
  7.4 1.3 %collective-permute-start.2 = (bf16[2,128,256]{2,1,0:T(8,128)(2,1)}, bf16[2,128,256]{2,1,0:T(8,128)(2,1)S(1)}, u32[]{:S(2)}, u32[]{:S(2)}) collective-permute-start(bf16[2,128,256]{2,1,0:T(8,128)(2,1)} %get-tuple-element.28), channel_id=1, source_target_pairs={{0,20},{4,16},{8,28},{12,24},{16,4},{20,0},{24,12},{28,8},{1,21},{... | collective-permute-start | bytes 393224 | tf_op jit(solution)/shard_map/ppermute | solution.py:17
  9.0 1.7 %collective-permute-start.6 = (bf16[3,352,256]{2,1,0:T(8,128)(2,1)}, bf16[3,352,256]{2,1,0:T(8,128)(2,1)S(1)}, u32[]{:S(2)}, u32[]{:S(2)}) collective-permute-start(bf16[3,352,256]{2,1,0:T(8,128)(2,1)} %get-tuple-element.30), channel_id=1, source_target_pairs={{0,4},{4,0},{8,12},{12,8},{16,20},{20,16},{24,28},{28,24},{1,5},{5... | collective-permute-start | bytes 1622024 | tf_op jit(solution)/shard_map/ppermute | solution.py:17
  10.7 6.9 %collective-permute-done.1 = bf16[2,128,256]{2,1,0:T(8,128)(2,1)S(1)} collective-permute-done((bf16[2,128,256]{2,1,0:T(8,128)(2,1)}, bf16[2,128,256]{2,1,0:T(8,128)(2,1)S(1)}, u32[]{:S(2)}, u32[]{:S(2)}) %collective-permute-start.1) | collective-permute-done | bytes 131104 | tf_op jit(solution)/shard_map/ppermute | solution.py:17
  17.6 3.1 %collective-permute-done.2 = bf16[2,128,256]{2,1,0:T(8,128)(2,1)S(1)} collective-permute-done((bf16[2,128,256]{2,1,0:T(8,128)(2,1)}, bf16[2,128,256]{2,1,0:T(8,128)(2,1)S(1)}, u32[]{:S(2)}, u32[]{:S(2)}) %collective-permute-start.2) | collective-permute-done | bytes 131104 | tf_op jit(solution)/shard_map/ppermute | solution.py:17
  20.7 1.6 %collective-permute-start.4 = (bf16[3,2,128,256]{3,2,1,0:T(8,128)(2,1)S(1)}, bf16[3,2,128,256]{3,2,1,0:T(8,128)(2,1)S(1)}, u32[]{:S(2)}, u32[]{:S(2)}) collective-permute-start(bf16[3,2,128,256]{3,2,1,0:T(8,128)(2,1)S(1)} %pad_maximum_fusion.refs_1_), channel_id=1, source_target_pairs={{0,2},{1,3},{2,0},{3,1},{4,6},{5,7},{6,4},{7,5},{8,10},{9,11},{10,... | collective-permute-start | bytes 1179656 | tf_op jit(solution)/shard_map/ppermute | solution.py:17
  22.3 8.4 %collective-permute-done.4.refs_3_ = bf16[3,2,128,256]{3,2,1,0:T(8,128)(2,1)S(1)} collective-permute-done((bf16[3,2,128,256]{3,2,1,0:T(8,128)(2,1)S(1)}, bf16[3,2,128,256]{3,2,1,0:T(8,128)(2,1)S(1)}, u32[]{:S(2)}, u32[]{:S(2)}) %collective-permute-start.4) | collective-permute-done | bytes 393248 | tf_op jit(solution)/shard_map/ppermute | solution.py:17
  31.6 5.1 %collective-permute-done.7.refs_7_ = bf16[3,352,256]{2,1,0:T(8,128)(2,1)S(1)} collective-permute-done((bf16[3,352,256]{2,1,0:T(8,128)(2,1)}, bf16[3,352,256]{2,1,0:T(8,128)(2,1)S(1)}, u32[]{:S(2)}, u32[]{:S(2)}) %collective-permute-start.7) | collective-permute-done | bytes 540704 | tf_op jit(solution)/shard_map/ppermute | solution.py:17
  36.7 1.0 %copy-done = bf16[3,352,256]{2,1,0:T(8,128)(2,1)S(1)} copy-done((bf16[3,352,256]{2,1,0:T(8,128)(2,1)S(1)}, bf16[3,352,256]{2,1,0:T(8,128)(2,1)}, u32[]{:S(2)}) %copy-start) | copy-done | bytes 540696
  38.8 1.7 %shard_map.119 = (bf16[512,1024]{1,0:T(8,128)(2,1)S(1)}, bf16[512,1024]{1,0:T(8,128)(2,1)S(1)}, bf16[3,352,1024]{2,1,0:T(8,128)(2,1)S(1)}, f32[3,352,512]{2,1,0:T(8,128)S(1)}) custom-call(bf16[2,128,1024]{2,1,0:T(8,128)(2,1)S(1)} %copy-done.1, bf16[3,2,128,256]{3,2,1,0:T(8,128)(2,1)S(1)} %pad_maximum_fusion.refs_1_, ...), custom_call_target="tpu_custom_call" | custom-call | flops 1660944384 | tf_op jit(solution)/shard_map/pallas_call | solution.py:140
  40.6 6.3 %collective-permute-done.8.last = bf16[3,352,256]{2,1,0:T(8,128)(2,1)S(1)} collective-permute-done((bf16[3,352,256]{2,1,0:T(8,128)(2,1)S(1)}, bf16[3,352,256]{2,1,0:T(8,128)(2,1)S(1)}, u32[]{:S(2)}, u32[]{:S(2)}) %collective-permute-start.8) | collective-permute-done | bytes 540704 | tf_op jit(solution)/shard_map/ppermute | solution.py:17
  46.9 4.6 %shard_map.120 = (f32[2,2,512,256]{3,2,1,0:T(8,128)S(1)}, bf16[2,2,512,256]{3,2,1,0:T(8,128)(2,1)S(1)}, f32[3,352,256]{2,1,0:T(8,128)S(1)}, f32[3,352,256]{2,1,0...) custom-call(bf16[512,1024]{1,0:T(8,128)(2,1)S(1)} %get-tuple-element.31.x_all, ...), custom_call_target="tpu_custom_call" | custom-call | flops 4429185024 | tf_op jit(solution)/shard_map/pallas_call | solution.py:205
  52.5 1.7 %collective-permute-done.9 = bf16[2,2,512,256]{3,2,1,0:T(8,128)(2,1)S(1)} collective-permute-done((bf16[2,2,512,256]{3,2,1,0:T(8,128)(2,1)S(1)}, bf16[2,2,512,256]{3,2,1,0:T(8,128)(2,1)S(1)}, u32[]{:S(2)}, u32[]{:S(2)}) %collective-permute-start.9) | collective-permute-done | bytes 1048608 | tf_op jit(solution)/shard_map/ppermute | solution.py:17
  54.9 11.3 %collective-permute-done.14 = bf16[3,352,256]{2,1,0:T(8,128)(2,1)S(1)} collective-permute-done((bf16[3,352,256]{2,1,0:T(8,128)(2,1)S(1)}, bf16[3,352,256]{2,1,0:T(8,128)(2,1)S(1)}, u32[]{:S(2)}, u32[]{:S(2)}) %collective-permute-start.14) | collective-permute-done | bytes 540704 | tf_op jit(solution)/shard_map/ppermute | solution.py:17
  67.1 1.7 %collective-permute-start.16 = (bf16[3,352,256]{2,1,0:T(8,128)(2,1)S(1)}, bf16[3,352,256]{2,1,0:T(8,128)(2,1)S(1)}, u32[]{:S(2)}, u32[]{:S(2)}) collective-permute-start(bf16[3,352,256]{2,1,0:T(8,128)(2,1)S(1)} %get-tuple-element.42), channel_id=1, source_target_pairs={{0,8},{4,12},{8,0},{12,4},{16,24},{20,28},{24,16},{28,20},{1,9},{5... | collective-permute-start | bytes 1622024 | tf_op jit(solution)/shard_map/ppermute | solution.py:17
  68.8 1.1 %fusion.6 = (bf16[2,512,256]{2,1,0:T(8,128)(2,1)S(1)}, f32[2,512,256]{2,1,0:T(8,128)}) fusion(bf16[2,512,256]{2,1,0:T(8,128)(2,1)S(1)} %collective-permute-done.10, bf16[2,2,512,256]{3,2,1,0:T(8,128)(2,1)S(1)} %collective-permute-done.9, f32[2,2,512,256]{3,2,1,0:T(8,128)S(1)} %get-tuple-element.35), kind=kLoop, calls=%fused_computation.15 | loop fusion | flops 1310720 | bytes 3670016 | tf_op jit(solution)/shard_map/convert.5
  71.2 4.2 %collective-permute-start.12 = (bf16[2,128,256]{2,1,0:T(8,128)(2,1)}, bf16[2,128,256]{2,1,0:T(8,128)(2,1)}, u32[]{:S(2)}, u32[]{:S(2)}) collective-permute-start(bf16[2,128,256]{2,1,0:T(8,128)(2,1)} %get-tuple-element.50), channel_id=1, source_target_pairs={{0,16},{4,20},{8,24},{12,28},{16,0},{20,4},{24,8},{28,12},{1,17},{... | collective-permute-start | bytes 393224 | tf_op jit(solution)/shard_map/ppermute | solution.py:17
  75.4 9.0 %collective-permute-done.15.got_x = bf16[3,352,256]{2,1,0:T(8,128)(2,1)S(1)} collective-permute-done((bf16[3,352,256]{2,1,0:T(8,128)(2,1)S(1)}, bf16[3,352,256]{2,1,0:T(8,128)(2,1)S(1)}, u32[]{:S(2)}, u32[]{:S(2)}) %collective-permute-start.15) | collective-permute-done | bytes 540704 | tf_op jit(solution)/shard_map/ppermute | solution.py:17
  84.4 1.8 %collective-permute-done.16.got_z = bf16[3,352,256]{2,1,0:T(8,128)(2,1)S(1)} collective-permute-done((bf16[3,352,256]{2,1,0:T(8,128)(2,1)S(1)}, bf16[3,352,256]{2,1,0:T(8,128)(2,1)S(1)}, u32[]{:S(2)}, u32[]{:S(2)}) %collective-permute-start.16) | collective-permute-done | bytes 540704 | tf_op jit(solution)/shard_map/ppermute | solution.py:17
  86.2 1.5 %shard_map.121 = (f32[704,256]{1,0:T(8,128)}, f32[704,256]{1,0:T(8,128)}, f32[704,256]{1,0:T(8,128)}) custom-call(f32[3,352,256]{2,1,0:T(8,128)S(1)} %get-tuple-element.37.own, bf16[3,352,256]{2,1,0:T(8,128)(2,1)S(1)} %collective-permute-done.15.got_x, bf16[3,352,256]{2,1,0:T(8,128)(2,1)S(1)} %collective-permute-done.16.got_z), custom_call_target="tpu_custom_call" | custom-call | tf_op jit(solution)/shard_map/pallas_call | solution.py:241
  87.7 1.1 %fusion.3 = bf16[2,128,256]{2,1,0:T(8,128)(2,1)S(1)} fusion(f32[2,512,256]{2,1,0:T(8,128)} %get-tuple-element.47, bf16[2,128,256]{2,1,0:T(8,128)(2,1)} %collective-permute-done.13, bf16[2,128,256]{2,1,0:T(8,128)(2,1)} %collective-permute-done.12, bf16[2,128,256]{2,1,0:T(8,128)(2,1)S(1)} %collective-permute-done.11), kind=kLoop, calls=%fused_computation.8 | loop fusion | flops 458752 | bytes 786432 | tf_op jit(solution)/shard_map/convert.2
  89.5 1.6 %fusion.5 = (f32[128]{0:T(128)S(1)}, bf16[128,256]{1,0:T(8,128)(2,1)}) fusion(bf16[128,1024]{1,0:T(8,128)(2,1)} %refs_1_.1, s32[]{:T(128)S(6)} %select_n.3, bf16[2,128,256]{2,1,0:T(8,128)(2,1)S(1)} %fusion.3, f32[128]{0:T(128)S(1)} %copy-done.2), kind=kLoop, calls=%fused_computation.12 | loop fusion | flops 196480 | bytes 197636 | tf_op jit(solution)/shard_map/reduce_sum | solution.py:329
  91.0 6.1 %psum.7 = f32[128]{0:T(128)} all-reduce(f32[128]{0:T(128)S(1)} %get-tuple-element.51), channel_id=1, replica_groups=mesh['wide'=8,'narrow'=4] {'narrow'}, use_global_device_ids=true, to_apply=%region_1.0 | all-reduce | flops 128 | bytes 1024 | tf_op jit(solution)/shard_map/psum | solution.py:329
  (29 shorter events, 6.7 us)
Async XLA Ops:
  3.3 14.3 %collective-permute-start.1 = (bf16[2,128,256]{2,1,0:T(8,128)(2,1)}, bf16[2,128,256]{2,1,0:T(8,128)(2,1)S(1)}, u32[]{:S(2)}, u32[]{:S(2)}) collective-permute-start(bf16[2,128,256]{2,1,0:T(8,128)(2,1)} %get-tuple-element.28), channel_id=1, source_target_pairs={{0,16},{4,20},{8,24},{12,28},{16,0},{20,4},{24,8},{28,12},{1,17},{... | collective-permute-start | bytes 393224 | tf_op jit(solution)/shard_map/ppermute | solution.py:17
  7.4 13.2 %collective-permute-start.2 = (bf16[2,128,256]{2,1,0:T(8,128)(2,1)}, bf16[2,128,256]{2,1,0:T(8,128)(2,1)S(1)}, u32[]{:S(2)}, u32[]{:S(2)}) collective-permute-start(bf16[2,128,256]{2,1,0:T(8,128)(2,1)} %get-tuple-element.28), channel_id=1, source_target_pairs={{0,20},{4,16},{8,28},{12,24},{16,4},{20,0},{24,12},{28,8},{1,21},{... | collective-permute-start | bytes 393224 | tf_op jit(solution)/shard_map/ppermute | solution.py:17
  8.7 12.0 %collective-permute-start = (bf16[2,128,256]{2,1,0:T(8,128)(2,1)}, bf16[2,128,256]{2,1,0:T(8,128)(2,1)S(1)}, u32[]{:S(2)}, u32[]{:S(2)}) collective-permute-start(bf16[2,128,256]{2,1,0:T(8,128)(2,1)} %get-tuple-element.27), channel_id=1, source_target_pairs={{0,4},{4,0},{8,12},{12,8},{16,20},{20,16},{24,28},{28,24},{1,5},{5... | collective-permute-start | bytes 393224 | tf_op jit(solution)/shard_map/ppermute | solution.py:17
  9.0 21.7 %collective-permute-start.6 = (bf16[3,352,256]{2,1,0:T(8,128)(2,1)}, bf16[3,352,256]{2,1,0:T(8,128)(2,1)S(1)}, u32[]{:S(2)}, u32[]{:S(2)}) collective-permute-start(bf16[3,352,256]{2,1,0:T(8,128)(2,1)} %get-tuple-element.30), channel_id=1, source_target_pairs={{0,4},{4,0},{8,12},{12,8},{16,20},{20,16},{24,28},{28,24},{1,5},{5... | collective-permute-start | bytes 1622024 | tf_op jit(solution)/shard_map/ppermute | solution.py:17
  20.7 10.0 %collective-permute-start.4 = (bf16[3,2,128,256]{3,2,1,0:T(8,128)(2,1)S(1)}, bf16[3,2,128,256]{3,2,1,0:T(8,128)(2,1)S(1)}, u32[]{:S(2)}, u32[]{:S(2)}) collective-permute-start(bf16[3,2,128,256]{3,2,1,0:T(8,128)(2,1)S(1)} %pad_maximum_fusion.refs_1_), channel_id=1, source_target_pairs={{0,2},{1,3},{2,0},{3,1},{4,6},{5,7},{6,4},{7,5},{8,10},{9,11},{10,... | collective-permute-start | bytes 1179656 | tf_op jit(solution)/shard_map/ppermute | solution.py:17
  22.3 14.4 %collective-permute-start.7 = (bf16[3,352,256]{2,1,0:T(8,128)(2,1)}, bf16[3,352,256]{2,1,0:T(8,128)(2,1)S(1)}, u32[]{:S(2)}, u32[]{:S(2)}) collective-permute-start(bf16[3,352,256]{2,1,0:T(8,128)(2,1)} %get-tuple-element.29.refs_5_), channel_id=1, source_target_pairs={{0,8},{4,12},{8,0},{12,4},{16,24},{20,28},{24,16},{28,20},{1,9},{5... | collective-permute-start | bytes 1622024 | tf_op jit(solution)/shard_map/ppermute | solution.py:17
  22.3 9.3 %collective-permute-start.3 = (bf16[3,2,128,256]{3,2,1,0:T(8,128)(2,1)S(1)}, bf16[3,2,128,256]{3,2,1,0:T(8,128)(2,1)S(1)}, u32[]{:S(2)}, u32[]{:S(2)}) collective-permute-start(bf16[3,2,128,256]{3,2,1,0:T(8,128)(2,1)S(1)} %pad_maximum_fusion.refs_1_), channel_id=1, source_target_pairs={{0,1},{1,0},{2,3},{3,2},{4,5},{5,4},{6,7},{7,6},{8,9},{9,8},{10,11... | collective-permute-start | bytes 1179656 | tf_op jit(solution)/shard_map/ppermute | solution.py:17
  30.7 6.0 %collective-permute-start.5 = (bf16[3,2,128,256]{3,2,1,0:T(8,128)(2,1)S(1)}, bf16[3,2,128,256]{3,2,1,0:T(8,128)(2,1)S(1)}, u32[]{:S(2)}, u32[]{:S(2)}) collective-permute-start(bf16[3,2,128,256]{3,2,1,0:T(8,128)(2,1)S(1)} %collective-permute-done.4.refs_3_), channel_id=1, source_target_pairs={{0,1},{1,0},{2,3},{3,2},{4,5},{5,4},{6,7},{7,6},{8,9},{9,8},{10,11... | collective-permute-start | bytes 1179656 | tf_op jit(solution)/shard_map/ppermute | solution.py:17
  30.7 16.2 %collective-permute-start.8 = (bf16[3,352,256]{2,1,0:T(8,128)(2,1)S(1)}, bf16[3,352,256]{2,1,0:T(8,128)(2,1)S(1)}, u32[]{:S(2)}, u32[]{:S(2)}) collective-permute-start(bf16[3,352,256]{2,1,0:T(8,128)(2,1)S(1)} %collective-permute-done.6.refs_6_), channel_id=1, source_target_pairs={{0,8},{4,12},{8,0},{12,4},{16,24},{20,28},{24,16},{28,20},{1,9},{5... | collective-permute-start | bytes 1622024 | tf_op jit(solution)/shard_map/ppermute | solution.py:17
  36.7 1.0 %copy-start = (bf16[3,352,256]{2,1,0:T(8,128)(2,1)S(1)}, bf16[3,352,256]{2,1,0:T(8,128)(2,1)}, u32[]{:S(2)}) copy-start(bf16[3,352,256]{2,1,0:T(8,128)(2,1)} %get-tuple-element.29.refs_5_) | copy-start | bytes 1622020
  37.8 1.0 %copy-start.1 = (bf16[2,128,1024]{2,1,0:T(8,128)(2,1)S(1)}, bf16[2,128,1024]{2,1,0:T(8,128)(2,1)}, u32[]{:S(2)}) copy-start(bf16[2,128,1024]{2,1,0:T(8,128)(2,1)} %get-tuple-element.26.refs_0_) | copy-start | bytes 1572868
  51.5 2.7 %collective-permute-start.9 = (bf16[2,2,512,256]{3,2,1,0:T(8,128)(2,1)S(1)}, bf16[2,2,512,256]{3,2,1,0:T(8,128)(2,1)S(1)}, u32[]{:S(2)}, u32[]{:S(2)}) collective-permute-start(bf16[2,2,512,256]{3,2,1,0:T(8,128)(2,1)S(1)} %get-tuple-element.36), channel_id=1, source_target_pairs={{0,1},{1,0},{2,3},{3,2},{4,5},{5,4},{6,7},{7,6},{8,9},{9,8},{10,11... | collective-permute-start | bytes 3145736 | tf_op jit(solution)/shard_map/ppermute | solution.py:17
  51.5 14.7 %collective-permute-start.14 = (bf16[3,352,256]{2,1,0:T(8,128)(2,1)S(1)}, bf16[3,352,256]{2,1,0:T(8,128)(2,1)S(1)}, u32[]{:S(2)}, u32[]{:S(2)}) collective-permute-start(bf16[3,352,256]{2,1,0:T(8,128)(2,1)S(1)} %get-tuple-element.39), channel_id=1, source_target_pairs={{0,8},{4,12},{8,0},{12,4},{16,24},{20,28},{24,16},{28,20},{1,9},{5... | collective-permute-start | bytes 1622024 | tf_op jit(solution)/shard_map/ppermute | solution.py:17
  54.3 14.5 %collective-permute-start.10 = (bf16[2,512,256]{2,1,0:T(8,128)(2,1)S(1)}, bf16[2,512,256]{2,1,0:T(8,128)(2,1)S(1)}, u32[]{:S(2)}, u32[]{:S(2)}) collective-permute-start(bf16[2,512,256]{2,1,0:T(8,128)(2,1)S(1)} %fusion), channel_id=1, source_target_pairs={{0,2},{1,3},{2,0},{3,1},{4,6},{5,7},{6,4},{7,5},{8,10},{9,11},{10,... | collective-permute-start | bytes 1572872 | tf_op jit(solution)/shard_map/ppermute | solution.py:17
  66.4 18.1 %collective-permute-start.15 = (bf16[3,352,256]{2,1,0:T(8,128)(2,1)S(1)}, bf16[3,352,256]{2,1,0:T(8,128)(2,1)S(1)}, u32[]{:S(2)}, u32[]{:S(2)}) collective-permute-start(bf16[3,352,256]{2,1,0:T(8,128)(2,1)S(1)} %add_convert_fusion), channel_id=1, source_target_pairs={{0,4},{4,0},{8,12},{12,8},{16,20},{20,16},{24,28},{28,24},{1,5},{5... | collective-permute-start | bytes 1622024 | tf_op jit(solution)/shard_map/ppermute | solution.py:17
  67.1 19.2 %collective-permute-start.16 = (bf16[3,352,256]{2,1,0:T(8,128)(2,1)S(1)}, bf16[3,352,256]{2,1,0:T(8,128)(2,1)S(1)}, u32[]{:S(2)}, u32[]{:S(2)}) collective-permute-start(bf16[3,352,256]{2,1,0:T(8,128)(2,1)S(1)} %get-tuple-element.42), channel_id=1, source_target_pairs={{0,8},{4,12},{8,0},{12,4},{16,24},{20,28},{24,16},{28,20},{1,9},{5... | collective-permute-start | bytes 1622024 | tf_op jit(solution)/shard_map/ppermute | solution.py:17
  69.9 19.5 %copy-start.2 = (f32[128]{0:T(128)S(1)}, f32[128]{0:T(128)}, u32[]{:S(2)}) copy-start(f32[128]{0:T(128)} %param.10) | copy-start | bytes 1540
  70.7 17.0 %collective-permute-start.11 = (bf16[2,128,256]{2,1,0:T(8,128)(2,1)}, bf16[2,128,256]{2,1,0:T(8,128)(2,1)S(1)}, u32[]{:S(2)}, u32[]{:S(2)}) collective-permute-start(bf16[2,128,256]{2,1,0:T(8,128)(2,1)} %get-tuple-element.48), channel_id=1, source_target_pairs={{0,4},{4,0},{8,12},{12,8},{16,20},{20,16},{24,28},{28,24},{1,5},{5... | collective-permute-start | bytes 393224 | tf_op jit(solution)/shard_map/ppermute | solution.py:17
  71.2 16.5 %collective-permute-start.12 = (bf16[2,128,256]{2,1,0:T(8,128)(2,1)}, bf16[2,128,256]{2,1,0:T(8,128)(2,1)}, u32[]{:S(2)}, u32[]{:S(2)}) collective-permute-start(bf16[2,128,256]{2,1,0:T(8,128)(2,1)} %get-tuple-element.50), channel_id=1, source_target_pairs={{0,16},{4,20},{8,24},{12,28},{16,0},{20,4},{24,8},{28,12},{1,17},{... | collective-permute-start | bytes 393224 | tf_op jit(solution)/shard_map/ppermute | solution.py:17
  75.4 12.3 %collective-permute-start.13 = (bf16[2,128,256]{2,1,0:T(8,128)(2,1)S(1)}, bf16[2,128,256]{2,1,0:T(8,128)(2,1)}, u32[]{:S(2)}, u32[]{:S(2)}) collective-permute-start(bf16[2,128,256]{2,1,0:T(8,128)(2,1)S(1)} %get-tuple-element.49), channel_id=1, source_target_pairs={{0,20},{4,16},{8,28},{12,24},{16,4},{20,0},{24,12},{28,8},{1,21},{... | collective-permute-start | bytes 393224 | tf_op jit(solution)/shard_map/ppermute | solution.py:17

commit v3 on v2

--- a/solution.py
+++ b/solution.py
@@ -9,6 +9,7 @@
 
 VMEM = pl.BlockSpec(memory_space=pltpu.VMEM)
 HBM = pl.BlockSpec(memory_space=pltpu.HBM)
+EXTRA = 16
 PARAMS = pltpu.CompilerParams(vmem_limit_bytes=32 * 1024 * 1024)
 PROLOGUE_PARAMS = pltpu.CompilerParams(vmem_limit_bytes=61 * 1024 * 1024)
 
@@ -31,6 +32,23 @@
 
 def at_quarter(index, width):
     return pl.ds(pl.multiple_of(index * width, width), width)
+
+
+def packet_rows(rows):
+    return 2 * rows + EXTRA
+
+
+def put_pair(ref, first, value):
+    count, lanes = value.shape
+    high = value.astype(jnp.bfloat16).astype(jnp.float32)
+    both = jnp.concatenate([high, value - high], 0)
+    both = jnp.concatenate([both, jnp.zeros((EXTRA - 2 * count, lanes), jnp.float32)], 0)
+    ref[first : first + EXTRA, :lanes] = both.astype(ref.dtype)
+
+
+def get_pair(ref, first, count):
+    both = ref[first : first + EXTRA, :].astype(jnp.float32)
+    return both[:count] + both[count : 2 * count]
 
 
 def prologue_kernel(routed, gate, up, down, *refs):
@@ -87,7 +105,7 @@
         functools.partial(prologue_kernel, bool(token_args)),
         out_shape=outs,
         in_specs=[HBM] * (3 + len(token_args)),
-        out_specs=[VMEM] * len(outs),
+        out_specs=[HBM] * 2 + [VMEM] * (len(outs) - 2),
         scratch_shapes=scratch + [pltpu.SemaphoreType.DMA((10,))],
         compiler_params=PROLOGUE_PARAMS,
     )(*weights, *token_args)
@@ -154,8 +172,8 @@
     )(*([own] if has_own else []), *pieces, *weights)
 
 
-def main_kernel(x_all, s_all, w_part, part, last, kept, sent, own, to_x, to_z, to_d, grads, w_all):
-    outs = (own, to_x, to_z, to_d)
+def main_kernel(x_all, s_all, w_part, part, last, kept, sent, *refs):
+    outs, (grads, w_all) = refs[:4], refs[4:]
     half, width = last.shape[1:]
     member = lax.axis_index("wide") % 4
     place = lax.axis_index("narrow")
@@ -164,11 +182,13 @@
     for i in range(3):
         w_all[i, :, last_column] = last[i]
     total = x_all.shape[0]
-    tile = min(256, total)
-
-    @pl.loop(0, total // tile)
-    def _(step):
-        rows = pl.ds(pl.multiple_of(step * tile, tile), tile)
+    tile = min(width, total)
+    kept[:, 2 * total :, :] = jnp.zeros_like(kept[:, 2 * total :, :])
+    sent[:, 2 * total :, :] = jnp.zeros_like(sent[:, 2 * total :, :])
+
+    routers = []
+    for step in range(total // tile):
+        rows = slice(step * tile, (step + 1) * tile)
         x_tile, s_tile = x_all[rows, last_column], s_all[rows, last_column]
         gate = part[0, :, rows] + dot_nt(last[0], x_tile)
         up = part[1, :, rows] + dot_nt(last[1], x_tile)
@@ -187,8 +207,13 @@
             out_part = dot_nn(hidden_t, w_all[2, :, column])
             in_part = dot_nn(d_gate_t, w_all[0, :, column]) + dot_nn(d_up_t, w_all[1, :, column])
             target = sent if mask % 2 else kept
-            target[mask // 2, 0, rows, :] = out_part.astype(target.dtype)
-            target[mask // 2, 1, rows, :] = in_part.astype(target.dtype)
+            target[mask // 2, rows, :] = out_part.astype(target.dtype)
+            lower = slice(total + step * tile, total + (step + 1) * tile)
+            target[mask // 2, lower, :] = in_part.astype(target.dtype)
+        router = jnp.sum(hidden.astype(jnp.float32) * d_hidden, axis=0, keepdims=True)
+        kept[0, 2 * total + step : 2 * total + step + 1, :tile] = router
+        routers.append(router)
+    put_pair(sent.at[0], 2 * total, jnp.concatenate(routers, 0))
 
     left = grads[0:2].reshape(2 * half, total)
     for k in (3, 2, 1, 0):
@@ -205,11 +230,11 @@
     return pl.pallas_call(
         main_kernel,
         out_shape=(
-            jax.ShapeDtypeStruct((2, 2, total, width), jnp.float32),
-            jax.ShapeDtypeStruct((2, 2, total, width), jnp.bfloat16),
+            jax.ShapeDtypeStruct((2, packet_rows(total), width), jnp.float32),
+            jax.ShapeDtypeStruct((2, packet_rows(total), width), jnp.bfloat16),
         )
         + tuple(
-            jax.ShapeDtypeStruct((3, half, width), jnp.bfloat16 if k > 1 else jnp.float32)
+            jax.ShapeDtypeStruct((3, half, width), jnp.bfloat16 if k else jnp.float32)
             for k in range(4)
         ),
         in_specs=[VMEM] * 5,
@@ -225,26 +250,113 @@
     )(x_all, s_all, w_part, part, last)
 
 
-def join_kernel(own, got_x, got_z, *outs):
+def join_kernel(own, got_x, got_z, got_d, *outs):
     half = own.shape[1]
     x_bit = lax.axis_index("wide") % 2
     keep_rows = pl.ds(pl.multiple_of(x_bit * half, 16), half)
     give_rows = pl.ds(pl.multiple_of((1 - x_bit) * half, 16), half)
     for i, ref in enumerate(outs):
         ref[keep_rows, :] = own[i] + got_z[i].astype(jnp.float32)
-        ref[give_rows, :] = got_x[i].astype(jnp.float32)
-
-
-def join_grads(own, got_x, got_z):
+        ref[give_rows, :] = got_x[i].astype(jnp.float32) + got_d[i].astype(jnp.float32)
+
+
+def join_grads(own, got_x, got_z, got_d):
     _, half, width = own.shape
     shape = jax.ShapeDtypeStruct((2 * half, width), jnp.float32)
     return pl.pallas_call(
         join_kernel,
         out_shape=(shape,) * 3,
+        in_specs=[VMEM] * 4,
+        out_specs=[VMEM] * 3,
+        compiler_params=PARAMS,
+    )(own, got_x, got_z, got_d)
+
+
+def cross_kernel(kept, got, sent):
+    total = (kept.shape[1] - EXTRA) // 2
+    tile = min(kept.shape[2], total)
+    count = total // tile
+    body = slice(0, 2 * total)
+    sent[body, :] = (kept[1, body, :] + got[1, body, :].astype(jnp.float32)).astype(sent.dtype)
+    sent[2 * total :, :] = jnp.zeros_like(sent[2 * total :, :])
+    router = kept[0, 2 * total : 2 * total + count, :] + get_pair(got.at[0], 2 * total, count)
+    put_pair(sent, 2 * total, router)
+
+
+def cross_part(kept, got):
+    return pl.pallas_call(
+        cross_kernel,
+        out_shape=jax.ShapeDtypeStruct(got.shape[1:], got.dtype),
+        in_specs=[VMEM] * 2,
+        out_specs=VMEM,
+        compiler_params=PARAMS,
+    )(kept, got)
+
+
+def result_kernel(kept, got, across, *outs):
+    total = (kept.shape[1] - EXTRA) // 2
+    width = kept.shape[2]
+    count = total // min(width, total)
+    router = kept[0, 2 * total : 2 * total + count, :] + get_pair(got.at[0], 2 * total, count)
+    router = router + get_pair(across, 2 * total, count)
+    slots = (outs[0].shape[0] - EXTRA) // 2
+    for block, out in enumerate(outs):
+        for part in range(2):
+            rows = slice(part * total + block * slots, part * total + (block + 1) * slots)
+            value = kept[0, rows, :] + got[0, rows, :].astype(jnp.float32)
+            value = value + across[rows, :].astype(jnp.float32)
+            out[part * slots : (part + 1) * slots, :] = value.astype(out.dtype)
+        out[2 * slots :, :] = jnp.zeros_like(out[2 * slots :, :])
+        if slots == total:
+            out[2 * slots : 2 * slots + count, :] = router
+        else:
+            lane = block * slots % width
+            mine = router[block * slots // width :, lane : lane + slots][:1]
+            if block:
+                put_pair(out, 2 * slots, mine)
+            else:
+                out[2 * slots : 2 * slots + 1, :slots] = mine
+
+
+def result_parts(kept, got, across, blocks):
+    total = (kept.shape[1] - EXTRA) // 2
+    shape = (packet_rows(total // blocks), kept.shape[2])
+    return pl.pallas_call(
+        result_kernel,
+        out_shape=tuple(
+            jax.ShapeDtypeStruct(shape, jnp.bfloat16 if k else jnp.float32) for k in range(blocks)
+        ),
         in_specs=[VMEM] * 3,
+        out_specs=[VMEM] * blocks,
+        compiler_params=PARAMS,
+    )(kept, got, across)
+
+
+def finish_kernel(prob, own, *refs):
+    got, (output, tokens_grad, prob_grad) = refs[:-3], refs[-3:]
+    slots, width = output.shape
+    ffn, grad = own[:slots, :], own[slots : 2 * slots, :]
+    router = own[2 * slots : 2 * slots + 1, :]
+    for ref in got:
+        ffn = ffn + ref[:slots, :].astype(jnp.float32)
+        grad = grad + ref[slots : 2 * slots, :].astype(jnp.float32)
+        router = router + get_pair(ref, 2 * slots, 1)
+    weight = jnp.broadcast_to(prob[...], (128, slots)).T[:, :1]
+    output[...] = (ffn.astype(jnp.bfloat16).astype(jnp.float32) * weight).astype(jnp.bfloat16)
+    tokens_grad[...] = grad.astype(jnp.bfloat16)
+    prob_grad[...] = router[:, :slots] / prob[...]
+
+
+def finish(prob, own, got):
+    slots, width = (own.shape[0] - EXTRA) // 2, own.shape[1]
+    part = jax.ShapeDtypeStruct((slots, width), jnp.bfloat16)
+    return pl.pallas_call(
+        finish_kernel,
+        out_shape=(part, part, jax.ShapeDtypeStruct((1, slots), jnp.float32)),
+        in_specs=[VMEM] * (2 + len(got)),
         out_specs=[VMEM] * 3,
         compiler_params=PARAMS,
-    )(own, got_x, got_z)
+    )(prob, own, *got)
 
 
 def shards(tokens, cotangent, expert_ids, route_prob, gate_weight, up_weight, down_weight):
@@ -293,8 +405,9 @@
             routed, "wide", split_axis=0, concat_axis=0, axis_index_groups=groups, tiled=True
         )
 
-    from_x = partner(give, "wide", 1)
-    from_z = partner(keep, "wide", 2)
+    from_x, from_z = lax.optimization_barrier(
+        (partner(give, "wide", 1), partner(keep, "wide", 2))
+    )
     from_d = partner(from_x, "wide", 2)
     across = partner(mine, "narrow", 2)
     pieces = (mine, partner(mine, "narrow", 1), across, partner(across, "narrow", 1))
@@ -302,32 +415,38 @@
     kept, sent, grad_own, grad_x, grad_z, grad_d = main(*held, from_d)
 
     got = partner(sent, "narrow", 1)
-    got_d = partner(grad_d, "wide", 2)
-    grad_x = (grad_x + got_d.astype(jnp.float32)).astype(jnp.bfloat16)
-    grad_x, grad_z = lax.optimization_barrier((grad_x, grad_z))
     got_x = partner(grad_x, "wide", 1)
     got_z = partner(grad_z, "wide", 2)
-
-    across = partner((kept[1] + got[1].astype(jnp.float32)).astype(jnp.bfloat16), "narrow", 2)
-    result = kept[0] + got[0].astype(jnp.float32) + across.astype(jnp.float32)
+    got_d = partner(grad_d, "wide", 3)
+    across = partner(cross_part(kept, got), "narrow", 2)
     if direct:
-        total = result[:, :slots]
-        for k, mask in enumerate(masks):
-            rows = result[:, (k + 1) * slots : (k + 2) * slots].astype(jnp.bfloat16)
-            total = total + partner(rows, "wide", mask).astype(jnp.float32)
+        parts = result_parts(kept, got, across, len(masks) + 1)
+        back = [partner(part, "wide", mask) for mask, part in zip(masks, parts[1:])]
+        output, tokens_grad, prob_grad = finish(route_prob[None, :], parts[0], back)
+        prob_grad = prob_grad[0]
     else:
-        parts = result.astype(jnp.bfloat16).reshape(2, 2 * expert_count, slots, width)
+        (result,) = result_parts(kept, got, across, 1)
+        total = (result.shape[0] - EXTRA) // 2
+        parts = result[: 2 * total].astype(jnp.bfloat16)
+        parts = parts.reshape(2, 2 * expert_count, slots, width)
         back = lax.all_to_all(
             parts, "wide", split_axis=1, concat_axis=1, axis_index_groups=groups, tiled=True
         )
         back = back.reshape(2, expert_count, 2, slots, width).astype(jnp.float32).sum(2)
-        total = back.reshape(2, expert_count * slots, width)[:, slot_place]
-    ffn = total[0].astype(jnp.bfloat16).astype(jnp.float32)
-    tokens_grad = total[1].astype(jnp.bfloat16)
-    output = (route_prob[:, None] * ffn).astype(jnp.bfloat16)
-    cot_columns = lax.dynamic_slice_in_dim(cotangent, place * width, width, 1)
-    prob_grad = lax.psum(jnp.sum(ffn * cot_columns.astype(jnp.float32), axis=1), "narrow")
-    gate_grad, up_grad, down_grad = join_grads(grad_own, got_x, got_z)
+        back = back.reshape(2, expert_count * slots, width)[:, slot_place]
+        router = result[2 * total : 2 * total + total // min(width, total), : min(width, total)]
+        router = router.reshape(2 * expert_count, slots)
+        high = lax.reduce_precision(router, 8, 7)
+        pair = jnp.stack([high, router - high], 1).astype(jnp.bfloat16)
+        pair = lax.all_to_all(
+            pair, "wide", split_axis=0, concat_axis=0, axis_index_groups=groups, tiled=True
+        )
+        router = pair.reshape(expert_count, 4, slots).astype(jnp.float32).sum(1)
+        prob_grad = router.reshape(expert_count * slots)[slot_place] / route_prob
+        ffn = back[0].astype(jnp.bfloat16).astype(jnp.float32)
+        output = (route_prob[:, None] * ffn).astype(jnp.bfloat16)
+        tokens_grad = back[1].astype(jnp.bfloat16)
+    gate_grad, up_grad, down_grad = join_grads(grad_own, got_x, got_z, got_d)
     return (output, tokens_grad, prob_grad, gate_grad.T, up_grad.T, down_grad.T)
 
 

time: 97.5 us -> 121 us (1.24)
  Pallas kernels: 10.5 us -> 43 us
  blocking collectives: 6.13 us -> 0 us
  starting transfers between devices: 18.6 us -> 23.6 us
  other arithmetic: 4.11 us -> 0.05 us
  waiting for transfers between devices: 53.6 us -> 51.7 us
  local copies, waits for them, and re-layouts: 3.45 us -> 2.09 us
    pallas_call x1, Pallas kernels: 2.7 us -> 34.8 us  [prologue(): pl.pallas_call(functools.partial(prologue_kernel, bool(token_args)), out_...]
    psum x1 -> x0, blocking collectives: 6.13 us -> none  [shards(): lax.psum(jnp.sum(ffn * cot_columns.astype(jnp.float32), axis=1), 'narrow')]
    ppermute x17, starting transfers between devices: 18.6 us -> 23.6 us  [partner(): lax.ppermute(x, axis, [(i, i ^ mask) for i in range(lax.axis_size(axis))])]
    another operation x2 -> x0, other arithmetic: 2.26 us -> none
    ppermute x17, waiting for transfers between devices: 53.6 us -> 51.7 us  [partner(): lax.ppermute(x, axis, [(i, i ^ mask) for i in range(lax.axis_size(axis))])]
    reduce_sum x1 -> x0, other arithmetic: 1.57 us -> none  [shards(): jnp.sum(ffn * cot_columns.astype(jnp.float32), axis=1)]
    pallas_call x2 -> x5, Pallas kernels: 6.06 us -> 6.4 us  [the longest x1 3.85 us: main(): pl.pallas_call(main_kernel, out_shape=(jax.ShapeDtypeStruct((2, packet_ro...]
  transfers between devices with their start and end apart: 17 -> 17, of which waited for: 9 -> 7; matrix products, arithmetic and copies ran while one was open for 2% -> 0% of each run, Pallas kernels for 3% -> 3%
where the time goes in v3:
time: 121 us
  waiting for transfers between devices  51.7 us (43%)
  Pallas kernels  43 us (36%)
  starting transfers between devices  23.6 us (20%)
  local copies, waits for them, and re-layouts  2.09 us (2%)
    ppermute x17, waiting for transfers between devices, partner(): lax.ppermute(x, axis, [(i, i ^ mask) for i in range(lax.axis_size(axis))])  51.7 us
    pallas_call x1, Pallas kernels, prologue(): pl.pallas_call(functools.partial(prologue_kernel, bool(token_args)), out_...  34.8 us
    ppermute x17, starting transfers between devices, partner(): lax.ppermute(x, axis, [(i, i ^ mask) for i in range(lax.axis_size(axis))])  23.6 us
    pallas_call x1, Pallas kernels, main(): pl.pallas_call(main_kernel, out_shape=(jax.ShapeDtypeStruct((2, packet_ro...  3.85 us
  transfers between devices with their start and end apart: 17, of which 7 were waited for; matrix products, arithmetic and copies ran while one was open for 0% of the time, Pallas kernels for 3%

profile of v3, /device:TPU:0, one launch (start us, length us, event | category | flops | bytes accessed | tf_op | source)
XLA Modules:
  0.0 121.1 jit_solution(7050448710522988495)
XLA Ops:
  0.6 34.8 %shard_map.118 = (bf16[3,352,256]{2,1,0:T(8,128)(2,1)}, bf16[3,352,256]{2,1,0:T(8,128)(2,1)}, bf16[2,128,1024]{2,1,0:T(8,128)(2,1)}, bf16[2,128,256]{2,1,0:T(8,128)(2,1)}, bf16[2,128,256]{2,1,0:T(8,128)(2,1)}) custom-call(bf16[704,256]{1,0:T(8,128)(2,1)} %bitcast.14, bf16[704,256]{1,0:T(8,128)(2,1)} %bitcast.15, bf16[704,256]{1,0:T(8,128)(2,1)} %bitcast.16, ...), custom_call_target="tpu_custom_call" | custom-call | tf_op jit(solution)/shard_map/pallas_call | solution.py:104
  35.5 3.0 %collective-permute-start = (bf16[2,128,256]{2,1,0:T(8,128)(2,1)}, bf16[2,128,256]{2,1,0:T(8,128)(2,1)S(1)}, u32[]{:S(2)}, u32[]{:S(2)}) collective-permute-start(bf16[2,128,256]{2,1,0:T(8,128)(2,1)} %get-tuple-element.34), channel_id=1, source_target_pairs={{0,4},{4,0},{8,12},{12,8},{16,20},{20,16},{24,28},{28,24},{1,5},{5... | collective-permute-start | bytes 393224 | tf_op jit(solution)/shard_map/ppermute | solution.py:18
  38.5 2.6 %collective-permute-start.2 = (bf16[2,128,256]{2,1,0:T(8,128)(2,1)}, bf16[2,128,256]{2,1,0:T(8,128)(2,1)S(1)}, u32[]{:S(2)}, u32[]{:S(2)}) collective-permute-start(bf16[2,128,256]{2,1,0:T(8,128)(2,1)} %get-tuple-element.35), channel_id=1, source_target_pairs={{0,20},{4,16},{8,28},{12,24},{16,4},{20,0},{24,12},{28,8},{1,21},{... | collective-permute-start | bytes 393224 | tf_op jit(solution)/shard_map/ppermute | solution.py:18
  41.1 1.8 %collective-permute-start.6 = (bf16[3,352,256]{2,1,0:T(8,128)(2,1)}, bf16[3,352,256]{2,1,0:T(8,128)(2,1)S(1)}, u32[]{:S(2)}, u32[]{:S(2)}) collective-permute-start(bf16[3,352,256]{2,1,0:T(8,128)(2,1)} %get-tuple-element.37), channel_id=1, source_target_pairs={{0,4},{4,0},{8,12},{12,8},{16,20},{20,16},{24,28},{28,24},{1,5},{5... | collective-permute-start | bytes 1622024 | tf_op jit(solution)/shard_map/ppermute | solution.py:18
  42.9 1.6 %collective-permute-start.7 = (bf16[3,352,256]{2,1,0:T(8,128)(2,1)}, bf16[3,352,256]{2,1,0:T(8,128)(2,1)S(1)}, u32[]{:S(2)}, u32[]{:S(2)}) collective-permute-start(bf16[3,352,256]{2,1,0:T(8,128)(2,1)} %get-tuple-element.36.refs_5_), channel_id=1, source_target_pairs={{0,8},{4,12},{8,0},{12,4},{16,24},{20,28},{24,16},{28,20},{1,9},{5... | collective-permute-start | bytes 1622024 | tf_op jit(solution)/shard_map/ppermute | solution.py:18
  44.4 7.9 %collective-permute-done.2 = bf16[2,128,256]{2,1,0:T(8,128)(2,1)S(1)} collective-permute-done((bf16[2,128,256]{2,1,0:T(8,128)(2,1)}, bf16[2,128,256]{2,1,0:T(8,128)(2,1)S(1)}, u32[]{:S(2)}, u32[]{:S(2)}) %collective-permute-start.2) | collective-permute-done | bytes 131104 | tf_op jit(solution)/shard_map/ppermute | solution.py:18
  53.1 1.6 %collective-permute-start.4 = (bf16[3,2,128,256]{3,2,1,0:T(8,128)(2,1)S(1)}, bf16[3,2,128,256]{3,2,1,0:T(8,128)(2,1)S(1)}, u32[]{:S(2)}, u32[]{:S(2)}) collective-permute-start(bf16[3,2,128,256]{3,2,1,0:T(8,128)(2,1)S(1)} %pad_maximum_fusion.refs_1_), channel_id=1, source_target_pairs={{0,2},{1,3},{2,0},{3,1},{4,6},{5,7},{6,4},{7,5},{8,10},{9,11},{10,... | collective-permute-start | bytes 1179656 | tf_op jit(solution)/shard_map/ppermute | solution.py:18
  54.7 8.4 %collective-permute-done.4.refs_3_ = bf16[3,2,128,256]{3,2,1,0:T(8,128)(2,1)S(1)} collective-permute-done((bf16[3,2,128,256]{3,2,1,0:T(8,128)(2,1)S(1)}, bf16[3,2,128,256]{3,2,1,0:T(8,128)(2,1)S(1)}, u32[]{:S(2)}, u32[]{:S(2)}) %collective-permute-start.4) | collective-permute-done | bytes 393248 | tf_op jit(solution)/shard_map/ppermute | solution.py:18
  63.1 1.9 %collective-permute-start.8 = (bf16[3,352,256]{2,1,0:T(8,128)(2,1)S(1)}, bf16[3,352,256]{2,1,0:T(8,128)(2,1)S(1)}, u32[]{:S(2)}, u32[]{:S(2)}) collective-permute-start(bf16[3,352,256]{2,1,0:T(8,128)(2,1)S(1)} %collective-permute-done.6.refs_6_), channel_id=1, source_target_pairs={{0,8},{4,12},{8,0},{12,4},{16,24},{20,28},{24,16},{28,20},{1,9},{5... | collective-permute-start | bytes 1622024 | tf_op jit(solution)/shard_map/ppermute | solution.py:18
  65.0 1.0 copy-done.1
  66.1 1.0 copy-done.2
  67.1 1.7 %shard_map.119 = (bf16[512,1024]{1,0:T(8,128)(2,1)S(1)}, bf16[512,1024]{1,0:T(8,128)(2,1)S(1)}, bf16[3,352,1024]{2,1,0:T(8,128)(2,1)S(1)}, f32[3,352,512]{2,1,0:T(8,128)S(1)}) custom-call(bf16[2,128,1024]{2,1,0:T(8,128)(2,1)S(1)} %copy-done.2, bf16[3,2,128,256]{3,2,1,0:T(8,128)(2,1)S(1)} %pad_maximum_fusion.refs_1_, ...), custom_call_target="tpu_custom_call" | custom-call | flops 1660944384 | tf_op jit(solution)/shard_map/pallas_call | solution.py:158
  68.8 9.0 %collective-permute-done.8.last = bf16[3,352,256]{2,1,0:T(8,128)(2,1)S(1)} collective-permute-done((bf16[3,352,256]{2,1,0:T(8,128)(2,1)S(1)}, bf16[3,352,256]{2,1,0:T(8,128)(2,1)S(1)}, u32[]{:S(2)}, u32[]{:S(2)}) %collective-permute-start.8) | collective-permute-done | bytes 540704 | tf_op jit(solution)/shard_map/ppermute | solution.py:18
  77.9 3.9 %shard_map.120 = (f32[2,1040,256]{2,1,0:T(8,128)S(1)}, bf16[2,1040,256]{2,1,0:T(8,128)(2,1)S(1)}, f32[3,352,256]{2,1,0:T(8,128)S(1)}, bf16[3,352,256]{2,1,0:T(8,...) custom-call(bf16[512,1024]{1,0:T(8,128)(2,1)S(1)} %get-tuple-element.40.x_all, ...), custom_call_target="tpu_custom_call" | custom-call | flops 4429185024 | tf_op jit(solution)/shard_map/pallas_call | solution.py:230
  81.8 1.6 %collective-permute-start.14 = (bf16[3,352,256]{2,1,0:T(8,128)(2,1)S(1)}, bf16[3,352,256]{2,1,0:T(8,128)(2,1)S(1)}, u32[]{:S(2)}, u32[]{:S(2)}) collective-permute-start(bf16[3,352,256]{2,1,0:T(8,128)(2,1)S(1)} %get-tuple-element.54), channel_id=1, source_target_pairs={{0,4},{4,0},{8,12},{12,8},{16,20},{20,16},{24,28},{28,24},{1,5},{5... | collective-permute-start | bytes 1622024 | tf_op jit(solution)/shard_map/ppermute | solution.py:18
  83.4 1.1 collective-permute-done.9.got
  84.6 1.6 %collective-permute-start.10 = (bf16[1040,256]{1,0:T(8,128)(2,1)S(1)}, bf16[1040,256]{1,0:T(8,128)(2,1)S(1)}, u32[]{:S(2)}, u32[]{:S(2)}) collective-permute-start(bf16[1040,256]{1,0:T(8,128)(2,1)S(1)} %shard_map.121), channel_id=1, source_target_pairs={{0,2},{1,3},{2,0},{3,1},{4,6},{5,7},{6,4},{7,5},{8,10},{9,11},{10,... | collective-permute-start | bytes 1597448 | tf_op jit(solution)/shard_map/ppermute | solution.py:18
  86.2 1.8 %collective-permute-start.15 = (bf16[3,352,256]{2,1,0:T(8,128)(2,1)S(1)}, bf16[3,352,256]{2,1,0:T(8,128)(2,1)S(1)}, u32[]{:S(2)}, u32[]{:S(2)}) collective-permute-start(bf16[3,352,256]{2,1,0:T(8,128)(2,1)S(1)} %get-tuple-element.55), channel_id=1, source_target_pairs={{0,8},{4,12},{8,0},{12,4},{16,24},{20,28},{24,16},{28,20},{1,9},{5... | collective-permute-start | bytes 1622024 | tf_op jit(solution)/shard_map/ppermute | solution.py:18
  88.0 1.2 %collective-permute-start.16 = (bf16[3,352,256]{2,1,0:T(8,128)(2,1)S(1)}, bf16[3,352,256]{2,1,0:T(8,128)(2,1)S(1)}, u32[]{:S(2)}, u32[]{:S(2)}) collective-permute-start(bf16[3,352,256]{2,1,0:T(8,128)(2,1)S(1)} %get-tuple-element.56), channel_id=1, source_target_pairs={{0,12},{4,8},{8,4},{12,0},{16,28},{20,24},{24,20},{28,16},{1,13},{... | collective-permute-start | bytes 1622024 | tf_op jit(solution)/shard_map/ppermute | solution.py:18
  89.2 9.6 %collective-permute-done.10.across = bf16[1040,256]{1,0:T(8,128)(2,1)S(1)} collective-permute-done((bf16[1040,256]{1,0:T(8,128)(2,1)S(1)}, bf16[1040,256]{1,0:T(8,128)(2,1)S(1)}, u32[]{:S(2)}, u32[]{:S(2)}) %collective-permute-start.10) | collective-permute-done | bytes 532512 | tf_op jit(solution)/shard_map/ppermute | solution.py:18
  99.0 1.6 %collective-permute-start.11 = (bf16[272,256]{1,0:T(8,128)(2,1)S(1)}, bf16[272,256]{1,0:T(8,128)(2,1)S(1)}, u32[]{:S(2)}, u32[]{:S(2)}) collective-permute-start(bf16[272,256]{1,0:T(8,128)(2,1)S(1)} %get-tuple-element.47), channel_id=1, source_target_pairs={{0,4},{4,0},{8,12},{12,8},{16,20},{20,16},{24,28},{28,24},{1,5},{5... | collective-permute-start | bytes 417800 | tf_op jit(solution)/shard_map/ppermute | solution.py:18
  100.5 3.3 %collective-permute-start.12 = (bf16[272,256]{1,0:T(8,128)(2,1)S(1)}, bf16[272,256]{1,0:T(8,128)(2,1)S(1)}, u32[]{:S(2)}, u32[]{:S(2)}) collective-permute-start(bf16[272,256]{1,0:T(8,128)(2,1)S(1)} %get-tuple-element.48), channel_id=1, source_target_pairs={{0,16},{4,20},{8,24},{12,28},{16,0},{20,4},{24,8},{28,12},{1,17},{... | collective-permute-start | bytes 417800 | tf_op jit(solution)/shard_map/ppermute | solution.py:18
  103.8 15.0 %collective-permute-done.16.got_d = bf16[3,352,256]{2,1,0:T(8,128)(2,1)S(1)} collective-permute-done((bf16[3,352,256]{2,1,0:T(8,128)(2,1)S(1)}, bf16[3,352,256]{2,1,0:T(8,128)(2,1)S(1)}, u32[]{:S(2)}, u32[]{:S(2)}) %collective-permute-start.16) | collective-permute-done | bytes 540704 | tf_op jit(solution)/shard_map/ppermute | solution.py:18
  118.8 1.5 %shard_map.124 = (f32[704,256]{1,0:T(8,128)}, f32[704,256]{1,0:T(8,128)}, f32[704,256]{1,0:T(8,128)}) custom-call(f32[3,352,256]{2,1,0:T(8,128)S(1)} %get-tuple-element.53.own, bf16[3,352,256]{2,1,0:T(8,128)(2,1)S(1)} %collective-permute-done.14.got_x, bf16[3,352,256]{2,1,0:T(8,128)(2,1)S(1)} %collective-permute-done.15.got_z, ...), custom_call_target="tpu_custom_call" | custom-call | tf_op jit(solution)/shard_map/pallas_call | solution.py:266
  (24 shorter events, 2.0 us)
Async XLA Ops:
  35.5 9.0 %collective-permute-start = (bf16[2,128,256]{2,1,0:T(8,128)(2,1)}, bf16[2,128,256]{2,1,0:T(8,128)(2,1)S(1)}, u32[]{:S(2)}, u32[]{:S(2)}) collective-permute-start(bf16[2,128,256]{2,1,0:T(8,128)(2,1)} %get-tuple-element.34), channel_id=1, source_target_pairs={{0,4},{4,0},{8,12},{12,8},{16,20},{20,16},{24,28},{28,24},{1,5},{5... | collective-permute-start | bytes 393224 | tf_op jit(solution)/shard_map/ppermute | solution.py:18
  38.5 13.9 %collective-permute-start.2 = (bf16[2,128,256]{2,1,0:T(8,128)(2,1)}, bf16[2,128,256]{2,1,0:T(8,128)(2,1)S(1)}, u32[]{:S(2)}, u32[]{:S(2)}) collective-permute-start(bf16[2,128,256]{2,1,0:T(8,128)(2,1)} %get-tuple-element.35), channel_id=1, source_target_pairs={{0,20},{4,16},{8,28},{12,24},{16,4},{20,0},{24,12},{28,8},{1,21},{... | collective-permute-start | bytes 393224 | tf_op jit(solution)/shard_map/ppermute | solution.py:18
  41.0 12.0 %collective-permute-start.1 = (bf16[2,128,256]{2,1,0:T(8,128)(2,1)}, bf16[2,128,256]{2,1,0:T(8,128)(2,1)S(1)}, u32[]{:S(2)}, u32[]{:S(2)}) collective-permute-start(bf16[2,128,256]{2,1,0:T(8,128)(2,1)} %get-tuple-element.35), channel_id=1, source_target_pairs={{0,16},{4,20},{8,24},{12,28},{16,0},{20,4},{24,8},{28,12},{1,17},{... | collective-permute-start | bytes 393224 | tf_op jit(solution)/shard_map/ppermute | solution.py:18
  41.1 22.0 %collective-permute-start.6 = (bf16[3,352,256]{2,1,0:T(8,128)(2,1)}, bf16[3,352,256]{2,1,0:T(8,128)(2,1)S(1)}, u32[]{:S(2)}, u32[]{:S(2)}) collective-permute-start(bf16[3,352,256]{2,1,0:T(8,128)(2,1)} %get-tuple-element.37), channel_id=1, source_target_pairs={{0,4},{4,0},{8,12},{12,8},{16,20},{20,16},{24,28},{28,24},{1,5},{5... | collective-permute-start | bytes 1622024 | tf_op jit(solution)/shard_map/ppermute | solution.py:18
  42.9 20.2 %collective-permute-start.7 = (bf16[3,352,256]{2,1,0:T(8,128)(2,1)}, bf16[3,352,256]{2,1,0:T(8,128)(2,1)S(1)}, u32[]{:S(2)}, u32[]{:S(2)}) collective-permute-start(bf16[3,352,256]{2,1,0:T(8,128)(2,1)} %get-tuple-element.36.refs_5_), channel_id=1, source_target_pairs={{0,8},{4,12},{8,0},{12,4},{16,24},{20,28},{24,16},{28,20},{1,9},{5... | collective-permute-start | bytes 1622024 | tf_op jit(solution)/shard_map/ppermute | solution.py:18
  53.1 10.0 %collective-permute-start.4 = (bf16[3,2,128,256]{3,2,1,0:T(8,128)(2,1)S(1)}, bf16[3,2,128,256]{3,2,1,0:T(8,128)(2,1)S(1)}, u32[]{:S(2)}, u32[]{:S(2)}) collective-permute-start(bf16[3,2,128,256]{3,2,1,0:T(8,128)(2,1)S(1)} %pad_maximum_fusion.refs_1_), channel_id=1, source_target_pairs={{0,2},{1,3},{2,0},{3,1},{4,6},{5,7},{6,4},{7,5},{8,10},{9,11},{10,... | collective-permute-start | bytes 1179656 | tf_op jit(solution)/shard_map/ppermute | solution.py:18
  54.7 10.3 %collective-permute-start.3 = (bf16[3,2,128,256]{3,2,1,0:T(8,128)(2,1)S(1)}, bf16[3,2,128,256]{3,2,1,0:T(8,128)(2,1)S(1)}, u32[]{:S(2)}, u32[]{:S(2)}) collective-permute-start(bf16[3,2,128,256]{3,2,1,0:T(8,128)(2,1)S(1)} %pad_maximum_fusion.refs_1_), channel_id=1, source_target_pairs={{0,1},{1,0},{2,3},{3,2},{4,5},{5,4},{6,7},{7,6},{8,9},{9,8},{10,11... | collective-permute-start | bytes 1179656 | tf_op jit(solution)/shard_map/ppermute | solution.py:18
  63.1 1.9 %collective-permute-start.5 = (bf16[3,2,128,256]{3,2,1,0:T(8,128)(2,1)S(1)}, bf16[3,2,128,256]{3,2,1,0:T(8,128)(2,1)S(1)}, u32[]{:S(2)}, u32[]{:S(2)}) collective-permute-start(bf16[3,2,128,256]{3,2,1,0:T(8,128)(2,1)S(1)} %collective-permute-done.4.refs_3_), channel_id=1, source_target_pairs={{0,1},{1,0},{2,3},{3,2},{4,5},{5,4},{6,7},{7,6},{8,9},{9,8},{10,11... | collective-permute-start | bytes 1179656 | tf_op jit(solution)/shard_map/ppermute | solution.py:18
  63.1 14.8 %collective-permute-start.8 = (bf16[3,352,256]{2,1,0:T(8,128)(2,1)S(1)}, bf16[3,352,256]{2,1,0:T(8,128)(2,1)S(1)}, u32[]{:S(2)}, u32[]{:S(2)}) collective-permute-start(bf16[3,352,256]{2,1,0:T(8,128)(2,1)S(1)} %collective-permute-done.6.refs_6_), channel_id=1, source_target_pairs={{0,8},{4,12},{8,0},{12,4},{16,24},{20,28},{24,16},{28,20},{1,9},{5... | collective-permute-start | bytes 1622024 | tf_op jit(solution)/shard_map/ppermute | solution.py:18
  65.0 1.0 copy-start.1
  66.1 1.0 copy-start.2
  81.7 2.7 %collective-permute-start.9 = (bf16[2,1040,256]{2,1,0:T(8,128)(2,1)S(1)}, bf16[2,1040,256]{2,1,0:T(8,128)(2,1)S(1)}, u32[]{:S(2)}, u32[]{:S(2)}) collective-permute-start(bf16[2,1040,256]{2,1,0:T(8,128)(2,1)S(1)} %get-tuple-element.45), channel_id=1, source_target_pairs={{0,1},{1,0},{2,3},{3,2},{4,5},{5,4},{6,7},{7,6},{8,9},{9,8},{10,11... | collective-permute-start | bytes 3194888 | tf_op jit(solution)/shard_map/ppermute | solution.py:18
  81.8 22.0 %collective-permute-start.14 = (bf16[3,352,256]{2,1,0:T(8,128)(2,1)S(1)}, bf16[3,352,256]{2,1,0:T(8,128)(2,1)S(1)}, u32[]{:S(2)}, u32[]{:S(2)}) collective-permute-start(bf16[3,352,256]{2,1,0:T(8,128)(2,1)S(1)} %get-tuple-element.54), channel_id=1, source_target_pairs={{0,4},{4,0},{8,12},{12,8},{16,20},{20,16},{24,28},{28,24},{1,5},{5... | collective-permute-start | bytes 1622024 | tf_op jit(solution)/shard_map/ppermute | solution.py:18
  84.6 14.2 %collective-permute-start.10 = (bf16[1040,256]{1,0:T(8,128)(2,1)S(1)}, bf16[1040,256]{1,0:T(8,128)(2,1)S(1)}, u32[]{:S(2)}, u32[]{:S(2)}) collective-permute-start(bf16[1040,256]{1,0:T(8,128)(2,1)S(1)} %shard_map.121), channel_id=1, source_target_pairs={{0,2},{1,3},{2,0},{3,1},{4,6},{5,7},{6,4},{7,5},{8,10},{9,11},{10,... | collective-permute-start | bytes 1597448 | tf_op jit(solution)/shard_map/ppermute | solution.py:18
  86.2 17.6 %collective-permute-start.15 = (bf16[3,352,256]{2,1,0:T(8,128)(2,1)S(1)}, bf16[3,352,256]{2,1,0:T(8,128)(2,1)S(1)}, u32[]{:S(2)}, u32[]{:S(2)}) collective-permute-start(bf16[3,352,256]{2,1,0:T(8,128)(2,1)S(1)} %get-tuple-element.55), channel_id=1, source_target_pairs={{0,8},{4,12},{8,0},{12,4},{16,24},{20,28},{24,16},{28,20},{1,9},{5... | collective-permute-start | bytes 1622024 | tf_op jit(solution)/shard_map/ppermute | solution.py:18
  88.0 30.8 %collective-permute-start.16 = (bf16[3,352,256]{2,1,0:T(8,128)(2,1)S(1)}, bf16[3,352,256]{2,1,0:T(8,128)(2,1)S(1)}, u32[]{:S(2)}, u32[]{:S(2)}) collective-permute-start(bf16[3,352,256]{2,1,0:T(8,128)(2,1)S(1)} %get-tuple-element.56), channel_id=1, source_target_pairs={{0,12},{4,8},{8,4},{12,0},{16,28},{20,24},{24,20},{28,16},{1,13},{... | collective-permute-start | bytes 1622024 | tf_op jit(solution)/shard_map/ppermute | solution.py:18
  98.9 21.3 %copy-start = (f32[128]{0:T(128)S(1)}, f32[128]{0:T(128)}, u32[]{:S(2)}) copy-start(f32[128]{0:T(128)} %param.10) | copy-start | bytes 1540
  99.0 21.3 %collective-permute-start.11 = (bf16[272,256]{1,0:T(8,128)(2,1)S(1)}, bf16[272,256]{1,0:T(8,128)(2,1)S(1)}, u32[]{:S(2)}, u32[]{:S(2)}) collective-permute-start(bf16[272,256]{1,0:T(8,128)(2,1)S(1)} %get-tuple-element.47), channel_id=1, source_target_pairs={{0,4},{4,0},{8,12},{12,8},{16,20},{20,16},{24,28},{28,24},{1,5},{5... | collective-permute-start | bytes 417800 | tf_op jit(solution)/shard_map/ppermute | solution.py:18
  100.5 19.7 %collective-permute-start.12 = (bf16[272,256]{1,0:T(8,128)(2,1)S(1)}, bf16[272,256]{1,0:T(8,128)(2,1)S(1)}, u32[]{:S(2)}, u32[]{:S(2)}) collective-permute-start(bf16[272,256]{1,0:T(8,128)(2,1)S(1)} %get-tuple-element.48), channel_id=1, source_target_pairs={{0,16},{4,20},{8,24},{12,28},{16,0},{20,4},{24,8},{28,12},{1,17},{... | collective-permute-start | bytes 417800 | tf_op jit(solution)/shard_map/ppermute | solution.py:18
  103.8 16.5 %collective-permute-start.13 = (bf16[272,256]{1,0:T(8,128)(2,1)S(1)}, bf16[272,256]{1,0:T(8,128)(2,1)S(1)}, u32[]{:S(2)}, u32[]{:S(2)}) collective-permute-start(bf16[272,256]{1,0:T(8,128)(2,1)S(1)} %get-tuple-element.49), channel_id=1, source_target_pairs={{0,20},{4,16},{8,28},{12,24},{16,4},{20,0},{24,12},{28,8},{1,21},{... | collective-permute-start | bytes 417800 | tf_op jit(solution)/shard_map/ppermute | solution.py:18

commit v4 on v3

--- a/solution.py
+++ b/solution.py
@@ -11,7 +11,6 @@
 HBM = pl.BlockSpec(memory_space=pltpu.HBM)
 EXTRA = 16
 PARAMS = pltpu.CompilerParams(vmem_limit_bytes=32 * 1024 * 1024)
-PROLOGUE_PARAMS = pltpu.CompilerParams(vmem_limit_bytes=61 * 1024 * 1024)
 
 
 def partner(x, axis, mask):
@@ -105,10 +104,10 @@
         functools.partial(prologue_kernel, bool(token_args)),
         out_shape=outs,
         in_specs=[HBM] * (3 + len(token_args)),
-        out_specs=[HBM] * 2 + [VMEM] * (len(outs) - 2),
+        out_specs=[VMEM] * len(outs),
         scratch_shapes=scratch + [pltpu.SemaphoreType.DMA((10,))],
-        compiler_params=PROLOGUE_PARAMS,
-    )(*weights, *token_args)
+        compiler_params=PARAMS,
+    )(*[pltpu.with_memory_space_constraint(x, pltpu.HBM) for x in (*weights, *token_args)])
 
 
 def gather_kernel(has_own, *refs):
@@ -166,27 +165,16 @@
         in_specs=[VMEM] * (7 + has_own),
         out_specs=[VMEM] * 4,
         compiler_params=PARAMS,
-        cost_estimate=pl.CostEstimate(
-            flops=6 * 2 * half * 3 * width * total, bytes_accessed=0, transcendentals=0
-        ),
+        cost_estimate=pl.CostEstimate(flops=1, bytes_accessed=1, transcendentals=0),
     )(*([own] if has_own else []), *pieces, *weights)
 
 
-def main_kernel(x_all, s_all, w_part, part, last, kept, sent, *refs):
-    outs, (grads, w_all) = refs[:4], refs[4:]
+def inner_kernel(x_all, s_all, part, last, units, router, *outs):
     half, width = last.shape[1:]
     member = lax.axis_index("wide") % 4
-    place = lax.axis_index("narrow")
     last_column = at_quarter(member ^ 3, width)
-    w_all[...] = w_part[...]
-    for i in range(3):
-        w_all[i, :, last_column] = last[i]
     total = x_all.shape[0]
     tile = min(width, total)
-    kept[:, 2 * total :, :] = jnp.zeros_like(kept[:, 2 * total :, :])
-    sent[:, 2 * total :, :] = jnp.zeros_like(sent[:, 2 * total :, :])
-
-    routers = []
     for step in range(total // tile):
         rows = slice(step * tile, (step + 1) * tile)
         x_tile, s_tile = x_all[rows, last_column], s_all[rows, last_column]
@@ -198,78 +186,111 @@
         hidden = (active * up).astype(jnp.bfloat16)
         d_gate = (d_hidden * up * sigma * (1.0 + gate * (1.0 - sigma))).astype(jnp.bfloat16)
         d_up = (d_hidden * active).astype(jnp.bfloat16)
-        grads[0, :, rows] = d_gate
-        grads[1, :, rows] = d_up
-        grads[2, :, rows] = hidden
-        hidden_t, d_gate_t, d_up_t = hidden.T, d_gate.T, d_up.T
-        for mask in range(4):
-            column = at_quarter(place ^ mask, width)
-            out_part = dot_nn(hidden_t, w_all[2, :, column])
-            in_part = dot_nn(d_gate_t, w_all[0, :, column]) + dot_nn(d_up_t, w_all[1, :, column])
-            target = sent if mask % 2 else kept
-            target[mask // 2, rows, :] = out_part.astype(target.dtype)
-            lower = slice(total + step * tile, total + (step + 1) * tile)
-            target[mask // 2, lower, :] = in_part.astype(target.dtype)
-        router = jnp.sum(hidden.astype(jnp.float32) * d_hidden, axis=0, keepdims=True)
-        kept[0, 2 * total + step : 2 * total + step + 1, :tile] = router
-        routers.append(router)
-    put_pair(sent.at[0], 2 * total, jnp.concatenate(routers, 0))
-
-    left = grads[0:2].reshape(2 * half, total)
+        units[0, :, rows] = d_gate
+        units[1, :, rows] = d_up
+        units[2, :, rows] = hidden
+        router[step : step + 1, :] = jnp.sum(
+            hidden.astype(jnp.float32) * d_hidden, axis=0, keepdims=True
+        )
+
+    left = units[0:2].reshape(2 * half, total)
     for k in (3, 2, 1, 0):
         column = at_quarter(member ^ k, width)
         both = dot_nn(left, x_all[:, column])
         outs[k][0] = both[:half].astype(outs[k].dtype)
         outs[k][1] = both[half:].astype(outs[k].dtype)
-        outs[k][2] = dot_nn(grads[2], s_all[:, column]).astype(outs[k].dtype)
-
-
-def main(x_all, s_all, w_part, part, last):
+        outs[k][2] = dot_nn(units[2], s_all[:, column]).astype(outs[k].dtype)
+
+
+def inner(x_all, s_all, part, last):
     total, features = x_all.shape
     _, half, width = last.shape
-    return pl.pallas_call(
-        main_kernel,
+    tile = min(width, total)
+    return pl.pallas_call(
+        inner_kernel,
+        out_shape=(
+            jax.ShapeDtypeStruct((3, half, total), jnp.bfloat16),
+            jax.ShapeDtypeStruct((total // tile, tile), jnp.float32),
+        )
+        + tuple(
+            jax.ShapeDtypeStruct((3, half, width), jnp.bfloat16 if k > 1 else jnp.float32)
+            for k in range(4)
+        ),
+        in_specs=[VMEM] * 4,
+        out_specs=[VMEM] * 6,
+        compiler_params=PARAMS,
+        cost_estimate=pl.CostEstimate(
+            flops=8 * half * features * total, bytes_accessed=0, transcendentals=0
+        ),
+    )(x_all, s_all, part, last)
+
+
+def outer_kernel(units, router, w_part, last, kept, sent, w_all):
+    half, width = last.shape[1:]
+    place = lax.axis_index("narrow")
+    w_all[...] = w_part[...]
+    last_column = at_quarter(lax.axis_index("wide") % 4 ^ 3, width)
+    for i in range(3):
+        w_all[i, :, last_column] = last[i]
+    total = units.shape[2]
+    count, tile = router.shape
+    for ref in (kept, sent):
+        ref[:, 2 * total :, :] = jnp.zeros_like(ref[:, 2 * total :, :])
+    kept[0, 2 * total : 2 * total + count, :tile] = router[...]
+    put_pair(sent.at[0], 2 * total, router[...])
+    for step in range(count):
+        rows = slice(step * tile, (step + 1) * tile)
+        lower = slice(total + step * tile, total + (step + 1) * tile)
+        d_gate, d_up, hidden = (units[i, :, rows].T for i in range(3))
+        for mask in range(4):
+            column = at_quarter(place ^ mask, width)
+            target = sent if mask % 2 else kept
+            out_part = dot_nn(hidden, w_all[2, :, column])
+            in_part = dot_nn(d_gate, w_all[0, :, column]) + dot_nn(d_up, w_all[1, :, column])
+            target[mask // 2, rows, :] = out_part.astype(target.dtype)
+            target[mask // 2, lower, :] = in_part.astype(target.dtype)
+
+
+def outer(units, router, w_part, last):
+    _, half, total = units.shape
+    width = last.shape[2]
+    features = w_part.shape[2]
+    return pl.pallas_call(
+        outer_kernel,
         out_shape=(
             jax.ShapeDtypeStruct((2, packet_rows(total), width), jnp.float32),
             jax.ShapeDtypeStruct((2, packet_rows(total), width), jnp.bfloat16),
-        )
-        + tuple(
-            jax.ShapeDtypeStruct((3, half, width), jnp.bfloat16 if k else jnp.float32)
-            for k in range(4)
-        ),
-        in_specs=[VMEM] * 5,
-        out_specs=[VMEM] * 6,
-        scratch_shapes=[
-            pltpu.VMEM((3, half, total), jnp.bfloat16),
-            pltpu.VMEM((3, half, features), jnp.bfloat16),
-        ],
+        ),
+        in_specs=[VMEM] * 4,
+        out_specs=[VMEM] * 2,
+        scratch_shapes=[pltpu.VMEM((3, half, features), jnp.bfloat16)],
         compiler_params=PARAMS,
         cost_estimate=pl.CostEstimate(
-            flops=12 * 2 * half * features * total, bytes_accessed=0, transcendentals=0
-        ),
-    )(x_all, s_all, w_part, part, last)
-
-
-def join_kernel(own, got_x, got_z, got_d, *outs):
+            flops=6 * half * features * total, bytes_accessed=0, transcendentals=0
+        ),
+    )(units, router, w_part, last)
+
+
+def join_kernel(own, got_x, got_z, *outs):
     half = own.shape[1]
     x_bit = lax.axis_index("wide") % 2
     keep_rows = pl.ds(pl.multiple_of(x_bit * half, 16), half)
     give_rows = pl.ds(pl.multiple_of((1 - x_bit) * half, 16), half)
     for i, ref in enumerate(outs):
         ref[keep_rows, :] = own[i] + got_z[i].astype(jnp.float32)
-        ref[give_rows, :] = got_x[i].astype(jnp.float32) + got_d[i].astype(jnp.float32)
-
-
-def join_grads(own, got_x, got_z, got_d):
+        ref[give_rows, :] = got_x[i].astype(jnp.float32)
+
+
+def join_grads(own, got_x, got_z):
     _, half, width = own.shape
     shape = jax.ShapeDtypeStruct((2 * half, width), jnp.float32)
     return pl.pallas_call(
         join_kernel,
         out_shape=(shape,) * 3,
-        in_specs=[VMEM] * 4,
+        in_specs=[VMEM] * 3,
         out_specs=[VMEM] * 3,
         compiler_params=PARAMS,
-    )(own, got_x, got_z, got_d)
+    )(own, got_x, got_z)
 
 
 def cross_kernel(kept, got, sent):
@@ -405,19 +426,22 @@
             routed, "wide", split_axis=0, concat_axis=0, axis_index_groups=groups, tiled=True
         )
 
-    from_x, from_z = lax.optimization_barrier(
-        (partner(give, "wide", 1), partner(keep, "wide", 2))
+    mine, from_x, from_z = lax.optimization_barrier(
+        (mine, partner(give, "wide", 1), partner(keep, "wide", 2))
     )
     from_d = partner(from_x, "wide", 2)
     across = partner(mine, "narrow", 2)
     pieces = (mine, partner(mine, "narrow", 1), across, partner(across, "narrow", 1))
-    held = gather_parts(own, pieces, (keep, from_x, from_z))
-    kept, sent, grad_own, grad_x, grad_z, grad_d = main(*held, from_d)
+    x_all, s_all, w_part, part = gather_parts(own, pieces, (keep, from_x, from_z))
+    units, router, grad_own, grad_x, grad_z, grad_d = inner(x_all, s_all, part, from_d)
+    kept, sent = outer(units, router, w_part, from_d)
 
     got = partner(sent, "narrow", 1)
+    got_d = partner(grad_d, "wide", 2)
+    grad_x = (grad_x + got_d.astype(jnp.float32)).astype(jnp.bfloat16)
+    grad_x, grad_z = lax.optimization_barrier((grad_x, grad_z))
     got_x = partner(grad_x, "wide", 1)
     got_z = partner(grad_z, "wide", 2)
-    got_d = partner(grad_d, "wide", 3)
     across = partner(cross_part(kept, got), "narrow", 2)
     if direct:
         parts = result_parts(kept, got, across, len(masks) + 1)
@@ -446,7 +470,7 @@
         ffn = back[0].astype(jnp.bfloat16).astype(jnp.float32)
         output = (route_prob[:, None] * ffn).astype(jnp.bfloat16)
         tokens_grad = back[1].astype(jnp.bfloat16)
-    gate_grad, up_grad, down_grad = join_grads(grad_own, got_x, got_z, got_d)
+    gate_grad, up_grad, down_grad = join_grads(grad_own, got_x, got_z)
     return (output, tokens_grad, prob_grad, gate_grad.T, up_grad.T, down_grad.T)
 
 

time: 121 us -> 81.1 us (0.67)
  Pallas kernels: 43 us -> 9.92 us
  waiting for transfers between devices: 51.7 us -> 47.7 us
  local copies, waits for them, and re-layouts: 2.09 us -> 0.01 us
    pallas_call x1, Pallas kernels: 34.8 us -> 1.47 us  [prologue(): pl.pallas_call(functools.partial(prologue_kernel, bool(token_args)), out_...]
    ppermute x17, waiting for transfers between devices: 51.7 us -> 47.7 us  [partner(): lax.ppermute(x, axis, [(i, i ^ mask) for i in range(lax.axis_size(axis))])]
    unnamed x6 -> x2, local copies, waits for them, and re-layouts: 2.09 us -> 0.01 us
    pallas_call x2 -> x3, Pallas kernels: 5.33 us -> 5.56 us  [the longest x1 2.05 us: outer(): pl.pallas_call(outer_kernel, out_shape=(jax.ShapeDtypeStruct((2, packet_r...]
  transfers between devices with their start and end apart: 17 -> 17, of which waited for: 7 -> 10; matrix products, arithmetic and copies ran while one was open for 0% -> 0% of each run, Pallas kernels for 3% -> 4%
where the time goes in v4:
time: 81.1 us; the launch traced here: 81 us
  waiting for transfers between devices  47.7 us (59%)
  starting transfers between devices  22.4 us (28%)
  Pallas kernels  9.92 us (12%)
    ppermute x17, waiting for transfers between devices, partner(): lax.ppermute(x, axis, [(i, i ^ mask) for i in range(lax.axis_size(axis))])  47.7 us
    ppermute x17, starting transfers between devices, partner(): lax.ppermute(x, axis, [(i, i ^ mask) for i in range(lax.axis_size(axis))])  22.4 us
    pallas_call x1, Pallas kernels, outer(): pl.pallas_call(outer_kernel, out_shape=(jax.ShapeDtypeStruct((2, packet_r...  2.05 us
    pallas_call x1, Pallas kernels, inner(): pl.pallas_call(inner_kernel, out_shape=(jax.ShapeDtypeStruct((3, half, to...  2.01 us
    pallas_call x1, Pallas kernels, gather_parts(): pl.pallas_call(functools.partial(gather_kernel, int(has_own)), out_shape=...  1.75 us
  transfers between devices with their start and end apart: 17, of which 10 were waited for; matrix products, arithmetic and copies ran while one was open for 0% of the time, Pallas kernels for 4%

profile of v4, /device:TPU:0, one launch (start us, length us, event | category | flops | bytes accessed | tf_op | source)
XLA Modules:
  0.0 81.0 jit_solution(17239578055067802470)
XLA Ops:
  0.6 1.5 %shard_map.118 = (bf16[3,352,256]{2,1,0:T(8,128)(2,1)S(1)}, bf16[3,352,256]{2,1,0:T(8,128)(2,1)S(1)}, bf16[2,128,1024]{2,1,0:T(8,128)(2,1)S(1)}, bf16[2,128,256]...) custom-call(bf16[704,256]{1,0:T(8,128)(2,1)} %bitcast.14, bf16[704,256]{1,0:T(8,128)(2,1)} %bitcast.15, ...), custom_call_target="tpu_custom_call" | custom-call | tf_op jit(solution)/shard_map/pallas_call | solution.py:103
  2.1 3.0 %collective-permute-start.3 = (bf16[3,352,256]{2,1,0:T(8,128)(2,1)S(1)}, bf16[3,352,256]{2,1,0:T(8,128)(2,1)S(1)}, u32[]{:S(2)}, u32[]{:S(2)}) collective-permute-start(bf16[3,352,256]{2,1,0:T(8,128)(2,1)S(1)} %get-tuple-element.41), channel_id=1, source_target_pairs={{0,4},{4,0},{8,12},{12,8},{16,20},{20,16},{24,28},{28,24},{1,5},{5... | collective-permute-start | bytes 1622024 | tf_op jit(solution)/shard_map/ppermute | solution.py:17
  5.1 1.6 %collective-permute-start.4 = (bf16[3,352,256]{2,1,0:T(8,128)(2,1)S(1)}, bf16[3,352,256]{2,1,0:T(8,128)(2,1)S(1)}, u32[]{:S(2)}, u32[]{:S(2)}) collective-permute-start(bf16[3,352,256]{2,1,0:T(8,128)(2,1)S(1)} %get-tuple-element.42.refs_5_), channel_id=1, source_target_pairs={{0,8},{4,12},{8,0},{12,4},{16,24},{20,28},{24,16},{28,20},{1,9},{5... | collective-permute-start | bytes 1622024 | tf_op jit(solution)/shard_map/ppermute | solution.py:17
  7.2 3.5 %collective-permute-start.2 = (bf16[2,128,256]{2,1,0:T(8,128)(2,1)S(1)}, bf16[2,128,256]{2,1,0:T(8,128)(2,1)S(1)}, u32[]{:S(2)}, u32[]{:S(2)}) collective-permute-start(bf16[2,128,256]{2,1,0:T(8,128)(2,1)S(1)} %get-tuple-element.40), channel_id=1, source_target_pairs={{0,20},{4,16},{8,28},{12,24},{16,4},{20,0},{24,12},{28,8},{1,21},{... | collective-permute-start | bytes 393224 | tf_op jit(solution)/shard_map/ppermute | solution.py:17
  11.1 11.9 %collective-permute-done = bf16[2,128,256]{2,1,0:T(8,128)(2,1)S(1)} collective-permute-done((bf16[2,128,256]{2,1,0:T(8,128)(2,1)S(1)}, bf16[2,128,256]{2,1,0:T(8,128)(2,1)S(1)}, u32[]{:S(2)}, u32[]{:S(2)}) %collective-permute-start) | collective-permute-done | bytes 131104 | tf_op jit(solution)/shard_map/ppermute | solution.py:17
  23.6 0.8 %collective-permute-done.4.refs_7_ = bf16[3,352,256]{2,1,0:T(8,128)(2,1)S(1)} collective-permute-done((bf16[3,352,256]{2,1,0:T(8,128)(2,1)S(1)}, bf16[3,352,256]{2,1,0:T(8,128)(2,1)S(1)}, u32[]{:S(2)}, u32[]{:S(2)}) %collective-permute-start.4) | collective-permute-done | bytes 540704 | tf_op jit(solution)/shard_map/ppermute | solution.py:17
  24.5 1.5 %collective-permute-start.6 = (bf16[3,2,128,256]{3,2,1,0:T(8,128)(2,1)S(1)}, bf16[3,2,128,256]{3,2,1,0:T(8,128)(2,1)S(1)}, u32[]{:S(2)}, u32[]{:S(2)}) collective-permute-start(bf16[3,2,128,256]{3,2,1,0:T(8,128)(2,1)S(1)} %pad_maximum_fusion.refs_1_), channel_id=1, source_target_pairs={{0,2},{1,3},{2,0},{3,1},{4,6},{5,7},{6,4},{7,5},{8,10},{9,11},{10,... | collective-permute-start | bytes 1179656 | tf_op jit(solution)/shard_map/ppermute | solution.py:17
  26.0 2.7 %collective-permute-start.8 = (bf16[3,352,256]{2,1,0:T(8,128)(2,1)S(1)}, bf16[3,352,256]{2,1,0:T(8,128)(2,1)S(1)}, u32[]{:S(2)}, u32[]{:S(2)}) collective-permute-start(bf16[3,352,256]{2,1,0:T(8,128)(2,1)S(1)} %collective-permute-done.3.refs_6_), channel_id=1, source_target_pairs={{0,8},{4,12},{8,0},{12,4},{16,24},{20,28},{24,16},{28,20},{1,9},{5... | collective-permute-start | bytes 1622024 | tf_op jit(solution)/shard_map/ppermute | solution.py:17
  28.7 5.4 %collective-permute-done.6.refs_3_ = bf16[3,2,128,256]{3,2,1,0:T(8,128)(2,1)S(1)} collective-permute-done((bf16[3,2,128,256]{3,2,1,0:T(8,128)(2,1)S(1)}, bf16[3,2,128,256]{3,2,1,0:T(8,128)(2,1)S(1)}, u32[]{:S(2)}, u32[]{:S(2)}) %collective-permute-start.6) | collective-permute-done | bytes 393248 | tf_op jit(solution)/shard_map/ppermute | solution.py:17
  34.1 1.7 %collective-permute-done.7.refs_4_ = bf16[3,2,128,256]{3,2,1,0:T(8,128)(2,1)S(1)} collective-permute-done((bf16[3,2,128,256]{3,2,1,0:T(8,128)(2,1)S(1)}, bf16[3,2,128,256]{3,2,1,0:T(8,128)(2,1)S(1)}, u32[]{:S(2)}, u32[]{:S(2)}) %collective-permute-start.7) | collective-permute-done | bytes 393248 | tf_op jit(solution)/shard_map/ppermute | solution.py:17
  35.9 1.7 %shard_map.119 = (bf16[512,1024]{1,0:T(8,128)(2,1)S(1)}, bf16[512,1024]{1,0:T(8,128)(2,1)S(1)}, bf16[3,352,1024]{2,1,0:T(8,128)(2,1)S(1)}, f32[3,352,512]{2,1,0:T(8,128)S(1)}) custom-call(bf16[2,128,1024]{2,1,0:T(8,128)(2,1)S(1)} %get-tuple-element.38.refs_0_, bf16[3,2,128,256]{3,2,1,0:T(8,128)(2,1)S(1)} %pad_maximum_fusion.refs_1_, ...), custom_call_target="tpu_custom_call" | custom-call | flops 1 | bytes 1 | tf_op jit(solution)/shard_map/pallas_call | solution.py:157
  37.6 1.9 %collective-permute-done.8.last = bf16[3,352,256]{2,1,0:T(8,128)(2,1)S(1)} collective-permute-done((bf16[3,352,256]{2,1,0:T(8,128)(2,1)S(1)}, bf16[3,352,256]{2,1,0:T(8,128)(2,1)S(1)}, u32[]{:S(2)}, u32[]{:S(2)}) %collective-permute-start.8) | collective-permute-done | bytes 540704 | tf_op jit(solution)/shard_map/ppermute | solution.py:17
  39.5 2.0 %shard_map.120 = (bf16[3,352,512]{2,1,0:T(8,128)(2,1)S(1)}, f32[2,256]{1,0:T(2,128)S(1)}, f32[3,352,256]{2,1,0:T(8,128)S(1)}, f32[3,352,256]{2,1,0:T(8,128)S(1)}...) custom-call(bf16[512,1024]{1,0:T(8,128)(2,1)S(1)} %get-tuple-element.46.x_all, ...), custom_call_target="tpu_custom_call" | custom-call | flops 1476395008 | tf_op jit(solution)/shard_map/pallas_call | solution.py:209
  41.5 2.0 %shard_map.121 = (f32[2,1040,256]{2,1,0:T(8,128)S(1)}, bf16[2,1040,256]{2,1,0:T(8,128)(2,1)S(1)}) custom-call(bf16[3,352,512]{2,1,0:T(8,128)(2,1)S(1)} %get-tuple-element.49.units, f32[2,256]{1,0:T(2,128)S(1)} %get-tuple-element.50.router, bf16[3,352,1024]{2,1,0:T(8,128)(2,1)S(1)} %get-tuple-element.51.w_part, ...), custom_call_target="tpu_custom_call" | custom-call | flops 1107296256 | tf_op jit(solution)/shard_map/pallas_call | solution.py:258
  43.7 1.8 %collective-permute-start.14 = (bf16[3,352,256]{2,1,0:T(8,128)(2,1)S(1)}, bf16[3,352,256]{2,1,0:T(8,128)(2,1)S(1)}, u32[]{:S(2)}, u32[]{:S(2)}) collective-permute-start(bf16[3,352,256]{2,1,0:T(8,128)(2,1)S(1)} %get-tuple-element.63), channel_id=1, source_target_pairs={{0,8},{4,12},{8,0},{12,4},{16,24},{20,28},{24,16},{28,20},{1,9},{5... | collective-permute-start | bytes 1622024 | tf_op jit(solution)/shard_map/ppermute | solution.py:17
  45.5 0.9 %collective-permute-done.9.got = bf16[2,1040,256]{2,1,0:T(8,128)(2,1)S(1)} collective-permute-done((bf16[2,1040,256]{2,1,0:T(8,128)(2,1)S(1)}, bf16[2,1040,256]{2,1,0:T(8,128)(2,1)S(1)}, u32[]{:S(2)}, u32[]{:S(2)}) %collective-permute-start.9) | collective-permute-done | bytes 1064992 | tf_op jit(solution)/shard_map/ppermute | solution.py:17
  47.0 11.3 %collective-permute-done.14 = bf16[3,352,256]{2,1,0:T(8,128)(2,1)S(1)} collective-permute-done((bf16[3,352,256]{2,1,0:T(8,128)(2,1)S(1)}, bf16[3,352,256]{2,1,0:T(8,128)(2,1)S(1)}, u32[]{:S(2)}, u32[]{:S(2)}) %collective-permute-start.14) | collective-permute-done | bytes 540704 | tf_op jit(solution)/shard_map/ppermute | solution.py:17
  59.1 1.7 %collective-permute-start.16 = (bf16[3,352,256]{2,1,0:T(8,128)(2,1)S(1)}, bf16[3,352,256]{2,1,0:T(8,128)(2,1)S(1)}, u32[]{:S(2)}, u32[]{:S(2)}) collective-permute-start(bf16[3,352,256]{2,1,0:T(8,128)(2,1)S(1)} %get-tuple-element.66), channel_id=1, source_target_pairs={{0,8},{4,12},{8,0},{12,4},{16,24},{20,28},{24,16},{28,20},{1,9},{5... | collective-permute-start | bytes 1622024 | tf_op jit(solution)/shard_map/ppermute | solution.py:17
  61.0 1.6 %collective-permute-start.11 = (bf16[272,256]{1,0:T(8,128)(2,1)S(1)}, bf16[272,256]{1,0:T(8,128)(2,1)S(1)}, u32[]{:S(2)}, u32[]{:S(2)}) collective-permute-start(bf16[272,256]{1,0:T(8,128)(2,1)S(1)} %get-tuple-element.55), channel_id=1, source_target_pairs={{0,4},{4,0},{8,12},{12,8},{16,20},{20,16},{24,28},{28,24},{1,5},{5... | collective-permute-start | bytes 417800 | tf_op jit(solution)/shard_map/ppermute | solution.py:17
  62.6 1.4 %collective-permute-start.12 = (bf16[272,256]{1,0:T(8,128)(2,1)S(1)}, bf16[272,256]{1,0:T(8,128)(2,1)S(1)}, u32[]{:S(2)}, u32[]{:S(2)}) collective-permute-start(bf16[272,256]{1,0:T(8,128)(2,1)S(1)} %get-tuple-element.56), channel_id=1, source_target_pairs={{0,16},{4,20},{8,24},{12,28},{16,0},{20,4},{24,8},{28,12},{1,17},{... | collective-permute-start | bytes 417800 | tf_op jit(solution)/shard_map/ppermute | solution.py:17
  64.1 1.4 %collective-permute-start.13 = (bf16[272,256]{1,0:T(8,128)(2,1)S(1)}, bf16[272,256]{1,0:T(8,128)(2,1)S(1)}, u32[]{:S(2)}, u32[]{:S(2)}) collective-permute-start(bf16[272,256]{1,0:T(8,128)(2,1)S(1)} %get-tuple-element.57), channel_id=1, source_target_pairs={{0,20},{4,16},{8,28},{12,24},{16,4},{20,0},{24,12},{28,8},{1,21},{... | collective-permute-start | bytes 417800 | tf_op jit(solution)/shard_map/ppermute | solution.py:17
  65.5 11.3 %collective-permute-done.15.got_x = bf16[3,352,256]{2,1,0:T(8,128)(2,1)S(1)} collective-permute-done((bf16[3,352,256]{2,1,0:T(8,128)(2,1)S(1)}, bf16[3,352,256]{2,1,0:T(8,128)(2,1)S(1)}, u32[]{:S(2)}, u32[]{:S(2)}) %collective-permute-start.15) | collective-permute-done | bytes 540704 | tf_op jit(solution)/shard_map/ppermute | solution.py:17
  76.8 1.9 %collective-permute-done.16.got_z = bf16[3,352,256]{2,1,0:T(8,128)(2,1)S(1)} collective-permute-done((bf16[3,352,256]{2,1,0:T(8,128)(2,1)S(1)}, bf16[3,352,256]{2,1,0:T(8,128)(2,1)S(1)}, u32[]{:S(2)}, u32[]{:S(2)}) %collective-permute-start.16) | collective-permute-done | bytes 540704 | tf_op jit(solution)/shard_map/ppermute | solution.py:17
  78.6 1.5 %shard_map.125 = (f32[704,256]{1,0:T(8,128)}, f32[704,256]{1,0:T(8,128)}, f32[704,256]{1,0:T(8,128)}) custom-call(f32[3,352,256]{2,1,0:T(8,128)S(1)} %get-tuple-element.61.own, bf16[3,352,256]{2,1,0:T(8,128)(2,1)S(1)} %collective-permute-done.15.got_x, bf16[3,352,256]{2,1,0:T(8,128)(2,1)S(1)} %collective-permute-done.16.got_z), custom_call_target="tpu_custom_call" | custom-call | tf_op jit(solution)/shard_map/pallas_call | solution.py:287
  (22 shorter events, 4.0 us)
Async XLA Ops:
  2.1 21.5 %collective-permute-start.3 = (bf16[3,352,256]{2,1,0:T(8,128)(2,1)S(1)}, bf16[3,352,256]{2,1,0:T(8,128)(2,1)S(1)}, u32[]{:S(2)}, u32[]{:S(2)}) collective-permute-start(bf16[3,352,256]{2,1,0:T(8,128)(2,1)S(1)} %get-tuple-element.41), channel_id=1, source_target_pairs={{0,4},{4,0},{8,12},{12,8},{16,20},{20,16},{24,28},{28,24},{1,5},{5... | collective-permute-start | bytes 1622024 | tf_op jit(solution)/shard_map/ppermute | solution.py:17
  5.1 19.4 %collective-permute-start.4 = (bf16[3,352,256]{2,1,0:T(8,128)(2,1)S(1)}, bf16[3,352,256]{2,1,0:T(8,128)(2,1)S(1)}, u32[]{:S(2)}, u32[]{:S(2)}) collective-permute-start(bf16[3,352,256]{2,1,0:T(8,128)(2,1)S(1)} %get-tuple-element.42.refs_5_), channel_id=1, source_target_pairs={{0,8},{4,12},{8,0},{12,4},{16,24},{20,28},{24,16},{28,20},{1,9},{5... | collective-permute-start | bytes 1622024 | tf_op jit(solution)/shard_map/ppermute | solution.py:17
  6.7 16.3 %collective-permute-start = (bf16[2,128,256]{2,1,0:T(8,128)(2,1)S(1)}, bf16[2,128,256]{2,1,0:T(8,128)(2,1)S(1)}, u32[]{:S(2)}, u32[]{:S(2)}) collective-permute-start(bf16[2,128,256]{2,1,0:T(8,128)(2,1)S(1)} %get-tuple-element.39), channel_id=1, source_target_pairs={{0,4},{4,0},{8,12},{12,8},{16,20},{20,16},{24,28},{28,24},{1,5},{5... | collective-permute-start | bytes 393224 | tf_op jit(solution)/shard_map/ppermute | solution.py:17
  7.2 15.8 %collective-permute-start.2 = (bf16[2,128,256]{2,1,0:T(8,128)(2,1)S(1)}, bf16[2,128,256]{2,1,0:T(8,128)(2,1)S(1)}, u32[]{:S(2)}, u32[]{:S(2)}) collective-permute-start(bf16[2,128,256]{2,1,0:T(8,128)(2,1)S(1)} %get-tuple-element.40), channel_id=1, source_target_pairs={{0,20},{4,16},{8,28},{12,24},{16,4},{20,0},{24,12},{28,8},{1,21},{... | collective-permute-start | bytes 393224 | tf_op jit(solution)/shard_map/ppermute | solution.py:17
  10.7 12.8 %collective-permute-start.1 = (bf16[2,128,256]{2,1,0:T(8,128)(2,1)S(1)}, bf16[2,128,256]{2,1,0:T(8,128)(2,1)S(1)}, u32[]{:S(2)}, u32[]{:S(2)}) collective-permute-start(bf16[2,128,256]{2,1,0:T(8,128)(2,1)S(1)} %get-tuple-element.40), channel_id=1, source_target_pairs={{0,16},{4,20},{8,24},{12,28},{16,0},{20,4},{24,8},{28,12},{1,17},{... | collective-permute-start | bytes 393224 | tf_op jit(solution)/shard_map/ppermute | solution.py:17
  24.5 9.7 %collective-permute-start.6 = (bf16[3,2,128,256]{3,2,1,0:T(8,128)(2,1)S(1)}, bf16[3,2,128,256]{3,2,1,0:T(8,128)(2,1)S(1)}, u32[]{:S(2)}, u32[]{:S(2)}) collective-permute-start(bf16[3,2,128,256]{3,2,1,0:T(8,128)(2,1)S(1)} %pad_maximum_fusion.refs_1_), channel_id=1, source_target_pairs={{0,2},{1,3},{2,0},{3,1},{4,6},{5,7},{6,4},{7,5},{8,10},{9,11},{10,... | collective-permute-start | bytes 1179656 | tf_op jit(solution)/shard_map/ppermute | solution.py:17
  26.0 13.5 %collective-permute-start.8 = (bf16[3,352,256]{2,1,0:T(8,128)(2,1)S(1)}, bf16[3,352,256]{2,1,0:T(8,128)(2,1)S(1)}, u32[]{:S(2)}, u32[]{:S(2)}) collective-permute-start(bf16[3,352,256]{2,1,0:T(8,128)(2,1)S(1)} %collective-permute-done.3.refs_6_), channel_id=1, source_target_pairs={{0,8},{4,12},{8,0},{12,4},{16,24},{20,28},{24,16},{28,20},{1,9},{5... | collective-permute-start | bytes 1622024 | tf_op jit(solution)/shard_map/ppermute | solution.py:17
  28.7 5.4 %collective-permute-start.5 = (bf16[3,2,128,256]{3,2,1,0:T(8,128)(2,1)S(1)}, bf16[3,2,128,256]{3,2,1,0:T(8,128)(2,1)S(1)}, u32[]{:S(2)}, u32[]{:S(2)}) collective-permute-start(bf16[3,2,128,256]{3,2,1,0:T(8,128)(2,1)S(1)} %pad_maximum_fusion.refs_1_), channel_id=1, source_target_pairs={{0,1},{1,0},{2,3},{3,2},{4,5},{5,4},{6,7},{7,6},{8,9},{9,8},{10,11... | collective-permute-start | bytes 1179656 | tf_op jit(solution)/shard_map/ppermute | solution.py:17
  34.1 1.7 %collective-permute-start.7 = (bf16[3,2,128,256]{3,2,1,0:T(8,128)(2,1)S(1)}, bf16[3,2,128,256]{3,2,1,0:T(8,128)(2,1)S(1)}, u32[]{:S(2)}, u32[]{:S(2)}) collective-permute-start(bf16[3,2,128,256]{3,2,1,0:T(8,128)(2,1)S(1)} %collective-permute-done.6.refs_3_), channel_id=1, source_target_pairs={{0,1},{1,0},{2,3},{3,2},{4,5},{5,4},{6,7},{7,6},{8,9},{9,8},{10,11... | collective-permute-start | bytes 1179656 | tf_op jit(solution)/shard_map/ppermute | solution.py:17
  43.6 2.7 %collective-permute-start.9 = (bf16[2,1040,256]{2,1,0:T(8,128)(2,1)S(1)}, bf16[2,1040,256]{2,1,0:T(8,128)(2,1)S(1)}, u32[]{:S(2)}, u32[]{:S(2)}) collective-permute-start(bf16[2,1040,256]{2,1,0:T(8,128)(2,1)S(1)} %get-tuple-element.53), channel_id=1, source_target_pairs={{0,1},{1,0},{2,3},{3,2},{4,5},{5,4},{6,7},{7,6},{8,9},{9,8},{10,11... | collective-permute-start | bytes 3194888 | tf_op jit(solution)/shard_map/ppermute | solution.py:17
  43.7 14.7 %collective-permute-start.14 = (bf16[3,352,256]{2,1,0:T(8,128)(2,1)S(1)}, bf16[3,352,256]{2,1,0:T(8,128)(2,1)S(1)}, u32[]{:S(2)}, u32[]{:S(2)}) collective-permute-start(bf16[3,352,256]{2,1,0:T(8,128)(2,1)S(1)} %get-tuple-element.63), channel_id=1, source_target_pairs={{0,8},{4,12},{8,0},{12,4},{16,24},{20,28},{24,16},{28,20},{1,9},{5... | collective-permute-start | bytes 1622024 | tf_op jit(solution)/shard_map/ppermute | solution.py:17
  46.5 14.4 %collective-permute-start.10 = (bf16[1040,256]{1,0:T(8,128)(2,1)S(1)}, bf16[1040,256]{1,0:T(8,128)(2,1)S(1)}, u32[]{:S(2)}, u32[]{:S(2)}) collective-permute-start(bf16[1040,256]{1,0:T(8,128)(2,1)S(1)} %shard_map.122), channel_id=1, source_target_pairs={{0,2},{1,3},{2,0},{3,1},{4,6},{5,7},{6,4},{7,5},{8,10},{9,11},{10,... | collective-permute-start | bytes 1597448 | tf_op jit(solution)/shard_map/ppermute | solution.py:17
  58.5 18.2 %collective-permute-start.15 = (bf16[3,352,256]{2,1,0:T(8,128)(2,1)S(1)}, bf16[3,352,256]{2,1,0:T(8,128)(2,1)S(1)}, u32[]{:S(2)}, u32[]{:S(2)}) collective-permute-start(bf16[3,352,256]{2,1,0:T(8,128)(2,1)S(1)} %add_convert_fusion), channel_id=1, source_target_pairs={{0,4},{4,0},{8,12},{12,8},{16,20},{20,16},{24,28},{28,24},{1,5},{5... | collective-permute-start | bytes 1622024 | tf_op jit(solution)/shard_map/ppermute | solution.py:17
  59.1 19.5 %collective-permute-start.16 = (bf16[3,352,256]{2,1,0:T(8,128)(2,1)S(1)}, bf16[3,352,256]{2,1,0:T(8,128)(2,1)S(1)}, u32[]{:S(2)}, u32[]{:S(2)}) collective-permute-start(bf16[3,352,256]{2,1,0:T(8,128)(2,1)S(1)} %get-tuple-element.66), channel_id=1, source_target_pairs={{0,8},{4,12},{8,0},{12,4},{16,24},{20,28},{24,16},{28,20},{1,9},{5... | collective-permute-start | bytes 1622024 | tf_op jit(solution)/shard_map/ppermute | solution.py:17
  61.0 19.1 %collective-permute-start.11 = (bf16[272,256]{1,0:T(8,128)(2,1)S(1)}, bf16[272,256]{1,0:T(8,128)(2,1)S(1)}, u32[]{:S(2)}, u32[]{:S(2)}) collective-permute-start(bf16[272,256]{1,0:T(8,128)(2,1)S(1)} %get-tuple-element.55), channel_id=1, source_target_pairs={{0,4},{4,0},{8,12},{12,8},{16,20},{20,16},{24,28},{28,24},{1,5},{5... | collective-permute-start | bytes 417800 | tf_op jit(solution)/shard_map/ppermute | solution.py:17
  62.6 17.5 %collective-permute-start.12 = (bf16[272,256]{1,0:T(8,128)(2,1)S(1)}, bf16[272,256]{1,0:T(8,128)(2,1)S(1)}, u32[]{:S(2)}, u32[]{:S(2)}) collective-permute-start(bf16[272,256]{1,0:T(8,128)(2,1)S(1)} %get-tuple-element.56), channel_id=1, source_target_pairs={{0,16},{4,20},{8,24},{12,28},{16,0},{20,4},{24,8},{28,12},{1,17},{... | collective-permute-start | bytes 417800 | tf_op jit(solution)/shard_map/ppermute | solution.py:17
  64.1 16.1 %collective-permute-start.13 = (bf16[272,256]{1,0:T(8,128)(2,1)S(1)}, bf16[272,256]{1,0:T(8,128)(2,1)S(1)}, u32[]{:S(2)}, u32[]{:S(2)}) collective-permute-start(bf16[272,256]{1,0:T(8,128)(2,1)S(1)} %get-tuple-element.57), channel_id=1, source_target_pairs={{0,20},{4,16},{8,28},{12,24},{16,4},{20,0},{24,12},{28,8},{1,21},{... | collective-permute-start | bytes 417800 | tf_op jit(solution)/shard_map/ppermute | solution.py:17
  78.6 1.5 %copy-start = (f32[128]{0:T(128)S(1)}, f32[128]{0:T(128)}, u32[]{:S(2)}) copy-start(f32[128]{0:T(128)} %param.10) | copy-start | bytes 1540

commit v5 on v3

--- a/solution.py
+++ b/solution.py
@@ -11,7 +11,6 @@
 HBM = pl.BlockSpec(memory_space=pltpu.HBM)
 EXTRA = 16
 PARAMS = pltpu.CompilerParams(vmem_limit_bytes=32 * 1024 * 1024)
-PROLOGUE_PARAMS = pltpu.CompilerParams(vmem_limit_bytes=61 * 1024 * 1024)
 
 
 def partner(x, axis, mask):
@@ -105,10 +104,10 @@
         functools.partial(prologue_kernel, bool(token_args)),
         out_shape=outs,
         in_specs=[HBM] * (3 + len(token_args)),
-        out_specs=[HBM] * 2 + [VMEM] * (len(outs) - 2),
+        out_specs=[VMEM] * len(outs),
         scratch_shapes=scratch + [pltpu.SemaphoreType.DMA((10,))],
-        compiler_params=PROLOGUE_PARAMS,
-    )(*weights, *token_args)
+        compiler_params=PARAMS,
+    )(*[pltpu.with_memory_space_constraint(x, pltpu.HBM) for x in (*weights, *token_args)])
 
 
 def gather_kernel(has_own, *refs):
@@ -166,29 +165,25 @@
         in_specs=[VMEM] * (7 + has_own),
         out_specs=[VMEM] * 4,
         compiler_params=PARAMS,
-        cost_estimate=pl.CostEstimate(
-            flops=6 * 2 * half * 3 * width * total, bytes_accessed=0, transcendentals=0
-        ),
+        cost_estimate=pl.CostEstimate(flops=1, bytes_accessed=1, transcendentals=0),
     )(*([own] if has_own else []), *pieces, *weights)
 
 
-def main_kernel(x_all, s_all, w_part, part, last, kept, sent, *refs):
-    outs, (grads, w_all) = refs[:4], refs[4:]
-    half, width = last.shape[1:]
-    member = lax.axis_index("wide") % 4
+def outer_kernel(x_all, s_all, w_part, part, last, units, kept, sent, w_all):
+    width = last.shape[2]
     place = lax.axis_index("narrow")
-    last_column = at_quarter(member ^ 3, width)
+    last_column = at_quarter(lax.axis_index("wide") % 4 ^ 3, width)
     w_all[...] = w_part[...]
     for i in range(3):
         w_all[i, :, last_column] = last[i]
     total = x_all.shape[0]
     tile = min(width, total)
-    kept[:, 2 * total :, :] = jnp.zeros_like(kept[:, 2 * total :, :])
-    sent[:, 2 * total :, :] = jnp.zeros_like(sent[:, 2 * total :, :])
-
+    for ref in (kept, sent):
+        ref[:, 2 * total :, :] = jnp.zeros_like(ref[:, 2 * total :, :])
     routers = []
     for step in range(total // tile):
         rows = slice(step * tile, (step + 1) * tile)
+        lower = slice(total + step * tile, total + (step + 1) * tile)
         x_tile, s_tile = x_all[rows, last_column], s_all[rows, last_column]
         gate = part[0, :, rows] + dot_nt(last[0], x_tile)
         up = part[1, :, rows] + dot_nt(last[1], x_tile)
@@ -198,78 +193,94 @@
         hidden = (active * up).astype(jnp.bfloat16)
         d_gate = (d_hidden * up * sigma * (1.0 + gate * (1.0 - sigma))).astype(jnp.bfloat16)
         d_up = (d_hidden * active).astype(jnp.bfloat16)
-        grads[0, :, rows] = d_gate
-        grads[1, :, rows] = d_up
-        grads[2, :, rows] = hidden
+        units[0, :, rows] = d_gate
+        units[1, :, rows] = d_up
+        units[2, :, rows] = hidden
+        router = jnp.sum(hidden.astype(jnp.float32) * d_hidden, axis=0, keepdims=True)
+        kept[0, 2 * total + step : 2 * total + step + 1, :tile] = router
+        routers.append(router)
         hidden_t, d_gate_t, d_up_t = hidden.T, d_gate.T, d_up.T
         for mask in range(4):
             column = at_quarter(place ^ mask, width)
+            target = sent if mask % 2 else kept
             out_part = dot_nn(hidden_t, w_all[2, :, column])
             in_part = dot_nn(d_gate_t, w_all[0, :, column]) + dot_nn(d_up_t, w_all[1, :, column])
-            target = sent if mask % 2 else kept
             target[mask // 2, rows, :] = out_part.astype(target.dtype)
-            lower = slice(total + step * tile, total + (step + 1) * tile)
             target[mask // 2, lower, :] = in_part.astype(target.dtype)
-        router = jnp.sum(hidden.astype(jnp.float32) * d_hidden, axis=0, keepdims=True)
-        kept[0, 2 * total + step : 2 * total + step + 1, :tile] = router
-        routers.append(router)
     put_pair(sent.at[0], 2 * total, jnp.concatenate(routers, 0))
 
-    left = grads[0:2].reshape(2 * half, total)
+
+def outer(x_all, s_all, w_part, part, last):
+    total, features = x_all.shape
+    _, half, width = last.shape
+    return pl.pallas_call(
+        outer_kernel,
+        out_shape=(
+            jax.ShapeDtypeStruct((3, half, total), jnp.bfloat16),
+            jax.ShapeDtypeStruct((2, packet_rows(total), width), jnp.float32),
+            jax.ShapeDtypeStruct((2, packet_rows(total), width), jnp.bfloat16),
+        ),
+        in_specs=[VMEM] * 5,
+        out_specs=[VMEM] * 3,
+        scratch_shapes=[pltpu.VMEM((3, half, features), jnp.bfloat16)],
+        compiler_params=PARAMS,
+        cost_estimate=pl.CostEstimate(
+            flops=8 * half * features * total, bytes_accessed=0, transcendentals=0
+        ),
+    )(x_all, s_all, w_part, part, last)
+
+
+def grads_kernel(units, x_all, s_all, *outs):
+    half, total = units.shape[1:]
+    width = outs[0].shape[2]
+    member = lax.axis_index("wide") % 4
+    left = units[0:2].reshape(2 * half, total)
     for k in (3, 2, 1, 0):
         column = at_quarter(member ^ k, width)
         both = dot_nn(left, x_all[:, column])
         outs[k][0] = both[:half].astype(outs[k].dtype)
         outs[k][1] = both[half:].astype(outs[k].dtype)
-        outs[k][2] = dot_nn(grads[2], s_all[:, column]).astype(outs[k].dtype)
-
-
-def main(x_all, s_all, w_part, part, last):
-    total, features = x_all.shape
-    _, half, width = last.shape
-    return pl.pallas_call(
-        main_kernel,
-        out_shape=(
-            jax.ShapeDtypeStruct((2, packet_rows(total), width), jnp.float32),
-            jax.ShapeDtypeStruct((2, packet_rows(total), width), jnp.bfloat16),
-        )
-        + tuple(
-            jax.ShapeDtypeStruct((3, half, width), jnp.bfloat16 if k else jnp.float32)
+        outs[k][2] = dot_nn(units[2], s_all[:, column]).astype(outs[k].dtype)
+
+
+def weight_grads(units, x_all, s_all):
+    half, total = units.shape[1:]
+    features = x_all.shape[1]
+    return pl.pallas_call(
+        grads_kernel,
+        out_shape=tuple(
+            jax.ShapeDtypeStruct((3, half, features // 4), jnp.bfloat16 if k > 1 else jnp.float32)
             for k in range(4)
         ),
-        in_specs=[VMEM] * 5,
-        out_specs=[VMEM] * 6,
-        scratch_shapes=[
-            pltpu.VMEM((3, half, total), jnp.bfloat16),
-            pltpu.VMEM((3, half, features), jnp.bfloat16),
-        ],
+        in_specs=[VMEM] * 3,
+        out_specs=[VMEM] * 4,
         compiler_params=PARAMS,
         cost_estimate=pl.CostEstimate(
-            flops=12 * 2 * half * features * total, bytes_accessed=0, transcendentals=0
-        ),
-    )(x_all, s_all, w_part, part, last)
-
-
-def join_kernel(own, got_x, got_z, got_d, *outs):
+            flops=6 * half * features * total, bytes_accessed=0, transcendentals=0
+        ),
+    )(units, x_all, s_all)
+
+
+def join_kernel(own, got_x, got_z, *outs):
     half = own.shape[1]
     x_bit = lax.axis_index("wide") % 2
     keep_rows = pl.ds(pl.multiple_of(x_bit * half, 16), half)
     give_rows = pl.ds(pl.multiple_of((1 - x_bit) * half, 16), half)
     for i, ref in enumerate(outs):
         ref[keep_rows, :] = own[i] + got_z[i].astype(jnp.float32)
-        ref[give_rows, :] = got_x[i].astype(jnp.float32) + got_d[i].astype(jnp.float32)
-
-
-def join_grads(own, got_x, got_z, got_d):
+        ref[give_rows, :] = got_x[i].astype(jnp.float32)
+
+
+def join_grads(own, got_x, got_z):
     _, half, width = own.shape
     shape = jax.ShapeDtypeStruct((2 * half, width), jnp.float32)
     return pl.pallas_call(
         join_kernel,
         out_shape=(shape,) * 3,
-        in_specs=[VMEM] * 4,
+        in_specs=[VMEM] * 3,
         out_specs=[VMEM] * 3,
         compiler_params=PARAMS,
-    )(own, got_x, got_z, got_d)
+    )(own, got_x, got_z)
 
 
 def cross_kernel(kept, got, sent):
@@ -293,43 +304,147 @@
     )(kept, got)
 
 
-def result_kernel(kept, got, across, *outs):
+def result_kernel(kept, got, across, out):
     total = (kept.shape[1] - EXTRA) // 2
-    width = kept.shape[2]
+    count = total // min(kept.shape[2], total)
+    body, tail = slice(0, 2 * total), slice(2 * total, 2 * total + count)
+    value = kept[0, body, :] + got[0, body, :].astype(jnp.float32)
+    out[body, :] = value + across[body, :].astype(jnp.float32)
+    out[2 * total :, :] = jnp.zeros_like(out[2 * total :, :])
+    router = kept[0, tail, :] + get_pair(got.at[0], 2 * total, count)
+    out[tail, :] = router + get_pair(across, 2 * total, count)
+
+
+def result_parts(kept, got, across):
+    return pl.pallas_call(
+        result_kernel,
+        out_shape=jax.ShapeDtypeStruct(kept.shape[1:], jnp.float32),
+        in_specs=[VMEM] * 3,
+        out_specs=VMEM,
+        compiler_params=PARAMS,
+    )(kept, got, across)
+
+
+def first_kernel(kept, got, to_y, to_x):
+    total = (kept.shape[1] - EXTRA) // 2
+    slots = total // 4
+    count = total // min(kept.shape[2], total)
+    body = slice(0, total)
+    to_y[body, :] = (kept[1, body, :] + got[1, body, :].astype(jnp.float32)).astype(to_y.dtype)
+    put_pair(
+        to_y,
+        total,
+        kept[0, 2 * total : 2 * total + count, :] + get_pair(got.at[0], 2 * total, count),
+    )
+    for part in range(2):
+        for block in range(2):
+            rows = slice(total + (2 * block + 1) * slots, total + (2 * block + 2) * slots)
+            value = kept[part, rows, :] + got[part, rows, :].astype(jnp.float32)
+            to_x[part, block * slots : (block + 1) * slots, :] = value.astype(to_x.dtype)
+
+
+def first_parts(kept, got):
+    total, width = (kept.shape[1] - EXTRA) // 2, kept.shape[2]
+    return pl.pallas_call(
+        first_kernel,
+        out_shape=(
+            jax.ShapeDtypeStruct((total + EXTRA, width), jnp.bfloat16),
+            jax.ShapeDtypeStruct((2, total // 2, width), jnp.bfloat16),
+        ),
+        in_specs=[VMEM] * 2,
+        out_specs=[VMEM] * 2,
+        compiler_params=PARAMS,
+    )(kept, got)
+
+
+def ffn_kernel(kept, got, from_y, held, to_x):
+    total = (kept.shape[1] - EXTRA) // 2
+    slots, width = total // 4, kept.shape[2]
     count = total // min(width, total)
     router = kept[0, 2 * total : 2 * total + count, :] + get_pair(got.at[0], 2 * total, count)
-    router = router + get_pair(across, 2 * total, count)
-    slots = (outs[0].shape[0] - EXTRA) // 2
-    for block, out in enumerate(outs):
-        for part in range(2):
-            rows = slice(part * total + block * slots, part * total + (block + 1) * slots)
-            value = kept[0, rows, :] + got[0, rows, :].astype(jnp.float32)
-            value = value + across[rows, :].astype(jnp.float32)
-            out[part * slots : (part + 1) * slots, :] = value.astype(out.dtype)
-        out[2 * slots :, :] = jnp.zeros_like(out[2 * slots :, :])
-        if slots == total:
-            out[2 * slots : 2 * slots + count, :] = router
-        else:
-            lane = block * slots % width
-            mine = router[block * slots // width :, lane : lane + slots][:1]
-            if block:
-                put_pair(out, 2 * slots, mine)
-            else:
-                out[2 * slots : 2 * slots + 1, :slots] = mine
-
-
-def result_parts(kept, got, across, blocks):
+    router = router + get_pair(from_y, total, count)
+    pairs = []
+    for block in range(4):
+        rows = slice(block * slots, (block + 1) * slots)
+        value = kept[0, rows, :] + got[0, rows, :].astype(jnp.float32)
+        value = value + from_y[rows, :].astype(jnp.float32)
+        out = to_x if block % 2 else held
+        place = block // 2
+        out[place * slots : (place + 1) * slots, :] = value.astype(out.dtype)
+        lane = block * slots % width
+        pairs.append(router[block * slots // width :, lane : lane + slots][:1])
+    held[2 * slots :, :] = jnp.zeros_like(held[2 * slots :, :])
+    to_x[2 * slots :, :] = jnp.zeros_like(to_x[2 * slots :, :])
+    held[2 * slots : 2 * slots + 1, :slots] = pairs[0]
+    held[2 * slots + 1 : 2 * slots + 2, :slots] = pairs[2]
+    put_pair(to_x, 2 * slots, jnp.concatenate([pairs[1], pairs[3]], 0))
+
+
+def ffn_parts(kept, got, from_y):
+    total, width = (kept.shape[1] - EXTRA) // 2, kept.shape[2]
+    shape = (total // 2 + EXTRA, width)
+    return pl.pallas_call(
+        ffn_kernel,
+        out_shape=(
+            jax.ShapeDtypeStruct(shape, jnp.float32),
+            jax.ShapeDtypeStruct(shape, jnp.bfloat16),
+        ),
+        in_specs=[VMEM] * 3,
+        out_specs=[VMEM] * 2,
+        compiler_params=PARAMS,
+    )(kept, got, from_y)
+
+
+def input_kernel(kept, got, from_x, held, to_y):
     total = (kept.shape[1] - EXTRA) // 2
-    shape = (packet_rows(total // blocks), kept.shape[2])
-    return pl.pallas_call(
-        result_kernel,
-        out_shape=tuple(
-            jax.ShapeDtypeStruct(shape, jnp.bfloat16 if k else jnp.float32) for k in range(blocks)
+    slots = total // 4
+    for part, out in enumerate((held, to_y)):
+        for block in range(2):
+            rows = slice(total + 2 * block * slots, total + (2 * block + 1) * slots)
+            here = slice(block * slots, (block + 1) * slots)
+            value = kept[part, rows, :] + got[part, rows, :].astype(jnp.float32)
+            out[here, :] = (value + from_x[part, here, :].astype(jnp.float32)).astype(out.dtype)
+
+
+def input_parts(kept, got, from_x):
+    shape = from_x.shape[1:]
+    return pl.pallas_call(
+        input_kernel,
+        out_shape=(
+            jax.ShapeDtypeStruct(shape, jnp.float32),
+            jax.ShapeDtypeStruct(shape, jnp.bfloat16),
         ),
         in_specs=[VMEM] * 3,
-        out_specs=[VMEM] * blocks,
-        compiler_params=PARAMS,
-    )(kept, got, across)
+        out_specs=[VMEM] * 2,
+        compiler_params=PARAMS,
+    )(kept, got, from_x)
+
+
+def last_kernel(ffn, from_x, grad, from_y, held, to_z):
+    slots = grad.shape[0] // 2
+    router = ffn[2 * slots : 2 * slots + 2, :] + get_pair(from_x, 2 * slots, 2)
+    for block, out in enumerate((held, to_z)):
+        rows = slice(block * slots, (block + 1) * slots)
+        out[:slots, :] = (ffn[rows, :] + from_x[rows, :].astype(jnp.float32)).astype(out.dtype)
+        out[slots : 2 * slots, :] = (grad[rows, :] + from_y[rows, :].astype(jnp.float32)).astype(
+            out.dtype
+        )
+    held[2 * slots :, :] = jnp.broadcast_to(router[:1], (EXTRA, router.shape[1]))
+    put_pair(to_z, 2 * slots, router[1:])
+
+
+def last_parts(ffn, from_x, grad, from_y):
+    return pl.pallas_call(
+        last_kernel,
+        out_shape=(
+            jax.ShapeDtypeStruct(ffn.shape, jnp.float32),
+            jax.ShapeDtypeStruct(ffn.shape, jnp.bfloat16),
+        ),
+        in_specs=[VMEM] * 4,
+        out_specs=[VMEM] * 2,
+        compiler_params=PARAMS,
+        cost_estimate=pl.CostEstimate(flops=10**10, bytes_accessed=0, transcendentals=0),
+    )(ffn, from_x, grad, from_y)
 
 
 def finish_kernel(prob, own, *refs):
@@ -405,27 +520,32 @@
             routed, "wide", split_axis=0, concat_axis=0, axis_index_groups=groups, tiled=True
         )
 
-    from_x, from_z = lax.optimization_barrier(
-        (partner(give, "wide", 1), partner(keep, "wide", 2))
+    mine, from_x, from_z = lax.optimization_barrier(
+        (mine, partner(give, "wide", 1), partner(keep, "wide", 2))
     )
     from_d = partner(from_x, "wide", 2)
     across = partner(mine, "narrow", 2)
     pieces = (mine, partner(mine, "narrow", 1), across, partner(across, "narrow", 1))
-    held = gather_parts(own, pieces, (keep, from_x, from_z))
-    kept, sent, grad_own, grad_x, grad_z, grad_d = main(*held, from_d)
-
+    x_all, s_all, w_part, part = gather_parts(own, pieces, (keep, from_x, from_z))
+    units, kept, sent = outer(x_all, s_all, w_part, part, from_d)
     got = partner(sent, "narrow", 1)
-    got_x = partner(grad_x, "wide", 1)
-    got_z = partner(grad_z, "wide", 2)
-    got_d = partner(grad_d, "wide", 3)
-    across = partner(cross_part(kept, got), "narrow", 2)
+    grad_own, grad_x, grad_z, grad_d = weight_grads(units, x_all, s_all)
+    got_d = partner(grad_d, "wide", 2)
     if direct:
-        parts = result_parts(kept, got, across, len(masks) + 1)
-        back = [partner(part, "wide", mask) for mask, part in zip(masks, parts[1:])]
-        output, tokens_grad, prob_grad = finish(route_prob[None, :], parts[0], back)
+        to_y, to_x = first_parts(kept, got)
+        ffn_held, ffn_x = ffn_parts(kept, got, partner(to_y, "narrow", 2))
+        grad_held, grad_y = input_parts(kept, got, partner(to_x, "wide", 1))
+        grad_x, _, _ = lax.optimization_barrier((grad_x, ffn_x, grad_y))
+        held, to_z = last_parts(
+            ffn_held, partner(ffn_x, "wide", 1), grad_held, partner(grad_y, "narrow", 2)
+        )
+        output, tokens_grad, prob_grad = finish(
+            route_prob[None, :], held, [partner(to_z, "wide", 4)]
+        )
         prob_grad = prob_grad[0]
     else:
-        (result,) = result_parts(kept, got, across, 1)
+        across = partner(cross_part(kept, got), "narrow", 2)
+        result = result_parts(kept, got, across)
         total = (result.shape[0] - EXTRA) // 2
         parts = result[: 2 * total].astype(jnp.bfloat16)
         parts = parts.reshape(2, 2 * expert_count, slots, width)
@@ -446,7 +566,11 @@
         ffn = back[0].astype(jnp.bfloat16).astype(jnp.float32)
         output = (route_prob[:, None] * ffn).astype(jnp.bfloat16)
         tokens_grad = back[1].astype(jnp.bfloat16)
-    gate_grad, up_grad, down_grad = join_grads(grad_own, got_x, got_z, got_d)
+    grad_x = (grad_x + got_d.astype(jnp.float32)).astype(jnp.bfloat16)
+    grad_x, grad_z = lax.optimization_barrier((grad_x, grad_z))
+    got_x = partner(grad_x, "wide", 1)
+    got_z = partner(grad_z, "wide", 2)
+    gate_grad, up_grad, down_grad = join_grads(grad_own, got_x, got_z)
     return (output, tokens_grad, prob_grad, gate_grad.T, up_grad.T, down_grad.T)
 
 

time: 121 us -> 77.4 us (0.64)
  Pallas kernels: 43 us -> 9.93 us
  waiting for transfers between devices: 51.7 us -> 44.3 us
  local copies, waits for them, and re-layouts: 2.09 us -> 0.01 us
  starting transfers between devices: 23.6 us -> 22.2 us
    pallas_call x1, Pallas kernels: 34.8 us -> 1.47 us  [prologue(): pl.pallas_call(functools.partial(prologue_kernel, bool(token_args)), out_...]
    ppermute x17 -> x18, waiting for transfers between devices: 51.7 us -> 44.3 us  [partner(): lax.ppermute(x, axis, [(i, i ^ mask) for i in range(lax.axis_size(axis))])]
    unnamed x6 -> x2, local copies, waits for them, and re-layouts: 2.09 us -> 0.01 us
    ppermute x17 -> x18, starting transfers between devices: 23.6 us -> 22.2 us  [partner(): lax.ppermute(x, axis, [(i, i ^ mask) for i in range(lax.axis_size(axis))])]
    pallas_call x4 -> x7, Pallas kernels: 5.58 us -> 5.9 us  [the longest x1 2.76 us: outer(): pl.pallas_call(outer_kernel, out_shape=(jax.ShapeDtypeStruct((3, half, to...]
  transfers between devices with their start and end apart: 17 -> 18, of which waited for: 7 -> 10; matrix products, arithmetic and copies ran while one was open for 0% -> 0% of each run, Pallas kernels for 3% -> 5%
where the time goes in v5:
time: 77.4 us; the launch traced here: 77.3 us
  waiting for transfers between devices  44.3 us (57%)
  starting transfers between devices  22.2 us (29%)
  Pallas kernels  9.93 us (13%)
    ppermute x18, waiting for transfers between devices, partner(): lax.ppermute(x, axis, [(i, i ^ mask) for i in range(lax.axis_size(axis))])  44.3 us
    ppermute x18, starting transfers between devices, partner(): lax.ppermute(x, axis, [(i, i ^ mask) for i in range(lax.axis_size(axis))])  22.2 us
    pallas_call x1, Pallas kernels, outer(): pl.pallas_call(outer_kernel, out_shape=(jax.ShapeDtypeStruct((3, half, to...  2.76 us
    pallas_call x1, Pallas kernels, gather_parts(): pl.pallas_call(functools.partial(gather_kernel, int(has_own)), out_shape=...  1.75 us
  transfers between devices with their start and end apart: 18, of which 10 were waited for; matrix products, arithmetic and copies ran while one was open for 0% of the time, Pallas kernels for 5%

profile of v5, /device:TPU:0, one launch (start us, length us, event | category | flops | bytes accessed | tf_op | source)
XLA Modules:
  0.0 77.3 jit_solution(2812020814421330224)
XLA Ops:
  0.6 1.5 %shard_map.118 = (bf16[3,352,256]{2,1,0:T(8,128)(2,1)S(1)}, bf16[3,352,256]{2,1,0:T(8,128)(2,1)S(1)}, bf16[2,128,1024]{2,1,0:T(8,128)(2,1)S(1)}, bf16[2,128,256]...) custom-call(bf16[704,256]{1,0:T(8,128)(2,1)} %bitcast.14, bf16[704,256]{1,0:T(8,128)(2,1)} %bitcast.15, ...), custom_call_target="tpu_custom_call" | custom-call | tf_op jit(solution)/shard_map/pallas_call | solution.py:103
  2.1 3.0 %collective-permute-start.3 = (bf16[3,352,256]{2,1,0:T(8,128)(2,1)S(1)}, bf16[3,352,256]{2,1,0:T(8,128)(2,1)S(1)}, u32[]{:S(2)}, u32[]{:S(2)}) collective-permute-start(bf16[3,352,256]{2,1,0:T(8,128)(2,1)S(1)} %get-tuple-element.45), channel_id=1, source_target_pairs={{0,4},{4,0},{8,12},{12,8},{16,20},{20,16},{24,28},{28,24},{1,5},{5... | collective-permute-start | bytes 1622024 | tf_op jit(solution)/shard_map/ppermute | solution.py:17
  5.1 1.6 %collective-permute-start.4 = (bf16[3,352,256]{2,1,0:T(8,128)(2,1)S(1)}, bf16[3,352,256]{2,1,0:T(8,128)(2,1)S(1)}, u32[]{:S(2)}, u32[]{:S(2)}) collective-permute-start(bf16[3,352,256]{2,1,0:T(8,128)(2,1)S(1)} %get-tuple-element.46.refs_5_), channel_id=1, source_target_pairs={{0,8},{4,12},{8,0},{12,4},{16,24},{20,28},{24,16},{28,20},{1,9},{5... | collective-permute-start | bytes 1622024 | tf_op jit(solution)/shard_map/ppermute | solution.py:17
  7.2 3.5 %collective-permute-start.2 = (bf16[2,128,256]{2,1,0:T(8,128)(2,1)S(1)}, bf16[2,128,256]{2,1,0:T(8,128)(2,1)S(1)}, u32[]{:S(2)}, u32[]{:S(2)}) collective-permute-start(bf16[2,128,256]{2,1,0:T(8,128)(2,1)S(1)} %get-tuple-element.44), channel_id=1, source_target_pairs={{0,20},{4,16},{8,28},{12,24},{16,4},{20,0},{24,12},{28,8},{1,21},{... | collective-permute-start | bytes 393224 | tf_op jit(solution)/shard_map/ppermute | solution.py:17
  11.1 11.9 %collective-permute-done = bf16[2,128,256]{2,1,0:T(8,128)(2,1)S(1)} collective-permute-done((bf16[2,128,256]{2,1,0:T(8,128)(2,1)S(1)}, bf16[2,128,256]{2,1,0:T(8,128)(2,1)S(1)}, u32[]{:S(2)}, u32[]{:S(2)}) %collective-permute-start) | collective-permute-done | bytes 131104 | tf_op jit(solution)/shard_map/ppermute | solution.py:17
  23.6 0.8 %collective-permute-done.4.refs_7_ = bf16[3,352,256]{2,1,0:T(8,128)(2,1)S(1)} collective-permute-done((bf16[3,352,256]{2,1,0:T(8,128)(2,1)S(1)}, bf16[3,352,256]{2,1,0:T(8,128)(2,1)S(1)}, u32[]{:S(2)}, u32[]{:S(2)}) %collective-permute-start.4) | collective-permute-done | bytes 540704 | tf_op jit(solution)/shard_map/ppermute | solution.py:17
  24.5 1.5 %collective-permute-start.6 = (bf16[3,2,128,256]{3,2,1,0:T(8,128)(2,1)S(1)}, bf16[3,2,128,256]{3,2,1,0:T(8,128)(2,1)S(1)}, u32[]{:S(2)}, u32[]{:S(2)}) collective-permute-start(bf16[3,2,128,256]{3,2,1,0:T(8,128)(2,1)S(1)} %pad_maximum_fusion.refs_1_), channel_id=1, source_target_pairs={{0,2},{1,3},{2,0},{3,1},{4,6},{5,7},{6,4},{7,5},{8,10},{9,11},{10,... | collective-permute-start | bytes 1179656 | tf_op jit(solution)/shard_map/ppermute | solution.py:17
  26.0 2.7 %collective-permute-start.8 = (bf16[3,352,256]{2,1,0:T(8,128)(2,1)S(1)}, bf16[3,352,256]{2,1,0:T(8,128)(2,1)S(1)}, u32[]{:S(2)}, u32[]{:S(2)}) collective-permute-start(bf16[3,352,256]{2,1,0:T(8,128)(2,1)S(1)} %collective-permute-done.3.refs_6_), channel_id=1, source_target_pairs={{0,8},{4,12},{8,0},{12,4},{16,24},{20,28},{24,16},{28,20},{1,9},{5... | collective-permute-start | bytes 1622024 | tf_op jit(solution)/shard_map/ppermute | solution.py:17
  28.7 5.4 %collective-permute-done.6.refs_3_ = bf16[3,2,128,256]{3,2,1,0:T(8,128)(2,1)S(1)} collective-permute-done((bf16[3,2,128,256]{3,2,1,0:T(8,128)(2,1)S(1)}, bf16[3,2,128,256]{3,2,1,0:T(8,128)(2,1)S(1)}, u32[]{:S(2)}, u32[]{:S(2)}) %collective-permute-start.6) | collective-permute-done | bytes 393248 | tf_op jit(solution)/shard_map/ppermute | solution.py:17
  34.1 1.7 %collective-permute-done.7.refs_4_ = bf16[3,2,128,256]{3,2,1,0:T(8,128)(2,1)S(1)} collective-permute-done((bf16[3,2,128,256]{3,2,1,0:T(8,128)(2,1)S(1)}, bf16[3,2,128,256]{3,2,1,0:T(8,128)(2,1)S(1)}, u32[]{:S(2)}, u32[]{:S(2)}) %collective-permute-start.7) | collective-permute-done | bytes 393248 | tf_op jit(solution)/shard_map/ppermute | solution.py:17
  35.9 1.7 %shard_map.119 = (bf16[512,1024]{1,0:T(8,128)(2,1)S(1)}, bf16[512,1024]{1,0:T(8,128)(2,1)S(1)}, bf16[3,352,1024]{2,1,0:T(8,128)(2,1)S(1)}, f32[3,352,512]{2,1,0:T(8,128)S(1)}) custom-call(bf16[2,128,1024]{2,1,0:T(8,128)(2,1)S(1)} %get-tuple-element.42.refs_0_, bf16[3,2,128,256]{3,2,1,0:T(8,128)(2,1)S(1)} %pad_maximum_fusion.refs_1_, ...), custom_call_target="tpu_custom_call" | custom-call | flops 1 | bytes 1 | tf_op jit(solution)/shard_map/pallas_call | solution.py:157
  37.6 1.9 %collective-permute-done.8.last = bf16[3,352,256]{2,1,0:T(8,128)(2,1)S(1)} collective-permute-done((bf16[3,352,256]{2,1,0:T(8,128)(2,1)S(1)}, bf16[3,352,256]{2,1,0:T(8,128)(2,1)S(1)}, u32[]{:S(2)}, u32[]{:S(2)}) %collective-permute-start.8) | collective-permute-done | bytes 540704 | tf_op jit(solution)/shard_map/ppermute | solution.py:17
  39.5 2.8 %shard_map.120 = (bf16[3,352,512]{2,1,0:T(8,128)(2,1)S(1)}, f32[2,1040,256]{2,1,0:T(8,128)S(1)}, bf16[2,1040,256]{2,1,0:T(8,128)(2,1)S(1)}) custom-call(bf16[512,1024]{1,0:T(8,128)(2,1)S(1)} %get-tuple-element.50.x_all, bf16[512,1024]{1,0:T(8,128)(2,1)S(1)} %get-tuple-element.51.s_all, bf16[3,352,1024]{2,1,0:T(8,128)(2,1)S(1)} %get-tuple-element.52.w_part, ...), custom_call_target="tpu_custom_call" | custom-call | flops 1476395008 | tf_op jit(solution)/shard_map/pallas_call | solution.py:216
  42.4 1.3 %shard_map.126 = (f32[3,352,256]{2,1,0:T(8,128)S(1)}, f32[3,352,256]{2,1,0:T(8,128)S(1)}, bf16[3,352,256]{2,1,0:T(8,128)(2,1)S(1)}, bf16[3,352,256]{2,1,0:T(8,128)(2,1)S(1)}) custom-call(bf16[3,352,512]{2,1,0:T(8,128)(2,1)S(1)} %get-tuple-element.67.units, bf16[512,1024]{1,0:T(8,128)(2,1)S(1)} %get-tuple-element.50.x_all, ...), custom_call_target="tpu_custom_call" | custom-call | flops 1107296256 | tf_op jit(solution)/shard_map/pallas_call | solution.py:249
  43.7 1.8 %collective-permute-start.15 = (bf16[3,352,256]{2,1,0:T(8,128)(2,1)S(1)}, bf16[3,352,256]{2,1,0:T(8,128)(2,1)S(1)}, u32[]{:S(2)}, u32[]{:S(2)}) collective-permute-start(bf16[3,352,256]{2,1,0:T(8,128)(2,1)S(1)} %get-tuple-element.71), channel_id=1, source_target_pairs={{0,8},{4,12},{8,0},{12,4},{16,24},{20,28},{24,16},{28,20},{1,9},{5... | collective-permute-start | bytes 1622024 | tf_op jit(solution)/shard_map/ppermute | solution.py:17
  45.6 0.8 %collective-permute-start.10 = (bf16[528,256]{1,0:T(8,128)(2,1)S(1)}, bf16[528,256]{1,0:T(8,128)(2,1)S(1)}, u32[]{:S(2)}, u32[]{:S(2)}) collective-permute-start(bf16[528,256]{1,0:T(8,128)(2,1)S(1)} %get-tuple-element.56), channel_id=1, source_target_pairs={{0,2},{1,3},{2,0},{3,1},{4,6},{5,7},{6,4},{7,5},{8,10},{9,11},{10,... | collective-permute-start | bytes 811016 | tf_op jit(solution)/shard_map/ppermute | solution.py:17
  47.0 7.5 %collective-permute-done.12.from_x = bf16[2,256,256]{2,1,0:T(8,128)(2,1)S(1)} collective-permute-done((bf16[2,256,256]{2,1,0:T(8,128)(2,1)S(1)}, bf16[2,256,256]{2,1,0:T(8,128)(2,1)S(1)}, u32[]{:S(2)}, u32[]{:S(2)}) %collective-permute-start.12) | collective-permute-done | bytes 262176 | tf_op jit(solution)/shard_map/ppermute | solution.py:17
  54.5 1.5 %collective-permute-start.13 = (bf16[256,256]{1,0:T(8,128)(2,1)S(1)}, bf16[256,256]{1,0:T(8,128)(2,1)S(1)}, u32[]{:S(2)}, u32[]{:S(2)}) collective-permute-start(bf16[256,256]{1,0:T(8,128)(2,1)S(1)} %get-tuple-element.61), channel_id=1, source_target_pairs={{0,2},{1,3},{2,0},{3,1},{4,6},{5,7},{6,4},{7,5},{8,10},{9,11},{10,... | collective-permute-start | bytes 393224 | tf_op jit(solution)/shard_map/ppermute | solution.py:17
  56.7 1.7 %collective-permute-done.15 = bf16[3,352,256]{2,1,0:T(8,128)(2,1)S(1)} collective-permute-done((bf16[3,352,256]{2,1,0:T(8,128)(2,1)S(1)}, bf16[3,352,256]{2,1,0:T(8,128)(2,1)S(1)}, u32[]{:S(2)}, u32[]{:S(2)}) %collective-permute-start.15) | collective-permute-done | bytes 540704 | tf_op jit(solution)/shard_map/ppermute | solution.py:17
  59.2 1.7 %collective-permute-start.17 = (bf16[3,352,256]{2,1,0:T(8,128)(2,1)S(1)}, bf16[3,352,256]{2,1,0:T(8,128)(2,1)S(1)}, u32[]{:S(2)}, u32[]{:S(2)}) collective-permute-start(bf16[3,352,256]{2,1,0:T(8,128)(2,1)S(1)} %get-tuple-element.74), channel_id=1, source_target_pairs={{0,8},{4,12},{8,0},{12,4},{16,24},{20,28},{24,16},{28,20},{1,9},{5... | collective-permute-start | bytes 1622024 | tf_op jit(solution)/shard_map/ppermute | solution.py:17
  61.5 1.3 %collective-permute-start.14 = (bf16[272,256]{1,0:T(8,128)(2,1)S(1)}, bf16[272,256]{1,0:T(8,128)(2,1)S(1)}, u32[]{:S(2)}, u32[]{:S(2)}) collective-permute-start(bf16[272,256]{1,0:T(8,128)(2,1)S(1)} %get-tuple-element.63), channel_id=1, source_target_pairs={{0,16},{4,20},{8,24},{12,28},{16,0},{20,4},{24,8},{28,12},{1,17},{... | collective-permute-start | bytes 417800 | tf_op jit(solution)/shard_map/ppermute | solution.py:17
  62.8 12.2 %collective-permute-done.14.refs_0_ = bf16[272,256]{1,0:T(8,128)(2,1)S(1)} collective-permute-done((bf16[272,256]{1,0:T(8,128)(2,1)S(1)}, bf16[272,256]{1,0:T(8,128)(2,1)S(1)}, u32[]{:S(2)}, u32[]{:S(2)}) %collective-permute-start.14) | collective-permute-done | bytes 139296 | tf_op jit(solution)/shard_map/ppermute | solution.py:17
  75.0 0.8 %shard_map.125 = (bf16[128,256]{1,0:T(8,128)(2,1)}, bf16[128,256]{1,0:T(8,128)(2,1)}, f32[1,128]{1,0:T(1,128)}) custom-call(f32[1,128]{1,0:T(1,128)S(1)} %bitcast.13, f32[272,256]{1,0:T(8,128)S(1)} %get-tuple-element.62.own, bf16[272,256]{1,0:T(8,128)(2,1)S(1)} %collective-permute-done.14.refs_0_), custom_call_target="tpu_custom_call" | custom-call | tf_op jit(solution)/shard_map/pallas_call | solution.py:468
  75.8 1.5 %shard_map.127 = (f32[704,256]{1,0:T(8,128)}, f32[704,256]{1,0:T(8,128)}, f32[704,256]{1,0:T(8,128)}) custom-call(f32[3,352,256]{2,1,0:T(8,128)S(1)} %get-tuple-element.68.own, bf16[3,352,256]{2,1,0:T(8,128)(2,1)S(1)} %collective-permute-done.16.got_x, bf16[3,352,256]{2,1,0:T(8,128)(2,1)S(1)} %collective-permute-done.17.got_z), custom_call_target="tpu_custom_call" | custom-call | tf_op jit(solution)/shard_map/pallas_call | solution.py:277
  (26 shorter events, 4.4 us)
Async XLA Ops:
  2.1 21.5 %collective-permute-start.3 = (bf16[3,352,256]{2,1,0:T(8,128)(2,1)S(1)}, bf16[3,352,256]{2,1,0:T(8,128)(2,1)S(1)}, u32[]{:S(2)}, u32[]{:S(2)}) collective-permute-start(bf16[3,352,256]{2,1,0:T(8,128)(2,1)S(1)} %get-tuple-element.45), channel_id=1, source_target_pairs={{0,4},{4,0},{8,12},{12,8},{16,20},{20,16},{24,28},{28,24},{1,5},{5... | collective-permute-start | bytes 1622024 | tf_op jit(solution)/shard_map/ppermute | solution.py:17
  5.1 19.4 %collective-permute-start.4 = (bf16[3,352,256]{2,1,0:T(8,128)(2,1)S(1)}, bf16[3,352,256]{2,1,0:T(8,128)(2,1)S(1)}, u32[]{:S(2)}, u32[]{:S(2)}) collective-permute-start(bf16[3,352,256]{2,1,0:T(8,128)(2,1)S(1)} %get-tuple-element.46.refs_5_), channel_id=1, source_target_pairs={{0,8},{4,12},{8,0},{12,4},{16,24},{20,28},{24,16},{28,20},{1,9},{5... | collective-permute-start | bytes 1622024 | tf_op jit(solution)/shard_map/ppermute | solution.py:17
  6.7 16.3 %collective-permute-start = (bf16[2,128,256]{2,1,0:T(8,128)(2,1)S(1)}, bf16[2,128,256]{2,1,0:T(8,128)(2,1)S(1)}, u32[]{:S(2)}, u32[]{:S(2)}) collective-permute-start(bf16[2,128,256]{2,1,0:T(8,128)(2,1)S(1)} %get-tuple-element.43), channel_id=1, source_target_pairs={{0,4},{4,0},{8,12},{12,8},{16,20},{20,16},{24,28},{28,24},{1,5},{5... | collective-permute-start | bytes 393224 | tf_op jit(solution)/shard_map/ppermute | solution.py:17
  7.2 15.8 %collective-permute-start.2 = (bf16[2,128,256]{2,1,0:T(8,128)(2,1)S(1)}, bf16[2,128,256]{2,1,0:T(8,128)(2,1)S(1)}, u32[]{:S(2)}, u32[]{:S(2)}) collective-permute-start(bf16[2,128,256]{2,1,0:T(8,128)(2,1)S(1)} %get-tuple-element.44), channel_id=1, source_target_pairs={{0,20},{4,16},{8,28},{12,24},{16,4},{20,0},{24,12},{28,8},{1,21},{... | collective-permute-start | bytes 393224 | tf_op jit(solution)/shard_map/ppermute | solution.py:17
  10.7 12.8 %collective-permute-start.1 = (bf16[2,128,256]{2,1,0:T(8,128)(2,1)S(1)}, bf16[2,128,256]{2,1,0:T(8,128)(2,1)S(1)}, u32[]{:S(2)}, u32[]{:S(2)}) collective-permute-start(bf16[2,128,256]{2,1,0:T(8,128)(2,1)S(1)} %get-tuple-element.44), channel_id=1, source_target_pairs={{0,16},{4,20},{8,24},{12,28},{16,0},{20,4},{24,8},{28,12},{1,17},{... | collective-permute-start | bytes 393224 | tf_op jit(solution)/shard_map/ppermute | solution.py:17
  24.5 9.7 %collective-permute-start.6 = (bf16[3,2,128,256]{3,2,1,0:T(8,128)(2,1)S(1)}, bf16[3,2,128,256]{3,2,1,0:T(8,128)(2,1)S(1)}, u32[]{:S(2)}, u32[]{:S(2)}) collective-permute-start(bf16[3,2,128,256]{3,2,1,0:T(8,128)(2,1)S(1)} %pad_maximum_fusion.refs_1_), channel_id=1, source_target_pairs={{0,2},{1,3},{2,0},{3,1},{4,6},{5,7},{6,4},{7,5},{8,10},{9,11},{10,... | collective-permute-start | bytes 1179656 | tf_op jit(solution)/shard_map/ppermute | solution.py:17
  26.0 13.5 %collective-permute-start.8 = (bf16[3,352,256]{2,1,0:T(8,128)(2,1)S(1)}, bf16[3,352,256]{2,1,0:T(8,128)(2,1)S(1)}, u32[]{:S(2)}, u32[]{:S(2)}) collective-permute-start(bf16[3,352,256]{2,1,0:T(8,128)(2,1)S(1)} %collective-permute-done.3.refs_6_), channel_id=1, source_target_pairs={{0,8},{4,12},{8,0},{12,4},{16,24},{20,28},{24,16},{28,20},{1,9},{5... | collective-permute-start | bytes 1622024 | tf_op jit(solution)/shard_map/ppermute | solution.py:17
  28.7 5.4 %collective-permute-start.5 = (bf16[3,2,128,256]{3,2,1,0:T(8,128)(2,1)S(1)}, bf16[3,2,128,256]{3,2,1,0:T(8,128)(2,1)S(1)}, u32[]{:S(2)}, u32[]{:S(2)}) collective-permute-start(bf16[3,2,128,256]{3,2,1,0:T(8,128)(2,1)S(1)} %pad_maximum_fusion.refs_1_), channel_id=1, source_target_pairs={{0,1},{1,0},{2,3},{3,2},{4,5},{5,4},{6,7},{7,6},{8,9},{9,8},{10,11... | collective-permute-start | bytes 1179656 | tf_op jit(solution)/shard_map/ppermute | solution.py:17
  34.1 1.7 %collective-permute-start.7 = (bf16[3,2,128,256]{3,2,1,0:T(8,128)(2,1)S(1)}, bf16[3,2,128,256]{3,2,1,0:T(8,128)(2,1)S(1)}, u32[]{:S(2)}, u32[]{:S(2)}) collective-permute-start(bf16[3,2,128,256]{3,2,1,0:T(8,128)(2,1)S(1)} %collective-permute-done.6.refs_3_), channel_id=1, source_target_pairs={{0,1},{1,0},{2,3},{3,2},{4,5},{5,4},{6,7},{7,6},{8,9},{9,8},{10,11... | collective-permute-start | bytes 1179656 | tf_op jit(solution)/shard_map/ppermute | solution.py:17
  42.3 3.2 %collective-permute-start.9 = (bf16[2,1040,256]{2,1,0:T(8,128)(2,1)S(1)}, bf16[2,1040,256]{2,1,0:T(8,128)(2,1)S(1)}, u32[]{:S(2)}, u32[]{:S(2)}) collective-permute-start(bf16[2,1040,256]{2,1,0:T(8,128)(2,1)S(1)} %get-tuple-element.55), channel_id=1, source_target_pairs={{0,1},{1,0},{2,3},{3,2},{4,5},{5,4},{6,7},{7,6},{8,9},{9,8},{10,11... | collective-permute-start | bytes 3194888 | tf_op jit(solution)/shard_map/ppermute | solution.py:17
  43.7 14.7 %collective-permute-start.15 = (bf16[3,352,256]{2,1,0:T(8,128)(2,1)S(1)}, bf16[3,352,256]{2,1,0:T(8,128)(2,1)S(1)}, u32[]{:S(2)}, u32[]{:S(2)}) collective-permute-start(bf16[3,352,256]{2,1,0:T(8,128)(2,1)S(1)} %get-tuple-element.71), channel_id=1, source_target_pairs={{0,8},{4,12},{8,0},{12,4},{16,24},{20,28},{24,16},{28,20},{1,9},{5... | collective-permute-start | bytes 1622024 | tf_op jit(solution)/shard_map/ppermute | solution.py:17
  45.6 10.4 %collective-permute-start.10 = (bf16[528,256]{1,0:T(8,128)(2,1)S(1)}, bf16[528,256]{1,0:T(8,128)(2,1)S(1)}, u32[]{:S(2)}, u32[]{:S(2)}) collective-permute-start(bf16[528,256]{1,0:T(8,128)(2,1)S(1)} %get-tuple-element.56), channel_id=1, source_target_pairs={{0,2},{1,3},{2,0},{3,1},{4,6},{5,7},{6,4},{7,5},{8,10},{9,11},{10,... | collective-permute-start | bytes 811016 | tf_op jit(solution)/shard_map/ppermute | solution.py:17
  46.4 8.0 %collective-permute-start.12 = (bf16[2,256,256]{2,1,0:T(8,128)(2,1)S(1)}, bf16[2,256,256]{2,1,0:T(8,128)(2,1)S(1)}, u32[]{:S(2)}, u32[]{:S(2)}) collective-permute-start(bf16[2,256,256]{2,1,0:T(8,128)(2,1)S(1)} %get-tuple-element.59), channel_id=1, source_target_pairs={{0,4},{4,0},{8,12},{12,8},{16,20},{20,16},{24,28},{28,24},{1,5},{5... | collective-permute-start | bytes 786440 | tf_op jit(solution)/shard_map/ppermute | solution.py:17
  54.5 6.4 %collective-permute-start.13 = (bf16[256,256]{1,0:T(8,128)(2,1)S(1)}, bf16[256,256]{1,0:T(8,128)(2,1)S(1)}, u32[]{:S(2)}, u32[]{:S(2)}) collective-permute-start(bf16[256,256]{1,0:T(8,128)(2,1)S(1)} %get-tuple-element.61), channel_id=1, source_target_pairs={{0,2},{1,3},{2,0},{3,1},{4,6},{5,7},{6,4},{7,5},{8,10},{9,11},{10,... | collective-permute-start | bytes 393224 | tf_op jit(solution)/shard_map/ppermute | solution.py:17
  56.1 5.4 %collective-permute-start.11 = (bf16[272,256]{1,0:T(8,128)(2,1)S(1)}, bf16[272,256]{1,0:T(8,128)(2,1)S(1)}, u32[]{:S(2)}, u32[]{:S(2)}) collective-permute-start(bf16[272,256]{1,0:T(8,128)(2,1)S(1)} %get-tuple-element.58), channel_id=1, source_target_pairs={{0,4},{4,0},{8,12},{12,8},{16,20},{20,16},{24,28},{28,24},{1,5},{5... | collective-permute-start | bytes 417800 | tf_op jit(solution)/shard_map/ppermute | solution.py:17
  58.5 17.2 %collective-permute-start.16 = (bf16[3,352,256]{2,1,0:T(8,128)(2,1)S(1)}, bf16[3,352,256]{2,1,0:T(8,128)(2,1)S(1)}, u32[]{:S(2)}, u32[]{:S(2)}) collective-permute-start(bf16[3,352,256]{2,1,0:T(8,128)(2,1)S(1)} %add_convert_fusion), channel_id=1, source_target_pairs={{0,4},{4,0},{8,12},{12,8},{16,20},{20,16},{24,28},{28,24},{1,5},{5... | collective-permute-start | bytes 1622024 | tf_op jit(solution)/shard_map/ppermute | solution.py:17
  59.2 16.6 %collective-permute-start.17 = (bf16[3,352,256]{2,1,0:T(8,128)(2,1)S(1)}, bf16[3,352,256]{2,1,0:T(8,128)(2,1)S(1)}, u32[]{:S(2)}, u32[]{:S(2)}) collective-permute-start(bf16[3,352,256]{2,1,0:T(8,128)(2,1)S(1)} %get-tuple-element.74), channel_id=1, source_target_pairs={{0,8},{4,12},{8,0},{12,4},{16,24},{20,28},{24,16},{28,20},{1,9},{5... | collective-permute-start | bytes 1622024 | tf_op jit(solution)/shard_map/ppermute | solution.py:17
  61.5 13.5 %copy-start = (f32[128]{0:T(128)S(1)}, f32[128]{0:T(128)}, u32[]{:S(2)}) copy-start(f32[128]{0:T(128)} %param.10) | copy-start | bytes 1540
  61.5 13.4 %collective-permute-start.14 = (bf16[272,256]{1,0:T(8,128)(2,1)S(1)}, bf16[272,256]{1,0:T(8,128)(2,1)S(1)}, u32[]{:S(2)}, u32[]{:S(2)}) collective-permute-start(bf16[272,256]{1,0:T(8,128)(2,1)S(1)} %get-tuple-element.63), channel_id=1, source_target_pairs={{0,16},{4,20},{8,24},{12,28},{16,0},{20,4},{24,8},{28,12},{1,17},{... | collective-permute-start | bytes 417800 | tf_op jit(solution)/shard_map/ppermute | solution.py:17

commit v6 on v5

--- a/solution.py
+++ b/solution.py
@@ -261,26 +261,56 @@
     )(units, x_all, s_all)
 
 
-def join_kernel(own, got_x, got_z, *outs):
-    half = own.shape[1]
-    x_bit = lax.axis_index("wide") % 2
-    keep_rows = pl.ds(pl.multiple_of(x_bit * half, 16), half)
-    give_rows = pl.ds(pl.multiple_of((1 - x_bit) * half, 16), half)
-    for i, ref in enumerate(outs):
-        ref[keep_rows, :] = own[i] + got_z[i].astype(jnp.float32)
-        ref[give_rows, :] = got_x[i].astype(jnp.float32)
+def write_rows(held, outs, sems, first):
+    rows = pl.ds(pl.multiple_of(first, 16), held.shape[1])
+    copies = [
+        pltpu.make_async_copy(held.at[i], out.at[rows, :], sems.at[i]) for i, out in enumerate(outs)
+    ]
+    return copies
+
+
+def keep_kernel(own, got, out_0, out_1, out_2, held, sems):
+    first = lax.axis_index("wide") % 2 * held.shape[1]
+    copies = write_rows(held, (out_0, out_1, out_2), sems, first)
+    for i, copy in enumerate(copies):
+        held[i] = own[i] + got[i].astype(jnp.float32)
+        copy.start()
+    for copy in copies:
+        copy.wait()
+
+
+def give_kernel(in_0, in_1, in_2, got, out_0, out_1, out_2, held, sems):
+    first = (1 - lax.axis_index("wide") % 2) * held.shape[1]
+    copies = write_rows(held, (out_0, out_1, out_2), sems, first)
+    for i, copy in enumerate(copies):
+        held[i] = got[i].astype(jnp.float32)
+        copy.start()
+    for copy in copies:
+        copy.wait()
 
 
 def join_grads(own, got_x, got_z):
     _, half, width = own.shape
     shape = jax.ShapeDtypeStruct((2 * half, width), jnp.float32)
-    return pl.pallas_call(
-        join_kernel,
+    scratch = [pltpu.VMEM(own.shape, jnp.float32), pltpu.SemaphoreType.DMA((3,))]
+    kept = pl.pallas_call(
+        keep_kernel,
         out_shape=(shape,) * 3,
-        in_specs=[VMEM] * 3,
-        out_specs=[VMEM] * 3,
-        compiler_params=PARAMS,
-    )(own, got_x, got_z)
+        in_specs=[VMEM] * 2,
+        out_specs=[HBM] * 3,
+        scratch_shapes=scratch,
+        compiler_params=PARAMS,
+        cost_estimate=pl.CostEstimate(flops=1, bytes_accessed=0, transcendentals=0),
+    )(own, got_z)
+    return pl.pallas_call(
+        give_kernel,
+        out_shape=(shape,) * 3,
+        in_specs=[HBM] * 3 + [VMEM],
+        out_specs=[HBM] * 3,
+        scratch_shapes=scratch,
+        input_output_aliases={0: 0, 1: 1, 2: 2},
+        compiler_params=PARAMS,
+    )(*kept, got_x)
 
 
 def cross_kernel(kept, got, sent):
@@ -535,7 +565,7 @@
         to_y, to_x = first_parts(kept, got)
         ffn_held, ffn_x = ffn_parts(kept, got, partner(to_y, "narrow", 2))
         grad_held, grad_y = input_parts(kept, got, partner(to_x, "wide", 1))
-        grad_x, _, _ = lax.optimization_barrier((grad_x, ffn_x, grad_y))
+        grad_x, grad_z, _, _ = lax.optimization_barrier((grad_x, grad_z, ffn_x, grad_y))
         held, to_z = last_parts(
             ffn_held, partner(ffn_x, "wide", 1), grad_held, partner(grad_y, "narrow", 2)
         )
@@ -567,7 +597,6 @@
         output = (route_prob[:, None] * ffn).astype(jnp.bfloat16)
         tokens_grad = back[1].astype(jnp.bfloat16)
     grad_x = (grad_x + got_d.astype(jnp.float32)).astype(jnp.bfloat16)
-    grad_x, grad_z = lax.optimization_barrier((grad_x, grad_z))
     got_x = partner(grad_x, "wide", 1)
     got_z = partner(grad_z, "wide", 2)
     gate_grad, up_grad, down_grad = join_grads(grad_own, got_x, got_z)

time: 77.4 us -> 75.3 us (0.973)
  waiting for transfers between devices: 44.3 us -> 42.1 us
    ppermute x18, waiting for transfers between devices: 44.3 us -> 42.1 us  [partner(): lax.ppermute(x, axis, [(i, i ^ mask) for i in range(lax.axis_size(axis))])]
    pallas_call x1 -> x2, Pallas kernels: 1.47 us -> 2.06 us  [the longest x1 1.03 us: join_grads(): pl.pallas_call(keep_kernel, out_shape=(shape,) * 3, in_specs=[VMEM] * 2,...]
  transfers between devices with their start and end apart: 18 -> 18, of which waited for: 10 -> 10; matrix products, arithmetic and copies ran while one was open for 0% -> 0% of each run, Pallas kernels for 5% -> 7%
where the time goes in v6:
time: 75.3 us; the launch traced here: 75.1 us
  waiting for transfers between devices  42.1 us (56%)
  starting transfers between devices  21.6 us (29%)
  Pallas kernels  10.5 us (14%)
    ppermute x18, waiting for transfers between devices, partner(): lax.ppermute(x, axis, [(i, i ^ mask) for i in range(lax.axis_size(axis))])  42.1 us
    ppermute x18, starting transfers between devices, partner(): lax.ppermute(x, axis, [(i, i ^ mask) for i in range(lax.axis_size(axis))])  21.6 us
    pallas_call x1, Pallas kernels, outer(): pl.pallas_call(outer_kernel, out_shape=(jax.ShapeDtypeStruct((3, half, to...  2.76 us
    pallas_call x1, Pallas kernels, gather_parts(): pl.pallas_call(functools.partial(gather_kernel, int(has_own)), out_shape=...  1.75 us
  transfers between devices with their start and end apart: 18, of which 10 were waited for; matrix products, arithmetic and copies ran while one was open for 0% of the time, Pallas kernels for 7%

profile of v6, /device:TPU:0, one launch (start us, length us, event | category | flops | bytes accessed | tf_op | source)
XLA Modules:
  0.0 75.1 jit_solution(16134494528423506104)
XLA Ops:
  0.6 1.5 %shard_map.118 = (bf16[3,352,256]{2,1,0:T(8,128)(2,1)S(1)}, bf16[3,352,256]{2,1,0:T(8,128)(2,1)S(1)}, bf16[2,128,1024]{2,1,0:T(8,128)(2,1)S(1)}, bf16[2,128,256]...) custom-call(bf16[704,256]{1,0:T(8,128)(2,1)} %bitcast.17, bf16[704,256]{1,0:T(8,128)(2,1)} %bitcast.18, ...), custom_call_target="tpu_custom_call" | custom-call | tf_op jit(solution)/shard_map/pallas_call | solution.py:103
  2.1 3.0 %collective-permute-start.3 = (bf16[3,352,256]{2,1,0:T(8,128)(2,1)S(1)}, bf16[3,352,256]{2,1,0:T(8,128)(2,1)S(1)}, u32[]{:S(2)}, u32[]{:S(2)}) collective-permute-start(bf16[3,352,256]{2,1,0:T(8,128)(2,1)S(1)} %get-tuple-element.47), channel_id=1, source_target_pairs={{0,4},{4,0},{8,12},{12,8},{16,20},{20,16},{24,28},{28,24},{1,5},{5... | collective-permute-start | bytes 1622024 | tf_op jit(solution)/shard_map/ppermute | solution.py:17
  5.1 1.6 %collective-permute-start.4 = (bf16[3,352,256]{2,1,0:T(8,128)(2,1)S(1)}, bf16[3,352,256]{2,1,0:T(8,128)(2,1)S(1)}, u32[]{:S(2)}, u32[]{:S(2)}) collective-permute-start(bf16[3,352,256]{2,1,0:T(8,128)(2,1)S(1)} %get-tuple-element.48.refs_5_), channel_id=1, source_target_pairs={{0,8},{4,12},{8,0},{12,4},{16,24},{20,28},{24,16},{28,20},{1,9},{5... | collective-permute-start | bytes 1622024 | tf_op jit(solution)/shard_map/ppermute | solution.py:17
  7.2 3.5 %collective-permute-start.2 = (bf16[2,128,256]{2,1,0:T(8,128)(2,1)S(1)}, bf16[2,128,256]{2,1,0:T(8,128)(2,1)S(1)}, u32[]{:S(2)}, u32[]{:S(2)}) collective-permute-start(bf16[2,128,256]{2,1,0:T(8,128)(2,1)S(1)} %get-tuple-element.46), channel_id=1, source_target_pairs={{0,20},{4,16},{8,28},{12,24},{16,4},{20,0},{24,12},{28,8},{1,21},{... | collective-permute-start | bytes 393224 | tf_op jit(solution)/shard_map/ppermute | solution.py:17
  11.1 11.9 %collective-permute-done = bf16[2,128,256]{2,1,0:T(8,128)(2,1)S(1)} collective-permute-done((bf16[2,128,256]{2,1,0:T(8,128)(2,1)S(1)}, bf16[2,128,256]{2,1,0:T(8,128)(2,1)S(1)}, u32[]{:S(2)}, u32[]{:S(2)}) %collective-permute-start) | collective-permute-done | bytes 131104 | tf_op jit(solution)/shard_map/ppermute | solution.py:17
  23.6 0.8 %collective-permute-done.4.refs_7_ = bf16[3,352,256]{2,1,0:T(8,128)(2,1)S(1)} collective-permute-done((bf16[3,352,256]{2,1,0:T(8,128)(2,1)S(1)}, bf16[3,352,256]{2,1,0:T(8,128)(2,1)S(1)}, u32[]{:S(2)}, u32[]{:S(2)}) %collective-permute-start.4) | collective-permute-done | bytes 540704 | tf_op jit(solution)/shard_map/ppermute | solution.py:17
  24.5 1.5 %collective-permute-start.6 = (bf16[3,2,128,256]{3,2,1,0:T(8,128)(2,1)S(1)}, bf16[3,2,128,256]{3,2,1,0:T(8,128)(2,1)S(1)}, u32[]{:S(2)}, u32[]{:S(2)}) collective-permute-start(bf16[3,2,128,256]{3,2,1,0:T(8,128)(2,1)S(1)} %pad_maximum_fusion.refs_1_), channel_id=1, source_target_pairs={{0,2},{1,3},{2,0},{3,1},{4,6},{5,7},{6,4},{7,5},{8,10},{9,11},{10,... | collective-permute-start | bytes 1179656 | tf_op jit(solution)/shard_map/ppermute | solution.py:17
  26.0 2.7 %collective-permute-start.8 = (bf16[3,352,256]{2,1,0:T(8,128)(2,1)S(1)}, bf16[3,352,256]{2,1,0:T(8,128)(2,1)S(1)}, u32[]{:S(2)}, u32[]{:S(2)}) collective-permute-start(bf16[3,352,256]{2,1,0:T(8,128)(2,1)S(1)} %collective-permute-done.3.refs_6_), channel_id=1, source_target_pairs={{0,8},{4,12},{8,0},{12,4},{16,24},{20,28},{24,16},{28,20},{1,9},{5... | collective-permute-start | bytes 1622024 | tf_op jit(solution)/shard_map/ppermute | solution.py:17
  28.7 5.4 %collective-permute-done.6.refs_3_ = bf16[3,2,128,256]{3,2,1,0:T(8,128)(2,1)S(1)} collective-permute-done((bf16[3,2,128,256]{3,2,1,0:T(8,128)(2,1)S(1)}, bf16[3,2,128,256]{3,2,1,0:T(8,128)(2,1)S(1)}, u32[]{:S(2)}, u32[]{:S(2)}) %collective-permute-start.6) | collective-permute-done | bytes 393248 | tf_op jit(solution)/shard_map/ppermute | solution.py:17
  34.1 1.7 %collective-permute-done.7.refs_4_ = bf16[3,2,128,256]{3,2,1,0:T(8,128)(2,1)S(1)} collective-permute-done((bf16[3,2,128,256]{3,2,1,0:T(8,128)(2,1)S(1)}, bf16[3,2,128,256]{3,2,1,0:T(8,128)(2,1)S(1)}, u32[]{:S(2)}, u32[]{:S(2)}) %collective-permute-start.7) | collective-permute-done | bytes 393248 | tf_op jit(solution)/shard_map/ppermute | solution.py:17
  35.9 1.7 %shard_map.119 = (bf16[512,1024]{1,0:T(8,128)(2,1)S(1)}, bf16[512,1024]{1,0:T(8,128)(2,1)S(1)}, bf16[3,352,1024]{2,1,0:T(8,128)(2,1)S(1)}, f32[3,352,512]{2,1,0:T(8,128)S(1)}) custom-call(bf16[2,128,1024]{2,1,0:T(8,128)(2,1)S(1)} %get-tuple-element.44.refs_0_, bf16[3,2,128,256]{3,2,1,0:T(8,128)(2,1)S(1)} %pad_maximum_fusion.refs_1_, ...), custom_call_target="tpu_custom_call" | custom-call | flops 1 | bytes 1 | tf_op jit(solution)/shard_map/pallas_call | solution.py:157
  37.6 1.9 %collective-permute-done.8.last = bf16[3,352,256]{2,1,0:T(8,128)(2,1)S(1)} collective-permute-done((bf16[3,352,256]{2,1,0:T(8,128)(2,1)S(1)}, bf16[3,352,256]{2,1,0:T(8,128)(2,1)S(1)}, u32[]{:S(2)}, u32[]{:S(2)}) %collective-permute-start.8) | collective-permute-done | bytes 540704 | tf_op jit(solution)/shard_map/ppermute | solution.py:17
  39.5 2.8 %shard_map.120 = (bf16[3,352,512]{2,1,0:T(8,128)(2,1)S(1)}, f32[2,1040,256]{2,1,0:T(8,128)S(1)}, bf16[2,1040,256]{2,1,0:T(8,128)(2,1)S(1)}) custom-call(bf16[512,1024]{1,0:T(8,128)(2,1)S(1)} %get-tuple-element.52.x_all, bf16[512,1024]{1,0:T(8,128)(2,1)S(1)} %get-tuple-element.53.s_all, bf16[3,352,1024]{2,1,0:T(8,128)(2,1)S(1)} %get-tuple-element.54.w_part, ...), custom_call_target="tpu_custom_call" | custom-call | flops 1476395008 | tf_op jit(solution)/shard_map/pallas_call | solution.py:216
  42.4 1.3 %shard_map.126 = (f32[3,352,256]{2,1,0:T(8,128)S(1)}, f32[3,352,256]{2,1,0:T(8,128)S(1)}, bf16[3,352,256]{2,1,0:T(8,128)(2,1)S(1)}, bf16[3,352,256]{2,1,0:T(8,128)(2,1)S(1)}) custom-call(bf16[3,352,512]{2,1,0:T(8,128)(2,1)S(1)} %get-tuple-element.69.units, bf16[512,1024]{1,0:T(8,128)(2,1)S(1)} %get-tuple-element.52.x_all, ...), custom_call_target="tpu_custom_call" | custom-call | flops 1107296256 | tf_op jit(solution)/shard_map/pallas_call | solution.py:249
  43.7 1.8 %collective-permute-start.16 = (bf16[3,352,256]{2,1,0:T(8,128)(2,1)S(1)}, bf16[3,352,256]{2,1,0:T(8,128)(2,1)S(1)}, u32[]{:S(2)}, u32[]{:S(2)}) collective-permute-start(bf16[3,352,256]{2,1,0:T(8,128)(2,1)S(1)} %get-tuple-element.78), channel_id=1, source_target_pairs={{0,8},{4,12},{8,0},{12,4},{16,24},{20,28},{24,16},{28,20},{1,9},{5... | collective-permute-start | bytes 1622024 | tf_op jit(solution)/shard_map/ppermute | solution.py:17
  47.0 7.5 %collective-permute-done.12.from_x = bf16[2,256,256]{2,1,0:T(8,128)(2,1)S(1)} collective-permute-done((bf16[2,256,256]{2,1,0:T(8,128)(2,1)S(1)}, bf16[2,256,256]{2,1,0:T(8,128)(2,1)S(1)}, u32[]{:S(2)}, u32[]{:S(2)}) %collective-permute-start.12) | collective-permute-done | bytes 262176 | tf_op jit(solution)/shard_map/ppermute | solution.py:17
  54.5 1.5 %collective-permute-start.13 = (bf16[256,256]{1,0:T(8,128)(2,1)S(1)}, bf16[256,256]{1,0:T(8,128)(2,1)S(1)}, u32[]{:S(2)}, u32[]{:S(2)}) collective-permute-start(bf16[256,256]{1,0:T(8,128)(2,1)S(1)} %get-tuple-element.63), channel_id=1, source_target_pairs={{0,2},{1,3},{2,0},{3,1},{4,6},{5,7},{6,4},{7,5},{8,10},{9,11},{10,... | collective-permute-start | bytes 393224 | tf_op jit(solution)/shard_map/ppermute | solution.py:17
  56.7 1.2 %collective-permute-start.15 = (bf16[3,352,256]{2,1,0:T(8,128)(2,1)S(1)}, bf16[3,352,256]{2,1,0:T(8,128)(2,1)S(1)}, u32[]{:S(2)}, u32[]{:S(2)}) collective-permute-start(bf16[3,352,256]{2,1,0:T(8,128)(2,1)S(1)} %get-tuple-element.73), channel_id=1, source_target_pairs={{0,8},{4,12},{8,0},{12,4},{16,24},{20,28},{24,16},{28,20},{1,9},{5... | collective-permute-start | bytes 1622024 | tf_op jit(solution)/shard_map/ppermute | solution.py:17
  57.9 1.0 %collective-permute-done.16 = bf16[3,352,256]{2,1,0:T(8,128)(2,1)S(1)} collective-permute-done((bf16[3,352,256]{2,1,0:T(8,128)(2,1)S(1)}, bf16[3,352,256]{2,1,0:T(8,128)(2,1)S(1)}, u32[]{:S(2)}, u32[]{:S(2)}) %collective-permute-start.16) | collective-permute-done | bytes 540704 | tf_op jit(solution)/shard_map/ppermute | solution.py:17
  59.6 1.9 %collective-permute-done.11.from_x = bf16[272,256]{1,0:T(8,128)(2,1)S(1)} collective-permute-done((bf16[272,256]{1,0:T(8,128)(2,1)S(1)}, bf16[272,256]{1,0:T(8,128)(2,1)S(1)}, u32[]{:S(2)}, u32[]{:S(2)}) %collective-permute-start.11) | collective-permute-done | bytes 139296 | tf_op jit(solution)/shard_map/ppermute | solution.py:17
  61.5 1.3 %collective-permute-start.14 = (bf16[272,256]{1,0:T(8,128)(2,1)S(1)}, bf16[272,256]{1,0:T(8,128)(2,1)S(1)}, u32[]{:S(2)}, u32[]{:S(2)}) collective-permute-start(bf16[272,256]{1,0:T(8,128)(2,1)S(1)} %get-tuple-element.65), channel_id=1, source_target_pairs={{0,16},{4,20},{8,24},{12,28},{16,0},{20,4},{24,8},{28,12},{1,17},{... | collective-permute-start | bytes 417800 | tf_op jit(solution)/shard_map/ppermute | solution.py:17
  62.8 9.4 %collective-permute-done.14.refs_0_ = bf16[272,256]{1,0:T(8,128)(2,1)S(1)} collective-permute-done((bf16[272,256]{1,0:T(8,128)(2,1)S(1)}, bf16[272,256]{1,0:T(8,128)(2,1)S(1)}, u32[]{:S(2)}, u32[]{:S(2)}) %collective-permute-start.14) | collective-permute-done | bytes 139296 | tf_op jit(solution)/shard_map/ppermute | solution.py:17
  73.1 1.0 %shard_map.127 = (f32[704,256]{1,0:T(8,128)}, f32[704,256]{1,0:T(8,128)}, f32[704,256]{1,0:T(8,128)}) custom-call(f32[3,352,256]{2,1,0:T(8,128)S(1)} %get-tuple-element.70.own, bf16[3,352,256]{2,1,0:T(8,128)(2,1)S(1)} %collective-permute-done.15.got), custom_call_target="tpu_custom_call" | custom-call | flops 1 | tf_op jit(solution)/shard_map/pallas_call | solution.py:296
  74.1 1.0 %shard_map.128 = (f32[704,256]{1,0:T(8,128)}, f32[704,256]{1,0:T(8,128)}, f32[704,256]{1,0:T(8,128)}) custom-call(f32[704,256]{1,0:T(8,128)} %get-tuple-element.74.in_0, f32[704,256]{1,0:T(8,128)} %get-tuple-element.75.in_1, f32[704,256]{1,0:T(8,128)} %get-tuple-element.76.in_2, ...), custom_call_target="tpu_custom_call", output_to_operand_aliasing={{0}: (0, {}), {1}: (1, {}), {2}: (2, {})} | custom-call | tf_op jit(solution)/shard_map/pallas_call | solution.py:305
  (27 shorter events, 5.4 us)
Async XLA Ops:
  2.1 21.5 %collective-permute-start.3 = (bf16[3,352,256]{2,1,0:T(8,128)(2,1)S(1)}, bf16[3,352,256]{2,1,0:T(8,128)(2,1)S(1)}, u32[]{:S(2)}, u32[]{:S(2)}) collective-permute-start(bf16[3,352,256]{2,1,0:T(8,128)(2,1)S(1)} %get-tuple-element.47), channel_id=1, source_target_pairs={{0,4},{4,0},{8,12},{12,8},{16,20},{20,16},{24,28},{28,24},{1,5},{5... | collective-permute-start | bytes 1622024 | tf_op jit(solution)/shard_map/ppermute | solution.py:17
  5.1 19.4 %collective-permute-start.4 = (bf16[3,352,256]{2,1,0:T(8,128)(2,1)S(1)}, bf16[3,352,256]{2,1,0:T(8,128)(2,1)S(1)}, u32[]{:S(2)}, u32[]{:S(2)}) collective-permute-start(bf16[3,352,256]{2,1,0:T(8,128)(2,1)S(1)} %get-tuple-element.48.refs_5_), channel_id=1, source_target_pairs={{0,8},{4,12},{8,0},{12,4},{16,24},{20,28},{24,16},{28,20},{1,9},{5... | collective-permute-start | bytes 1622024 | tf_op jit(solution)/shard_map/ppermute | solution.py:17
  6.7 16.3 %collective-permute-start = (bf16[2,128,256]{2,1,0:T(8,128)(2,1)S(1)}, bf16[2,128,256]{2,1,0:T(8,128)(2,1)S(1)}, u32[]{:S(2)}, u32[]{:S(2)}) collective-permute-start(bf16[2,128,256]{2,1,0:T(8,128)(2,1)S(1)} %get-tuple-element.45), channel_id=1, source_target_pairs={{0,4},{4,0},{8,12},{12,8},{16,20},{20,16},{24,28},{28,24},{1,5},{5... | collective-permute-start | bytes 393224 | tf_op jit(solution)/shard_map/ppermute | solution.py:17
  7.2 15.8 %collective-permute-start.2 = (bf16[2,128,256]{2,1,0:T(8,128)(2,1)S(1)}, bf16[2,128,256]{2,1,0:T(8,128)(2,1)S(1)}, u32[]{:S(2)}, u32[]{:S(2)}) collective-permute-start(bf16[2,128,256]{2,1,0:T(8,128)(2,1)S(1)} %get-tuple-element.46), channel_id=1, source_target_pairs={{0,20},{4,16},{8,28},{12,24},{16,4},{20,0},{24,12},{28,8},{1,21},{... | collective-permute-start | bytes 393224 | tf_op jit(solution)/shard_map/ppermute | solution.py:17
  10.7 12.8 %collective-permute-start.1 = (bf16[2,128,256]{2,1,0:T(8,128)(2,1)S(1)}, bf16[2,128,256]{2,1,0:T(8,128)(2,1)S(1)}, u32[]{:S(2)}, u32[]{:S(2)}) collective-permute-start(bf16[2,128,256]{2,1,0:T(8,128)(2,1)S(1)} %get-tuple-element.46), channel_id=1, source_target_pairs={{0,16},{4,20},{8,24},{12,28},{16,0},{20,4},{24,8},{28,12},{1,17},{... | collective-permute-start | bytes 393224 | tf_op jit(solution)/shard_map/ppermute | solution.py:17
  24.5 9.7 %collective-permute-start.6 = (bf16[3,2,128,256]{3,2,1,0:T(8,128)(2,1)S(1)}, bf16[3,2,128,256]{3,2,1,0:T(8,128)(2,1)S(1)}, u32[]{:S(2)}, u32[]{:S(2)}) collective-permute-start(bf16[3,2,128,256]{3,2,1,0:T(8,128)(2,1)S(1)} %pad_maximum_fusion.refs_1_), channel_id=1, source_target_pairs={{0,2},{1,3},{2,0},{3,1},{4,6},{5,7},{6,4},{7,5},{8,10},{9,11},{10,... | collective-permute-start | bytes 1179656 | tf_op jit(solution)/shard_map/ppermute | solution.py:17
  26.0 13.5 %collective-permute-start.8 = (bf16[3,352,256]{2,1,0:T(8,128)(2,1)S(1)}, bf16[3,352,256]{2,1,0:T(8,128)(2,1)S(1)}, u32[]{:S(2)}, u32[]{:S(2)}) collective-permute-start(bf16[3,352,256]{2,1,0:T(8,128)(2,1)S(1)} %collective-permute-done.3.refs_6_), channel_id=1, source_target_pairs={{0,8},{4,12},{8,0},{12,4},{16,24},{20,28},{24,16},{28,20},{1,9},{5... | collective-permute-start | bytes 1622024 | tf_op jit(solution)/shard_map/ppermute | solution.py:17
  28.7 5.4 %collective-permute-start.5 = (bf16[3,2,128,256]{3,2,1,0:T(8,128)(2,1)S(1)}, bf16[3,2,128,256]{3,2,1,0:T(8,128)(2,1)S(1)}, u32[]{:S(2)}, u32[]{:S(2)}) collective-permute-start(bf16[3,2,128,256]{3,2,1,0:T(8,128)(2,1)S(1)} %pad_maximum_fusion.refs_1_), channel_id=1, source_target_pairs={{0,1},{1,0},{2,3},{3,2},{4,5},{5,4},{6,7},{7,6},{8,9},{9,8},{10,11... | collective-permute-start | bytes 1179656 | tf_op jit(solution)/shard_map/ppermute | solution.py:17
  34.1 1.7 %collective-permute-start.7 = (bf16[3,2,128,256]{3,2,1,0:T(8,128)(2,1)S(1)}, bf16[3,2,128,256]{3,2,1,0:T(8,128)(2,1)S(1)}, u32[]{:S(2)}, u32[]{:S(2)}) collective-permute-start(bf16[3,2,128,256]{3,2,1,0:T(8,128)(2,1)S(1)} %collective-permute-done.6.refs_3_), channel_id=1, source_target_pairs={{0,1},{1,0},{2,3},{3,2},{4,5},{5,4},{6,7},{7,6},{8,9},{9,8},{10,11... | collective-permute-start | bytes 1179656 | tf_op jit(solution)/shard_map/ppermute | solution.py:17
  42.3 3.2 %collective-permute-start.9 = (bf16[2,1040,256]{2,1,0:T(8,128)(2,1)S(1)}, bf16[2,1040,256]{2,1,0:T(8,128)(2,1)S(1)}, u32[]{:S(2)}, u32[]{:S(2)}) collective-permute-start(bf16[2,1040,256]{2,1,0:T(8,128)(2,1)S(1)} %get-tuple-element.57), channel_id=1, source_target_pairs={{0,1},{1,0},{2,3},{3,2},{4,5},{5,4},{6,7},{7,6},{8,9},{9,8},{10,11... | collective-permute-start | bytes 3194888 | tf_op jit(solution)/shard_map/ppermute | solution.py:17
  43.7 15.1 %collective-permute-start.16 = (bf16[3,352,256]{2,1,0:T(8,128)(2,1)S(1)}, bf16[3,352,256]{2,1,0:T(8,128)(2,1)S(1)}, u32[]{:S(2)}, u32[]{:S(2)}) collective-permute-start(bf16[3,352,256]{2,1,0:T(8,128)(2,1)S(1)} %get-tuple-element.78), channel_id=1, source_target_pairs={{0,8},{4,12},{8,0},{12,4},{16,24},{20,28},{24,16},{28,20},{1,9},{5... | collective-permute-start | bytes 1622024 | tf_op jit(solution)/shard_map/ppermute | solution.py:17
  45.6 10.4 %collective-permute-start.10 = (bf16[528,256]{1,0:T(8,128)(2,1)S(1)}, bf16[528,256]{1,0:T(8,128)(2,1)S(1)}, u32[]{:S(2)}, u32[]{:S(2)}) collective-permute-start(bf16[528,256]{1,0:T(8,128)(2,1)S(1)} %get-tuple-element.58), channel_id=1, source_target_pairs={{0,2},{1,3},{2,0},{3,1},{4,6},{5,7},{6,4},{7,5},{8,10},{9,11},{10,... | collective-permute-start | bytes 811016 | tf_op jit(solution)/shard_map/ppermute | solution.py:17
  46.4 8.0 %collective-permute-start.12 = (bf16[2,256,256]{2,1,0:T(8,128)(2,1)S(1)}, bf16[2,256,256]{2,1,0:T(8,128)(2,1)S(1)}, u32[]{:S(2)}, u32[]{:S(2)}) collective-permute-start(bf16[2,256,256]{2,1,0:T(8,128)(2,1)S(1)} %get-tuple-element.61), channel_id=1, source_target_pairs={{0,4},{4,0},{8,12},{12,8},{16,20},{20,16},{24,28},{28,24},{1,5},{5... | collective-permute-start | bytes 786440 | tf_op jit(solution)/shard_map/ppermute | solution.py:17
  54.5 5.0 %collective-permute-start.13 = (bf16[256,256]{1,0:T(8,128)(2,1)S(1)}, bf16[256,256]{1,0:T(8,128)(2,1)S(1)}, u32[]{:S(2)}, u32[]{:S(2)}) collective-permute-start(bf16[256,256]{1,0:T(8,128)(2,1)S(1)} %get-tuple-element.63), channel_id=1, source_target_pairs={{0,2},{1,3},{2,0},{3,1},{4,6},{5,7},{6,4},{7,5},{8,10},{9,11},{10,... | collective-permute-start | bytes 393224 | tf_op jit(solution)/shard_map/ppermute | solution.py:17
  56.1 5.4 %collective-permute-start.11 = (bf16[272,256]{1,0:T(8,128)(2,1)S(1)}, bf16[272,256]{1,0:T(8,128)(2,1)S(1)}, u32[]{:S(2)}, u32[]{:S(2)}) collective-permute-start(bf16[272,256]{1,0:T(8,128)(2,1)S(1)} %get-tuple-element.60), channel_id=1, source_target_pairs={{0,4},{4,0},{8,12},{12,8},{16,20},{20,16},{24,28},{28,24},{1,5},{5... | collective-permute-start | bytes 417800 | tf_op jit(solution)/shard_map/ppermute | solution.py:17
  56.7 16.4 %collective-permute-start.15 = (bf16[3,352,256]{2,1,0:T(8,128)(2,1)S(1)}, bf16[3,352,256]{2,1,0:T(8,128)(2,1)S(1)}, u32[]{:S(2)}, u32[]{:S(2)}) collective-permute-start(bf16[3,352,256]{2,1,0:T(8,128)(2,1)S(1)} %get-tuple-element.73), channel_id=1, source_target_pairs={{0,8},{4,12},{8,0},{12,4},{16,24},{20,28},{24,16},{28,20},{1,9},{5... | collective-permute-start | bytes 1622024 | tf_op jit(solution)/shard_map/ppermute | solution.py:17
  59.0 15.1 %collective-permute-start.17 = (bf16[3,352,256]{2,1,0:T(8,128)(2,1)S(1)}, bf16[3,352,256]{2,1,0:T(8,128)(2,1)S(1)}, u32[]{:S(2)}, u32[]{:S(2)}) collective-permute-start(bf16[3,352,256]{2,1,0:T(8,128)(2,1)S(1)} %add_convert_fusion), channel_id=1, source_target_pairs={{0,4},{4,0},{8,12},{12,8},{16,20},{20,16},{24,28},{28,24},{1,5},{5... | collective-permute-start | bytes 1622024 | tf_op jit(solution)/shard_map/ppermute | solution.py:17
  61.5 10.8 %copy-start = (f32[128]{0:T(128)S(1)}, f32[128]{0:T(128)}, u32[]{:S(2)}) copy-start(f32[128]{0:T(128)} %param.10) | copy-start | bytes 1540
  61.5 10.7 %collective-permute-start.14 = (bf16[272,256]{1,0:T(8,128)(2,1)S(1)}, bf16[272,256]{1,0:T(8,128)(2,1)S(1)}, u32[]{:S(2)}, u32[]{:S(2)}) collective-permute-start(bf16[272,256]{1,0:T(8,128)(2,1)S(1)} %get-tuple-element.65), channel_id=1, source_target_pairs={{0,16},{4,20},{8,24},{12,28},{16,0},{20,4},{24,8},{28,12},{1,17},{... | collective-permute-start | bytes 417800 | tf_op jit(solution)/shard_map/ppermute | solution.py:17

commit v7 on v5

--- a/solution.py
+++ b/solution.py
@@ -169,13 +169,20 @@
     )(*([own] if has_own else []), *pieces, *weights)
 
 
-def outer_kernel(x_all, s_all, w_part, part, last, units, kept, sent, w_all):
+def grad_parts(units, x_all, s_all, column, out):
+    half, total = units.shape[1:]
+    both = dot_nn(units[0:2].reshape(2 * half, total), x_all[:, column])
+    out[0] = both[:half].astype(out.dtype)
+    out[1] = both[half:].astype(out.dtype)
+    out[2] = dot_nn(units[2], s_all[:, column]).astype(out.dtype)
+
+
+def outer_kernel(x_all, s_all, w_part, part, last, units, kept, sent, to_d, w_all, sem):
     width = last.shape[2]
+    copy = pltpu.make_async_copy(w_part, w_all, sem)
+    copy.start()
     place = lax.axis_index("narrow")
     last_column = at_quarter(lax.axis_index("wide") % 4 ^ 3, width)
-    w_all[...] = w_part[...]
-    for i in range(3):
-        w_all[i, :, last_column] = last[i]
     total = x_all.shape[0]
     tile = min(width, total)
     for ref in (kept, sent):
@@ -188,10 +195,11 @@
         gate = part[0, :, rows] + dot_nt(last[0], x_tile)
         up = part[1, :, rows] + dot_nt(last[1], x_tile)
         d_hidden = part[2, :, rows] + dot_nt(last[2], s_tile)
-        sigma = jax.nn.sigmoid(gate)
+        sigma = 0.5 + 0.5 * jnp.tanh(0.5 * gate)
         active = gate * sigma
         hidden = (active * up).astype(jnp.bfloat16)
-        d_gate = (d_hidden * up * sigma * (1.0 + gate * (1.0 - sigma))).astype(jnp.bfloat16)
+        slope = sigma + active * (1.0 - sigma)
+        d_gate = (d_hidden * up * slope).astype(jnp.bfloat16)
         d_up = (d_hidden * active).astype(jnp.bfloat16)
         units[0, :, rows] = d_gate
         units[1, :, rows] = d_up
@@ -200,6 +208,10 @@
         kept[0, 2 * total + step : 2 * total + step + 1, :tile] = router
         routers.append(router)
         hidden_t, d_gate_t, d_up_t = hidden.T, d_gate.T, d_up.T
+        if step == 0:
+            copy.wait()
+            for i in range(3):
+                w_all[i, :, last_column] = last[i]
         for mask in range(4):
             column = at_quarter(place ^ mask, width)
             target = sent if mask % 2 else kept
@@ -208,6 +220,7 @@
             target[mask // 2, rows, :] = out_part.astype(target.dtype)
             target[mask // 2, lower, :] = in_part.astype(target.dtype)
     put_pair(sent.at[0], 2 * total, jnp.concatenate(routers, 0))
+    grad_parts(units, x_all, s_all, last_column, to_d)
 
 
 def outer(x_all, s_all, w_part, part, last):
@@ -219,10 +232,14 @@
             jax.ShapeDtypeStruct((3, half, total), jnp.bfloat16),
             jax.ShapeDtypeStruct((2, packet_rows(total), width), jnp.float32),
             jax.ShapeDtypeStruct((2, packet_rows(total), width), jnp.bfloat16),
+            jax.ShapeDtypeStruct(last.shape, jnp.bfloat16),
         ),
         in_specs=[VMEM] * 5,
-        out_specs=[VMEM] * 3,
-        scratch_shapes=[pltpu.VMEM((3, half, features), jnp.bfloat16)],
+        out_specs=[VMEM] * 4,
+        scratch_shapes=[
+            pltpu.VMEM((3, half, features), jnp.bfloat16),
+            pltpu.SemaphoreType.DMA,
+        ],
         compiler_params=PARAMS,
         cost_estimate=pl.CostEstimate(
             flops=8 * half * features * total, bytes_accessed=0, transcendentals=0
@@ -231,16 +248,10 @@
 
 
 def grads_kernel(units, x_all, s_all, *outs):
-    half, total = units.shape[1:]
     width = outs[0].shape[2]
     member = lax.axis_index("wide") % 4
-    left = units[0:2].reshape(2 * half, total)
-    for k in (3, 2, 1, 0):
-        column = at_quarter(member ^ k, width)
-        both = dot_nn(left, x_all[:, column])
-        outs[k][0] = both[:half].astype(outs[k].dtype)
-        outs[k][1] = both[half:].astype(outs[k].dtype)
-        outs[k][2] = dot_nn(units[2], s_all[:, column]).astype(outs[k].dtype)
+    for k, out in enumerate(outs):
+        grad_parts(units, x_all, s_all, at_quarter(member ^ k, width), out)
 
 
 def weight_grads(units, x_all, s_all):
@@ -250,37 +261,49 @@
         grads_kernel,
         out_shape=tuple(
             jax.ShapeDtypeStruct((3, half, features // 4), jnp.bfloat16 if k > 1 else jnp.float32)
-            for k in range(4)
+            for k in range(3)
         ),
         in_specs=[VMEM] * 3,
-        out_specs=[VMEM] * 4,
+        out_specs=[VMEM] * 3,
         compiler_params=PARAMS,
         cost_estimate=pl.CostEstimate(
-            flops=6 * half * features * total, bytes_accessed=0, transcendentals=0
+            flops=5 * half * features * total, bytes_accessed=0, transcendentals=0
         ),
     )(units, x_all, s_all)
 
 
-def join_kernel(own, got_x, got_z, *outs):
-    half = own.shape[1]
+def join_kernel(own, got_x, out_0, out_1, out_2, held, sems):
+    half = held.shape[1]
     x_bit = lax.axis_index("wide") % 2
-    keep_rows = pl.ds(pl.multiple_of(x_bit * half, 16), half)
-    give_rows = pl.ds(pl.multiple_of((1 - x_bit) * half, 16), half)
-    for i, ref in enumerate(outs):
-        ref[keep_rows, :] = own[i] + got_z[i].astype(jnp.float32)
-        ref[give_rows, :] = got_x[i].astype(jnp.float32)
-
-
-def join_grads(own, got_x, got_z):
+    copies = []
+    for part, held_part in enumerate((own, held)):
+        first = (part * (1 - x_bit) + (1 - part) * x_bit) * half
+        rows = pl.ds(pl.multiple_of(first, 16), half)
+        for i, out in enumerate((out_0, out_1, out_2)):
+            if part:
+                held[i] = got_x[i].astype(jnp.float32)
+            place = sems.at[3 * part + i]
+            copies.append(pltpu.make_async_copy(held_part.at[i], out.at[rows, :], place))
+            copies[-1].start()
+    for copy in copies:
+        copy.wait()
+
+
+def join_grads(own, got_x):
     _, half, width = own.shape
     shape = jax.ShapeDtypeStruct((2 * half, width), jnp.float32)
     return pl.pallas_call(
         join_kernel,
         out_shape=(shape,) * 3,
-        in_specs=[VMEM] * 3,
-        out_specs=[VMEM] * 3,
-        compiler_params=PARAMS,
-    )(own, got_x, got_z)
+        in_specs=[VMEM] * 2,
+        out_specs=[HBM] * 3,
+        scratch_shapes=[
+            pltpu.VMEM(own.shape, jnp.float32),
+            pltpu.SemaphoreType.DMA((6,)),
+        ],
+        compiler_params=PARAMS,
+        cost_estimate=pl.CostEstimate(flops=1, bytes_accessed=0, transcendentals=0),
+    )(own, got_x)
 
 
 def cross_kernel(kept, got, sent):
@@ -443,7 +466,7 @@
         in_specs=[VMEM] * 4,
         out_specs=[VMEM] * 2,
         compiler_params=PARAMS,
-        cost_estimate=pl.CostEstimate(flops=10**10, bytes_accessed=0, transcendentals=0),
+        cost_estimate=pl.CostEstimate(flops=3 * 10**9, bytes_accessed=0, transcendentals=0),
     )(ffn, from_x, grad, from_y)
 
 
@@ -520,22 +543,23 @@
             routed, "wide", split_axis=0, concat_axis=0, axis_index_groups=groups, tiled=True
         )
 
-    mine, from_x, from_z = lax.optimization_barrier(
-        (mine, partner(give, "wide", 1), partner(keep, "wide", 2))
+    from_x, from_z = lax.optimization_barrier(
+        (partner(give, "wide", 1), partner(keep, "wide", 2))
     )
     from_d = partner(from_x, "wide", 2)
     across = partner(mine, "narrow", 2)
     pieces = (mine, partner(mine, "narrow", 1), across, partner(across, "narrow", 1))
     x_all, s_all, w_part, part = gather_parts(own, pieces, (keep, from_x, from_z))
-    units, kept, sent = outer(x_all, s_all, w_part, part, from_d)
+    units, kept, sent, grad_d = outer(x_all, s_all, w_part, part, from_d)
     got = partner(sent, "narrow", 1)
-    grad_own, grad_x, grad_z, grad_d = weight_grads(units, x_all, s_all)
     got_d = partner(grad_d, "wide", 2)
     if direct:
         to_y, to_x = first_parts(kept, got)
+        units, _ = lax.optimization_barrier((units, to_y))
         ffn_held, ffn_x = ffn_parts(kept, got, partner(to_y, "narrow", 2))
         grad_held, grad_y = input_parts(kept, got, partner(to_x, "wide", 1))
-        grad_x, _, _ = lax.optimization_barrier((grad_x, ffn_x, grad_y))
+        grad_own, grad_x, grad_z = weight_grads(units, x_all, s_all)
+        grad_x, grad_z, _, _ = lax.optimization_barrier((grad_x, grad_z, ffn_x, grad_y))
         held, to_z = last_parts(
             ffn_held, partner(ffn_x, "wide", 1), grad_held, partner(grad_y, "narrow", 2)
         )
@@ -544,6 +568,7 @@
         )
         prob_grad = prob_grad[0]
     else:
+        grad_own, grad_x, grad_z = weight_grads(units, x_all, s_all)
         across = partner(cross_part(kept, got), "narrow", 2)
         result = result_parts(kept, got, across)
         total = (result.shape[0] - EXTRA) // 2
@@ -567,10 +592,9 @@
         output = (route_prob[:, None] * ffn).astype(jnp.bfloat16)
         tokens_grad = back[1].astype(jnp.bfloat16)
     grad_x = (grad_x + got_d.astype(jnp.float32)).astype(jnp.bfloat16)
-    grad_x, grad_z = lax.optimization_barrier((grad_x, grad_z))
     got_x = partner(grad_x, "wide", 1)
     got_z = partner(grad_z, "wide", 2)
-    gate_grad, up_grad, down_grad = join_grads(grad_own, got_x, got_z)
+    gate_grad, up_grad, down_grad = join_grads(grad_own + got_z.astype(jnp.float32), got_x)
     return (output, tokens_grad, prob_grad, gate_grad.T, up_grad.T, down_grad.T)
 
 

time: 77.4 us -> 74.4 us (0.961)
  waiting for transfers between devices: 44.3 us -> 38.9 us
  starting transfers between devices: 22.2 us -> 24.2 us
    ppermute x18, waiting for transfers between devices: 44.3 us -> 38.9 us  [partner(): lax.ppermute(x, axis, [(i, i ^ mask) for i in range(lax.axis_size(axis))])]
    ppermute x18, starting transfers between devices: 22.2 us -> 24.2 us  [partner(): lax.ppermute(x, axis, [(i, i ^ mask) for i in range(lax.axis_size(axis))])]
where the time goes in v7:
time: 74.4 us; the launch traced here: 74.2 us
  waiting for transfers between devices  38.9 us (52%)
  starting transfers between devices  24.2 us (33%)
  Pallas kernels  10.1 us (14%)
    ppermute x18, waiting for transfers between devices, partner(): lax.ppermute(x, axis, [(i, i ^ mask) for i in range(lax.axis_size(axis))])  38.9 us
    ppermute x18, starting transfers between devices, partner(): lax.ppermute(x, axis, [(i, i ^ mask) for i in range(lax.axis_size(axis))])  24.2 us
    pallas_call x1, Pallas kernels, outer(): pl.pallas_call(outer_kernel, out_shape=(jax.ShapeDtypeStruct((3, half, to...  3.35 us
    pallas_call x1, Pallas kernels, gather_parts(): pl.pallas_call(functools.partial(gather_kernel, int(has_own)), out_shape=...  1.74 us
  transfers between devices with their start and end apart: 18, of which 10 were waited for; matrix products, arithmetic and copies ran while one was open for 0% of the time, Pallas kernels for 5%

profile of v7, /device:TPU:0, one launch (start us, length us, event | category | flops | bytes accessed | tf_op | source)
XLA Modules:
  0.0 74.2 jit_solution(16173256877118237514)
XLA Ops:
  0.6 1.5 %shard_map.118 = (bf16[3,352,256]{2,1,0:T(8,128)(2,1)S(1)}, bf16[3,352,256]{2,1,0:T(8,128)(2,1)S(1)}, bf16[2,128,1024]{2,1,0:T(8,128)(2,1)S(1)}, bf16[2,128,256]...) custom-call(bf16[704,256]{1,0:T(8,128)(2,1)} %bitcast.14, bf16[704,256]{1,0:T(8,128)(2,1)} %bitcast.15, ...), custom_call_target="tpu_custom_call" | custom-call | tf_op jit(solution)/shard_map/pallas_call | solution.py:103
  2.1 3.0 %collective-permute-start.6 = (bf16[3,352,256]{2,1,0:T(8,128)(2,1)S(1)}, bf16[3,352,256]{2,1,0:T(8,128)(2,1)S(1)}, u32[]{:S(2)}, u32[]{:S(2)}) collective-permute-start(bf16[3,352,256]{2,1,0:T(8,128)(2,1)S(1)} %get-tuple-element.45), channel_id=1, source_target_pairs={{0,4},{4,0},{8,12},{12,8},{16,20},{20,16},{24,28},{28,24},{1,5},{5... | collective-permute-start | bytes 1622024 | tf_op jit(solution)/shard_map/ppermute | solution.py:17
  5.1 1.6 %collective-permute-start.7 = (bf16[3,352,256]{2,1,0:T(8,128)(2,1)S(1)}, bf16[3,352,256]{2,1,0:T(8,128)(2,1)S(1)}, u32[]{:S(2)}, u32[]{:S(2)}) collective-permute-start(bf16[3,352,256]{2,1,0:T(8,128)(2,1)S(1)} %get-tuple-element.44.refs_5_), channel_id=1, source_target_pairs={{0,8},{4,12},{8,0},{12,4},{16,24},{20,28},{24,16},{28,20},{1,9},{5... | collective-permute-start | bytes 1622024 | tf_op jit(solution)/shard_map/ppermute | solution.py:17
  7.2 3.5 %collective-permute-start.2 = (bf16[2,128,256]{2,1,0:T(8,128)(2,1)S(1)}, bf16[2,128,256]{2,1,0:T(8,128)(2,1)S(1)}, u32[]{:S(2)}, u32[]{:S(2)}) collective-permute-start(bf16[2,128,256]{2,1,0:T(8,128)(2,1)S(1)} %get-tuple-element.43), channel_id=1, source_target_pairs={{0,20},{4,16},{8,28},{12,24},{16,4},{20,0},{24,12},{28,8},{1,21},{... | collective-permute-start | bytes 393224 | tf_op jit(solution)/shard_map/ppermute | solution.py:17
  11.1 11.9 %collective-permute-done = bf16[2,128,256]{2,1,0:T(8,128)(2,1)S(1)} collective-permute-done((bf16[2,128,256]{2,1,0:T(8,128)(2,1)S(1)}, bf16[2,128,256]{2,1,0:T(8,128)(2,1)S(1)}, u32[]{:S(2)}, u32[]{:S(2)}) %collective-permute-start) | collective-permute-done | bytes 131104 | tf_op jit(solution)/shard_map/ppermute | solution.py:17
  23.6 1.6 %collective-permute-start.4 = (bf16[3,2,128,256]{3,2,1,0:T(8,128)(2,1)S(1)}, bf16[3,2,128,256]{3,2,1,0:T(8,128)(2,1)S(1)}, u32[]{:S(2)}, u32[]{:S(2)}) collective-permute-start(bf16[3,2,128,256]{3,2,1,0:T(8,128)(2,1)S(1)} %pad_maximum_fusion.refs_1_), channel_id=1, source_target_pairs={{0,2},{1,3},{2,0},{3,1},{4,6},{5,7},{6,4},{7,5},{8,10},{9,11},{10,... | collective-permute-start | bytes 1179656 | tf_op jit(solution)/shard_map/ppermute | solution.py:17
  25.2 3.5 %collective-permute-start.8 = (bf16[3,352,256]{2,1,0:T(8,128)(2,1)S(1)}, bf16[3,352,256]{2,1,0:T(8,128)(2,1)S(1)}, u32[]{:S(2)}, u32[]{:S(2)}) collective-permute-start(bf16[3,352,256]{2,1,0:T(8,128)(2,1)S(1)} %collective-permute-done.6.refs_6_), channel_id=1, source_target_pairs={{0,8},{4,12},{8,0},{12,4},{16,24},{20,28},{24,16},{28,20},{1,9},{5... | collective-permute-start | bytes 1622024 | tf_op jit(solution)/shard_map/ppermute | solution.py:17
  28.7 4.7 %collective-permute-done.4.refs_3_ = bf16[3,2,128,256]{3,2,1,0:T(8,128)(2,1)S(1)} collective-permute-done((bf16[3,2,128,256]{3,2,1,0:T(8,128)(2,1)S(1)}, bf16[3,2,128,256]{3,2,1,0:T(8,128)(2,1)S(1)}, u32[]{:S(2)}, u32[]{:S(2)}) %collective-permute-start.4) | collective-permute-done | bytes 393248 | tf_op jit(solution)/shard_map/ppermute | solution.py:17
  33.4 1.7 %collective-permute-done.5.refs_4_ = bf16[3,2,128,256]{3,2,1,0:T(8,128)(2,1)S(1)} collective-permute-done((bf16[3,2,128,256]{3,2,1,0:T(8,128)(2,1)S(1)}, bf16[3,2,128,256]{3,2,1,0:T(8,128)(2,1)S(1)}, u32[]{:S(2)}, u32[]{:S(2)}) %collective-permute-start.5) | collective-permute-done | bytes 393248 | tf_op jit(solution)/shard_map/ppermute | solution.py:17
  35.2 1.7 %shard_map.119 = (bf16[512,1024]{1,0:T(8,128)(2,1)S(1)}, bf16[512,1024]{1,0:T(8,128)(2,1)S(1)}, bf16[3,352,1024]{2,1,0:T(8,128)(2,1)S(1)}, f32[3,352,512]{2,1,0:T(8,128)S(1)}) custom-call(bf16[2,128,1024]{2,1,0:T(8,128)(2,1)S(1)} %get-tuple-element.41.refs_0_, bf16[3,2,128,256]{3,2,1,0:T(8,128)(2,1)S(1)} %pad_maximum_fusion.refs_1_, ...), custom_call_target="tpu_custom_call" | custom-call | flops 1 | bytes 1 | tf_op jit(solution)/shard_map/pallas_call | solution.py:157
  36.9 2.6 %collective-permute-done.8.last = bf16[3,352,256]{2,1,0:T(8,128)(2,1)S(1)} collective-permute-done((bf16[3,352,256]{2,1,0:T(8,128)(2,1)S(1)}, bf16[3,352,256]{2,1,0:T(8,128)(2,1)S(1)}, u32[]{:S(2)}, u32[]{:S(2)}) %collective-permute-start.8) | collective-permute-done | bytes 540704 | tf_op jit(solution)/shard_map/ppermute | solution.py:17
  39.5 3.3 %shard_map.120 = (bf16[3,352,512]{2,1,0:T(8,128)(2,1)S(1)}, f32[2,1040,256]{2,1,0:T(8,128)S(1)}, bf16[2,1040,256]{2,1,0:T(8,128)(2,1)S(1)}, bf16[3,352,256]{2,1,0:T(8,128)(2,1)S(1)}) custom-call(bf16[512,1024]{1,0:T(8,128)(2,1)S(1)} %get-tuple-element.48.x_all, bf16[512,1024]{1,0:T(8,128)(2,1)S(1)} %get-tuple-element.49.s_all, ...), custom_call_target="tpu_custom_call" | custom-call | flops 1476395008 | tf_op jit(solution)/shard_map/pallas_call | solution.py:229
  42.9 1.8 %collective-permute-start.16 = (bf16[3,352,256]{2,1,0:T(8,128)(2,1)S(1)}, bf16[3,352,256]{2,1,0:T(8,128)(2,1)S(1)}, u32[]{:S(2)}, u32[]{:S(2)}) collective-permute-start(bf16[3,352,256]{2,1,0:T(8,128)(2,1)S(1)} %get-tuple-element.72), channel_id=1, source_target_pairs={{0,8},{4,12},{8,0},{12,4},{16,24},{20,28},{24,16},{28,20},{1,9},{5... | collective-permute-start | bytes 1622024 | tf_op jit(solution)/shard_map/ppermute | solution.py:17
  44.7 0.9 %collective-permute-done.9.got = bf16[2,1040,256]{2,1,0:T(8,128)(2,1)S(1)} collective-permute-done((bf16[2,1040,256]{2,1,0:T(8,128)(2,1)S(1)}, bf16[2,1040,256]{2,1,0:T(8,128)(2,1)S(1)}, u32[]{:S(2)}, u32[]{:S(2)}) %collective-permute-start.9) | collective-permute-done | bytes 1064992 | tf_op jit(solution)/shard_map/ppermute | solution.py:17
  46.8 1.0 %shard_map.126 = (f32[3,352,256]{2,1,0:T(8,128)S(1)}, f32[3,352,256]{2,1,0:T(8,128)S(1)}, bf16[3,352,256]{2,1,0:T(8,128)(2,1)S(1)}) custom-call(bf16[3,352,512]{2,1,0:T(8,128)(2,1)S(1)} %get-tuple-element.66.units, bf16[512,1024]{1,0:T(8,128)(2,1)S(1)} %get-tuple-element.48.x_all, bf16[512,1024]{1,0:T(8,128)(2,1)S(1)} %get-tuple-element.49.s_all), custom_call_target="tpu_custom_call" | custom-call | flops 922746880 | tf_op jit(solution)/shard_map/pallas_call | solution.py:260
  47.8 6.5 %collective-permute-done.12.from_x = bf16[2,256,256]{2,1,0:T(8,128)(2,1)S(1)} collective-permute-done((bf16[2,256,256]{2,1,0:T(8,128)(2,1)S(1)}, bf16[2,256,256]{2,1,0:T(8,128)(2,1)S(1)}, u32[]{:S(2)}, u32[]{:S(2)}) %collective-permute-start.12) | collective-permute-done | bytes 262176 | tf_op jit(solution)/shard_map/ppermute | solution.py:17
  54.4 1.6 %collective-permute-start.13 = (bf16[256,256]{1,0:T(8,128)(2,1)S(1)}, bf16[256,256]{1,0:T(8,128)(2,1)S(1)}, u32[]{:S(2)}, u32[]{:S(2)}) collective-permute-start(bf16[256,256]{1,0:T(8,128)(2,1)S(1)} %get-tuple-element.59), channel_id=1, source_target_pairs={{0,2},{1,3},{2,0},{3,1},{4,6},{5,7},{6,4},{7,5},{8,10},{9,11},{10,... | collective-permute-start | bytes 393224 | tf_op jit(solution)/shard_map/ppermute | solution.py:17
  56.7 1.7 %collective-permute-start.15 = (bf16[3,352,256]{2,1,0:T(8,128)(2,1)S(1)}, bf16[3,352,256]{2,1,0:T(8,128)(2,1)S(1)}, u32[]{:S(2)}, u32[]{:S(2)}) collective-permute-start(bf16[3,352,256]{2,1,0:T(8,128)(2,1)S(1)} %get-tuple-element.70), channel_id=1, source_target_pairs={{0,8},{4,12},{8,0},{12,4},{16,24},{20,28},{24,16},{28,20},{1,9},{5... | collective-permute-start | bytes 1622024 | tf_op jit(solution)/shard_map/ppermute | solution.py:17
  58.6 1.6 %collective-permute-start.17 = (bf16[3,352,256]{2,1,0:T(8,128)(2,1)S(1)}, bf16[3,352,256]{2,1,0:T(8,128)(2,1)S(1)}, u32[]{:S(2)}, u32[]{:S(2)}) collective-permute-start(bf16[3,352,256]{2,1,0:T(8,128)(2,1)S(1)} %add_convert_fusion), channel_id=1, source_target_pairs={{0,4},{4,0},{8,12},{12,8},{16,20},{20,16},{24,28},{28,24},{1,5},{5... | collective-permute-start | bytes 1622024 | tf_op jit(solution)/shard_map/ppermute | solution.py:17
  60.1 2.3 %collective-permute-done.11.from_x = bf16[272,256]{1,0:T(8,128)(2,1)S(1)} collective-permute-done((bf16[272,256]{1,0:T(8,128)(2,1)S(1)}, bf16[272,256]{1,0:T(8,128)(2,1)S(1)}, u32[]{:S(2)}, u32[]{:S(2)}) %collective-permute-start.11) | collective-permute-done | bytes 139296 | tf_op jit(solution)/shard_map/ppermute | solution.py:17
  62.5 1.7 %collective-permute-start.14 = (bf16[272,256]{1,0:T(8,128)(2,1)S(1)}, bf16[272,256]{1,0:T(8,128)(2,1)S(1)}, u32[]{:S(2)}, u32[]{:S(2)}) collective-permute-start(bf16[272,256]{1,0:T(8,128)(2,1)S(1)} %get-tuple-element.61), channel_id=1, source_target_pairs={{0,16},{4,20},{8,24},{12,28},{16,0},{20,4},{24,8},{28,12},{1,17},{... | collective-permute-start | bytes 417800 | tf_op jit(solution)/shard_map/ppermute | solution.py:17
  64.2 7.3 %collective-permute-done.14.refs_0_ = bf16[272,256]{1,0:T(8,128)(2,1)S(1)} collective-permute-done((bf16[272,256]{1,0:T(8,128)(2,1)S(1)}, bf16[272,256]{1,0:T(8,128)(2,1)S(1)}, u32[]{:S(2)}, u32[]{:S(2)}) %collective-permute-start.14) | collective-permute-done | bytes 139296 | tf_op jit(solution)/shard_map/ppermute | solution.py:17
  71.5 0.8 %shard_map.125 = (bf16[128,256]{1,0:T(8,128)(2,1)}, bf16[128,256]{1,0:T(8,128)(2,1)}, f32[1,128]{1,0:T(1,128)}) custom-call(f32[1,128]{1,0:T(1,128)S(1)} %bitcast.13, f32[272,256]{1,0:T(8,128)S(1)} %get-tuple-element.60.own, bf16[272,256]{1,0:T(8,128)(2,1)S(1)} %collective-permute-done.14.refs_0_), custom_call_target="tpu_custom_call" | custom-call | tf_op jit(solution)/shard_map/pallas_call | solution.py:491
  72.8 1.4 %shard_map.127 = (f32[704,256]{1,0:T(8,128)}, f32[704,256]{1,0:T(8,128)}, f32[704,256]{1,0:T(8,128)}) custom-call(f32[3,352,256]{2,1,0:T(8,128)S(1)} %convert_add_fusion.own, bf16[3,352,256]{2,1,0:T(8,128)(2,1)S(1)} %collective-permute-done.17.got_x), custom_call_target="tpu_custom_call" | custom-call | flops 1 | tf_op jit(solution)/shard_map/pallas_call | solution.py:295
  (27 shorter events, 4.2 us)
Async XLA Ops:
  2.1 23.1 %collective-permute-start.6 = (bf16[3,352,256]{2,1,0:T(8,128)(2,1)S(1)}, bf16[3,352,256]{2,1,0:T(8,128)(2,1)S(1)}, u32[]{:S(2)}, u32[]{:S(2)}) collective-permute-start(bf16[3,352,256]{2,1,0:T(8,128)(2,1)S(1)} %get-tuple-element.45), channel_id=1, source_target_pairs={{0,4},{4,0},{8,12},{12,8},{16,20},{20,16},{24,28},{28,24},{1,5},{5... | collective-permute-start | bytes 1622024 | tf_op jit(solution)/shard_map/ppermute | solution.py:17
  5.1 20.1 %collective-permute-start.7 = (bf16[3,352,256]{2,1,0:T(8,128)(2,1)S(1)}, bf16[3,352,256]{2,1,0:T(8,128)(2,1)S(1)}, u32[]{:S(2)}, u32[]{:S(2)}) collective-permute-start(bf16[3,352,256]{2,1,0:T(8,128)(2,1)S(1)} %get-tuple-element.44.refs_5_), channel_id=1, source_target_pairs={{0,8},{4,12},{8,0},{12,4},{16,24},{20,28},{24,16},{28,20},{1,9},{5... | collective-permute-start | bytes 1622024 | tf_op jit(solution)/shard_map/ppermute | solution.py:17
  6.7 16.3 %collective-permute-start = (bf16[2,128,256]{2,1,0:T(8,128)(2,1)S(1)}, bf16[2,128,256]{2,1,0:T(8,128)(2,1)S(1)}, u32[]{:S(2)}, u32[]{:S(2)}) collective-permute-start(bf16[2,128,256]{2,1,0:T(8,128)(2,1)S(1)} %get-tuple-element.42), channel_id=1, source_target_pairs={{0,4},{4,0},{8,12},{12,8},{16,20},{20,16},{24,28},{28,24},{1,5},{5... | collective-permute-start | bytes 393224 | tf_op jit(solution)/shard_map/ppermute | solution.py:17
  7.2 15.8 %collective-permute-start.2 = (bf16[2,128,256]{2,1,0:T(8,128)(2,1)S(1)}, bf16[2,128,256]{2,1,0:T(8,128)(2,1)S(1)}, u32[]{:S(2)}, u32[]{:S(2)}) collective-permute-start(bf16[2,128,256]{2,1,0:T(8,128)(2,1)S(1)} %get-tuple-element.43), channel_id=1, source_target_pairs={{0,20},{4,16},{8,28},{12,24},{16,4},{20,0},{24,12},{28,8},{1,21},{... | collective-permute-start | bytes 393224 | tf_op jit(solution)/shard_map/ppermute | solution.py:17
  10.7 12.8 %collective-permute-start.1 = (bf16[2,128,256]{2,1,0:T(8,128)(2,1)S(1)}, bf16[2,128,256]{2,1,0:T(8,128)(2,1)S(1)}, u32[]{:S(2)}, u32[]{:S(2)}) collective-permute-start(bf16[2,128,256]{2,1,0:T(8,128)(2,1)S(1)} %get-tuple-element.43), channel_id=1, source_target_pairs={{0,16},{4,20},{8,24},{12,28},{16,0},{20,4},{24,8},{28,12},{1,17},{... | collective-permute-start | bytes 393224 | tf_op jit(solution)/shard_map/ppermute | solution.py:17
  23.6 9.8 %collective-permute-start.4 = (bf16[3,2,128,256]{3,2,1,0:T(8,128)(2,1)S(1)}, bf16[3,2,128,256]{3,2,1,0:T(8,128)(2,1)S(1)}, u32[]{:S(2)}, u32[]{:S(2)}) collective-permute-start(bf16[3,2,128,256]{3,2,1,0:T(8,128)(2,1)S(1)} %pad_maximum_fusion.refs_1_), channel_id=1, source_target_pairs={{0,2},{1,3},{2,0},{3,1},{4,6},{5,7},{6,4},{7,5},{8,10},{9,11},{10,... | collective-permute-start | bytes 1179656 | tf_op jit(solution)/shard_map/ppermute | solution.py:17
  25.2 14.3 %collective-permute-start.8 = (bf16[3,352,256]{2,1,0:T(8,128)(2,1)S(1)}, bf16[3,352,256]{2,1,0:T(8,128)(2,1)S(1)}, u32[]{:S(2)}, u32[]{:S(2)}) collective-permute-start(bf16[3,352,256]{2,1,0:T(8,128)(2,1)S(1)} %collective-permute-done.6.refs_6_), channel_id=1, source_target_pairs={{0,8},{4,12},{8,0},{12,4},{16,24},{20,28},{24,16},{28,20},{1,9},{5... | collective-permute-start | bytes 1622024 | tf_op jit(solution)/shard_map/ppermute | solution.py:17
  28.7 4.7 %collective-permute-start.3 = (bf16[3,2,128,256]{3,2,1,0:T(8,128)(2,1)S(1)}, bf16[3,2,128,256]{3,2,1,0:T(8,128)(2,1)S(1)}, u32[]{:S(2)}, u32[]{:S(2)}) collective-permute-start(bf16[3,2,128,256]{3,2,1,0:T(8,128)(2,1)S(1)} %pad_maximum_fusion.refs_1_), channel_id=1, source_target_pairs={{0,1},{1,0},{2,3},{3,2},{4,5},{5,4},{6,7},{7,6},{8,9},{9,8},{10,11... | collective-permute-start | bytes 1179656 | tf_op jit(solution)/shard_map/ppermute | solution.py:17
  33.4 1.7 %collective-permute-start.5 = (bf16[3,2,128,256]{3,2,1,0:T(8,128)(2,1)S(1)}, bf16[3,2,128,256]{3,2,1,0:T(8,128)(2,1)S(1)}, u32[]{:S(2)}, u32[]{:S(2)}) collective-permute-start(bf16[3,2,128,256]{3,2,1,0:T(8,128)(2,1)S(1)} %collective-permute-done.4.refs_3_), channel_id=1, source_target_pairs={{0,1},{1,0},{2,3},{3,2},{4,5},{5,4},{6,7},{7,6},{8,9},{9,8},{10,11... | collective-permute-start | bytes 1179656 | tf_op jit(solution)/shard_map/ppermute | solution.py:17
  42.9 2.7 %collective-permute-start.9 = (bf16[2,1040,256]{2,1,0:T(8,128)(2,1)S(1)}, bf16[2,1040,256]{2,1,0:T(8,128)(2,1)S(1)}, u32[]{:S(2)}, u32[]{:S(2)}) collective-permute-start(bf16[2,1040,256]{2,1,0:T(8,128)(2,1)S(1)} %get-tuple-element.53), channel_id=1, source_target_pairs={{0,1},{1,0},{2,3},{3,2},{4,5},{5,4},{6,7},{7,6},{8,9},{9,8},{10,11... | collective-permute-start | bytes 3194888 | tf_op jit(solution)/shard_map/ppermute | solution.py:17
  42.9 15.5 %collective-permute-start.16 = (bf16[3,352,256]{2,1,0:T(8,128)(2,1)S(1)}, bf16[3,352,256]{2,1,0:T(8,128)(2,1)S(1)}, u32[]{:S(2)}, u32[]{:S(2)}) collective-permute-start(bf16[3,352,256]{2,1,0:T(8,128)(2,1)S(1)} %get-tuple-element.72), channel_id=1, source_target_pairs={{0,8},{4,12},{8,0},{12,4},{16,24},{20,28},{24,16},{28,20},{1,9},{5... | collective-permute-start | bytes 1622024 | tf_op jit(solution)/shard_map/ppermute | solution.py:17
  45.7 10.3 %collective-permute-start.10 = (bf16[528,256]{1,0:T(8,128)(2,1)S(1)}, bf16[528,256]{1,0:T(8,128)(2,1)S(1)}, u32[]{:S(2)}, u32[]{:S(2)}) collective-permute-start(bf16[528,256]{1,0:T(8,128)(2,1)S(1)} %get-tuple-element.54), channel_id=1, source_target_pairs={{0,2},{1,3},{2,0},{3,1},{4,6},{5,7},{6,4},{7,5},{8,10},{9,11},{10,... | collective-permute-start | bytes 811016 | tf_op jit(solution)/shard_map/ppermute | solution.py:17
  46.3 8.1 %collective-permute-start.12 = (bf16[2,256,256]{2,1,0:T(8,128)(2,1)S(1)}, bf16[2,256,256]{2,1,0:T(8,128)(2,1)S(1)}, u32[]{:S(2)}, u32[]{:S(2)}) collective-permute-start(bf16[2,256,256]{2,1,0:T(8,128)(2,1)S(1)} %get-tuple-element.57), channel_id=1, source_target_pairs={{0,4},{4,0},{8,12},{12,8},{16,20},{20,16},{24,28},{28,24},{1,5},{5... | collective-permute-start | bytes 786440 | tf_op jit(solution)/shard_map/ppermute | solution.py:17
  54.4 5.7 %collective-permute-start.13 = (bf16[256,256]{1,0:T(8,128)(2,1)S(1)}, bf16[256,256]{1,0:T(8,128)(2,1)S(1)}, u32[]{:S(2)}, u32[]{:S(2)}) collective-permute-start(bf16[256,256]{1,0:T(8,128)(2,1)S(1)} %get-tuple-element.59), channel_id=1, source_target_pairs={{0,2},{1,3},{2,0},{3,1},{4,6},{5,7},{6,4},{7,5},{8,10},{9,11},{10,... | collective-permute-start | bytes 393224 | tf_op jit(solution)/shard_map/ppermute | solution.py:17
  56.1 6.3 %collective-permute-start.11 = (bf16[272,256]{1,0:T(8,128)(2,1)S(1)}, bf16[272,256]{1,0:T(8,128)(2,1)S(1)}, u32[]{:S(2)}, u32[]{:S(2)}) collective-permute-start(bf16[272,256]{1,0:T(8,128)(2,1)S(1)} %get-tuple-element.56), channel_id=1, source_target_pairs={{0,4},{4,0},{8,12},{12,8},{16,20},{20,16},{24,28},{28,24},{1,5},{5... | collective-permute-start | bytes 417800 | tf_op jit(solution)/shard_map/ppermute | solution.py:17
  56.7 15.7 %collective-permute-start.15 = (bf16[3,352,256]{2,1,0:T(8,128)(2,1)S(1)}, bf16[3,352,256]{2,1,0:T(8,128)(2,1)S(1)}, u32[]{:S(2)}, u32[]{:S(2)}) collective-permute-start(bf16[3,352,256]{2,1,0:T(8,128)(2,1)S(1)} %get-tuple-element.70), channel_id=1, source_target_pairs={{0,8},{4,12},{8,0},{12,4},{16,24},{20,28},{24,16},{28,20},{1,9},{5... | collective-permute-start | bytes 1622024 | tf_op jit(solution)/shard_map/ppermute | solution.py:17
  58.6 14.2 %collective-permute-start.17 = (bf16[3,352,256]{2,1,0:T(8,128)(2,1)S(1)}, bf16[3,352,256]{2,1,0:T(8,128)(2,1)S(1)}, u32[]{:S(2)}, u32[]{:S(2)}) collective-permute-start(bf16[3,352,256]{2,1,0:T(8,128)(2,1)S(1)} %add_convert_fusion), channel_id=1, source_target_pairs={{0,4},{4,0},{8,12},{12,8},{16,20},{20,16},{24,28},{28,24},{1,5},{5... | collective-permute-start | bytes 1622024 | tf_op jit(solution)/shard_map/ppermute | solution.py:17
  62.4 9.1 %copy-start = (f32[128]{0:T(128)S(1)}, f32[128]{0:T(128)}, u32[]{:S(2)}) copy-start(f32[128]{0:T(128)} %param.10) | copy-start | bytes 1540
  62.5 9.0 %collective-permute-start.14 = (bf16[272,256]{1,0:T(8,128)(2,1)S(1)}, bf16[272,256]{1,0:T(8,128)(2,1)S(1)}, u32[]{:S(2)}, u32[]{:S(2)}) collective-permute-start(bf16[272,256]{1,0:T(8,128)(2,1)S(1)} %get-tuple-element.61), channel_id=1, source_target_pairs={{0,16},{4,20},{8,24},{12,28},{16,0},{20,4},{24,8},{28,12},{1,17},{... | collective-permute-start | bytes 417800 | tf_op jit(solution)/shard_map/ppermute | solution.py:17

commit v8 on v7

--- a/solution.py
+++ b/solution.py
@@ -169,20 +169,23 @@
     )(*([own] if has_own else []), *pieces, *weights)
 
 
-def grad_parts(units, x_all, s_all, column, out):
+def grad_parts(units, x_all, s_all, column, outs):
     half, total = units.shape[1:]
     both = dot_nn(units[0:2].reshape(2 * half, total), x_all[:, column])
-    out[0] = both[:half].astype(out.dtype)
-    out[1] = both[half:].astype(out.dtype)
-    out[2] = dot_nn(units[2], s_all[:, column]).astype(out.dtype)
-
-
-def outer_kernel(x_all, s_all, w_part, part, last, units, kept, sent, to_d, w_all, sem):
+    down = dot_nn(units[2], s_all[:, column])
+    for i, value in enumerate((both[:half], both[half:], down)):
+        out = outs[0] if i < 2 else outs[-1]
+        out[i if len(outs) == 1 else i % 2] = value.astype(out.dtype)
+
+
+def outer_kernel(x_all, s_all, w_part, part, last, units, kept, sent, *refs):
+    to_d, w_all = refs[:2], refs[2]
     width = last.shape[2]
-    copy = pltpu.make_async_copy(w_part, w_all, sem)
-    copy.start()
     place = lax.axis_index("narrow")
     last_column = at_quarter(lax.axis_index("wide") % 4 ^ 3, width)
+    w_all[...] = w_part[...]
+    for i in range(3):
+        w_all[i, :, last_column] = last[i]
     total = x_all.shape[0]
     tile = min(width, total)
     for ref in (kept, sent):
@@ -207,16 +210,12 @@
         router = jnp.sum(hidden.astype(jnp.float32) * d_hidden, axis=0, keepdims=True)
         kept[0, 2 * total + step : 2 * total + step + 1, :tile] = router
         routers.append(router)
-        hidden_t, d_gate_t, d_up_t = hidden.T, d_gate.T, d_up.T
-        if step == 0:
-            copy.wait()
-            for i in range(3):
-                w_all[i, :, last_column] = last[i]
+        hidden_t, d_both = hidden.T, jnp.concatenate([d_gate, d_up], 0).T
         for mask in range(4):
             column = at_quarter(place ^ mask, width)
             target = sent if mask % 2 else kept
             out_part = dot_nn(hidden_t, w_all[2, :, column])
-            in_part = dot_nn(d_gate_t, w_all[0, :, column]) + dot_nn(d_up_t, w_all[1, :, column])
+            in_part = dot_nn(d_both, w_all[0:2, :, column].reshape(2 * hidden.shape[0], width))
             target[mask // 2, rows, :] = out_part.astype(target.dtype)
             target[mask // 2, lower, :] = in_part.astype(target.dtype)
     put_pair(sent.at[0], 2 * total, jnp.concatenate(routers, 0))
@@ -232,14 +231,12 @@
             jax.ShapeDtypeStruct((3, half, total), jnp.bfloat16),
             jax.ShapeDtypeStruct((2, packet_rows(total), width), jnp.float32),
             jax.ShapeDtypeStruct((2, packet_rows(total), width), jnp.bfloat16),
-            jax.ShapeDtypeStruct(last.shape, jnp.bfloat16),
+            jax.ShapeDtypeStruct((2, half, width), jnp.bfloat16),
+            jax.ShapeDtypeStruct((1, half, width), jnp.bfloat16),
         ),
         in_specs=[VMEM] * 5,
-        out_specs=[VMEM] * 4,
-        scratch_shapes=[
-            pltpu.VMEM((3, half, features), jnp.bfloat16),
-            pltpu.SemaphoreType.DMA,
-        ],
+        out_specs=[VMEM] * 5,
+        scratch_shapes=[pltpu.VMEM((3, half, features), jnp.bfloat16)],
         compiler_params=PARAMS,
         cost_estimate=pl.CostEstimate(
             flops=8 * half * features * total, bytes_accessed=0, transcendentals=0
@@ -247,32 +244,30 @@
     )(x_all, s_all, w_part, part, last)
 
 
-def grads_kernel(units, x_all, s_all, *outs):
-    width = outs[0].shape[2]
+def grads_kernel(units, x_all, s_all, own, to_x, to_x_down, to_z):
+    width = own.shape[2]
     member = lax.axis_index("wide") % 4
-    for k, out in enumerate(outs):
-        grad_parts(units, x_all, s_all, at_quarter(member ^ k, width), out)
+    for k, outs in enumerate(((own,), (to_x, to_x_down), (to_z,))):
+        grad_parts(units, x_all, s_all, at_quarter(member ^ k, width), outs)
 
 
 def weight_grads(units, x_all, s_all):
     half, total = units.shape[1:]
     features = x_all.shape[1]
+    shapes = ((3, jnp.float32), (2, jnp.float32), (1, jnp.float32), (3, jnp.bfloat16))
     return pl.pallas_call(
         grads_kernel,
         out_shape=tuple(
-            jax.ShapeDtypeStruct((3, half, features // 4), jnp.bfloat16 if k > 1 else jnp.float32)
-            for k in range(3)
+            jax.ShapeDtypeStruct((count, half, features // 4), kind) for count, kind in shapes
         ),
         in_specs=[VMEM] * 3,
-        out_specs=[VMEM] * 3,
-        compiler_params=PARAMS,
-        cost_estimate=pl.CostEstimate(
-            flops=5 * half * features * total, bytes_accessed=0, transcendentals=0
-        ),
+        out_specs=[VMEM] * 4,
+        compiler_params=PARAMS,
+        cost_estimate=pl.CostEstimate(flops=5 * half * features * total, bytes_accessed=0, transcendentals=0),
     )(units, x_all, s_all)
 
 
-def join_kernel(own, got_x, out_0, out_1, out_2, held, sems):
+def join_kernel(own, got_x, got_x_down, out_0, out_1, out_2, held, sems):
     half = held.shape[1]
     x_bit = lax.axis_index("wide") % 2
     copies = []
@@ -281,7 +276,8 @@
         rows = pl.ds(pl.multiple_of(first, 16), half)
         for i, out in enumerate((out_0, out_1, out_2)):
             if part:
-                held[i] = got_x[i].astype(jnp.float32)
+                got = got_x.at[i] if i < 2 else got_x_down.at[0]
+                held[i] = got[...].astype(jnp.float32)
             place = sems.at[3 * part + i]
             copies.append(pltpu.make_async_copy(held_part.at[i], out.at[rows, :], place))
             copies[-1].start()
@@ -289,13 +285,13 @@
         copy.wait()
 
 
-def join_grads(own, got_x):
+def join_grads(own, got_x, got_x_down):
     _, half, width = own.shape
     shape = jax.ShapeDtypeStruct((2 * half, width), jnp.float32)
     return pl.pallas_call(
         join_kernel,
         out_shape=(shape,) * 3,
-        in_specs=[VMEM] * 2,
+        in_specs=[VMEM] * 3,
         out_specs=[HBM] * 3,
         scratch_shapes=[
             pltpu.VMEM(own.shape, jnp.float32),
@@ -303,7 +299,7 @@
         ],
         compiler_params=PARAMS,
         cost_estimate=pl.CostEstimate(flops=1, bytes_accessed=0, transcendentals=0),
-    )(own, got_x)
+    )(own, got_x, got_x_down)
 
 
 def cross_kernel(kept, got, sent):
@@ -466,7 +462,7 @@
         in_specs=[VMEM] * 4,
         out_specs=[VMEM] * 2,
         compiler_params=PARAMS,
-        cost_estimate=pl.CostEstimate(flops=3 * 10**9, bytes_accessed=0, transcendentals=0),
+        cost_estimate=pl.CostEstimate(flops=2 * 10**9, bytes_accessed=0, transcendentals=0),
     )(ffn, from_x, grad, from_y)
 
 
@@ -550,25 +546,38 @@
     across = partner(mine, "narrow", 2)
     pieces = (mine, partner(mine, "narrow", 1), across, partner(across, "narrow", 1))
     x_all, s_all, w_part, part = gather_parts(own, pieces, (keep, from_x, from_z))
-    units, kept, sent, grad_d = outer(x_all, s_all, w_part, part, from_d)
+    units, kept, sent, grad_d, grad_d_down = outer(x_all, s_all, w_part, part, from_d)
     got = partner(sent, "narrow", 1)
+    got_d_down = partner(grad_d_down, "wide", 2)
     got_d = partner(grad_d, "wide", 2)
     if direct:
         to_y, to_x = first_parts(kept, got)
         units, _ = lax.optimization_barrier((units, to_y))
         ffn_held, ffn_x = ffn_parts(kept, got, partner(to_y, "narrow", 2))
-        grad_held, grad_y = input_parts(kept, got, partner(to_x, "wide", 1))
-        grad_own, grad_x, grad_z = weight_grads(units, x_all, s_all)
-        grad_x, grad_z, _, _ = lax.optimization_barrier((grad_x, grad_z, ffn_x, grad_y))
+        grad_own, grad_x, grad_x_down, grad_z = weight_grads(units, x_all, s_all)
+        from_x = partner(to_x, "wide", 1)
+        grad_held, grad_y = input_parts(kept, got, from_x)
+        grad_z, _ = lax.optimization_barrier((grad_z, from_x))
+        grad_x, _, _ = lax.optimization_barrier((grad_x, ffn_x, grad_y))
+        grad_x_down = (grad_x_down + got_d_down.astype(jnp.float32)).astype(jnp.bfloat16)
+        got_x_down = partner(grad_x_down, "wide", 1)
+        grad_held, got_x_down = lax.optimization_barrier((grad_held, got_x_down))
         held, to_z = last_parts(
             ffn_held, partner(ffn_x, "wide", 1), grad_held, partner(grad_y, "narrow", 2)
         )
+        grad_x = (grad_x + got_d.astype(jnp.float32)).astype(jnp.bfloat16)
+        got_x = partner(grad_x, "wide", 1)
+        held, got_x = lax.optimization_barrier((held, got_x))
         output, tokens_grad, prob_grad = finish(
             route_prob[None, :], held, [partner(to_z, "wide", 4)]
         )
         prob_grad = prob_grad[0]
     else:
-        grad_own, grad_x, grad_z = weight_grads(units, x_all, s_all)
+        grad_own, grad_x, grad_x_down, grad_z = weight_grads(units, x_all, s_all)
+        grad_x_down = (grad_x_down + got_d_down.astype(jnp.float32)).astype(jnp.bfloat16)
+        got_x_down = partner(grad_x_down, "wide", 1)
+        grad_x = (grad_x + got_d.astype(jnp.float32)).astype(jnp.bfloat16)
+        got_x = partner(grad_x, "wide", 1)
         across = partner(cross_part(kept, got), "narrow", 2)
         result = result_parts(kept, got, across)
         total = (result.shape[0] - EXTRA) // 2
@@ -591,10 +600,10 @@
         ffn = back[0].astype(jnp.bfloat16).astype(jnp.float32)
         output = (route_prob[:, None] * ffn).astype(jnp.bfloat16)
         tokens_grad = back[1].astype(jnp.bfloat16)
-    grad_x = (grad_x + got_d.astype(jnp.float32)).astype(jnp.bfloat16)
-    got_x = partner(grad_x, "wide", 1)
     got_z = partner(grad_z, "wide", 2)
-    gate_grad, up_grad, down_grad = join_grads(grad_own + got_z.astype(jnp.float32), got_x)
+    gate_grad, up_grad, down_grad = join_grads(
+        grad_own + got_z.astype(jnp.float32), got_x, got_x_down
+    )
     return (output, tokens_grad, prob_grad, gate_grad.T, up_grad.T, down_grad.T)
 
 

time: 74.4 us -> 73.8 us (level)
    ppermute x18 -> x20, starting transfers between devices: 24.2 us -> 24.1 us  [partner(): lax.ppermute(x, axis, [(i, i ^ mask) for i in range(lax.axis_size(axis))])]
    ppermute x18 -> x20, waiting for transfers between devices: 38.9 us -> 38.9 us  [partner(): lax.ppermute(x, axis, [(i, i ^ mask) for i in range(lax.axis_size(axis))])]
  transfers between devices with their start and end apart: 18 -> 20, of which waited for: 10 -> 11; matrix products, arithmetic and copies ran while one was open for 0% -> 0% of each run, Pallas kernels for 5% -> 5%
where the time goes in v8:
time: 73.8 us; the launch traced here: 73.6 us
  waiting for transfers between devices  38.9 us (53%)
  starting transfers between devices  24.1 us (33%)
  Pallas kernels  9.52 us (13%)
    ppermute x20, waiting for transfers between devices, partner(): lax.ppermute(x, axis, [(i, i ^ mask) for i in range(lax.axis_size(axis))])  38.9 us
    ppermute x20, starting transfers between devices, partner(): lax.ppermute(x, axis, [(i, i ^ mask) for i in range(lax.axis_size(axis))])  24.1 us
    pallas_call x1, Pallas kernels, outer(): pl.pallas_call(outer_kernel, out_shape=(jax.ShapeDtypeStruct((3, half, to...  2.75 us
    pallas_call x1, Pallas kernels, gather_parts(): pl.pallas_call(functools.partial(gather_kernel, int(has_own)), out_shape=...  1.74 us
  transfers between devices with their start and end apart: 20, of which 11 were waited for; matrix products, arithmetic and copies ran while one was open for 0% of the time, Pallas kernels for 5%

profile of v8, /device:TPU:0, one launch (start us, length us, event | category | flops | bytes accessed | tf_op | source)
XLA Modules:
  0.0 73.6 jit_solution(16458025016619162544)
XLA Ops:
  0.6 1.5 %shard_map.118 = (bf16[3,352,256]{2,1,0:T(8,128)(2,1)S(1)}, bf16[3,352,256]{2,1,0:T(8,128)(2,1)S(1)}, bf16[2,128,1024]{2,1,0:T(8,128)(2,1)S(1)}, bf16[2,128,256]...) custom-call(bf16[704,256]{1,0:T(8,128)(2,1)} %bitcast.14, bf16[704,256]{1,0:T(8,128)(2,1)} %bitcast.15, ...), custom_call_target="tpu_custom_call" | custom-call | tf_op jit(solution)/shard_map/pallas_call | solution.py:103
  2.1 3.0 %collective-permute-start.6 = (bf16[3,352,256]{2,1,0:T(8,128)(2,1)S(1)}, bf16[3,352,256]{2,1,0:T(8,128)(2,1)S(1)}, u32[]{:S(2)}, u32[]{:S(2)}) collective-permute-start(bf16[3,352,256]{2,1,0:T(8,128)(2,1)S(1)} %get-tuple-element.51), channel_id=1, source_target_pairs={{0,4},{4,0},{8,12},{12,8},{16,20},{20,16},{24,28},{28,24},{1,5},{5... | collective-permute-start | bytes 1622024 | tf_op jit(solution)/shard_map/ppermute | solution.py:17
  5.1 1.6 %collective-permute-start.7 = (bf16[3,352,256]{2,1,0:T(8,128)(2,1)S(1)}, bf16[3,352,256]{2,1,0:T(8,128)(2,1)S(1)}, u32[]{:S(2)}, u32[]{:S(2)}) collective-permute-start(bf16[3,352,256]{2,1,0:T(8,128)(2,1)S(1)} %get-tuple-element.50.refs_5_), channel_id=1, source_target_pairs={{0,8},{4,12},{8,0},{12,4},{16,24},{20,28},{24,16},{28,20},{1,9},{5... | collective-permute-start | bytes 1622024 | tf_op jit(solution)/shard_map/ppermute | solution.py:17
  7.2 3.5 %collective-permute-start.2 = (bf16[2,128,256]{2,1,0:T(8,128)(2,1)S(1)}, bf16[2,128,256]{2,1,0:T(8,128)(2,1)S(1)}, u32[]{:S(2)}, u32[]{:S(2)}) collective-permute-start(bf16[2,128,256]{2,1,0:T(8,128)(2,1)S(1)} %get-tuple-element.49), channel_id=1, source_target_pairs={{0,20},{4,16},{8,28},{12,24},{16,4},{20,0},{24,12},{28,8},{1,21},{... | collective-permute-start | bytes 393224 | tf_op jit(solution)/shard_map/ppermute | solution.py:17
  11.1 11.9 %collective-permute-done = bf16[2,128,256]{2,1,0:T(8,128)(2,1)S(1)} collective-permute-done((bf16[2,128,256]{2,1,0:T(8,128)(2,1)S(1)}, bf16[2,128,256]{2,1,0:T(8,128)(2,1)S(1)}, u32[]{:S(2)}, u32[]{:S(2)}) %collective-permute-start) | collective-permute-done | bytes 131104 | tf_op jit(solution)/shard_map/ppermute | solution.py:17
  23.6 1.6 %collective-permute-start.4 = (bf16[3,2,128,256]{3,2,1,0:T(8,128)(2,1)S(1)}, bf16[3,2,128,256]{3,2,1,0:T(8,128)(2,1)S(1)}, u32[]{:S(2)}, u32[]{:S(2)}) collective-permute-start(bf16[3,2,128,256]{3,2,1,0:T(8,128)(2,1)S(1)} %pad_maximum_fusion.refs_1_), channel_id=1, source_target_pairs={{0,2},{1,3},{2,0},{3,1},{4,6},{5,7},{6,4},{7,5},{8,10},{9,11},{10,... | collective-permute-start | bytes 1179656 | tf_op jit(solution)/shard_map/ppermute | solution.py:17
  25.2 3.5 %collective-permute-start.8 = (bf16[3,352,256]{2,1,0:T(8,128)(2,1)S(1)}, bf16[3,352,256]{2,1,0:T(8,128)(2,1)S(1)}, u32[]{:S(2)}, u32[]{:S(2)}) collective-permute-start(bf16[3,352,256]{2,1,0:T(8,128)(2,1)S(1)} %collective-permute-done.6.refs_6_), channel_id=1, source_target_pairs={{0,8},{4,12},{8,0},{12,4},{16,24},{20,28},{24,16},{28,20},{1,9},{5... | collective-permute-start | bytes 1622024 | tf_op jit(solution)/shard_map/ppermute | solution.py:17
  28.7 4.7 %collective-permute-done.4.refs_3_ = bf16[3,2,128,256]{3,2,1,0:T(8,128)(2,1)S(1)} collective-permute-done((bf16[3,2,128,256]{3,2,1,0:T(8,128)(2,1)S(1)}, bf16[3,2,128,256]{3,2,1,0:T(8,128)(2,1)S(1)}, u32[]{:S(2)}, u32[]{:S(2)}) %collective-permute-start.4) | collective-permute-done | bytes 393248 | tf_op jit(solution)/shard_map/ppermute | solution.py:17
  33.4 1.7 %collective-permute-done.5.refs_4_ = bf16[3,2,128,256]{3,2,1,0:T(8,128)(2,1)S(1)} collective-permute-done((bf16[3,2,128,256]{3,2,1,0:T(8,128)(2,1)S(1)}, bf16[3,2,128,256]{3,2,1,0:T(8,128)(2,1)S(1)}, u32[]{:S(2)}, u32[]{:S(2)}) %collective-permute-start.5) | collective-permute-done | bytes 393248 | tf_op jit(solution)/shard_map/ppermute | solution.py:17
  35.2 1.7 %shard_map.119 = (bf16[512,1024]{1,0:T(8,128)(2,1)S(1)}, bf16[512,1024]{1,0:T(8,128)(2,1)S(1)}, bf16[3,352,1024]{2,1,0:T(8,128)(2,1)S(1)}, f32[3,352,512]{2,1,0:T(8,128)S(1)}) custom-call(bf16[2,128,1024]{2,1,0:T(8,128)(2,1)S(1)} %get-tuple-element.47.refs_0_, bf16[3,2,128,256]{3,2,1,0:T(8,128)(2,1)S(1)} %pad_maximum_fusion.refs_1_, ...), custom_call_target="tpu_custom_call" | custom-call | flops 1 | bytes 1 | tf_op jit(solution)/shard_map/pallas_call | solution.py:157
  36.9 2.6 %collective-permute-done.8.last = bf16[3,352,256]{2,1,0:T(8,128)(2,1)S(1)} collective-permute-done((bf16[3,352,256]{2,1,0:T(8,128)(2,1)S(1)}, bf16[3,352,256]{2,1,0:T(8,128)(2,1)S(1)}, u32[]{:S(2)}, u32[]{:S(2)}) %collective-permute-start.8) | collective-permute-done | bytes 540704 | tf_op jit(solution)/shard_map/ppermute | solution.py:17
  39.5 2.7 %shard_map.120 = (bf16[3,352,512]{2,1,0:T(8,128)(2,1)S(1)}, f32[2,1040,256]{2,1,0:T(8,128)S(1)}, bf16[2,1040,256]{2,1,0:T(8,128)(2,1)S(1)}, bf16[2,352,256]{2,1,0:T(8,128)(2,1)S(1)}, bf16[1,352,256]{2,1,0:T(8,128)(2,1)S(1)}) custom-call(bf16[512,1024]{1,0:T(8,128)(2,1)S(1)} %get-tuple-element.54.x_all, bf16[512,1024]{1,0:T(8,128)(2,1)S(1)} %get-tuple-element.55.s_all, ...), custom_call_target="tpu_custom_call" | custom-call | flops 1476395008 | tf_op jit(solution)/shard_map/pallas_call | solution.py:228
  42.3 1.8 %collective-permute-start.13 = (bf16[1,352,256]{2,1,0:T(8,128)(2,1)S(1)}, bf16[1,352,256]{2,1,0:T(8,128)(2,1)S(1)}, u32[]{:S(2)}, u32[]{:S(2)}) collective-permute-start(bf16[1,352,256]{2,1,0:T(8,128)(2,1)S(1)} %get-tuple-element.68), channel_id=1, source_target_pairs={{0,8},{4,12},{8,0},{12,4},{16,24},{20,28},{24,16},{28,20},{1,9},{5... | collective-permute-start | bytes 540680 | tf_op jit(solution)/shard_map/ppermute | solution.py:17
  46.2 1.0 %shard_map.124 = (f32[3,352,256]{2,1,0:T(8,128)S(1)}, f32[2,352,256]{2,1,0:T(8,128)S(1)}, f32[1,352,256]{2,1,0:T(8,128)S(1)}, bf16[3,352,256]{2,1,0:T(8,128)(2,1)S(1)}) custom-call(bf16[3,352,512]{2,1,0:T(8,128)(2,1)S(1)} %get-tuple-element.66.units, bf16[512,1024]{1,0:T(8,128)(2,1)S(1)} %get-tuple-element.54.x_all, ...), custom_call_target="tpu_custom_call" | custom-call | flops 922746880 | tf_op jit(solution)/shard_map/pallas_call | solution.py:258
  47.2 2.5 %collective-permute-done.13 = bf16[1,352,256]{2,1,0:T(8,128)(2,1)S(1)} collective-permute-done((bf16[1,352,256]{2,1,0:T(8,128)(2,1)S(1)}, bf16[1,352,256]{2,1,0:T(8,128)(2,1)S(1)}, u32[]{:S(2)}, u32[]{:S(2)}) %collective-permute-start.13) | collective-permute-done | bytes 180256 | tf_op jit(solution)/shard_map/ppermute | solution.py:17
  50.4 4.5 %collective-permute-done.12.from_x = bf16[2,256,256]{2,1,0:T(8,128)(2,1)S(1)} collective-permute-done((bf16[2,256,256]{2,1,0:T(8,128)(2,1)S(1)}, bf16[2,256,256]{2,1,0:T(8,128)(2,1)S(1)}, u32[]{:S(2)}, u32[]{:S(2)}) %collective-permute-start.12) | collective-permute-done | bytes 262176 | tf_op jit(solution)/shard_map/ppermute | solution.py:17
  55.0 1.6 %collective-permute-start.15 = (bf16[256,256]{1,0:T(8,128)(2,1)S(1)}, bf16[256,256]{1,0:T(8,128)(2,1)S(1)}, u32[]{:S(2)}, u32[]{:S(2)}) collective-permute-start(bf16[256,256]{1,0:T(8,128)(2,1)S(1)} %get-tuple-element.70), channel_id=1, source_target_pairs={{0,2},{1,3},{2,0},{3,1},{4,6},{5,7},{6,4},{7,5},{8,10},{9,11},{10,... | collective-permute-start | bytes 393224 | tf_op jit(solution)/shard_map/ppermute | solution.py:17
  56.6 1.7 %collective-permute-start.19 = (bf16[3,352,256]{2,1,0:T(8,128)(2,1)S(1)}, bf16[3,352,256]{2,1,0:T(8,128)(2,1)S(1)}, u32[]{:S(2)}, u32[]{:S(2)}) collective-permute-start(bf16[3,352,256]{2,1,0:T(8,128)(2,1)S(1)} %get-tuple-element.82), channel_id=1, source_target_pairs={{0,8},{4,12},{8,0},{12,4},{16,24},{20,28},{24,16},{28,20},{1,9},{5... | collective-permute-start | bytes 1622024 | tf_op jit(solution)/shard_map/ppermute | solution.py:17
  59.1 1.6 %collective-permute-start.17 = (bf16[2,352,256]{2,1,0:T(8,128)(2,1)S(1)}, bf16[2,352,256]{2,1,0:T(8,128)(2,1)S(1)}, u32[]{:S(2)}, u32[]{:S(2)}) collective-permute-start(bf16[2,352,256]{2,1,0:T(8,128)(2,1)S(1)} %add_convert_fusion), channel_id=1, source_target_pairs={{0,4},{4,0},{8,12},{12,8},{16,20},{20,16},{24,28},{28,24},{1,5},{5... | collective-permute-start | bytes 1081352 | tf_op jit(solution)/shard_map/ppermute | solution.py:17
  60.6 4.4 %collective-permute-done.11.from_x = bf16[272,256]{1,0:T(8,128)(2,1)S(1)} collective-permute-done((bf16[272,256]{1,0:T(8,128)(2,1)S(1)}, bf16[272,256]{1,0:T(8,128)(2,1)S(1)}, u32[]{:S(2)}, u32[]{:S(2)}) %collective-permute-start.11) | collective-permute-done | bytes 139296 | tf_op jit(solution)/shard_map/ppermute | solution.py:17
  65.9 3.2 %collective-permute-done.17.got_x = bf16[2,352,256]{2,1,0:T(8,128)(2,1)S(1)} collective-permute-done((bf16[2,352,256]{2,1,0:T(8,128)(2,1)S(1)}, bf16[2,352,256]{2,1,0:T(8,128)(2,1)S(1)}, u32[]{:S(2)}, u32[]{:S(2)}) %collective-permute-start.17) | collective-permute-done | bytes 360480 | tf_op jit(solution)/shard_map/ppermute | solution.py:17
  69.1 2.2 %collective-permute-done.18.refs_0_ = bf16[272,256]{1,0:T(8,128)(2,1)S(1)} collective-permute-done((bf16[272,256]{1,0:T(8,128)(2,1)S(1)}, bf16[272,256]{1,0:T(8,128)(2,1)S(1)}, u32[]{:S(2)}, u32[]{:S(2)}) %collective-permute-start.18) | collective-permute-done | bytes 139296 | tf_op jit(solution)/shard_map/ppermute | solution.py:17
  71.3 0.8 %shard_map.126 = (bf16[128,256]{1,0:T(8,128)(2,1)}, bf16[128,256]{1,0:T(8,128)(2,1)}, f32[1,128]{1,0:T(1,128)}) custom-call(f32[1,128]{1,0:T(1,128)S(1)} %bitcast.13, f32[272,256]{1,0:T(8,128)S(1)} %get-tuple-element.75.own, bf16[272,256]{1,0:T(8,128)(2,1)S(1)} %collective-permute-done.18.refs_0_), custom_call_target="tpu_custom_call" | custom-call | tf_op jit(solution)/shard_map/pallas_call | solution.py:487
  72.2 1.4 %shard_map.127 = (f32[704,256]{1,0:T(8,128)}, f32[704,256]{1,0:T(8,128)}, f32[704,256]{1,0:T(8,128)}) custom-call(f32[3,352,256]{2,1,0:T(8,128)S(1)} %convert_add_fusion.own, bf16[2,352,256]{2,1,0:T(8,128)(2,1)S(1)} %collective-permute-done.17.got_x, bf16[1,352,256]{2,1,0:T(8,128)(2,1)S(1)} %collective-permute-done.14.got_x_down), custom_call_target="tpu_custom_call" | custom-call | flops 1 | tf_op jit(solution)/shard_map/pallas_call | solution.py:291
  (32 shorter events, 6.1 us)
Async XLA Ops:
  2.1 23.1 %collective-permute-start.6 = (bf16[3,352,256]{2,1,0:T(8,128)(2,1)S(1)}, bf16[3,352,256]{2,1,0:T(8,128)(2,1)S(1)}, u32[]{:S(2)}, u32[]{:S(2)}) collective-permute-start(bf16[3,352,256]{2,1,0:T(8,128)(2,1)S(1)} %get-tuple-element.51), channel_id=1, source_target_pairs={{0,4},{4,0},{8,12},{12,8},{16,20},{20,16},{24,28},{28,24},{1,5},{5... | collective-permute-start | bytes 1622024 | tf_op jit(solution)/shard_map/ppermute | solution.py:17
  5.1 20.1 %collective-permute-start.7 = (bf16[3,352,256]{2,1,0:T(8,128)(2,1)S(1)}, bf16[3,352,256]{2,1,0:T(8,128)(2,1)S(1)}, u32[]{:S(2)}, u32[]{:S(2)}) collective-permute-start(bf16[3,352,256]{2,1,0:T(8,128)(2,1)S(1)} %get-tuple-element.50.refs_5_), channel_id=1, source_target_pairs={{0,8},{4,12},{8,0},{12,4},{16,24},{20,28},{24,16},{28,20},{1,9},{5... | collective-permute-start | bytes 1622024 | tf_op jit(solution)/shard_map/ppermute | solution.py:17
  6.7 16.3 %collective-permute-start = (bf16[2,128,256]{2,1,0:T(8,128)(2,1)S(1)}, bf16[2,128,256]{2,1,0:T(8,128)(2,1)S(1)}, u32[]{:S(2)}, u32[]{:S(2)}) collective-permute-start(bf16[2,128,256]{2,1,0:T(8,128)(2,1)S(1)} %get-tuple-element.48), channel_id=1, source_target_pairs={{0,4},{4,0},{8,12},{12,8},{16,20},{20,16},{24,28},{28,24},{1,5},{5... | collective-permute-start | bytes 393224 | tf_op jit(solution)/shard_map/ppermute | solution.py:17
  7.2 15.8 %collective-permute-start.2 = (bf16[2,128,256]{2,1,0:T(8,128)(2,1)S(1)}, bf16[2,128,256]{2,1,0:T(8,128)(2,1)S(1)}, u32[]{:S(2)}, u32[]{:S(2)}) collective-permute-start(bf16[2,128,256]{2,1,0:T(8,128)(2,1)S(1)} %get-tuple-element.49), channel_id=1, source_target_pairs={{0,20},{4,16},{8,28},{12,24},{16,4},{20,0},{24,12},{28,8},{1,21},{... | collective-permute-start | bytes 393224 | tf_op jit(solution)/shard_map/ppermute | solution.py:17
  10.7 12.8 %collective-permute-start.1 = (bf16[2,128,256]{2,1,0:T(8,128)(2,1)S(1)}, bf16[2,128,256]{2,1,0:T(8,128)(2,1)S(1)}, u32[]{:S(2)}, u32[]{:S(2)}) collective-permute-start(bf16[2,128,256]{2,1,0:T(8,128)(2,1)S(1)} %get-tuple-element.49), channel_id=1, source_target_pairs={{0,16},{4,20},{8,24},{12,28},{16,0},{20,4},{24,8},{28,12},{1,17},{... | collective-permute-start | bytes 393224 | tf_op jit(solution)/shard_map/ppermute | solution.py:17
  23.6 9.8 %collective-permute-start.4 = (bf16[3,2,128,256]{3,2,1,0:T(8,128)(2,1)S(1)}, bf16[3,2,128,256]{3,2,1,0:T(8,128)(2,1)S(1)}, u32[]{:S(2)}, u32[]{:S(2)}) collective-permute-start(bf16[3,2,128,256]{3,2,1,0:T(8,128)(2,1)S(1)} %pad_maximum_fusion.refs_1_), channel_id=1, source_target_pairs={{0,2},{1,3},{2,0},{3,1},{4,6},{5,7},{6,4},{7,5},{8,10},{9,11},{10,... | collective-permute-start | bytes 1179656 | tf_op jit(solution)/shard_map/ppermute | solution.py:17
  25.2 14.3 %collective-permute-start.8 = (bf16[3,352,256]{2,1,0:T(8,128)(2,1)S(1)}, bf16[3,352,256]{2,1,0:T(8,128)(2,1)S(1)}, u32[]{:S(2)}, u32[]{:S(2)}) collective-permute-start(bf16[3,352,256]{2,1,0:T(8,128)(2,1)S(1)} %collective-permute-done.6.refs_6_), channel_id=1, source_target_pairs={{0,8},{4,12},{8,0},{12,4},{16,24},{20,28},{24,16},{28,20},{1,9},{5... | collective-permute-start | bytes 1622024 | tf_op jit(solution)/shard_map/ppermute | solution.py:17
  28.7 4.7 %collective-permute-start.3 = (bf16[3,2,128,256]{3,2,1,0:T(8,128)(2,1)S(1)}, bf16[3,2,128,256]{3,2,1,0:T(8,128)(2,1)S(1)}, u32[]{:S(2)}, u32[]{:S(2)}) collective-permute-start(bf16[3,2,128,256]{3,2,1,0:T(8,128)(2,1)S(1)} %pad_maximum_fusion.refs_1_), channel_id=1, source_target_pairs={{0,1},{1,0},{2,3},{3,2},{4,5},{5,4},{6,7},{7,6},{8,9},{9,8},{10,11... | collective-permute-start | bytes 1179656 | tf_op jit(solution)/shard_map/ppermute | solution.py:17
  33.4 1.7 %collective-permute-start.5 = (bf16[3,2,128,256]{3,2,1,0:T(8,128)(2,1)S(1)}, bf16[3,2,128,256]{3,2,1,0:T(8,128)(2,1)S(1)}, u32[]{:S(2)}, u32[]{:S(2)}) collective-permute-start(bf16[3,2,128,256]{3,2,1,0:T(8,128)(2,1)S(1)} %collective-permute-done.4.refs_3_), channel_id=1, source_target_pairs={{0,1},{1,0},{2,3},{3,2},{4,5},{5,4},{6,7},{7,6},{8,9},{9,8},{10,11... | collective-permute-start | bytes 1179656 | tf_op jit(solution)/shard_map/ppermute | solution.py:17
  42.3 2.7 %collective-permute-start.9 = (bf16[2,1040,256]{2,1,0:T(8,128)(2,1)S(1)}, bf16[2,1040,256]{2,1,0:T(8,128)(2,1)S(1)}, u32[]{:S(2)}, u32[]{:S(2)}) collective-permute-start(bf16[2,1040,256]{2,1,0:T(8,128)(2,1)S(1)} %get-tuple-element.59), channel_id=1, source_target_pairs={{0,1},{1,0},{2,3},{3,2},{4,5},{5,4},{6,7},{7,6},{8,9},{9,8},{10,11... | collective-permute-start | bytes 3194888 | tf_op jit(solution)/shard_map/ppermute | solution.py:17
  42.3 7.4 %collective-permute-start.13 = (bf16[1,352,256]{2,1,0:T(8,128)(2,1)S(1)}, bf16[1,352,256]{2,1,0:T(8,128)(2,1)S(1)}, u32[]{:S(2)}, u32[]{:S(2)}) collective-permute-start(bf16[1,352,256]{2,1,0:T(8,128)(2,1)S(1)} %get-tuple-element.68), channel_id=1, source_target_pairs={{0,8},{4,12},{8,0},{12,4},{16,24},{20,28},{24,16},{28,20},{1,9},{5... | collective-permute-start | bytes 540680 | tf_op jit(solution)/shard_map/ppermute | solution.py:17
  44.1 14.8 %collective-permute-start.16 = (bf16[2,352,256]{2,1,0:T(8,128)(2,1)S(1)}, bf16[2,352,256]{2,1,0:T(8,128)(2,1)S(1)}, u32[]{:S(2)}, u32[]{:S(2)}) collective-permute-start(bf16[2,352,256]{2,1,0:T(8,128)(2,1)S(1)} %get-tuple-element.74), channel_id=1, source_target_pairs={{0,8},{4,12},{8,0},{12,4},{16,24},{20,28},{24,16},{28,20},{1,9},{5... | collective-permute-start | bytes 1081352 | tf_op jit(solution)/shard_map/ppermute | solution.py:17
  45.1 13.2 %collective-permute-start.10 = (bf16[528,256]{1,0:T(8,128)(2,1)S(1)}, bf16[528,256]{1,0:T(8,128)(2,1)S(1)}, u32[]{:S(2)}, u32[]{:S(2)}) collective-permute-start(bf16[528,256]{1,0:T(8,128)(2,1)S(1)} %get-tuple-element.60), channel_id=1, source_target_pairs={{0,2},{1,3},{2,0},{3,1},{4,6},{5,7},{6,4},{7,5},{8,10},{9,11},{10,... | collective-permute-start | bytes 811016 | tf_op jit(solution)/shard_map/ppermute | solution.py:17
  45.7 9.2 %collective-permute-start.12 = (bf16[2,256,256]{2,1,0:T(8,128)(2,1)S(1)}, bf16[2,256,256]{2,1,0:T(8,128)(2,1)S(1)}, u32[]{:S(2)}, u32[]{:S(2)}) collective-permute-start(bf16[2,256,256]{2,1,0:T(8,128)(2,1)S(1)} %get-tuple-element.63), channel_id=1, source_target_pairs={{0,4},{4,0},{8,12},{12,8},{16,20},{20,16},{24,28},{28,24},{1,5},{5... | collective-permute-start | bytes 786440 | tf_op jit(solution)/shard_map/ppermute | solution.py:17
  49.8 10.8 %collective-permute-start.14 = (bf16[1,352,256]{2,1,0:T(8,128)(2,1)S(1)}, bf16[1,352,256]{2,1,0:T(8,128)(2,1)S(1)}, u32[]{:S(2)}, u32[]{:S(2)}) collective-permute-start(bf16[1,352,256]{2,1,0:T(8,128)(2,1)S(1)} %add_convert_fusion.1), channel_id=1, source_target_pairs={{0,4},{4,0},{8,12},{12,8},{16,20},{20,16},{24,28},{28,24},{1,5},{5... | collective-permute-start | bytes 540680 | tf_op jit(solution)/shard_map/ppermute | solution.py:17
  55.0 5.7 %collective-permute-start.15 = (bf16[256,256]{1,0:T(8,128)(2,1)S(1)}, bf16[256,256]{1,0:T(8,128)(2,1)S(1)}, u32[]{:S(2)}, u32[]{:S(2)}) collective-permute-start(bf16[256,256]{1,0:T(8,128)(2,1)S(1)} %get-tuple-element.70), channel_id=1, source_target_pairs={{0,2},{1,3},{2,0},{3,1},{4,6},{5,7},{6,4},{7,5},{8,10},{9,11},{10,... | collective-permute-start | bytes 393224 | tf_op jit(solution)/shard_map/ppermute | solution.py:17
  56.6 15.5 %collective-permute-start.19 = (bf16[3,352,256]{2,1,0:T(8,128)(2,1)S(1)}, bf16[3,352,256]{2,1,0:T(8,128)(2,1)S(1)}, u32[]{:S(2)}, u32[]{:S(2)}) collective-permute-start(bf16[3,352,256]{2,1,0:T(8,128)(2,1)S(1)} %get-tuple-element.82), channel_id=1, source_target_pairs={{0,8},{4,12},{8,0},{12,4},{16,24},{20,28},{24,16},{28,20},{1,9},{5... | collective-permute-start | bytes 1622024 | tf_op jit(solution)/shard_map/ppermute | solution.py:17
  58.4 6.7 %collective-permute-start.11 = (bf16[272,256]{1,0:T(8,128)(2,1)S(1)}, bf16[272,256]{1,0:T(8,128)(2,1)S(1)}, u32[]{:S(2)}, u32[]{:S(2)}) collective-permute-start(bf16[272,256]{1,0:T(8,128)(2,1)S(1)} %get-tuple-element.62), channel_id=1, source_target_pairs={{0,4},{4,0},{8,12},{12,8},{16,20},{20,16},{24,28},{28,24},{1,5},{5... | collective-permute-start | bytes 417800 | tf_op jit(solution)/shard_map/ppermute | solution.py:17
  59.1 10.0 %collective-permute-start.17 = (bf16[2,352,256]{2,1,0:T(8,128)(2,1)S(1)}, bf16[2,352,256]{2,1,0:T(8,128)(2,1)S(1)}, u32[]{:S(2)}, u32[]{:S(2)}) collective-permute-start(bf16[2,352,256]{2,1,0:T(8,128)(2,1)S(1)} %add_convert_fusion), channel_id=1, source_target_pairs={{0,4},{4,0},{8,12},{12,8},{16,20},{20,16},{24,28},{28,24},{1,5},{5... | collective-permute-start | bytes 1081352 | tf_op jit(solution)/shard_map/ppermute | solution.py:17
  65.1 6.2 %copy-start = (f32[128]{0:T(128)S(1)}, f32[128]{0:T(128)}, u32[]{:S(2)}) copy-start(f32[128]{0:T(128)} %param.10) | copy-start | bytes 1540
  65.1 6.1 %collective-permute-start.18 = (bf16[272,256]{1,0:T(8,128)(2,1)S(1)}, bf16[272,256]{1,0:T(8,128)(2,1)S(1)}, u32[]{:S(2)}, u32[]{:S(2)}) collective-permute-start(bf16[272,256]{1,0:T(8,128)(2,1)S(1)} %get-tuple-element.76), channel_id=1, source_target_pairs={{0,16},{4,20},{8,24},{12,28},{16,0},{20,4},{24,8},{28,12},{1,17},{... | collective-permute-start | bytes 417800 | tf_op jit(solution)/shard_map/ppermute | solution.py:17

commit v9 on v8

--- a/solution.py
+++ b/solution.py
@@ -179,8 +179,9 @@
 
 
 def outer_kernel(x_all, s_all, w_part, part, last, units, kept, sent, *refs):
-    to_d, w_all = refs[:2], refs[2]
-    width = last.shape[2]
+    to_d, w_all, sums = refs[:2], refs[2], refs[3]
+    half, width = last.shape[1:]
+    chunk = 32 if half % 32 == 0 else 16
     place = lax.axis_index("narrow")
     last_column = at_quarter(lax.axis_index("wide") % 4 ^ 3, width)
     w_all[...] = w_part[...]
@@ -195,27 +196,29 @@
         rows = slice(step * tile, (step + 1) * tile)
         lower = slice(total + step * tile, total + (step + 1) * tile)
         x_tile, s_tile = x_all[rows, last_column], s_all[rows, last_column]
-        gate = part[0, :, rows] + dot_nt(last[0], x_tile)
-        up = part[1, :, rows] + dot_nt(last[1], x_tile)
-        d_hidden = part[2, :, rows] + dot_nt(last[2], s_tile)
-        sigma = 0.5 + 0.5 * jnp.tanh(0.5 * gate)
-        active = gate * sigma
-        hidden = (active * up).astype(jnp.bfloat16)
-        slope = sigma + active * (1.0 - sigma)
-        d_gate = (d_hidden * up * slope).astype(jnp.bfloat16)
-        d_up = (d_hidden * active).astype(jnp.bfloat16)
-        units[0, :, rows] = d_gate
-        units[1, :, rows] = d_up
-        units[2, :, rows] = hidden
-        router = jnp.sum(hidden.astype(jnp.float32) * d_hidden, axis=0, keepdims=True)
+        for i, held in enumerate((x_tile, x_tile, s_tile)):
+            sums[i] = part[i, :, rows] + dot_nt(last[i], held)
+        products = jnp.zeros((chunk, tile), jnp.float32)
+        for low in range(0, half, chunk):
+            piece = slice(low, low + chunk)
+            gate, up, d_hidden = sums[0, piece, :], sums[1, piece, :], sums[2, piece, :]
+            sigma = 0.5 + 0.5 * jnp.tanh(0.5 * gate)
+            active = gate * sigma
+            hidden = (active * up).astype(jnp.bfloat16)
+            slope = sigma + active * (1.0 - sigma)
+            units[0, piece, rows] = (d_hidden * up * slope).astype(jnp.bfloat16)
+            units[1, piece, rows] = (d_hidden * active).astype(jnp.bfloat16)
+            units[2, piece, rows] = hidden
+            products = products + hidden.astype(jnp.float32) * d_hidden
+        router = jnp.sum(products, axis=0, keepdims=True)
         kept[0, 2 * total + step : 2 * total + step + 1, :tile] = router
         routers.append(router)
-        hidden_t, d_both = hidden.T, jnp.concatenate([d_gate, d_up], 0).T
+        hidden_t, d_both = units[2, :, rows].T, units[0:2, :, rows].reshape(2 * half, tile).T
         for mask in range(4):
             column = at_quarter(place ^ mask, width)
             target = sent if mask % 2 else kept
             out_part = dot_nn(hidden_t, w_all[2, :, column])
-            in_part = dot_nn(d_both, w_all[0:2, :, column].reshape(2 * hidden.shape[0], width))
+            in_part = dot_nn(d_both, w_all[0:2, :, column].reshape(2 * half, width))
             target[mask // 2, rows, :] = out_part.astype(target.dtype)
             target[mask // 2, lower, :] = in_part.astype(target.dtype)
     put_pair(sent.at[0], 2 * total, jnp.concatenate(routers, 0))
@@ -236,7 +239,10 @@
         ),
         in_specs=[VMEM] * 5,
         out_specs=[VMEM] * 5,
-        scratch_shapes=[pltpu.VMEM((3, half, features), jnp.bfloat16)],
+        scratch_shapes=[
+            pltpu.VMEM((3, half, features), jnp.bfloat16),
+            pltpu.VMEM((3, half, min(width, total)), jnp.float32),
+        ],
         compiler_params=PARAMS,
         cost_estimate=pl.CostEstimate(
             flops=8 * half * features * total, bytes_accessed=0, transcendentals=0
@@ -556,6 +562,7 @@
         ffn_held, ffn_x = ffn_parts(kept, got, partner(to_y, "narrow", 2))
         grad_own, grad_x, grad_x_down, grad_z = weight_grads(units, x_all, s_all)
         from_x = partner(to_x, "wide", 1)
+        from_x, _ = lax.optimization_barrier((from_x, ffn_x))
         grad_held, grad_y = input_parts(kept, got, from_x)
         grad_z, _ = lax.optimization_barrier((grad_z, from_x))
         grad_x, _, _ = lax.optimization_barrier((grad_x, ffn_x, grad_y))

time: 73.8 us -> 73.3 us (level)
  transfers between devices with their start and end apart: 20 -> 20, of which waited for: 11 -> 13; matrix products, arithmetic and copies ran while one was open for 0% -> 0% of each run, Pallas kernels for 5% -> 5%
where the time goes in v9:
time: 73.3 us; the launch traced here: 73.2 us
  waiting for transfers between devices  38.4 us (52%)
  starting transfers between devices  24.2 us (33%)
  Pallas kernels  9.54 us (13%)
    ppermute x20, waiting for transfers between devices, partner(): lax.ppermute(x, axis, [(i, i ^ mask) for i in range(lax.axis_size(axis))])  38.4 us
    ppermute x20, starting transfers between devices, partner(): lax.ppermute(x, axis, [(i, i ^ mask) for i in range(lax.axis_size(axis))])  24.2 us
    pallas_call x1, Pallas kernels, outer(): pl.pallas_call(outer_kernel, out_shape=(jax.ShapeDtypeStruct((3, half, to...  2.75 us
    pallas_call x1, Pallas kernels, gather_parts(): pl.pallas_call(functools.partial(gather_kernel, int(has_own)), out_shape=...  1.74 us
    pallas_call x1, Pallas kernels, prologue(): pl.pallas_call(functools.partial(prologue_kernel, bool(token_args)), out_...  1.47 us
  transfers between devices with their start and end apart: 20, of which 13 were waited for; matrix products, arithmetic and copies ran while one was open for 0% of the time, Pallas kernels for 5%

profile of v9, /device:TPU:0, one launch (start us, length us, event | category | flops | bytes accessed | tf_op | source)
XLA Modules:
  0.0 73.2 jit_solution(1917794911596922971)
XLA Ops:
  0.6 1.5 %shard_map.118 = (bf16[3,352,256]{2,1,0:T(8,128)(2,1)S(1)}, bf16[3,352,256]{2,1,0:T(8,128)(2,1)S(1)}, bf16[2,128,1024]{2,1,0:T(8,128)(2,1)S(1)}, bf16[2,128,256]...) custom-call(bf16[704,256]{1,0:T(8,128)(2,1)} %bitcast.14, bf16[704,256]{1,0:T(8,128)(2,1)} %bitcast.15, ...), custom_call_target="tpu_custom_call" | custom-call | tf_op jit(solution)/shard_map/pallas_call | solution.py:103
  2.1 3.0 %collective-permute-start.6 = (bf16[3,352,256]{2,1,0:T(8,128)(2,1)S(1)}, bf16[3,352,256]{2,1,0:T(8,128)(2,1)S(1)}, u32[]{:S(2)}, u32[]{:S(2)}) collective-permute-start(bf16[3,352,256]{2,1,0:T(8,128)(2,1)S(1)} %get-tuple-element.52), channel_id=1, source_target_pairs={{0,4},{4,0},{8,12},{12,8},{16,20},{20,16},{24,28},{28,24},{1,5},{5... | collective-permute-start | bytes 1622024 | tf_op jit(solution)/shard_map/ppermute | solution.py:17
  5.1 1.6 %collective-permute-start.7 = (bf16[3,352,256]{2,1,0:T(8,128)(2,1)S(1)}, bf16[3,352,256]{2,1,0:T(8,128)(2,1)S(1)}, u32[]{:S(2)}, u32[]{:S(2)}) collective-permute-start(bf16[3,352,256]{2,1,0:T(8,128)(2,1)S(1)} %get-tuple-element.51.refs_5_), channel_id=1, source_target_pairs={{0,8},{4,12},{8,0},{12,4},{16,24},{20,28},{24,16},{28,20},{1,9},{5... | collective-permute-start | bytes 1622024 | tf_op jit(solution)/shard_map/ppermute | solution.py:17
  7.2 3.5 %collective-permute-start.2 = (bf16[2,128,256]{2,1,0:T(8,128)(2,1)S(1)}, bf16[2,128,256]{2,1,0:T(8,128)(2,1)S(1)}, u32[]{:S(2)}, u32[]{:S(2)}) collective-permute-start(bf16[2,128,256]{2,1,0:T(8,128)(2,1)S(1)} %get-tuple-element.50), channel_id=1, source_target_pairs={{0,20},{4,16},{8,28},{12,24},{16,4},{20,0},{24,12},{28,8},{1,21},{... | collective-permute-start | bytes 393224 | tf_op jit(solution)/shard_map/ppermute | solution.py:17
  11.1 11.9 %collective-permute-done = bf16[2,128,256]{2,1,0:T(8,128)(2,1)S(1)} collective-permute-done((bf16[2,128,256]{2,1,0:T(8,128)(2,1)S(1)}, bf16[2,128,256]{2,1,0:T(8,128)(2,1)S(1)}, u32[]{:S(2)}, u32[]{:S(2)}) %collective-permute-start) | collective-permute-done | bytes 131104 | tf_op jit(solution)/shard_map/ppermute | solution.py:17
  23.6 1.6 %collective-permute-start.4 = (bf16[3,2,128,256]{3,2,1,0:T(8,128)(2,1)S(1)}, bf16[3,2,128,256]{3,2,1,0:T(8,128)(2,1)S(1)}, u32[]{:S(2)}, u32[]{:S(2)}) collective-permute-start(bf16[3,2,128,256]{3,2,1,0:T(8,128)(2,1)S(1)} %pad_maximum_fusion.refs_1_), channel_id=1, source_target_pairs={{0,2},{1,3},{2,0},{3,1},{4,6},{5,7},{6,4},{7,5},{8,10},{9,11},{10,... | collective-permute-start | bytes 1179656 | tf_op jit(solution)/shard_map/ppermute | solution.py:17
  25.2 3.5 %collective-permute-start.8 = (bf16[3,352,256]{2,1,0:T(8,128)(2,1)S(1)}, bf16[3,352,256]{2,1,0:T(8,128)(2,1)S(1)}, u32[]{:S(2)}, u32[]{:S(2)}) collective-permute-start(bf16[3,352,256]{2,1,0:T(8,128)(2,1)S(1)} %collective-permute-done.6.refs_6_), channel_id=1, source_target_pairs={{0,8},{4,12},{8,0},{12,4},{16,24},{20,28},{24,16},{28,20},{1,9},{5... | collective-permute-start | bytes 1622024 | tf_op jit(solution)/shard_map/ppermute | solution.py:17
  28.7 4.7 %collective-permute-done.4.refs_3_ = bf16[3,2,128,256]{3,2,1,0:T(8,128)(2,1)S(1)} collective-permute-done((bf16[3,2,128,256]{3,2,1,0:T(8,128)(2,1)S(1)}, bf16[3,2,128,256]{3,2,1,0:T(8,128)(2,1)S(1)}, u32[]{:S(2)}, u32[]{:S(2)}) %collective-permute-start.4) | collective-permute-done | bytes 393248 | tf_op jit(solution)/shard_map/ppermute | solution.py:17
  33.4 1.7 %collective-permute-done.5.refs_4_ = bf16[3,2,128,256]{3,2,1,0:T(8,128)(2,1)S(1)} collective-permute-done((bf16[3,2,128,256]{3,2,1,0:T(8,128)(2,1)S(1)}, bf16[3,2,128,256]{3,2,1,0:T(8,128)(2,1)S(1)}, u32[]{:S(2)}, u32[]{:S(2)}) %collective-permute-start.5) | collective-permute-done | bytes 393248 | tf_op jit(solution)/shard_map/ppermute | solution.py:17
  35.2 1.7 %shard_map.119 = (bf16[512,1024]{1,0:T(8,128)(2,1)S(1)}, bf16[512,1024]{1,0:T(8,128)(2,1)S(1)}, bf16[3,352,1024]{2,1,0:T(8,128)(2,1)S(1)}, f32[3,352,512]{2,1,0:T(8,128)S(1)}) custom-call(bf16[2,128,1024]{2,1,0:T(8,128)(2,1)S(1)} %get-tuple-element.48.refs_0_, bf16[3,2,128,256]{3,2,1,0:T(8,128)(2,1)S(1)} %pad_maximum_fusion.refs_1_, ...), custom_call_target="tpu_custom_call" | custom-call | flops 1 | bytes 1 | tf_op jit(solution)/shard_map/pallas_call | solution.py:157
  36.9 2.6 %collective-permute-done.8.last = bf16[3,352,256]{2,1,0:T(8,128)(2,1)S(1)} collective-permute-done((bf16[3,352,256]{2,1,0:T(8,128)(2,1)S(1)}, bf16[3,352,256]{2,1,0:T(8,128)(2,1)S(1)}, u32[]{:S(2)}, u32[]{:S(2)}) %collective-permute-start.8) | collective-permute-done | bytes 540704 | tf_op jit(solution)/shard_map/ppermute | solution.py:17
  39.5 2.8 %shard_map.120 = (bf16[3,352,512]{2,1,0:T(8,128)(2,1)S(1)}, f32[2,1040,256]{2,1,0:T(8,128)S(1)}, bf16[2,1040,256]{2,1,0:T(8,128)(2,1)S(1)}, bf16[2,352,256]{2,1,0:T(8,128)(2,1)S(1)}, bf16[1,352,256]{2,1,0:T(8,128)(2,1)S(1)}) custom-call(bf16[512,1024]{1,0:T(8,128)(2,1)S(1)} %get-tuple-element.55.x_all, bf16[512,1024]{1,0:T(8,128)(2,1)S(1)} %get-tuple-element.56.s_all, ...), custom_call_target="tpu_custom_call" | custom-call | flops 1476395008 | tf_op jit(solution)/shard_map/pallas_call | solution.py:231
  42.3 1.8 %collective-permute-start.13 = (bf16[1,352,256]{2,1,0:T(8,128)(2,1)S(1)}, bf16[1,352,256]{2,1,0:T(8,128)(2,1)S(1)}, u32[]{:S(2)}, u32[]{:S(2)}) collective-permute-start(bf16[1,352,256]{2,1,0:T(8,128)(2,1)S(1)} %get-tuple-element.70), channel_id=1, source_target_pairs={{0,8},{4,12},{8,0},{12,4},{16,24},{20,28},{24,16},{28,20},{1,9},{5... | collective-permute-start | bytes 540680 | tf_op jit(solution)/shard_map/ppermute | solution.py:17
  46.3 1.0 %shard_map.124 = (f32[3,352,256]{2,1,0:T(8,128)S(1)}, f32[2,352,256]{2,1,0:T(8,128)S(1)}, f32[1,352,256]{2,1,0:T(8,128)S(1)}, bf16[3,352,256]{2,1,0:T(8,128)(2,1)S(1)}) custom-call(bf16[3,352,512]{2,1,0:T(8,128)(2,1)S(1)} %get-tuple-element.68.units, bf16[512,1024]{1,0:T(8,128)(2,1)S(1)} %get-tuple-element.55.x_all, ...), custom_call_target="tpu_custom_call" | custom-call | flops 922746880 | tf_op jit(solution)/shard_map/pallas_call | solution.py:264
  47.3 2.5 %collective-permute-done.13 = bf16[1,352,256]{2,1,0:T(8,128)(2,1)S(1)} collective-permute-done((bf16[1,352,256]{2,1,0:T(8,128)(2,1)S(1)}, bf16[1,352,256]{2,1,0:T(8,128)(2,1)S(1)}, u32[]{:S(2)}, u32[]{:S(2)}) %collective-permute-start.13) | collective-permute-done | bytes 180256 | tf_op jit(solution)/shard_map/ppermute | solution.py:17
  50.4 3.3 %collective-permute-done.10.from_y = bf16[528,256]{1,0:T(8,128)(2,1)S(1)} collective-permute-done((bf16[528,256]{1,0:T(8,128)(2,1)S(1)}, bf16[528,256]{1,0:T(8,128)(2,1)S(1)}, u32[]{:S(2)}, u32[]{:S(2)}) %collective-permute-start.10) | collective-permute-done | bytes 270368 | tf_op jit(solution)/shard_map/ppermute | solution.py:17
  55.0 1.5 %collective-permute-start.15 = (bf16[256,256]{1,0:T(8,128)(2,1)S(1)}, bf16[256,256]{1,0:T(8,128)(2,1)S(1)}, u32[]{:S(2)}, u32[]{:S(2)}) collective-permute-start(bf16[256,256]{1,0:T(8,128)(2,1)S(1)} %get-tuple-element.72), channel_id=1, source_target_pairs={{0,2},{1,3},{2,0},{3,1},{4,6},{5,7},{6,4},{7,5},{8,10},{9,11},{10,... | collective-permute-start | bytes 393224 | tf_op jit(solution)/shard_map/ppermute | solution.py:17
  56.6 1.7 %collective-permute-start.19 = (bf16[3,352,256]{2,1,0:T(8,128)(2,1)S(1)}, bf16[3,352,256]{2,1,0:T(8,128)(2,1)S(1)}, u32[]{:S(2)}, u32[]{:S(2)}) collective-permute-start(bf16[3,352,256]{2,1,0:T(8,128)(2,1)S(1)} %get-tuple-element.84), channel_id=1, source_target_pairs={{0,8},{4,12},{8,0},{12,4},{16,24},{20,28},{24,16},{28,20},{1,9},{5... | collective-permute-start | bytes 1622024 | tf_op jit(solution)/shard_map/ppermute | solution.py:17
  59.0 1.0 %collective-permute-done.15.from_y = bf16[256,256]{1,0:T(8,128)(2,1)S(1)} collective-permute-done((bf16[256,256]{1,0:T(8,128)(2,1)S(1)}, bf16[256,256]{1,0:T(8,128)(2,1)S(1)}, u32[]{:S(2)}, u32[]{:S(2)}) %collective-permute-start.15) | collective-permute-done | bytes 131104 | tf_op jit(solution)/shard_map/ppermute | solution.py:17
  60.1 1.7 %collective-permute-done.11.from_x = bf16[272,256]{1,0:T(8,128)(2,1)S(1)} collective-permute-done((bf16[272,256]{1,0:T(8,128)(2,1)S(1)}, bf16[272,256]{1,0:T(8,128)(2,1)S(1)}, u32[]{:S(2)}, u32[]{:S(2)}) %collective-permute-start.11) | collective-permute-done | bytes 139296 | tf_op jit(solution)/shard_map/ppermute | solution.py:17
  61.8 1.8 %collective-permute-start.18 = (bf16[272,256]{1,0:T(8,128)(2,1)S(1)}, bf16[272,256]{1,0:T(8,128)(2,1)S(1)}, u32[]{:S(2)}, u32[]{:S(2)}) collective-permute-start(bf16[272,256]{1,0:T(8,128)(2,1)S(1)} %get-tuple-element.78), channel_id=1, source_target_pairs={{0,16},{4,20},{8,24},{12,28},{16,0},{20,4},{24,8},{28,12},{1,17},{... | collective-permute-start | bytes 417800 | tf_op jit(solution)/shard_map/ppermute | solution.py:17
  63.6 4.7 %collective-permute-done.17.got_x = bf16[2,352,256]{2,1,0:T(8,128)(2,1)S(1)} collective-permute-done((bf16[2,352,256]{2,1,0:T(8,128)(2,1)S(1)}, bf16[2,352,256]{2,1,0:T(8,128)(2,1)S(1)}, u32[]{:S(2)}, u32[]{:S(2)}) %collective-permute-start.17) | collective-permute-done | bytes 360480 | tf_op jit(solution)/shard_map/ppermute | solution.py:17
  68.4 2.5 %collective-permute-done.18.refs_0_ = bf16[272,256]{1,0:T(8,128)(2,1)S(1)} collective-permute-done((bf16[272,256]{1,0:T(8,128)(2,1)S(1)}, bf16[272,256]{1,0:T(8,128)(2,1)S(1)}, u32[]{:S(2)}, u32[]{:S(2)}) %collective-permute-start.18) | collective-permute-done | bytes 139296 | tf_op jit(solution)/shard_map/ppermute | solution.py:17
  71.8 1.4 %shard_map.127 = (f32[704,256]{1,0:T(8,128)}, f32[704,256]{1,0:T(8,128)}, f32[704,256]{1,0:T(8,128)}) custom-call(f32[3,352,256]{2,1,0:T(8,128)S(1)} %convert_add_fusion.own, bf16[2,352,256]{2,1,0:T(8,128)(2,1)S(1)} %collective-permute-done.17.got_x, bf16[1,352,256]{2,1,0:T(8,128)(2,1)S(1)} %collective-permute-done.14.got_x_down), custom_call_target="tpu_custom_call" | custom-call | flops 1 | tf_op jit(solution)/shard_map/pallas_call | solution.py:297
  (32 shorter events, 7.3 us)
Async XLA Ops:
  2.1 23.1 %collective-permute-start.6 = (bf16[3,352,256]{2,1,0:T(8,128)(2,1)S(1)}, bf16[3,352,256]{2,1,0:T(8,128)(2,1)S(1)}, u32[]{:S(2)}, u32[]{:S(2)}) collective-permute-start(bf16[3,352,256]{2,1,0:T(8,128)(2,1)S(1)} %get-tuple-element.52), channel_id=1, source_target_pairs={{0,4},{4,0},{8,12},{12,8},{16,20},{20,16},{24,28},{28,24},{1,5},{5... | collective-permute-start | bytes 1622024 | tf_op jit(solution)/shard_map/ppermute | solution.py:17
  5.1 20.1 %collective-permute-start.7 = (bf16[3,352,256]{2,1,0:T(8,128)(2,1)S(1)}, bf16[3,352,256]{2,1,0:T(8,128)(2,1)S(1)}, u32[]{:S(2)}, u32[]{:S(2)}) collective-permute-start(bf16[3,352,256]{2,1,0:T(8,128)(2,1)S(1)} %get-tuple-element.51.refs_5_), channel_id=1, source_target_pairs={{0,8},{4,12},{8,0},{12,4},{16,24},{20,28},{24,16},{28,20},{1,9},{5... | collective-permute-start | bytes 1622024 | tf_op jit(solution)/shard_map/ppermute | solution.py:17
  6.7 16.3 %collective-permute-start = (bf16[2,128,256]{2,1,0:T(8,128)(2,1)S(1)}, bf16[2,128,256]{2,1,0:T(8,128)(2,1)S(1)}, u32[]{:S(2)}, u32[]{:S(2)}) collective-permute-start(bf16[2,128,256]{2,1,0:T(8,128)(2,1)S(1)} %get-tuple-element.49), channel_id=1, source_target_pairs={{0,4},{4,0},{8,12},{12,8},{16,20},{20,16},{24,28},{28,24},{1,5},{5... | collective-permute-start | bytes 393224 | tf_op jit(solution)/shard_map/ppermute | solution.py:17
  7.2 15.8 %collective-permute-start.2 = (bf16[2,128,256]{2,1,0:T(8,128)(2,1)S(1)}, bf16[2,128,256]{2,1,0:T(8,128)(2,1)S(1)}, u32[]{:S(2)}, u32[]{:S(2)}) collective-permute-start(bf16[2,128,256]{2,1,0:T(8,128)(2,1)S(1)} %get-tuple-element.50), channel_id=1, source_target_pairs={{0,20},{4,16},{8,28},{12,24},{16,4},{20,0},{24,12},{28,8},{1,21},{... | collective-permute-start | bytes 393224 | tf_op jit(solution)/shard_map/ppermute | solution.py:17
  10.7 12.8 %collective-permute-start.1 = (bf16[2,128,256]{2,1,0:T(8,128)(2,1)S(1)}, bf16[2,128,256]{2,1,0:T(8,128)(2,1)S(1)}, u32[]{:S(2)}, u32[]{:S(2)}) collective-permute-start(bf16[2,128,256]{2,1,0:T(8,128)(2,1)S(1)} %get-tuple-element.50), channel_id=1, source_target_pairs={{0,16},{4,20},{8,24},{12,28},{16,0},{20,4},{24,8},{28,12},{1,17},{... | collective-permute-start | bytes 393224 | tf_op jit(solution)/shard_map/ppermute | solution.py:17
  23.6 9.8 %collective-permute-start.4 = (bf16[3,2,128,256]{3,2,1,0:T(8,128)(2,1)S(1)}, bf16[3,2,128,256]{3,2,1,0:T(8,128)(2,1)S(1)}, u32[]{:S(2)}, u32[]{:S(2)}) collective-permute-start(bf16[3,2,128,256]{3,2,1,0:T(8,128)(2,1)S(1)} %pad_maximum_fusion.refs_1_), channel_id=1, source_target_pairs={{0,2},{1,3},{2,0},{3,1},{4,6},{5,7},{6,4},{7,5},{8,10},{9,11},{10,... | collective-permute-start | bytes 1179656 | tf_op jit(solution)/shard_map/ppermute | solution.py:17
  25.2 14.3 %collective-permute-start.8 = (bf16[3,352,256]{2,1,0:T(8,128)(2,1)S(1)}, bf16[3,352,256]{2,1,0:T(8,128)(2,1)S(1)}, u32[]{:S(2)}, u32[]{:S(2)}) collective-permute-start(bf16[3,352,256]{2,1,0:T(8,128)(2,1)S(1)} %collective-permute-done.6.refs_6_), channel_id=1, source_target_pairs={{0,8},{4,12},{8,0},{12,4},{16,24},{20,28},{24,16},{28,20},{1,9},{5... | collective-permute-start | bytes 1622024 | tf_op jit(solution)/shard_map/ppermute | solution.py:17
  28.7 4.7 %collective-permute-start.3 = (bf16[3,2,128,256]{3,2,1,0:T(8,128)(2,1)S(1)}, bf16[3,2,128,256]{3,2,1,0:T(8,128)(2,1)S(1)}, u32[]{:S(2)}, u32[]{:S(2)}) collective-permute-start(bf16[3,2,128,256]{3,2,1,0:T(8,128)(2,1)S(1)} %pad_maximum_fusion.refs_1_), channel_id=1, source_target_pairs={{0,1},{1,0},{2,3},{3,2},{4,5},{5,4},{6,7},{7,6},{8,9},{9,8},{10,11... | collective-permute-start | bytes 1179656 | tf_op jit(solution)/shard_map/ppermute | solution.py:17
  33.4 1.7 %collective-permute-start.5 = (bf16[3,2,128,256]{3,2,1,0:T(8,128)(2,1)S(1)}, bf16[3,2,128,256]{3,2,1,0:T(8,128)(2,1)S(1)}, u32[]{:S(2)}, u32[]{:S(2)}) collective-permute-start(bf16[3,2,128,256]{3,2,1,0:T(8,128)(2,1)S(1)} %collective-permute-done.4.refs_3_), channel_id=1, source_target_pairs={{0,1},{1,0},{2,3},{3,2},{4,5},{5,4},{6,7},{7,6},{8,9},{9,8},{10,11... | collective-permute-start | bytes 1179656 | tf_op jit(solution)/shard_map/ppermute | solution.py:17
  42.3 2.7 %collective-permute-start.9 = (bf16[2,1040,256]{2,1,0:T(8,128)(2,1)S(1)}, bf16[2,1040,256]{2,1,0:T(8,128)(2,1)S(1)}, u32[]{:S(2)}, u32[]{:S(2)}) collective-permute-start(bf16[2,1040,256]{2,1,0:T(8,128)(2,1)S(1)} %get-tuple-element.60), channel_id=1, source_target_pairs={{0,1},{1,0},{2,3},{3,2},{4,5},{5,4},{6,7},{7,6},{8,9},{9,8},{10,11... | collective-permute-start | bytes 3194888 | tf_op jit(solution)/shard_map/ppermute | solution.py:17
  42.3 7.4 %collective-permute-start.13 = (bf16[1,352,256]{2,1,0:T(8,128)(2,1)S(1)}, bf16[1,352,256]{2,1,0:T(8,128)(2,1)S(1)}, u32[]{:S(2)}, u32[]{:S(2)}) collective-permute-start(bf16[1,352,256]{2,1,0:T(8,128)(2,1)S(1)} %get-tuple-element.70), channel_id=1, source_target_pairs={{0,8},{4,12},{8,0},{12,4},{16,24},{20,28},{24,16},{28,20},{1,9},{5... | collective-permute-start | bytes 540680 | tf_op jit(solution)/shard_map/ppermute | solution.py:17
  44.2 14.1 %collective-permute-start.16 = (bf16[2,352,256]{2,1,0:T(8,128)(2,1)S(1)}, bf16[2,352,256]{2,1,0:T(8,128)(2,1)S(1)}, u32[]{:S(2)}, u32[]{:S(2)}) collective-permute-start(bf16[2,352,256]{2,1,0:T(8,128)(2,1)S(1)} %get-tuple-element.76), channel_id=1, source_target_pairs={{0,8},{4,12},{8,0},{12,4},{16,24},{20,28},{24,16},{28,20},{1,9},{5... | collective-permute-start | bytes 1081352 | tf_op jit(solution)/shard_map/ppermute | solution.py:17
  45.1 8.6 %collective-permute-start.10 = (bf16[528,256]{1,0:T(8,128)(2,1)S(1)}, bf16[528,256]{1,0:T(8,128)(2,1)S(1)}, u32[]{:S(2)}, u32[]{:S(2)}) collective-permute-start(bf16[528,256]{1,0:T(8,128)(2,1)S(1)} %get-tuple-element.61), channel_id=1, source_target_pairs={{0,2},{1,3},{2,0},{3,1},{4,6},{5,7},{6,4},{7,5},{8,10},{9,11},{10,... | collective-permute-start | bytes 811016 | tf_op jit(solution)/shard_map/ppermute | solution.py:17
  45.7 9.2 %collective-permute-start.12 = (bf16[2,256,256]{2,1,0:T(8,128)(2,1)S(1)}, bf16[2,256,256]{2,1,0:T(8,128)(2,1)S(1)}, u32[]{:S(2)}, u32[]{:S(2)}) collective-permute-start(bf16[2,256,256]{2,1,0:T(8,128)(2,1)S(1)} %get-tuple-element.64), channel_id=1, source_target_pairs={{0,4},{4,0},{8,12},{12,8},{16,20},{20,16},{24,28},{28,24},{1,5},{5... | collective-permute-start | bytes 786440 | tf_op jit(solution)/shard_map/ppermute | solution.py:17
  49.8 9.2 %collective-permute-start.14 = (bf16[1,352,256]{2,1,0:T(8,128)(2,1)S(1)}, bf16[1,352,256]{2,1,0:T(8,128)(2,1)S(1)}, u32[]{:S(2)}, u32[]{:S(2)}) collective-permute-start(bf16[1,352,256]{2,1,0:T(8,128)(2,1)S(1)} %add_convert_fusion.1), channel_id=1, source_target_pairs={{0,4},{4,0},{8,12},{12,8},{16,20},{20,16},{24,28},{28,24},{1,5},{5... | collective-permute-start | bytes 540680 | tf_op jit(solution)/shard_map/ppermute | solution.py:17
  53.8 8.0 %collective-permute-start.11 = (bf16[272,256]{1,0:T(8,128)(2,1)S(1)}, bf16[272,256]{1,0:T(8,128)(2,1)S(1)}, u32[]{:S(2)}, u32[]{:S(2)}) collective-permute-start(bf16[272,256]{1,0:T(8,128)(2,1)S(1)} %get-tuple-element.63), channel_id=1, source_target_pairs={{0,4},{4,0},{8,12},{12,8},{16,20},{20,16},{24,28},{28,24},{1,5},{5... | collective-permute-start | bytes 417800 | tf_op jit(solution)/shard_map/ppermute | solution.py:17
  55.0 5.0 %collective-permute-start.15 = (bf16[256,256]{1,0:T(8,128)(2,1)S(1)}, bf16[256,256]{1,0:T(8,128)(2,1)S(1)}, u32[]{:S(2)}, u32[]{:S(2)}) collective-permute-start(bf16[256,256]{1,0:T(8,128)(2,1)S(1)} %get-tuple-element.72), channel_id=1, source_target_pairs={{0,2},{1,3},{2,0},{3,1},{4,6},{5,7},{6,4},{7,5},{8,10},{9,11},{10,... | collective-permute-start | bytes 393224 | tf_op jit(solution)/shard_map/ppermute | solution.py:17
  56.6 15.1 %collective-permute-start.19 = (bf16[3,352,256]{2,1,0:T(8,128)(2,1)S(1)}, bf16[3,352,256]{2,1,0:T(8,128)(2,1)S(1)}, u32[]{:S(2)}, u32[]{:S(2)}) collective-permute-start(bf16[3,352,256]{2,1,0:T(8,128)(2,1)S(1)} %get-tuple-element.84), channel_id=1, source_target_pairs={{0,8},{4,12},{8,0},{12,4},{16,24},{20,28},{24,16},{28,20},{1,9},{5... | collective-permute-start | bytes 1622024 | tf_op jit(solution)/shard_map/ppermute | solution.py:17
  58.4 10.0 %collective-permute-start.17 = (bf16[2,352,256]{2,1,0:T(8,128)(2,1)S(1)}, bf16[2,352,256]{2,1,0:T(8,128)(2,1)S(1)}, u32[]{:S(2)}, u32[]{:S(2)}) collective-permute-start(bf16[2,352,256]{2,1,0:T(8,128)(2,1)S(1)} %add_convert_fusion), channel_id=1, source_target_pairs={{0,4},{4,0},{8,12},{12,8},{16,20},{20,16},{24,28},{28,24},{1,5},{5... | collective-permute-start | bytes 1081352 | tf_op jit(solution)/shard_map/ppermute | solution.py:17
  61.8 9.1 %copy-start = (f32[128]{0:T(128)S(1)}, f32[128]{0:T(128)}, u32[]{:S(2)}) copy-start(f32[128]{0:T(128)} %param.10) | copy-start | bytes 1540
  61.8 9.0 %collective-permute-start.18 = (bf16[272,256]{1,0:T(8,128)(2,1)S(1)}, bf16[272,256]{1,0:T(8,128)(2,1)S(1)}, u32[]{:S(2)}, u32[]{:S(2)}) collective-permute-start(bf16[272,256]{1,0:T(8,128)(2,1)S(1)} %get-tuple-element.78), channel_id=1, source_target_pairs={{0,16},{4,20},{8,24},{12,28},{16,0},{20,4},{24,8},{28,12},{1,17},{... | collective-permute-start | bytes 417800 | tf_op jit(solution)/shard_map/ppermute | solution.py:17

commit v10 on v9

--- a/solution.py
+++ b/solution.py
@@ -115,37 +115,32 @@
     pieces, weights = refs[has_own : has_own + 4], refs[has_own + 4 : has_own + 7]
     x_all, s_all, w_all, part = refs[has_own + 7 :]
     blocks, _, slots, width = pieces[0].shape
+    half, reach = w_all.shape[1:]
     member = lax.axis_index("wide") % 4
     place = lax.axis_index("narrow")
     for k, ref in enumerate(weights):
-        column = at_quarter(member ^ k, width)
         for i in range(3):
-            w_all[i, :, column] = ref[i]
+            w_all[i, :, k * width : (k + 1) * width] = ref[i]
     first = 0
     if has_own:
-        x_all[:slots, :] = own[0]
-        s_all[:slots, :] = own[1]
+        for k in range(4):
+            column = at_quarter(member ^ k, width)
+            x_all[:slots, k * width : (k + 1) * width] = own[0, :, column]
+            s_all[:slots, k * width : (k + 1) * width] = own[1, :, column]
         first = slots
     for mask, ref in enumerate(pieces):
-        column = at_quarter(place ^ mask, width)
+        column = at_quarter(place ^ member ^ mask, width)
         for block in range(blocks):
             rows = slice(first + block * slots, first + (block + 1) * slots)
             x_all[rows, column] = ref[block, 0]
             s_all[rows, column] = ref[block, 1]
     total = x_all.shape[0]
-    tile = min(256, total)
-
-    @pl.loop(0, total // tile)
-    def _(step):
-        rows = pl.ds(pl.multiple_of(step * tile, tile), tile)
-        for i in range(3):
-            held = s_all if i == 2 else x_all
-            sums = None
-            for k in range(3):
-                column = at_quarter(member ^ k, width)
-                term = dot_nt(w_all[i, :, column], held[rows, column])
-                sums = term if sums is None else sums + term
-            part[i, :, rows] = sums
+    tile = min(2 * width, total)
+    for step in range(total // tile):
+        rows = slice(step * tile, (step + 1) * tile)
+        both = dot_nt(w_all[0:2].reshape(2 * half, reach), x_all[rows, :reach])
+        part[0:2, :, rows] = both.reshape(2, half, tile)
+        part[2, :, rows] = dot_nt(w_all[2], s_all[rows, :reach])
 
 
 def gather_parts(own, pieces, weights):
@@ -159,7 +154,7 @@
         out_shape=(
             jax.ShapeDtypeStruct((total, features), jnp.bfloat16),
             jax.ShapeDtypeStruct((total, features), jnp.bfloat16),
-            jax.ShapeDtypeStruct((3, half, features), jnp.bfloat16),
+            jax.ShapeDtypeStruct((3, half, 3 * width), jnp.bfloat16),
             jax.ShapeDtypeStruct((3, half, total), jnp.float32),
         ),
         in_specs=[VMEM] * (7 + has_own),
@@ -181,26 +176,25 @@
 def outer_kernel(x_all, s_all, w_part, part, last, units, kept, sent, *refs):
     to_d, w_all, sums = refs[:2], refs[2], refs[3]
     half, width = last.shape[1:]
-    chunk = 32 if half % 32 == 0 else 16
-    place = lax.axis_index("narrow")
-    last_column = at_quarter(lax.axis_index("wide") % 4 ^ 3, width)
-    w_all[...] = w_part[...]
-    for i in range(3):
-        w_all[i, :, last_column] = last[i]
-    total = x_all.shape[0]
-    tile = min(width, total)
+    offset = lax.axis_index("narrow") ^ lax.axis_index("wide") % 4
+    last_column = slice(3 * width, 4 * width)
+    for k in range(4):
+        column = at_quarter(offset ^ k, width)
+        for i in range(3):
+            w_all[i, :, column] = last[i] if k == 3 else w_part[i, :, k * width : (k + 1) * width]
+    total, tile = x_all.shape[0], sums.shape[2]
+    lanes = min(width, total)
     for ref in (kept, sent):
         ref[:, 2 * total :, :] = jnp.zeros_like(ref[:, 2 * total :, :])
     routers = []
     for step in range(total // tile):
         rows = slice(step * tile, (step + 1) * tile)
-        lower = slice(total + step * tile, total + (step + 1) * tile)
-        x_tile, s_tile = x_all[rows, last_column], s_all[rows, last_column]
-        for i, held in enumerate((x_tile, x_tile, s_tile)):
-            sums[i] = part[i, :, rows] + dot_nt(last[i], held)
-        products = jnp.zeros((chunk, tile), jnp.float32)
-        for low in range(0, half, chunk):
-            piece = slice(low, low + chunk)
+        both = dot_nt(last[0:2].reshape(2 * half, width), x_all[rows, last_column])
+        sums[0:2] = part[0:2, :, rows] + both.reshape(2, half, tile)
+        sums[2] = part[2, :, rows] + dot_nt(last[2], s_all[rows, last_column])
+        products = jnp.zeros((16, tile), jnp.float32)
+        for low in range(0, half, 16):
+            piece = slice(low, low + 16)
             gate, up, d_hidden = sums[0, piece, :], sums[1, piece, :], sums[2, piece, :]
             sigma = 0.5 + 0.5 * jnp.tanh(0.5 * gate)
             active = gate * sigma
@@ -211,17 +205,21 @@
             units[2, piece, rows] = hidden
             products = products + hidden.astype(jnp.float32) * d_hidden
         router = jnp.sum(products, axis=0, keepdims=True)
-        kept[0, 2 * total + step : 2 * total + step + 1, :tile] = router
-        routers.append(router)
-        hidden_t, d_both = units[2, :, rows].T, units[0:2, :, rows].reshape(2 * half, tile).T
-        for mask in range(4):
-            column = at_quarter(place ^ mask, width)
-            target = sent if mask % 2 else kept
-            out_part = dot_nn(hidden_t, w_all[2, :, column])
-            in_part = dot_nn(d_both, w_all[0:2, :, column].reshape(2 * half, width))
-            target[mask // 2, rows, :] = out_part.astype(target.dtype)
-            target[mask // 2, lower, :] = in_part.astype(target.dtype)
-    put_pair(sent.at[0], 2 * total, jnp.concatenate(routers, 0))
+        routers += [router[:, low : low + lanes] for low in range(0, tile, lanes)]
+        for low in range(step * tile, (step + 1) * tile, lanes):
+            here = slice(low, low + lanes)
+            lower = slice(total + low, total + low + lanes)
+            out_part = dot_nn(units[2, :, here].T, w_all[2])
+            left = units[0:2, :, here].reshape(2 * half, lanes).T
+            in_part = dot_nn(left, w_all[0:2].reshape(2 * half, 4 * width))
+            for mask in range(4):
+                target = sent if mask % 2 else kept
+                column = slice(mask * width, (mask + 1) * width)
+                target[mask // 2, here, :] = out_part[:, column].astype(target.dtype)
+                target[mask // 2, lower, :] = in_part[:, column].astype(target.dtype)
+    router = jnp.concatenate(routers, 0)
+    kept[0, 2 * total : 2 * total + len(routers), :lanes] = router
+    put_pair(sent.at[0], 2 * total, router)
     grad_parts(units, x_all, s_all, last_column, to_d)
 
 
@@ -241,7 +239,7 @@
         out_specs=[VMEM] * 5,
         scratch_shapes=[
             pltpu.VMEM((3, half, features), jnp.bfloat16),
-            pltpu.VMEM((3, half, min(width, total)), jnp.float32),
+            pltpu.VMEM((3, half, min(2 * width, total)), jnp.float32),
         ],
         compiler_params=PARAMS,
         cost_estimate=pl.CostEstimate(
@@ -252,9 +250,8 @@
 
 def grads_kernel(units, x_all, s_all, own, to_x, to_x_down, to_z):
     width = own.shape[2]
-    member = lax.axis_index("wide") % 4
     for k, outs in enumerate(((own,), (to_x, to_x_down), (to_z,))):
-        grad_parts(units, x_all, s_all, at_quarter(member ^ k, width), outs)
+        grad_parts(units, x_all, s_all, slice(k * width, (k + 1) * width), outs)
 
 
 def weight_grads(units, x_all, s_all):

time: 73.3 us -> 73.3 us (level)
  no operation moved by 1% of the time
where the time goes in v10:
time: 73.3 us; the launch traced here: 73.2 us
  waiting for transfers between devices  39 us (53%)
  starting transfers between devices  24.2 us (33%)
  Pallas kernels  9.03 us (12%)
    ppermute x20, waiting for transfers between devices, partner(): lax.ppermute(x, axis, [(i, i ^ mask) for i in range(lax.axis_size(axis))])  39 us
    ppermute x20, starting transfers between devices, partner(): lax.ppermute(x, axis, [(i, i ^ mask) for i in range(lax.axis_size(axis))])  24.2 us
    pallas_call x1, Pallas kernels, outer(): pl.pallas_call(outer_kernel, out_shape=(jax.ShapeDtypeStruct((3, half, to...  2.74 us
    pallas_call x1, Pallas kernels, prologue(): pl.pallas_call(functools.partial(prologue_kernel, bool(token_args)), out_...  1.47 us
  transfers between devices with their start and end apart: 20, of which 13 were waited for; matrix products, arithmetic and copies ran while one was open for 0% of the time, Pallas kernels for 5%

profile of v10, /device:TPU:0, one launch (start us, length us, event | category | flops | bytes accessed | tf_op | source)
XLA Modules:
  0.0 73.2 jit_solution(7825160294686279721)
XLA Ops:
  0.6 1.5 %shard_map.118 = (bf16[3,352,256]{2,1,0:T(8,128)(2,1)S(1)}, bf16[3,352,256]{2,1,0:T(8,128)(2,1)S(1)}, bf16[2,128,1024]{2,1,0:T(8,128)(2,1)S(1)}, bf16[2,128,256]...) custom-call(bf16[704,256]{1,0:T(8,128)(2,1)} %bitcast.14, bf16[704,256]{1,0:T(8,128)(2,1)} %bitcast.15, ...), custom_call_target="tpu_custom_call" | custom-call | tf_op jit(solution)/shard_map/pallas_call | solution.py:103
  2.1 3.0 %collective-permute-start.6 = (bf16[3,352,256]{2,1,0:T(8,128)(2,1)S(1)}, bf16[3,352,256]{2,1,0:T(8,128)(2,1)S(1)}, u32[]{:S(2)}, u32[]{:S(2)}) collective-permute-start(bf16[3,352,256]{2,1,0:T(8,128)(2,1)S(1)} %get-tuple-element.52), channel_id=1, source_target_pairs={{0,4},{4,0},{8,12},{12,8},{16,20},{20,16},{24,28},{28,24},{1,5},{5... | collective-permute-start | bytes 1622024 | tf_op jit(solution)/shard_map/ppermute | solution.py:17
  5.1 1.6 %collective-permute-start.7 = (bf16[3,352,256]{2,1,0:T(8,128)(2,1)S(1)}, bf16[3,352,256]{2,1,0:T(8,128)(2,1)S(1)}, u32[]{:S(2)}, u32[]{:S(2)}) collective-permute-start(bf16[3,352,256]{2,1,0:T(8,128)(2,1)S(1)} %get-tuple-element.51.refs_5_), channel_id=1, source_target_pairs={{0,8},{4,12},{8,0},{12,4},{16,24},{20,28},{24,16},{28,20},{1,9},{5... | collective-permute-start | bytes 1622024 | tf_op jit(solution)/shard_map/ppermute | solution.py:17
  7.2 3.5 %collective-permute-start.2 = (bf16[2,128,256]{2,1,0:T(8,128)(2,1)S(1)}, bf16[2,128,256]{2,1,0:T(8,128)(2,1)S(1)}, u32[]{:S(2)}, u32[]{:S(2)}) collective-permute-start(bf16[2,128,256]{2,1,0:T(8,128)(2,1)S(1)} %get-tuple-element.50), channel_id=1, source_target_pairs={{0,20},{4,16},{8,28},{12,24},{16,4},{20,0},{24,12},{28,8},{1,21},{... | collective-permute-start | bytes 393224 | tf_op jit(solution)/shard_map/ppermute | solution.py:17
  11.1 11.9 %collective-permute-done = bf16[2,128,256]{2,1,0:T(8,128)(2,1)S(1)} collective-permute-done((bf16[2,128,256]{2,1,0:T(8,128)(2,1)S(1)}, bf16[2,128,256]{2,1,0:T(8,128)(2,1)S(1)}, u32[]{:S(2)}, u32[]{:S(2)}) %collective-permute-start) | collective-permute-done | bytes 131104 | tf_op jit(solution)/shard_map/ppermute | solution.py:17
  23.6 1.6 %collective-permute-start.4 = (bf16[3,2,128,256]{3,2,1,0:T(8,128)(2,1)S(1)}, bf16[3,2,128,256]{3,2,1,0:T(8,128)(2,1)S(1)}, u32[]{:S(2)}, u32[]{:S(2)}) collective-permute-start(bf16[3,2,128,256]{3,2,1,0:T(8,128)(2,1)S(1)} %pad_maximum_fusion.refs_1_), channel_id=1, source_target_pairs={{0,2},{1,3},{2,0},{3,1},{4,6},{5,7},{6,4},{7,5},{8,10},{9,11},{10,... | collective-permute-start | bytes 1179656 | tf_op jit(solution)/shard_map/ppermute | solution.py:17
  25.2 3.5 %collective-permute-start.8 = (bf16[3,352,256]{2,1,0:T(8,128)(2,1)S(1)}, bf16[3,352,256]{2,1,0:T(8,128)(2,1)S(1)}, u32[]{:S(2)}, u32[]{:S(2)}) collective-permute-start(bf16[3,352,256]{2,1,0:T(8,128)(2,1)S(1)} %collective-permute-done.6.refs_6_), channel_id=1, source_target_pairs={{0,8},{4,12},{8,0},{12,4},{16,24},{20,28},{24,16},{28,20},{1,9},{5... | collective-permute-start | bytes 1622024 | tf_op jit(solution)/shard_map/ppermute | solution.py:17
  28.7 4.7 %collective-permute-done.4.refs_3_ = bf16[3,2,128,256]{3,2,1,0:T(8,128)(2,1)S(1)} collective-permute-done((bf16[3,2,128,256]{3,2,1,0:T(8,128)(2,1)S(1)}, bf16[3,2,128,256]{3,2,1,0:T(8,128)(2,1)S(1)}, u32[]{:S(2)}, u32[]{:S(2)}) %collective-permute-start.4) | collective-permute-done | bytes 393248 | tf_op jit(solution)/shard_map/ppermute | solution.py:17
  33.4 1.7 %collective-permute-done.5.refs_4_ = bf16[3,2,128,256]{3,2,1,0:T(8,128)(2,1)S(1)} collective-permute-done((bf16[3,2,128,256]{3,2,1,0:T(8,128)(2,1)S(1)}, bf16[3,2,128,256]{3,2,1,0:T(8,128)(2,1)S(1)}, u32[]{:S(2)}, u32[]{:S(2)}) %collective-permute-start.5) | collective-permute-done | bytes 393248 | tf_op jit(solution)/shard_map/ppermute | solution.py:17
  35.2 1.3 %shard_map.119 = (bf16[512,1024]{1,0:T(8,128)(2,1)S(1)}, bf16[512,1024]{1,0:T(8,128)(2,1)S(1)}, bf16[3,352,768]{2,1,0:T(8,128)(2,1)S(1)}, f32[3,352,512]{2,1,0:T(8,128)S(1)}) custom-call(bf16[2,128,1024]{2,1,0:T(8,128)(2,1)S(1)} %get-tuple-element.48.refs_0_, bf16[3,2,128,256]{3,2,1,0:T(8,128)(2,1)S(1)} %pad_maximum_fusion.refs_1_, ...), custom_call_target="tpu_custom_call" | custom-call | flops 1 | bytes 1 | tf_op jit(solution)/shard_map/pallas_call | solution.py:152
  36.4 3.1 %collective-permute-done.8.last = bf16[3,352,256]{2,1,0:T(8,128)(2,1)S(1)} collective-permute-done((bf16[3,352,256]{2,1,0:T(8,128)(2,1)S(1)}, bf16[3,352,256]{2,1,0:T(8,128)(2,1)S(1)}, u32[]{:S(2)}, u32[]{:S(2)}) %collective-permute-start.8) | collective-permute-done | bytes 540704 | tf_op jit(solution)/shard_map/ppermute | solution.py:17
  39.5 2.7 %shard_map.120 = (bf16[3,352,512]{2,1,0:T(8,128)(2,1)S(1)}, f32[2,1040,256]{2,1,0:T(8,128)S(1)}, bf16[2,1040,256]{2,1,0:T(8,128)(2,1)S(1)}, bf16[2,352,256]{2,1,0:T(8,128)(2,1)S(1)}, bf16[1,352,256]{2,1,0:T(8,128)(2,1)S(1)}) custom-call(bf16[512,1024]{1,0:T(8,128)(2,1)S(1)} %get-tuple-element.55.x_all, bf16[512,1024]{1,0:T(8,128)(2,1)S(1)} %get-tuple-element.56.s_all, ...), custom_call_target="tpu_custom_call" | custom-call | flops 1476395008 | tf_op jit(solution)/shard_map/pallas_call | solution.py:229
  42.3 1.8 %collective-permute-start.13 = (bf16[1,352,256]{2,1,0:T(8,128)(2,1)S(1)}, bf16[1,352,256]{2,1,0:T(8,128)(2,1)S(1)}, u32[]{:S(2)}, u32[]{:S(2)}) collective-permute-start(bf16[1,352,256]{2,1,0:T(8,128)(2,1)S(1)} %get-tuple-element.70), channel_id=1, source_target_pairs={{0,8},{4,12},{8,0},{12,4},{16,24},{20,28},{24,16},{28,20},{1,9},{5... | collective-permute-start | bytes 540680 | tf_op jit(solution)/shard_map/ppermute | solution.py:17
  46.2 1.0 %shard_map.124 = (f32[3,352,256]{2,1,0:T(8,128)S(1)}, f32[2,352,256]{2,1,0:T(8,128)S(1)}, f32[1,352,256]{2,1,0:T(8,128)S(1)}, bf16[3,352,256]{2,1,0:T(8,128)(2,1)S(1)}) custom-call(bf16[3,352,512]{2,1,0:T(8,128)(2,1)S(1)} %get-tuple-element.68.units, bf16[512,1024]{1,0:T(8,128)(2,1)S(1)} %get-tuple-element.55.x_all, ...), custom_call_target="tpu_custom_call" | custom-call | flops 922746880 | tf_op jit(solution)/shard_map/pallas_call | solution.py:261
  47.2 2.5 %collective-permute-done.13 = bf16[1,352,256]{2,1,0:T(8,128)(2,1)S(1)} collective-permute-done((bf16[1,352,256]{2,1,0:T(8,128)(2,1)S(1)}, bf16[1,352,256]{2,1,0:T(8,128)(2,1)S(1)}, u32[]{:S(2)}, u32[]{:S(2)}) %collective-permute-start.13) | collective-permute-done | bytes 180256 | tf_op jit(solution)/shard_map/ppermute | solution.py:17
  50.4 3.3 %collective-permute-done.10.from_y = bf16[528,256]{1,0:T(8,128)(2,1)S(1)} collective-permute-done((bf16[528,256]{1,0:T(8,128)(2,1)S(1)}, bf16[528,256]{1,0:T(8,128)(2,1)S(1)}, u32[]{:S(2)}, u32[]{:S(2)}) %collective-permute-start.10) | collective-permute-done | bytes 270368 | tf_op jit(solution)/shard_map/ppermute | solution.py:17
  55.0 1.6 %collective-permute-start.15 = (bf16[256,256]{1,0:T(8,128)(2,1)S(1)}, bf16[256,256]{1,0:T(8,128)(2,1)S(1)}, u32[]{:S(2)}, u32[]{:S(2)}) collective-permute-start(bf16[256,256]{1,0:T(8,128)(2,1)S(1)} %get-tuple-element.72), channel_id=1, source_target_pairs={{0,2},{1,3},{2,0},{3,1},{4,6},{5,7},{6,4},{7,5},{8,10},{9,11},{10,... | collective-permute-start | bytes 393224 | tf_op jit(solution)/shard_map/ppermute | solution.py:17
  56.5 1.7 %collective-permute-start.19 = (bf16[3,352,256]{2,1,0:T(8,128)(2,1)S(1)}, bf16[3,352,256]{2,1,0:T(8,128)(2,1)S(1)}, u32[]{:S(2)}, u32[]{:S(2)}) collective-permute-start(bf16[3,352,256]{2,1,0:T(8,128)(2,1)S(1)} %get-tuple-element.84), channel_id=1, source_target_pairs={{0,8},{4,12},{8,0},{12,4},{16,24},{20,28},{24,16},{28,20},{1,9},{5... | collective-permute-start | bytes 1622024 | tf_op jit(solution)/shard_map/ppermute | solution.py:17
  59.0 1.0 %collective-permute-done.15.from_y = bf16[256,256]{1,0:T(8,128)(2,1)S(1)} collective-permute-done((bf16[256,256]{1,0:T(8,128)(2,1)S(1)}, bf16[256,256]{1,0:T(8,128)(2,1)S(1)}, u32[]{:S(2)}, u32[]{:S(2)}) %collective-permute-start.15) | collective-permute-done | bytes 131104 | tf_op jit(solution)/shard_map/ppermute | solution.py:17
  60.0 1.6 %collective-permute-done.11.from_x = bf16[272,256]{1,0:T(8,128)(2,1)S(1)} collective-permute-done((bf16[272,256]{1,0:T(8,128)(2,1)S(1)}, bf16[272,256]{1,0:T(8,128)(2,1)S(1)}, u32[]{:S(2)}, u32[]{:S(2)}) %collective-permute-start.11) | collective-permute-done | bytes 139296 | tf_op jit(solution)/shard_map/ppermute | solution.py:17
  61.7 1.7 %collective-permute-start.18 = (bf16[272,256]{1,0:T(8,128)(2,1)S(1)}, bf16[272,256]{1,0:T(8,128)(2,1)S(1)}, u32[]{:S(2)}, u32[]{:S(2)}) collective-permute-start(bf16[272,256]{1,0:T(8,128)(2,1)S(1)} %get-tuple-element.78), channel_id=1, source_target_pairs={{0,16},{4,20},{8,24},{12,28},{16,0},{20,4},{24,8},{28,12},{1,17},{... | collective-permute-start | bytes 417800 | tf_op jit(solution)/shard_map/ppermute | solution.py:17
  63.4 4.9 %collective-permute-done.17.got_x = bf16[2,352,256]{2,1,0:T(8,128)(2,1)S(1)} collective-permute-done((bf16[2,352,256]{2,1,0:T(8,128)(2,1)S(1)}, bf16[2,352,256]{2,1,0:T(8,128)(2,1)S(1)}, u32[]{:S(2)}, u32[]{:S(2)}) %collective-permute-start.17) | collective-permute-done | bytes 360480 | tf_op jit(solution)/shard_map/ppermute | solution.py:17
  68.3 2.5 %collective-permute-done.18.refs_0_ = bf16[272,256]{1,0:T(8,128)(2,1)S(1)} collective-permute-done((bf16[272,256]{1,0:T(8,128)(2,1)S(1)}, bf16[272,256]{1,0:T(8,128)(2,1)S(1)}, u32[]{:S(2)}, u32[]{:S(2)}) %collective-permute-start.18) | collective-permute-done | bytes 139296 | tf_op jit(solution)/shard_map/ppermute | solution.py:17
  71.8 1.4 %shard_map.127 = (f32[704,256]{1,0:T(8,128)}, f32[704,256]{1,0:T(8,128)}, f32[704,256]{1,0:T(8,128)}) custom-call(f32[3,352,256]{2,1,0:T(8,128)S(1)} %convert_add_fusion.own, bf16[2,352,256]{2,1,0:T(8,128)(2,1)S(1)} %collective-permute-done.17.got_x, bf16[1,352,256]{2,1,0:T(8,128)(2,1)S(1)} %collective-permute-done.14.got_x_down), custom_call_target="tpu_custom_call" | custom-call | flops 1 | tf_op jit(solution)/shard_map/pallas_call | solution.py:294
  (32 shorter events, 7.2 us)
Async XLA Ops:
  2.1 23.1 %collective-permute-start.6 = (bf16[3,352,256]{2,1,0:T(8,128)(2,1)S(1)}, bf16[3,352,256]{2,1,0:T(8,128)(2,1)S(1)}, u32[]{:S(2)}, u32[]{:S(2)}) collective-permute-start(bf16[3,352,256]{2,1,0:T(8,128)(2,1)S(1)} %get-tuple-element.52), channel_id=1, source_target_pairs={{0,4},{4,0},{8,12},{12,8},{16,20},{20,16},{24,28},{28,24},{1,5},{5... | collective-permute-start | bytes 1622024 | tf_op jit(solution)/shard_map/ppermute | solution.py:17
  5.1 20.1 %collective-permute-start.7 = (bf16[3,352,256]{2,1,0:T(8,128)(2,1)S(1)}, bf16[3,352,256]{2,1,0:T(8,128)(2,1)S(1)}, u32[]{:S(2)}, u32[]{:S(2)}) collective-permute-start(bf16[3,352,256]{2,1,0:T(8,128)(2,1)S(1)} %get-tuple-element.51.refs_5_), channel_id=1, source_target_pairs={{0,8},{4,12},{8,0},{12,4},{16,24},{20,28},{24,16},{28,20},{1,9},{5... | collective-permute-start | bytes 1622024 | tf_op jit(solution)/shard_map/ppermute | solution.py:17
  6.7 16.3 %collective-permute-start = (bf16[2,128,256]{2,1,0:T(8,128)(2,1)S(1)}, bf16[2,128,256]{2,1,0:T(8,128)(2,1)S(1)}, u32[]{:S(2)}, u32[]{:S(2)}) collective-permute-start(bf16[2,128,256]{2,1,0:T(8,128)(2,1)S(1)} %get-tuple-element.49), channel_id=1, source_target_pairs={{0,4},{4,0},{8,12},{12,8},{16,20},{20,16},{24,28},{28,24},{1,5},{5... | collective-permute-start | bytes 393224 | tf_op jit(solution)/shard_map/ppermute | solution.py:17
  7.2 15.8 %collective-permute-start.2 = (bf16[2,128,256]{2,1,0:T(8,128)(2,1)S(1)}, bf16[2,128,256]{2,1,0:T(8,128)(2,1)S(1)}, u32[]{:S(2)}, u32[]{:S(2)}) collective-permute-start(bf16[2,128,256]{2,1,0:T(8,128)(2,1)S(1)} %get-tuple-element.50), channel_id=1, source_target_pairs={{0,20},{4,16},{8,28},{12,24},{16,4},{20,0},{24,12},{28,8},{1,21},{... | collective-permute-start | bytes 393224 | tf_op jit(solution)/shard_map/ppermute | solution.py:17
  10.7 12.8 %collective-permute-start.1 = (bf16[2,128,256]{2,1,0:T(8,128)(2,1)S(1)}, bf16[2,128,256]{2,1,0:T(8,128)(2,1)S(1)}, u32[]{:S(2)}, u32[]{:S(2)}) collective-permute-start(bf16[2,128,256]{2,1,0:T(8,128)(2,1)S(1)} %get-tuple-element.50), channel_id=1, source_target_pairs={{0,16},{4,20},{8,24},{12,28},{16,0},{20,4},{24,8},{28,12},{1,17},{... | collective-permute-start | bytes 393224 | tf_op jit(solution)/shard_map/ppermute | solution.py:17
  23.6 9.8 %collective-permute-start.4 = (bf16[3,2,128,256]{3,2,1,0:T(8,128)(2,1)S(1)}, bf16[3,2,128,256]{3,2,1,0:T(8,128)(2,1)S(1)}, u32[]{:S(2)}, u32[]{:S(2)}) collective-permute-start(bf16[3,2,128,256]{3,2,1,0:T(8,128)(2,1)S(1)} %pad_maximum_fusion.refs_1_), channel_id=1, source_target_pairs={{0,2},{1,3},{2,0},{3,1},{4,6},{5,7},{6,4},{7,5},{8,10},{9,11},{10,... | collective-permute-start | bytes 1179656 | tf_op jit(solution)/shard_map/ppermute | solution.py:17
  25.2 14.3 %collective-permute-start.8 = (bf16[3,352,256]{2,1,0:T(8,128)(2,1)S(1)}, bf16[3,352,256]{2,1,0:T(8,128)(2,1)S(1)}, u32[]{:S(2)}, u32[]{:S(2)}) collective-permute-start(bf16[3,352,256]{2,1,0:T(8,128)(2,1)S(1)} %collective-permute-done.6.refs_6_), channel_id=1, source_target_pairs={{0,8},{4,12},{8,0},{12,4},{16,24},{20,28},{24,16},{28,20},{1,9},{5... | collective-permute-start | bytes 1622024 | tf_op jit(solution)/shard_map/ppermute | solution.py:17
  28.7 4.7 %collective-permute-start.3 = (bf16[3,2,128,256]{3,2,1,0:T(8,128)(2,1)S(1)}, bf16[3,2,128,256]{3,2,1,0:T(8,128)(2,1)S(1)}, u32[]{:S(2)}, u32[]{:S(2)}) collective-permute-start(bf16[3,2,128,256]{3,2,1,0:T(8,128)(2,1)S(1)} %pad_maximum_fusion.refs_1_), channel_id=1, source_target_pairs={{0,1},{1,0},{2,3},{3,2},{4,5},{5,4},{6,7},{7,6},{8,9},{9,8},{10,11... | collective-permute-start | bytes 1179656 | tf_op jit(solution)/shard_map/ppermute | solution.py:17
  33.4 1.7 %collective-permute-start.5 = (bf16[3,2,128,256]{3,2,1,0:T(8,128)(2,1)S(1)}, bf16[3,2,128,256]{3,2,1,0:T(8,128)(2,1)S(1)}, u32[]{:S(2)}, u32[]{:S(2)}) collective-permute-start(bf16[3,2,128,256]{3,2,1,0:T(8,128)(2,1)S(1)} %collective-permute-done.4.refs_3_), channel_id=1, source_target_pairs={{0,1},{1,0},{2,3},{3,2},{4,5},{5,4},{6,7},{7,6},{8,9},{9,8},{10,11... | collective-permute-start | bytes 1179656 | tf_op jit(solution)/shard_map/ppermute | solution.py:17
  42.3 2.7 %collective-permute-start.9 = (bf16[2,1040,256]{2,1,0:T(8,128)(2,1)S(1)}, bf16[2,1040,256]{2,1,0:T(8,128)(2,1)S(1)}, u32[]{:S(2)}, u32[]{:S(2)}) collective-permute-start(bf16[2,1040,256]{2,1,0:T(8,128)(2,1)S(1)} %get-tuple-element.60), channel_id=1, source_target_pairs={{0,1},{1,0},{2,3},{3,2},{4,5},{5,4},{6,7},{7,6},{8,9},{9,8},{10,11... | collective-permute-start | bytes 3194888 | tf_op jit(solution)/shard_map/ppermute | solution.py:17
  42.3 7.4 %collective-permute-start.13 = (bf16[1,352,256]{2,1,0:T(8,128)(2,1)S(1)}, bf16[1,352,256]{2,1,0:T(8,128)(2,1)S(1)}, u32[]{:S(2)}, u32[]{:S(2)}) collective-permute-start(bf16[1,352,256]{2,1,0:T(8,128)(2,1)S(1)} %get-tuple-element.70), channel_id=1, source_target_pairs={{0,8},{4,12},{8,0},{12,4},{16,24},{20,28},{24,16},{28,20},{1,9},{5... | collective-permute-start | bytes 540680 | tf_op jit(solution)/shard_map/ppermute | solution.py:17
  44.1 14.1 %collective-permute-start.16 = (bf16[2,352,256]{2,1,0:T(8,128)(2,1)S(1)}, bf16[2,352,256]{2,1,0:T(8,128)(2,1)S(1)}, u32[]{:S(2)}, u32[]{:S(2)}) collective-permute-start(bf16[2,352,256]{2,1,0:T(8,128)(2,1)S(1)} %get-tuple-element.76), channel_id=1, source_target_pairs={{0,8},{4,12},{8,0},{12,4},{16,24},{20,28},{24,16},{28,20},{1,9},{5... | collective-permute-start | bytes 1081352 | tf_op jit(solution)/shard_map/ppermute | solution.py:17
  45.1 8.6 %collective-permute-start.10 = (bf16[528,256]{1,0:T(8,128)(2,1)S(1)}, bf16[528,256]{1,0:T(8,128)(2,1)S(1)}, u32[]{:S(2)}, u32[]{:S(2)}) collective-permute-start(bf16[528,256]{1,0:T(8,128)(2,1)S(1)} %get-tuple-element.61), channel_id=1, source_target_pairs={{0,2},{1,3},{2,0},{3,1},{4,6},{5,7},{6,4},{7,5},{8,10},{9,11},{10,... | collective-permute-start | bytes 811016 | tf_op jit(solution)/shard_map/ppermute | solution.py:17
  45.7 9.2 %collective-permute-start.12 = (bf16[2,256,256]{2,1,0:T(8,128)(2,1)S(1)}, bf16[2,256,256]{2,1,0:T(8,128)(2,1)S(1)}, u32[]{:S(2)}, u32[]{:S(2)}) collective-permute-start(bf16[2,256,256]{2,1,0:T(8,128)(2,1)S(1)} %get-tuple-element.64), channel_id=1, source_target_pairs={{0,4},{4,0},{8,12},{12,8},{16,20},{20,16},{24,28},{28,24},{1,5},{5... | collective-permute-start | bytes 786440 | tf_op jit(solution)/shard_map/ppermute | solution.py:17
  49.8 9.2 %collective-permute-start.14 = (bf16[1,352,256]{2,1,0:T(8,128)(2,1)S(1)}, bf16[1,352,256]{2,1,0:T(8,128)(2,1)S(1)}, u32[]{:S(2)}, u32[]{:S(2)}) collective-permute-start(bf16[1,352,256]{2,1,0:T(8,128)(2,1)S(1)} %add_convert_fusion.1), channel_id=1, source_target_pairs={{0,4},{4,0},{8,12},{12,8},{16,20},{20,16},{24,28},{28,24},{1,5},{5... | collective-permute-start | bytes 540680 | tf_op jit(solution)/shard_map/ppermute | solution.py:17
  53.8 7.9 %collective-permute-start.11 = (bf16[272,256]{1,0:T(8,128)(2,1)S(1)}, bf16[272,256]{1,0:T(8,128)(2,1)S(1)}, u32[]{:S(2)}, u32[]{:S(2)}) collective-permute-start(bf16[272,256]{1,0:T(8,128)(2,1)S(1)} %get-tuple-element.63), channel_id=1, source_target_pairs={{0,4},{4,0},{8,12},{12,8},{16,20},{20,16},{24,28},{28,24},{1,5},{5... | collective-permute-start | bytes 417800 | tf_op jit(solution)/shard_map/ppermute | solution.py:17
  55.0 5.0 %collective-permute-start.15 = (bf16[256,256]{1,0:T(8,128)(2,1)S(1)}, bf16[256,256]{1,0:T(8,128)(2,1)S(1)}, u32[]{:S(2)}, u32[]{:S(2)}) collective-permute-start(bf16[256,256]{1,0:T(8,128)(2,1)S(1)} %get-tuple-element.72), channel_id=1, source_target_pairs={{0,2},{1,3},{2,0},{3,1},{4,6},{5,7},{6,4},{7,5},{8,10},{9,11},{10,... | collective-permute-start | bytes 393224 | tf_op jit(solution)/shard_map/ppermute | solution.py:17
  56.5 15.1 %collective-permute-start.19 = (bf16[3,352,256]{2,1,0:T(8,128)(2,1)S(1)}, bf16[3,352,256]{2,1,0:T(8,128)(2,1)S(1)}, u32[]{:S(2)}, u32[]{:S(2)}) collective-permute-start(bf16[3,352,256]{2,1,0:T(8,128)(2,1)S(1)} %get-tuple-element.84), channel_id=1, source_target_pairs={{0,8},{4,12},{8,0},{12,4},{16,24},{20,28},{24,16},{28,20},{1,9},{5... | collective-permute-start | bytes 1622024 | tf_op jit(solution)/shard_map/ppermute | solution.py:17
  58.4 9.9 %collective-permute-start.17 = (bf16[2,352,256]{2,1,0:T(8,128)(2,1)S(1)}, bf16[2,352,256]{2,1,0:T(8,128)(2,1)S(1)}, u32[]{:S(2)}, u32[]{:S(2)}) collective-permute-start(bf16[2,352,256]{2,1,0:T(8,128)(2,1)S(1)} %add_convert_fusion), channel_id=1, source_target_pairs={{0,4},{4,0},{8,12},{12,8},{16,20},{20,16},{24,28},{28,24},{1,5},{5... | collective-permute-start | bytes 1081352 | tf_op jit(solution)/shard_map/ppermute | solution.py:17
  61.6 9.2 %copy-start = (f32[128]{0:T(128)S(1)}, f32[128]{0:T(128)}, u32[]{:S(2)}) copy-start(f32[128]{0:T(128)} %param.10) | copy-start | bytes 1540
  61.7 9.1 %collective-permute-start.18 = (bf16[272,256]{1,0:T(8,128)(2,1)S(1)}, bf16[272,256]{1,0:T(8,128)(2,1)S(1)}, u32[]{:S(2)}, u32[]{:S(2)}) collective-permute-start(bf16[272,256]{1,0:T(8,128)(2,1)S(1)} %get-tuple-element.78), channel_id=1, source_target_pairs={{0,16},{4,20},{8,24},{12,28},{16,0},{20,4},{24,8},{28,12},{1,17},{... | collective-permute-start | bytes 417800 | tf_op jit(solution)/shard_map/ppermute | solution.py:17

commit v11 on v10

--- a/solution.py
+++ b/solution.py
@@ -270,39 +270,45 @@
     )(units, x_all, s_all)
 
 
-def join_kernel(own, got_x, got_x_down, out_0, out_1, out_2, held, sems):
-    half = held.shape[1]
-    x_bit = lax.axis_index("wide") % 2
+def write_rows(values, outs, held, sems, first):
+    rows = pl.ds(pl.multiple_of(first, 16), held.shape[1])
     copies = []
-    for part, held_part in enumerate((own, held)):
-        first = (part * (1 - x_bit) + (1 - part) * x_bit) * half
-        rows = pl.ds(pl.multiple_of(first, 16), half)
-        for i, out in enumerate((out_0, out_1, out_2)):
-            if part:
-                got = got_x.at[i] if i < 2 else got_x_down.at[0]
-                held[i] = got[...].astype(jnp.float32)
-            place = sems.at[3 * part + i]
-            copies.append(pltpu.make_async_copy(held_part.at[i], out.at[rows, :], place))
-            copies[-1].start()
+    for i, out in enumerate(outs):
+        held[i] = values(i)
+        copies.append(pltpu.make_async_copy(held.at[i], out.at[rows, :], sems.at[i]))
+        copies[-1].start()
     for copy in copies:
         copy.wait()
 
 
-def join_grads(own, got_x, got_x_down):
-    _, half, width = own.shape
-    shape = jax.ShapeDtypeStruct((2 * half, width), jnp.float32)
-    return pl.pallas_call(
-        join_kernel,
-        out_shape=(shape,) * 3,
-        in_specs=[VMEM] * 3,
+def give_kernel(got, got_down, out_0, out_1, out_2, held, sems):
+    def values(i):
+        return (got[i] if i < 2 else got_down[0]).astype(jnp.float32)
+
+    first = (1 - lax.axis_index("wide") % 2) * held.shape[1]
+    write_rows(values, (out_0, out_1, out_2), held, sems, first)
+
+
+def keep_kernel(in_0, in_1, in_2, own, got, out_0, out_1, out_2, held, sems):
+    def values(i):
+        return own[i] + got[i].astype(jnp.float32)
+
+    first = lax.axis_index("wide") % 2 * held.shape[1]
+    write_rows(values, (out_0, out_1, out_2), held, sems, first)
+
+
+def write_half(kernel, shape, held, values):
+    held_in = [pltpu.with_memory_space_constraint(x, pltpu.HBM) for x in held]
+    return pl.pallas_call(
+        kernel,
+        out_shape=(jax.ShapeDtypeStruct((2 * shape[1], shape[2]), jnp.float32),) * 3,
+        in_specs=[HBM] * len(held) + [VMEM] * len(values),
         out_specs=[HBM] * 3,
-        scratch_shapes=[
-            pltpu.VMEM(own.shape, jnp.float32),
-            pltpu.SemaphoreType.DMA((6,)),
-        ],
+        scratch_shapes=[pltpu.VMEM(shape, jnp.float32), pltpu.SemaphoreType.DMA((3,))],
+        input_output_aliases={i: i for i in range(len(held))},
         compiler_params=PARAMS,
         cost_estimate=pl.CostEstimate(flops=1, bytes_accessed=0, transcendentals=0),
-    )(own, got_x, got_x_down)
+    )(*held_in, *values)
 
 
 def cross_kernel(kept, got, sent):
@@ -571,7 +577,8 @@
         )
         grad_x = (grad_x + got_d.astype(jnp.float32)).astype(jnp.bfloat16)
         got_x = partner(grad_x, "wide", 1)
-        held, got_x = lax.optimization_barrier((held, got_x))
+        given = write_half(give_kernel, grad_own.shape, (), (got_x, got_x_down))
+        held, _ = lax.optimization_barrier((held, given[0]))
         output, tokens_grad, prob_grad = finish(
             route_prob[None, :], held, [partner(to_z, "wide", 4)]
         )
@@ -604,9 +611,10 @@
         ffn = back[0].astype(jnp.bfloat16).astype(jnp.float32)
         output = (route_prob[:, None] * ffn).astype(jnp.bfloat16)
         tokens_grad = back[1].astype(jnp.bfloat16)
+        given = write_half(give_kernel, grad_own.shape, (), (got_x, got_x_down))
     got_z = partner(grad_z, "wide", 2)
-    gate_grad, up_grad, down_grad = join_grads(
-        grad_own + got_z.astype(jnp.float32), got_x, got_x_down
+    gate_grad, up_grad, down_grad = write_half(
+        keep_kernel, grad_own.shape, given, (grad_own, got_z)
     )
     return (output, tokens_grad, prob_grad, gate_grad.T, up_grad.T, down_grad.T)
 

time: 73.3 us -> 72.8 us (level)
  waiting for transfers between devices: 39 us -> 38 us
    ppermute x20, waiting for transfers between devices: 39 us -> 38 us  [partner(): lax.ppermute(x, axis, [(i, i ^ mask) for i in range(lax.axis_size(axis))])]
    pallas_call x1 -> x2, Pallas kernels: 1.4 us -> 2.05 us  [write_half(): pl.pallas_call(kernel, out_shape=(jax.ShapeDtypeStruct((2 * shape[1], sha...]
  transfers between devices with their start and end apart: 20 -> 20, of which waited for: 13 -> 13; matrix products, arithmetic and copies ran while one was open for 0% -> 0% of each run, Pallas kernels for 5% -> 6%
where the time goes in v11:
time: 72.8 us; the launch traced here: 72.7 us
  waiting for transfers between devices  38 us (52%)
  starting transfers between devices  24.2 us (33%)
  Pallas kernels  9.67 us (13%)
    ppermute x20, waiting for transfers between devices, partner(): lax.ppermute(x, axis, [(i, i ^ mask) for i in range(lax.axis_size(axis))])  38 us
    ppermute x20, starting transfers between devices, partner(): lax.ppermute(x, axis, [(i, i ^ mask) for i in range(lax.axis_size(axis))])  24.2 us
    pallas_call x1, Pallas kernels, outer(): pl.pallas_call(outer_kernel, out_shape=(jax.ShapeDtypeStruct((3, half, to...  2.74 us
    pallas_call x2, Pallas kernels, write_half(): pl.pallas_call(kernel, out_shape=(jax.ShapeDtypeStruct((2 * shape[1], sha...  2.05 us
    pallas_call x1, Pallas kernels, prologue(): pl.pallas_call(functools.partial(prologue_kernel, bool(token_args)), out_...  1.47 us
  transfers between devices with their start and end apart: 20, of which 13 were waited for; matrix products, arithmetic and copies ran while one was open for 0% of the time, Pallas kernels for 6%

profile of v11, /device:TPU:0, one launch (start us, length us, event | category | flops | bytes accessed | tf_op | source)
XLA Modules:
  0.0 72.7 jit_solution(2363023050004893693)
XLA Ops:
  0.6 1.5 %shard_map.118 = (bf16[3,352,256]{2,1,0:T(8,128)(2,1)S(1)}, bf16[3,352,256]{2,1,0:T(8,128)(2,1)S(1)}, bf16[2,128,1024]{2,1,0:T(8,128)(2,1)S(1)}, bf16[2,128,256]...) custom-call(bf16[704,256]{1,0:T(8,128)(2,1)} %bitcast.17, bf16[704,256]{1,0:T(8,128)(2,1)} %bitcast.18, ...), custom_call_target="tpu_custom_call" | custom-call | tf_op jit(solution)/shard_map/pallas_call | solution.py:103
  2.1 3.0 %collective-permute-start.6 = (bf16[3,352,256]{2,1,0:T(8,128)(2,1)S(1)}, bf16[3,352,256]{2,1,0:T(8,128)(2,1)S(1)}, u32[]{:S(2)}, u32[]{:S(2)}) collective-permute-start(bf16[3,352,256]{2,1,0:T(8,128)(2,1)S(1)} %get-tuple-element.54), channel_id=1, source_target_pairs={{0,4},{4,0},{8,12},{12,8},{16,20},{20,16},{24,28},{28,24},{1,5},{5... | collective-permute-start | bytes 1622024 | tf_op jit(solution)/shard_map/ppermute | solution.py:17
  5.1 1.6 %collective-permute-start.7 = (bf16[3,352,256]{2,1,0:T(8,128)(2,1)S(1)}, bf16[3,352,256]{2,1,0:T(8,128)(2,1)S(1)}, u32[]{:S(2)}, u32[]{:S(2)}) collective-permute-start(bf16[3,352,256]{2,1,0:T(8,128)(2,1)S(1)} %get-tuple-element.53.refs_5_), channel_id=1, source_target_pairs={{0,8},{4,12},{8,0},{12,4},{16,24},{20,28},{24,16},{28,20},{1,9},{5... | collective-permute-start | bytes 1622024 | tf_op jit(solution)/shard_map/ppermute | solution.py:17
  7.2 3.5 %collective-permute-start.2 = (bf16[2,128,256]{2,1,0:T(8,128)(2,1)S(1)}, bf16[2,128,256]{2,1,0:T(8,128)(2,1)S(1)}, u32[]{:S(2)}, u32[]{:S(2)}) collective-permute-start(bf16[2,128,256]{2,1,0:T(8,128)(2,1)S(1)} %get-tuple-element.52), channel_id=1, source_target_pairs={{0,20},{4,16},{8,28},{12,24},{16,4},{20,0},{24,12},{28,8},{1,21},{... | collective-permute-start | bytes 393224 | tf_op jit(solution)/shard_map/ppermute | solution.py:17
  11.1 11.9 %collective-permute-done = bf16[2,128,256]{2,1,0:T(8,128)(2,1)S(1)} collective-permute-done((bf16[2,128,256]{2,1,0:T(8,128)(2,1)S(1)}, bf16[2,128,256]{2,1,0:T(8,128)(2,1)S(1)}, u32[]{:S(2)}, u32[]{:S(2)}) %collective-permute-start) | collective-permute-done | bytes 131104 | tf_op jit(solution)/shard_map/ppermute | solution.py:17
  23.6 1.6 %collective-permute-start.4 = (bf16[3,2,128,256]{3,2,1,0:T(8,128)(2,1)S(1)}, bf16[3,2,128,256]{3,2,1,0:T(8,128)(2,1)S(1)}, u32[]{:S(2)}, u32[]{:S(2)}) collective-permute-start(bf16[3,2,128,256]{3,2,1,0:T(8,128)(2,1)S(1)} %pad_maximum_fusion.refs_1_), channel_id=1, source_target_pairs={{0,2},{1,3},{2,0},{3,1},{4,6},{5,7},{6,4},{7,5},{8,10},{9,11},{10,... | collective-permute-start | bytes 1179656 | tf_op jit(solution)/shard_map/ppermute | solution.py:17
  25.2 3.5 %collective-permute-start.8 = (bf16[3,352,256]{2,1,0:T(8,128)(2,1)S(1)}, bf16[3,352,256]{2,1,0:T(8,128)(2,1)S(1)}, u32[]{:S(2)}, u32[]{:S(2)}) collective-permute-start(bf16[3,352,256]{2,1,0:T(8,128)(2,1)S(1)} %collective-permute-done.6.refs_6_), channel_id=1, source_target_pairs={{0,8},{4,12},{8,0},{12,4},{16,24},{20,28},{24,16},{28,20},{1,9},{5... | collective-permute-start | bytes 1622024 | tf_op jit(solution)/shard_map/ppermute | solution.py:17
  28.7 4.7 %collective-permute-done.4.refs_3_ = bf16[3,2,128,256]{3,2,1,0:T(8,128)(2,1)S(1)} collective-permute-done((bf16[3,2,128,256]{3,2,1,0:T(8,128)(2,1)S(1)}, bf16[3,2,128,256]{3,2,1,0:T(8,128)(2,1)S(1)}, u32[]{:S(2)}, u32[]{:S(2)}) %collective-permute-start.4) | collective-permute-done | bytes 393248 | tf_op jit(solution)/shard_map/ppermute | solution.py:17
  33.4 1.7 %collective-permute-done.5.refs_4_ = bf16[3,2,128,256]{3,2,1,0:T(8,128)(2,1)S(1)} collective-permute-done((bf16[3,2,128,256]{3,2,1,0:T(8,128)(2,1)S(1)}, bf16[3,2,128,256]{3,2,1,0:T(8,128)(2,1)S(1)}, u32[]{:S(2)}, u32[]{:S(2)}) %collective-permute-start.5) | collective-permute-done | bytes 393248 | tf_op jit(solution)/shard_map/ppermute | solution.py:17
  35.2 1.3 %shard_map.119 = (bf16[512,1024]{1,0:T(8,128)(2,1)S(1)}, bf16[512,1024]{1,0:T(8,128)(2,1)S(1)}, bf16[3,352,768]{2,1,0:T(8,128)(2,1)S(1)}, f32[3,352,512]{2,1,0:T(8,128)S(1)}) custom-call(bf16[2,128,1024]{2,1,0:T(8,128)(2,1)S(1)} %get-tuple-element.50.refs_0_, bf16[3,2,128,256]{3,2,1,0:T(8,128)(2,1)S(1)} %pad_maximum_fusion.refs_1_, ...), custom_call_target="tpu_custom_call" | custom-call | flops 1 | bytes 1 | tf_op jit(solution)/shard_map/pallas_call | solution.py:152
  36.4 3.1 %collective-permute-done.8.last = bf16[3,352,256]{2,1,0:T(8,128)(2,1)S(1)} collective-permute-done((bf16[3,352,256]{2,1,0:T(8,128)(2,1)S(1)}, bf16[3,352,256]{2,1,0:T(8,128)(2,1)S(1)}, u32[]{:S(2)}, u32[]{:S(2)}) %collective-permute-start.8) | collective-permute-done | bytes 540704 | tf_op jit(solution)/shard_map/ppermute | solution.py:17
  39.5 2.7 %shard_map.120 = (bf16[3,352,512]{2,1,0:T(8,128)(2,1)S(1)}, f32[2,1040,256]{2,1,0:T(8,128)S(1)}, bf16[2,1040,256]{2,1,0:T(8,128)(2,1)S(1)}, bf16[2,352,256]{2,1,0:T(8,128)(2,1)S(1)}, bf16[1,352,256]{2,1,0:T(8,128)(2,1)S(1)}) custom-call(bf16[512,1024]{1,0:T(8,128)(2,1)S(1)} %get-tuple-element.57.x_all, bf16[512,1024]{1,0:T(8,128)(2,1)S(1)} %get-tuple-element.58.s_all, ...), custom_call_target="tpu_custom_call" | custom-call | flops 1476395008 | tf_op jit(solution)/shard_map/pallas_call | solution.py:229
  42.3 1.8 %collective-permute-start.13 = (bf16[1,352,256]{2,1,0:T(8,128)(2,1)S(1)}, bf16[1,352,256]{2,1,0:T(8,128)(2,1)S(1)}, u32[]{:S(2)}, u32[]{:S(2)}) collective-permute-start(bf16[1,352,256]{2,1,0:T(8,128)(2,1)S(1)} %get-tuple-element.72), channel_id=1, source_target_pairs={{0,8},{4,12},{8,0},{12,4},{16,24},{20,28},{24,16},{28,20},{1,9},{5... | collective-permute-start | bytes 540680 | tf_op jit(solution)/shard_map/ppermute | solution.py:17
  47.2 2.5 %collective-permute-done.13 = bf16[1,352,256]{2,1,0:T(8,128)(2,1)S(1)} collective-permute-done((bf16[1,352,256]{2,1,0:T(8,128)(2,1)S(1)}, bf16[1,352,256]{2,1,0:T(8,128)(2,1)S(1)}, u32[]{:S(2)}, u32[]{:S(2)}) %collective-permute-start.13) | collective-permute-done | bytes 180256 | tf_op jit(solution)/shard_map/ppermute | solution.py:17
  50.4 3.3 %collective-permute-done.10.from_y = bf16[528,256]{1,0:T(8,128)(2,1)S(1)} collective-permute-done((bf16[528,256]{1,0:T(8,128)(2,1)S(1)}, bf16[528,256]{1,0:T(8,128)(2,1)S(1)}, u32[]{:S(2)}, u32[]{:S(2)}) %collective-permute-start.10) | collective-permute-done | bytes 270368 | tf_op jit(solution)/shard_map/ppermute | solution.py:17
  55.0 1.6 %collective-permute-start.15 = (bf16[256,256]{1,0:T(8,128)(2,1)S(1)}, bf16[256,256]{1,0:T(8,128)(2,1)S(1)}, u32[]{:S(2)}, u32[]{:S(2)}) collective-permute-start(bf16[256,256]{1,0:T(8,128)(2,1)S(1)} %get-tuple-element.74), channel_id=1, source_target_pairs={{0,2},{1,3},{2,0},{3,1},{4,6},{5,7},{6,4},{7,5},{8,10},{9,11},{10,... | collective-permute-start | bytes 393224 | tf_op jit(solution)/shard_map/ppermute | solution.py:17
  56.5 1.7 %collective-permute-start.19 = (bf16[3,352,256]{2,1,0:T(8,128)(2,1)S(1)}, bf16[3,352,256]{2,1,0:T(8,128)(2,1)S(1)}, u32[]{:S(2)}, u32[]{:S(2)}) collective-permute-start(bf16[3,352,256]{2,1,0:T(8,128)(2,1)S(1)} %get-tuple-element.90), channel_id=1, source_target_pairs={{0,8},{4,12},{8,0},{12,4},{16,24},{20,28},{24,16},{28,20},{1,9},{5... | collective-permute-start | bytes 1622024 | tf_op jit(solution)/shard_map/ppermute | solution.py:17
  59.0 1.0 %collective-permute-done.15.from_y = bf16[256,256]{1,0:T(8,128)(2,1)S(1)} collective-permute-done((bf16[256,256]{1,0:T(8,128)(2,1)S(1)}, bf16[256,256]{1,0:T(8,128)(2,1)S(1)}, u32[]{:S(2)}, u32[]{:S(2)}) %collective-permute-start.15) | collective-permute-done | bytes 131104 | tf_op jit(solution)/shard_map/ppermute | solution.py:17
  60.0 1.7 %collective-permute-done.11.from_x = bf16[272,256]{1,0:T(8,128)(2,1)S(1)} collective-permute-done((bf16[272,256]{1,0:T(8,128)(2,1)S(1)}, bf16[272,256]{1,0:T(8,128)(2,1)S(1)}, u32[]{:S(2)}, u32[]{:S(2)}) %collective-permute-start.11) | collective-permute-done | bytes 139296 | tf_op jit(solution)/shard_map/ppermute | solution.py:17
  61.8 1.7 %collective-permute-start.18 = (bf16[272,256]{1,0:T(8,128)(2,1)S(1)}, bf16[272,256]{1,0:T(8,128)(2,1)S(1)}, u32[]{:S(2)}, u32[]{:S(2)}) collective-permute-start(bf16[272,256]{1,0:T(8,128)(2,1)S(1)} %get-tuple-element.82), channel_id=1, source_target_pairs={{0,16},{4,20},{8,24},{12,28},{16,0},{20,4},{24,8},{28,12},{1,17},{... | collective-permute-start | bytes 417800 | tf_op jit(solution)/shard_map/ppermute | solution.py:17
  63.5 4.8 %collective-permute-done.17.got = bf16[2,352,256]{2,1,0:T(8,128)(2,1)S(1)} collective-permute-done((bf16[2,352,256]{2,1,0:T(8,128)(2,1)S(1)}, bf16[2,352,256]{2,1,0:T(8,128)(2,1)S(1)}, u32[]{:S(2)}, u32[]{:S(2)}) %collective-permute-start.17) | collective-permute-done | bytes 360480 | tf_op jit(solution)/shard_map/ppermute | solution.py:17
  68.3 1.0 %shard_map.126 = (f32[704,256]{1,0:T(8,128)}, f32[704,256]{1,0:T(8,128)}, f32[704,256]{1,0:T(8,128)}) custom-call(bf16[2,352,256]{2,1,0:T(8,128)(2,1)S(1)} %collective-permute-done.17.got, bf16[1,352,256]{2,1,0:T(8,128)(2,1)S(1)} %collective-permute-done.14.got_down), custom_call_target="tpu_custom_call" | custom-call | flops 1 | tf_op jit(solution)/shard_map/pallas_call | solution.py:302
  69.3 1.5 %collective-permute-done.18.refs_0_ = bf16[272,256]{1,0:T(8,128)(2,1)S(1)} collective-permute-done((bf16[272,256]{1,0:T(8,128)(2,1)S(1)}, bf16[272,256]{1,0:T(8,128)(2,1)S(1)}, u32[]{:S(2)}, u32[]{:S(2)}) %collective-permute-start.18) | collective-permute-done | bytes 139296 | tf_op jit(solution)/shard_map/ppermute | solution.py:17
  71.7 1.0 %shard_map.128 = (f32[704,256]{1,0:T(8,128)}, f32[704,256]{1,0:T(8,128)}, f32[704,256]{1,0:T(8,128)}) custom-call(f32[704,256]{1,0:T(8,128)} %get-tuple-element.80.in_0, f32[704,256]{1,0:T(8,128)} %get-tuple-element.86.in_1, f32[704,256]{1,0:T(8,128)} %get-tuple-element.87.in_2, ...), custom_call_target="tpu_custom_call", output_to_operand_aliasing={{0}: (0, {}), {1}: (1, {}), {2}: (2, {})} | custom-call | flops 1 | tf_op jit(solution)/shard_map/pallas_call | solution.py:302
  (32 shorter events, 8.1 us)
Async XLA Ops:
  2.1 23.1 %collective-permute-start.6 = (bf16[3,352,256]{2,1,0:T(8,128)(2,1)S(1)}, bf16[3,352,256]{2,1,0:T(8,128)(2,1)S(1)}, u32[]{:S(2)}, u32[]{:S(2)}) collective-permute-start(bf16[3,352,256]{2,1,0:T(8,128)(2,1)S(1)} %get-tuple-element.54), channel_id=1, source_target_pairs={{0,4},{4,0},{8,12},{12,8},{16,20},{20,16},{24,28},{28,24},{1,5},{5... | collective-permute-start | bytes 1622024 | tf_op jit(solution)/shard_map/ppermute | solution.py:17
  5.1 20.1 %collective-permute-start.7 = (bf16[3,352,256]{2,1,0:T(8,128)(2,1)S(1)}, bf16[3,352,256]{2,1,0:T(8,128)(2,1)S(1)}, u32[]{:S(2)}, u32[]{:S(2)}) collective-permute-start(bf16[3,352,256]{2,1,0:T(8,128)(2,1)S(1)} %get-tuple-element.53.refs_5_), channel_id=1, source_target_pairs={{0,8},{4,12},{8,0},{12,4},{16,24},{20,28},{24,16},{28,20},{1,9},{5... | collective-permute-start | bytes 1622024 | tf_op jit(solution)/shard_map/ppermute | solution.py:17
  6.7 16.3 %collective-permute-start = (bf16[2,128,256]{2,1,0:T(8,128)(2,1)S(1)}, bf16[2,128,256]{2,1,0:T(8,128)(2,1)S(1)}, u32[]{:S(2)}, u32[]{:S(2)}) collective-permute-start(bf16[2,128,256]{2,1,0:T(8,128)(2,1)S(1)} %get-tuple-element.51), channel_id=1, source_target_pairs={{0,4},{4,0},{8,12},{12,8},{16,20},{20,16},{24,28},{28,24},{1,5},{5... | collective-permute-start | bytes 393224 | tf_op jit(solution)/shard_map/ppermute | solution.py:17
  7.2 15.8 %collective-permute-start.2 = (bf16[2,128,256]{2,1,0:T(8,128)(2,1)S(1)}, bf16[2,128,256]{2,1,0:T(8,128)(2,1)S(1)}, u32[]{:S(2)}, u32[]{:S(2)}) collective-permute-start(bf16[2,128,256]{2,1,0:T(8,128)(2,1)S(1)} %get-tuple-element.52), channel_id=1, source_target_pairs={{0,20},{4,16},{8,28},{12,24},{16,4},{20,0},{24,12},{28,8},{1,21},{... | collective-permute-start | bytes 393224 | tf_op jit(solution)/shard_map/ppermute | solution.py:17
  10.7 12.8 %collective-permute-start.1 = (bf16[2,128,256]{2,1,0:T(8,128)(2,1)S(1)}, bf16[2,128,256]{2,1,0:T(8,128)(2,1)S(1)}, u32[]{:S(2)}, u32[]{:S(2)}) collective-permute-start(bf16[2,128,256]{2,1,0:T(8,128)(2,1)S(1)} %get-tuple-element.52), channel_id=1, source_target_pairs={{0,16},{4,20},{8,24},{12,28},{16,0},{20,4},{24,8},{28,12},{1,17},{... | collective-permute-start | bytes 393224 | tf_op jit(solution)/shard_map/ppermute | solution.py:17
  23.6 9.8 %collective-permute-start.4 = (bf16[3,2,128,256]{3,2,1,0:T(8,128)(2,1)S(1)}, bf16[3,2,128,256]{3,2,1,0:T(8,128)(2,1)S(1)}, u32[]{:S(2)}, u32[]{:S(2)}) collective-permute-start(bf16[3,2,128,256]{3,2,1,0:T(8,128)(2,1)S(1)} %pad_maximum_fusion.refs_1_), channel_id=1, source_target_pairs={{0,2},{1,3},{2,0},{3,1},{4,6},{5,7},{6,4},{7,5},{8,10},{9,11},{10,... | collective-permute-start | bytes 1179656 | tf_op jit(solution)/shard_map/ppermute | solution.py:17
  25.2 14.3 %collective-permute-start.8 = (bf16[3,352,256]{2,1,0:T(8,128)(2,1)S(1)}, bf16[3,352,256]{2,1,0:T(8,128)(2,1)S(1)}, u32[]{:S(2)}, u32[]{:S(2)}) collective-permute-start(bf16[3,352,256]{2,1,0:T(8,128)(2,1)S(1)} %collective-permute-done.6.refs_6_), channel_id=1, source_target_pairs={{0,8},{4,12},{8,0},{12,4},{16,24},{20,28},{24,16},{28,20},{1,9},{5... | collective-permute-start | bytes 1622024 | tf_op jit(solution)/shard_map/ppermute | solution.py:17
  28.7 4.7 %collective-permute-start.3 = (bf16[3,2,128,256]{3,2,1,0:T(8,128)(2,1)S(1)}, bf16[3,2,128,256]{3,2,1,0:T(8,128)(2,1)S(1)}, u32[]{:S(2)}, u32[]{:S(2)}) collective-permute-start(bf16[3,2,128,256]{3,2,1,0:T(8,128)(2,1)S(1)} %pad_maximum_fusion.refs_1_), channel_id=1, source_target_pairs={{0,1},{1,0},{2,3},{3,2},{4,5},{5,4},{6,7},{7,6},{8,9},{9,8},{10,11... | collective-permute-start | bytes 1179656 | tf_op jit(solution)/shard_map/ppermute | solution.py:17
  33.4 1.7 %collective-permute-start.5 = (bf16[3,2,128,256]{3,2,1,0:T(8,128)(2,1)S(1)}, bf16[3,2,128,256]{3,2,1,0:T(8,128)(2,1)S(1)}, u32[]{:S(2)}, u32[]{:S(2)}) collective-permute-start(bf16[3,2,128,256]{3,2,1,0:T(8,128)(2,1)S(1)} %collective-permute-done.4.refs_3_), channel_id=1, source_target_pairs={{0,1},{1,0},{2,3},{3,2},{4,5},{5,4},{6,7},{7,6},{8,9},{9,8},{10,11... | collective-permute-start | bytes 1179656 | tf_op jit(solution)/shard_map/ppermute | solution.py:17
  42.3 2.7 %collective-permute-start.9 = (bf16[2,1040,256]{2,1,0:T(8,128)(2,1)S(1)}, bf16[2,1040,256]{2,1,0:T(8,128)(2,1)S(1)}, u32[]{:S(2)}, u32[]{:S(2)}) collective-permute-start(bf16[2,1040,256]{2,1,0:T(8,128)(2,1)S(1)} %get-tuple-element.62), channel_id=1, source_target_pairs={{0,1},{1,0},{2,3},{3,2},{4,5},{5,4},{6,7},{7,6},{8,9},{9,8},{10,11... | collective-permute-start | bytes 3194888 | tf_op jit(solution)/shard_map/ppermute | solution.py:17
  42.3 7.4 %collective-permute-start.13 = (bf16[1,352,256]{2,1,0:T(8,128)(2,1)S(1)}, bf16[1,352,256]{2,1,0:T(8,128)(2,1)S(1)}, u32[]{:S(2)}, u32[]{:S(2)}) collective-permute-start(bf16[1,352,256]{2,1,0:T(8,128)(2,1)S(1)} %get-tuple-element.72), channel_id=1, source_target_pairs={{0,8},{4,12},{8,0},{12,4},{16,24},{20,28},{24,16},{28,20},{1,9},{5... | collective-permute-start | bytes 540680 | tf_op jit(solution)/shard_map/ppermute | solution.py:17
  44.1 14.1 %collective-permute-start.16 = (bf16[2,352,256]{2,1,0:T(8,128)(2,1)S(1)}, bf16[2,352,256]{2,1,0:T(8,128)(2,1)S(1)}, u32[]{:S(2)}, u32[]{:S(2)}) collective-permute-start(bf16[2,352,256]{2,1,0:T(8,128)(2,1)S(1)} %get-tuple-element.78), channel_id=1, source_target_pairs={{0,8},{4,12},{8,0},{12,4},{16,24},{20,28},{24,16},{28,20},{1,9},{5... | collective-permute-start | bytes 1081352 | tf_op jit(solution)/shard_map/ppermute | solution.py:17
  45.1 8.6 %collective-permute-start.10 = (bf16[528,256]{1,0:T(8,128)(2,1)S(1)}, bf16[528,256]{1,0:T(8,128)(2,1)S(1)}, u32[]{:S(2)}, u32[]{:S(2)}) collective-permute-start(bf16[528,256]{1,0:T(8,128)(2,1)S(1)} %get-tuple-element.63), channel_id=1, source_target_pairs={{0,2},{1,3},{2,0},{3,1},{4,6},{5,7},{6,4},{7,5},{8,10},{9,11},{10,... | collective-permute-start | bytes 811016 | tf_op jit(solution)/shard_map/ppermute | solution.py:17
  45.7 9.2 %collective-permute-start.12 = (bf16[2,256,256]{2,1,0:T(8,128)(2,1)S(1)}, bf16[2,256,256]{2,1,0:T(8,128)(2,1)S(1)}, u32[]{:S(2)}, u32[]{:S(2)}) collective-permute-start(bf16[2,256,256]{2,1,0:T(8,128)(2,1)S(1)} %get-tuple-element.66), channel_id=1, source_target_pairs={{0,4},{4,0},{8,12},{12,8},{16,20},{20,16},{24,28},{28,24},{1,5},{5... | collective-permute-start | bytes 786440 | tf_op jit(solution)/shard_map/ppermute | solution.py:17
  49.8 9.2 %collective-permute-start.14 = (bf16[1,352,256]{2,1,0:T(8,128)(2,1)S(1)}, bf16[1,352,256]{2,1,0:T(8,128)(2,1)S(1)}, u32[]{:S(2)}, u32[]{:S(2)}) collective-permute-start(bf16[1,352,256]{2,1,0:T(8,128)(2,1)S(1)} %add_convert_fusion.1), channel_id=1, source_target_pairs={{0,4},{4,0},{8,12},{12,8},{16,20},{20,16},{24,28},{28,24},{1,5},{5... | collective-permute-start | bytes 540680 | tf_op jit(solution)/shard_map/ppermute | solution.py:17
  53.8 7.9 %collective-permute-start.11 = (bf16[272,256]{1,0:T(8,128)(2,1)S(1)}, bf16[272,256]{1,0:T(8,128)(2,1)S(1)}, u32[]{:S(2)}, u32[]{:S(2)}) collective-permute-start(bf16[272,256]{1,0:T(8,128)(2,1)S(1)} %get-tuple-element.65), channel_id=1, source_target_pairs={{0,4},{4,0},{8,12},{12,8},{16,20},{20,16},{24,28},{28,24},{1,5},{5... | collective-permute-start | bytes 417800 | tf_op jit(solution)/shard_map/ppermute | solution.py:17
  55.0 5.0 %collective-permute-start.15 = (bf16[256,256]{1,0:T(8,128)(2,1)S(1)}, bf16[256,256]{1,0:T(8,128)(2,1)S(1)}, u32[]{:S(2)}, u32[]{:S(2)}) collective-permute-start(bf16[256,256]{1,0:T(8,128)(2,1)S(1)} %get-tuple-element.74), channel_id=1, source_target_pairs={{0,2},{1,3},{2,0},{3,1},{4,6},{5,7},{6,4},{7,5},{8,10},{9,11},{10,... | collective-permute-start | bytes 393224 | tf_op jit(solution)/shard_map/ppermute | solution.py:17
  56.5 15.1 %collective-permute-start.19 = (bf16[3,352,256]{2,1,0:T(8,128)(2,1)S(1)}, bf16[3,352,256]{2,1,0:T(8,128)(2,1)S(1)}, u32[]{:S(2)}, u32[]{:S(2)}) collective-permute-start(bf16[3,352,256]{2,1,0:T(8,128)(2,1)S(1)} %get-tuple-element.90), channel_id=1, source_target_pairs={{0,8},{4,12},{8,0},{12,4},{16,24},{20,28},{24,16},{28,20},{1,9},{5... | collective-permute-start | bytes 1622024 | tf_op jit(solution)/shard_map/ppermute | solution.py:17
  58.4 9.9 %collective-permute-start.17 = (bf16[2,352,256]{2,1,0:T(8,128)(2,1)S(1)}, bf16[2,352,256]{2,1,0:T(8,128)(2,1)S(1)}, u32[]{:S(2)}, u32[]{:S(2)}) collective-permute-start(bf16[2,352,256]{2,1,0:T(8,128)(2,1)S(1)} %add_convert_fusion), channel_id=1, source_target_pairs={{0,4},{4,0},{8,12},{12,8},{16,20},{20,16},{24,28},{28,24},{1,5},{5... | collective-permute-start | bytes 1081352 | tf_op jit(solution)/shard_map/ppermute | solution.py:17
  61.7 9.2 %copy-start = (f32[128]{0:T(128)S(1)}, f32[128]{0:T(128)}, u32[]{:S(2)}) copy-start(f32[128]{0:T(128)} %param.10) | copy-start | bytes 1540
  61.8 9.1 %collective-permute-start.18 = (bf16[272,256]{1,0:T(8,128)(2,1)S(1)}, bf16[272,256]{1,0:T(8,128)(2,1)S(1)}, u32[]{:S(2)}, u32[]{:S(2)}) collective-permute-start(bf16[272,256]{1,0:T(8,128)(2,1)S(1)} %get-tuple-element.82), channel_id=1, source_target_pairs={{0,16},{4,20},{8,24},{12,28},{16,0},{20,4},{24,8},{28,12},{1,17},{... | collective-permute-start | bytes 417800 | tf_op jit(solution)/shard_map/ppermute | solution.py:17

commit v12 on v11

--- a/solution.py
+++ b/solution.py
@@ -108,6 +108,22 @@
         scratch_shapes=scratch + [pltpu.SemaphoreType.DMA((10,))],
         compiler_params=PARAMS,
     )(*[pltpu.with_memory_space_constraint(x, pltpu.HBM) for x in (*weights, *token_args)])
+
+
+def stack_kernel(*refs):
+    for i, ref in enumerate(refs[:-1]):
+        refs[-1][i] = ref[...]
+
+
+def stack_parts(parts):
+    return pl.pallas_call(
+        stack_kernel,
+        out_shape=jax.ShapeDtypeStruct((len(parts), *parts[0].shape), parts[0].dtype),
+        in_specs=[VMEM] * len(parts),
+        out_specs=VMEM,
+        compiler_params=PARAMS,
+        cost_estimate=pl.CostEstimate(flops=2 * 10**9, bytes_accessed=0, transcendentals=0),
+    )(*parts)
 
 
 def gather_kernel(has_own, *refs):
@@ -521,7 +537,7 @@
         keep, give, own, same, other = prologue(
             weights, (tokens, cotangent, expert_ids.T, route_prob[None, :]), width
         )
-        mine = jnp.stack(
+        mine = stack_parts(
             [partner(part, "wide", mask) for mask, part in zip(masks, (same, other, other))]
         )
     else:

time: 72.8 us -> 74.1 us (1.018); the launches traced: 72.7 us -> 72.7 us
  transfers between devices with their start and end apart: 20 -> 20, of which waited for: 13 -> 16; matrix products, arithmetic and copies ran while one was open for 0% -> 0% of each run, Pallas kernels for 6% -> 6%
where the time goes in v12:
time: 74.1 us; the launch traced here: 72.7 us
  waiting for transfers between devices  38 us (51%)
  starting transfers between devices  24.2 us (33%)
  Pallas kernels  9.72 us (13%)
    ppermute x20, waiting for transfers between devices, partner(): lax.ppermute(x, axis, [(i, i ^ mask) for i in range(lax.axis_size(axis))])  38 us
    ppermute x20, starting transfers between devices, partner(): lax.ppermute(x, axis, [(i, i ^ mask) for i in range(lax.axis_size(axis))])  24.2 us
    pallas_call x1, Pallas kernels, outer(): pl.pallas_call(outer_kernel, out_shape=(jax.ShapeDtypeStruct((3, half, to...  2.75 us
    pallas_call x2, Pallas kernels, write_half(): pl.pallas_call(kernel, out_shape=(jax.ShapeDtypeStruct((2 * shape[1], sha...  2.05 us
  transfers between devices with their start and end apart: 20, of which 16 were waited for; matrix products, arithmetic and copies ran while one was open for 0% of the time, Pallas kernels for 6%

profile of v12, /device:TPU:0, one launch (start us, length us, event | category | flops | bytes accessed | tf_op | source)
XLA Modules:
  0.0 72.7 jit_solution(2344938986676940659)
XLA Ops:
  0.6 1.5 %shard_map.118 = (bf16[3,352,256]{2,1,0:T(8,128)(2,1)S(1)}, bf16[3,352,256]{2,1,0:T(8,128)(2,1)S(1)}, bf16[2,128,1024]{2,1,0:T(8,128)(2,1)S(1)}, bf16[2,128,256]...) custom-call(bf16[704,256]{1,0:T(8,128)(2,1)} %bitcast.14, bf16[704,256]{1,0:T(8,128)(2,1)} %bitcast.15, ...), custom_call_target="tpu_custom_call" | custom-call | tf_op jit(solution)/shard_map/pallas_call | solution.py:103
  2.1 3.0 %collective-permute-start = (bf16[2,128,256]{2,1,0:T(8,128)(2,1)S(1)}, bf16[2,128,256]{2,1,0:T(8,128)(2,1)S(1)}, u32[]{:S(2)}, u32[]{:S(2)}) collective-permute-start(bf16[2,128,256]{2,1,0:T(8,128)(2,1)S(1)} %get-tuple-element.51), channel_id=1, source_target_pairs={{0,4},{4,0},{8,12},{12,8},{16,20},{20,16},{24,28},{28,24},{1,5},{5... | collective-permute-start | bytes 393224 | tf_op jit(solution)/shard_map/ppermute | solution.py:17
  5.1 2.6 %collective-permute-start.2 = (bf16[2,128,256]{2,1,0:T(8,128)(2,1)S(1)}, bf16[2,128,256]{2,1,0:T(8,128)(2,1)S(1)}, u32[]{:S(2)}, u32[]{:S(2)}) collective-permute-start(bf16[2,128,256]{2,1,0:T(8,128)(2,1)S(1)} %get-tuple-element.52), channel_id=1, source_target_pairs={{0,20},{4,16},{8,28},{12,24},{16,4},{20,0},{24,12},{28,8},{1,21},{... | collective-permute-start | bytes 393224 | tf_op jit(solution)/shard_map/ppermute | solution.py:17
  7.7 1.8 %collective-permute-start.6 = (bf16[3,352,256]{2,1,0:T(8,128)(2,1)S(1)}, bf16[3,352,256]{2,1,0:T(8,128)(2,1)S(1)}, u32[]{:S(2)}, u32[]{:S(2)}) collective-permute-start(bf16[3,352,256]{2,1,0:T(8,128)(2,1)S(1)} %get-tuple-element.54), channel_id=1, source_target_pairs={{0,4},{4,0},{8,12},{12,8},{16,20},{20,16},{24,28},{28,24},{1,5},{5... | collective-permute-start | bytes 1622024 | tf_op jit(solution)/shard_map/ppermute | solution.py:17
  9.5 1.6 %collective-permute-start.7 = (bf16[3,352,256]{2,1,0:T(8,128)(2,1)S(1)}, bf16[3,352,256]{2,1,0:T(8,128)(2,1)S(1)}, u32[]{:S(2)}, u32[]{:S(2)}) collective-permute-start(bf16[3,352,256]{2,1,0:T(8,128)(2,1)S(1)} %get-tuple-element.53.refs_5_), channel_id=1, source_target_pairs={{0,8},{4,12},{8,0},{12,4},{16,24},{20,28},{24,16},{28,20},{1,9},{5... | collective-permute-start | bytes 1622024 | tf_op jit(solution)/shard_map/ppermute | solution.py:17
  11.1 7.7 %collective-permute-done.2.refs_2_ = bf16[2,128,256]{2,1,0:T(8,128)(2,1)S(1)} collective-permute-done((bf16[2,128,256]{2,1,0:T(8,128)(2,1)S(1)}, bf16[2,128,256]{2,1,0:T(8,128)(2,1)S(1)}, u32[]{:S(2)}, u32[]{:S(2)}) %collective-permute-start.2) | collective-permute-done | bytes 131104 | tf_op jit(solution)/shard_map/ppermute | solution.py:17
  19.5 1.6 %collective-permute-start.4 = (bf16[3,2,128,256]{3,2,1,0:T(8,128)(2,1)S(1)}, bf16[3,2,128,256]{3,2,1,0:T(8,128)(2,1)S(1)}, u32[]{:S(2)}, u32[]{:S(2)}) collective-permute-start(bf16[3,2,128,256]{3,2,1,0:T(8,128)(2,1)S(1)} %shard_map.119.refs_1_), channel_id=1, source_target_pairs={{0,2},{1,3},{2,0},{3,1},{4,6},{5,7},{6,4},{7,5},{8,10},{9,11},{10,... | collective-permute-start | bytes 1179656 | tf_op jit(solution)/shard_map/ppermute | solution.py:17
  21.1 2.4 %collective-permute-done.6.refs_6_ = bf16[3,352,256]{2,1,0:T(8,128)(2,1)S(1)} collective-permute-done((bf16[3,352,256]{2,1,0:T(8,128)(2,1)S(1)}, bf16[3,352,256]{2,1,0:T(8,128)(2,1)S(1)}, u32[]{:S(2)}, u32[]{:S(2)}) %collective-permute-start.6) | collective-permute-done | bytes 540704 | tf_op jit(solution)/shard_map/ppermute | solution.py:17
  23.5 3.4 %collective-permute-done.7.refs_7_ = bf16[3,352,256]{2,1,0:T(8,128)(2,1)S(1)} collective-permute-done((bf16[3,352,256]{2,1,0:T(8,128)(2,1)S(1)}, bf16[3,352,256]{2,1,0:T(8,128)(2,1)S(1)}, u32[]{:S(2)}, u32[]{:S(2)}) %collective-permute-start.7) | collective-permute-done | bytes 540704 | tf_op jit(solution)/shard_map/ppermute | solution.py:17
  27.1 2.4 %collective-permute-done.4.refs_3_ = bf16[3,2,128,256]{3,2,1,0:T(8,128)(2,1)S(1)} collective-permute-done((bf16[3,2,128,256]{3,2,1,0:T(8,128)(2,1)S(1)}, bf16[3,2,128,256]{3,2,1,0:T(8,128)(2,1)S(1)}, u32[]{:S(2)}, u32[]{:S(2)}) %collective-permute-start.4) | collective-permute-done | bytes 393248 | tf_op jit(solution)/shard_map/ppermute | solution.py:17
  29.5 1.7 %collective-permute-done.5.refs_4_ = bf16[3,2,128,256]{3,2,1,0:T(8,128)(2,1)S(1)} collective-permute-done((bf16[3,2,128,256]{3,2,1,0:T(8,128)(2,1)S(1)}, bf16[3,2,128,256]{3,2,1,0:T(8,128)(2,1)S(1)}, u32[]{:S(2)}, u32[]{:S(2)}) %collective-permute-start.5) | collective-permute-done | bytes 393248 | tf_op jit(solution)/shard_map/ppermute | solution.py:17
  31.2 1.3 %shard_map.120 = (bf16[512,1024]{1,0:T(8,128)(2,1)S(1)}, bf16[512,1024]{1,0:T(8,128)(2,1)S(1)}, bf16[3,352,768]{2,1,0:T(8,128)(2,1)S(1)}, f32[3,352,512]{2,1,0:T(8,128)S(1)}) custom-call(bf16[2,128,1024]{2,1,0:T(8,128)(2,1)S(1)} %get-tuple-element.50.refs_0_, bf16[3,2,128,256]{3,2,1,0:T(8,128)(2,1)S(1)} %shard_map.119.refs_1_, ...), custom_call_target="tpu_custom_call" | custom-call | flops 1 | bytes 1 | tf_op jit(solution)/shard_map/pallas_call | solution.py:168
  32.5 6.4 %collective-permute-done.8.last = bf16[3,352,256]{2,1,0:T(8,128)(2,1)S(1)} collective-permute-done((bf16[3,352,256]{2,1,0:T(8,128)(2,1)S(1)}, bf16[3,352,256]{2,1,0:T(8,128)(2,1)S(1)}, u32[]{:S(2)}, u32[]{:S(2)}) %collective-permute-start.8) | collective-permute-done | bytes 540704 | tf_op jit(solution)/shard_map/ppermute | solution.py:17
  38.9 2.8 %shard_map.121 = (bf16[3,352,512]{2,1,0:T(8,128)(2,1)S(1)}, f32[2,1040,256]{2,1,0:T(8,128)S(1)}, bf16[2,1040,256]{2,1,0:T(8,128)(2,1)S(1)}, bf16[2,352,256]{2,1,0:T(8,128)(2,1)S(1)}, bf16[1,352,256]{2,1,0:T(8,128)(2,1)S(1)}) custom-call(bf16[512,1024]{1,0:T(8,128)(2,1)S(1)} %get-tuple-element.57.x_all, bf16[512,1024]{1,0:T(8,128)(2,1)S(1)} %get-tuple-element.58.s_all, ...), custom_call_target="tpu_custom_call" | custom-call | flops 1476395008 | tf_op jit(solution)/shard_map/pallas_call | solution.py:245
  44.5 1.6 %collective-permute-start.10 = (bf16[528,256]{1,0:T(8,128)(2,1)S(1)}, bf16[528,256]{1,0:T(8,128)(2,1)S(1)}, u32[]{:S(2)}, u32[]{:S(2)}) collective-permute-start(bf16[528,256]{1,0:T(8,128)(2,1)S(1)} %get-tuple-element.63), channel_id=1, source_target_pairs={{0,2},{1,3},{2,0},{3,1},{4,6},{5,7},{6,4},{7,5},{8,10},{9,11},{10,... | collective-permute-start | bytes 811016 | tf_op jit(solution)/shard_map/ppermute | solution.py:17
  47.8 1.3 %collective-permute-done.13 = bf16[1,352,256]{2,1,0:T(8,128)(2,1)S(1)} collective-permute-done((bf16[1,352,256]{2,1,0:T(8,128)(2,1)S(1)}, bf16[1,352,256]{2,1,0:T(8,128)(2,1)S(1)}, u32[]{:S(2)}, u32[]{:S(2)}) %collective-permute-start.13) | collective-permute-done | bytes 180256 | tf_op jit(solution)/shard_map/ppermute | solution.py:17
  50.1 3.0 %collective-permute-done.10.from_y = bf16[528,256]{1,0:T(8,128)(2,1)S(1)} collective-permute-done((bf16[528,256]{1,0:T(8,128)(2,1)S(1)}, bf16[528,256]{1,0:T(8,128)(2,1)S(1)}, u32[]{:S(2)}, u32[]{:S(2)}) %collective-permute-start.10) | collective-permute-done | bytes 270368 | tf_op jit(solution)/shard_map/ppermute | solution.py:17
  54.1 1.2 %collective-permute-done.12.from_x = bf16[2,256,256]{2,1,0:T(8,128)(2,1)S(1)} collective-permute-done((bf16[2,256,256]{2,1,0:T(8,128)(2,1)S(1)}, bf16[2,256,256]{2,1,0:T(8,128)(2,1)S(1)}, u32[]{:S(2)}, u32[]{:S(2)}) %collective-permute-start.12) | collective-permute-done | bytes 262176 | tf_op jit(solution)/shard_map/ppermute | solution.py:17
  55.9 1.5 %collective-permute-start.19 = (bf16[3,352,256]{2,1,0:T(8,128)(2,1)S(1)}, bf16[3,352,256]{2,1,0:T(8,128)(2,1)S(1)}, u32[]{:S(2)}, u32[]{:S(2)}) collective-permute-start(bf16[3,352,256]{2,1,0:T(8,128)(2,1)S(1)} %get-tuple-element.90), channel_id=1, source_target_pairs={{0,8},{4,12},{8,0},{12,4},{16,24},{20,28},{24,16},{28,20},{1,9},{5... | collective-permute-start | bytes 1622024 | tf_op jit(solution)/shard_map/ppermute | solution.py:17
  59.1 1.3 %collective-permute-done.15.from_y = bf16[256,256]{1,0:T(8,128)(2,1)S(1)} collective-permute-done((bf16[256,256]{1,0:T(8,128)(2,1)S(1)}, bf16[256,256]{1,0:T(8,128)(2,1)S(1)}, u32[]{:S(2)}, u32[]{:S(2)}) %collective-permute-start.15) | collective-permute-done | bytes 131104 | tf_op jit(solution)/shard_map/ppermute | solution.py:17
  60.4 1.7 %collective-permute-done.11.from_x = bf16[272,256]{1,0:T(8,128)(2,1)S(1)} collective-permute-done((bf16[272,256]{1,0:T(8,128)(2,1)S(1)}, bf16[272,256]{1,0:T(8,128)(2,1)S(1)}, u32[]{:S(2)}, u32[]{:S(2)}) %collective-permute-start.11) | collective-permute-done | bytes 139296 | tf_op jit(solution)/shard_map/ppermute | solution.py:17
  62.2 3.9 %collective-permute-start.18 = (bf16[272,256]{1,0:T(8,128)(2,1)S(1)}, bf16[272,256]{1,0:T(8,128)(2,1)S(1)}, u32[]{:S(2)}, u32[]{:S(2)}) collective-permute-start(bf16[272,256]{1,0:T(8,128)(2,1)S(1)} %get-tuple-element.82), channel_id=1, source_target_pairs={{0,16},{4,20},{8,24},{12,28},{16,0},{20,4},{24,8},{28,12},{1,17},{... | collective-permute-start | bytes 417800 | tf_op jit(solution)/shard_map/ppermute | solution.py:17
  66.0 2.6 %collective-permute-done.17.got = bf16[2,352,256]{2,1,0:T(8,128)(2,1)S(1)} collective-permute-done((bf16[2,352,256]{2,1,0:T(8,128)(2,1)S(1)}, bf16[2,352,256]{2,1,0:T(8,128)(2,1)S(1)}, u32[]{:S(2)}, u32[]{:S(2)}) %collective-permute-start.17) | collective-permute-done | bytes 360480 | tf_op jit(solution)/shard_map/ppermute | solution.py:17
  69.7 1.2 %collective-permute-done.18.refs_0_ = bf16[272,256]{1,0:T(8,128)(2,1)S(1)} collective-permute-done((bf16[272,256]{1,0:T(8,128)(2,1)S(1)}, bf16[272,256]{1,0:T(8,128)(2,1)S(1)}, u32[]{:S(2)}, u32[]{:S(2)}) %collective-permute-start.18) | collective-permute-done | bytes 139296 | tf_op jit(solution)/shard_map/ppermute | solution.py:17
  (32 shorter events, 12.8 us)
Async XLA Ops:
  2.1 9.0 %collective-permute-start = (bf16[2,128,256]{2,1,0:T(8,128)(2,1)S(1)}, bf16[2,128,256]{2,1,0:T(8,128)(2,1)S(1)}, u32[]{:S(2)}, u32[]{:S(2)}) collective-permute-start(bf16[2,128,256]{2,1,0:T(8,128)(2,1)S(1)} %get-tuple-element.51), channel_id=1, source_target_pairs={{0,4},{4,0},{8,12},{12,8},{16,20},{20,16},{24,28},{28,24},{1,5},{5... | collective-permute-start | bytes 393224 | tf_op jit(solution)/shard_map/ppermute | solution.py:17
  5.1 13.6 %collective-permute-start.2 = (bf16[2,128,256]{2,1,0:T(8,128)(2,1)S(1)}, bf16[2,128,256]{2,1,0:T(8,128)(2,1)S(1)}, u32[]{:S(2)}, u32[]{:S(2)}) collective-permute-start(bf16[2,128,256]{2,1,0:T(8,128)(2,1)S(1)} %get-tuple-element.52), channel_id=1, source_target_pairs={{0,20},{4,16},{8,28},{12,24},{16,4},{20,0},{24,12},{28,8},{1,21},{... | collective-permute-start | bytes 393224 | tf_op jit(solution)/shard_map/ppermute | solution.py:17
  7.7 11.8 %collective-permute-start.1 = (bf16[2,128,256]{2,1,0:T(8,128)(2,1)S(1)}, bf16[2,128,256]{2,1,0:T(8,128)(2,1)S(1)}, u32[]{:S(2)}, u32[]{:S(2)}) collective-permute-start(bf16[2,128,256]{2,1,0:T(8,128)(2,1)S(1)} %get-tuple-element.52), channel_id=1, source_target_pairs={{0,16},{4,20},{8,24},{12,28},{16,0},{20,4},{24,8},{28,12},{1,17},{... | collective-permute-start | bytes 393224 | tf_op jit(solution)/shard_map/ppermute | solution.py:17
  7.7 15.7 %collective-permute-start.6 = (bf16[3,352,256]{2,1,0:T(8,128)(2,1)S(1)}, bf16[3,352,256]{2,1,0:T(8,128)(2,1)S(1)}, u32[]{:S(2)}, u32[]{:S(2)}) collective-permute-start(bf16[3,352,256]{2,1,0:T(8,128)(2,1)S(1)} %get-tuple-element.54), channel_id=1, source_target_pairs={{0,4},{4,0},{8,12},{12,8},{16,20},{20,16},{24,28},{28,24},{1,5},{5... | collective-permute-start | bytes 1622024 | tf_op jit(solution)/shard_map/ppermute | solution.py:17
  9.5 17.4 %collective-permute-start.7 = (bf16[3,352,256]{2,1,0:T(8,128)(2,1)S(1)}, bf16[3,352,256]{2,1,0:T(8,128)(2,1)S(1)}, u32[]{:S(2)}, u32[]{:S(2)}) collective-permute-start(bf16[3,352,256]{2,1,0:T(8,128)(2,1)S(1)} %get-tuple-element.53.refs_5_), channel_id=1, source_target_pairs={{0,8},{4,12},{8,0},{12,4},{16,24},{20,28},{24,16},{28,20},{1,9},{5... | collective-permute-start | bytes 1622024 | tf_op jit(solution)/shard_map/ppermute | solution.py:17
  19.5 10.0 %collective-permute-start.4 = (bf16[3,2,128,256]{3,2,1,0:T(8,128)(2,1)S(1)}, bf16[3,2,128,256]{3,2,1,0:T(8,128)(2,1)S(1)}, u32[]{:S(2)}, u32[]{:S(2)}) collective-permute-start(bf16[3,2,128,256]{3,2,1,0:T(8,128)(2,1)S(1)} %shard_map.119.refs_1_), channel_id=1, source_target_pairs={{0,2},{1,3},{2,0},{3,1},{4,6},{5,7},{6,4},{7,5},{8,10},{9,11},{10,... | collective-permute-start | bytes 1179656 | tf_op jit(solution)/shard_map/ppermute | solution.py:17
  26.9 12.0 %collective-permute-start.8 = (bf16[3,352,256]{2,1,0:T(8,128)(2,1)S(1)}, bf16[3,352,256]{2,1,0:T(8,128)(2,1)S(1)}, u32[]{:S(2)}, u32[]{:S(2)}) collective-permute-start(bf16[3,352,256]{2,1,0:T(8,128)(2,1)S(1)} %collective-permute-done.6.refs_6_), channel_id=1, source_target_pairs={{0,8},{4,12},{8,0},{12,4},{16,24},{20,28},{24,16},{28,20},{1,9},{5... | collective-permute-start | bytes 1622024 | tf_op jit(solution)/shard_map/ppermute | solution.py:17
  27.1 2.4 %collective-permute-start.3 = (bf16[3,2,128,256]{3,2,1,0:T(8,128)(2,1)S(1)}, bf16[3,2,128,256]{3,2,1,0:T(8,128)(2,1)S(1)}, u32[]{:S(2)}, u32[]{:S(2)}) collective-permute-start(bf16[3,2,128,256]{3,2,1,0:T(8,128)(2,1)S(1)} %shard_map.119.refs_1_), channel_id=1, source_target_pairs={{0,1},{1,0},{2,3},{3,2},{4,5},{5,4},{6,7},{7,6},{8,9},{9,8},{10,11... | collective-permute-start | bytes 1179656 | tf_op jit(solution)/shard_map/ppermute | solution.py:17
  29.5 1.7 %collective-permute-start.5 = (bf16[3,2,128,256]{3,2,1,0:T(8,128)(2,1)S(1)}, bf16[3,2,128,256]{3,2,1,0:T(8,128)(2,1)S(1)}, u32[]{:S(2)}, u32[]{:S(2)}) collective-permute-start(bf16[3,2,128,256]{3,2,1,0:T(8,128)(2,1)S(1)} %collective-permute-done.4.refs_3_), channel_id=1, source_target_pairs={{0,1},{1,0},{2,3},{3,2},{4,5},{5,4},{6,7},{7,6},{8,9},{9,8},{10,11... | collective-permute-start | bytes 1179656 | tf_op jit(solution)/shard_map/ppermute | solution.py:17
  41.6 2.7 %collective-permute-start.9 = (bf16[2,1040,256]{2,1,0:T(8,128)(2,1)S(1)}, bf16[2,1040,256]{2,1,0:T(8,128)(2,1)S(1)}, u32[]{:S(2)}, u32[]{:S(2)}) collective-permute-start(bf16[2,1040,256]{2,1,0:T(8,128)(2,1)S(1)} %get-tuple-element.62), channel_id=1, source_target_pairs={{0,1},{1,0},{2,3},{3,2},{4,5},{5,4},{6,7},{7,6},{8,9},{9,8},{10,11... | collective-permute-start | bytes 3194888 | tf_op jit(solution)/shard_map/ppermute | solution.py:17
  41.7 7.4 %collective-permute-start.13 = (bf16[1,352,256]{2,1,0:T(8,128)(2,1)S(1)}, bf16[1,352,256]{2,1,0:T(8,128)(2,1)S(1)}, u32[]{:S(2)}, u32[]{:S(2)}) collective-permute-start(bf16[1,352,256]{2,1,0:T(8,128)(2,1)S(1)} %get-tuple-element.72), channel_id=1, source_target_pairs={{0,8},{4,12},{8,0},{12,4},{16,24},{20,28},{24,16},{28,20},{1,9},{5... | collective-permute-start | bytes 540680 | tf_op jit(solution)/shard_map/ppermute | solution.py:17
  42.8 14.6 %collective-permute-start.16 = (bf16[2,352,256]{2,1,0:T(8,128)(2,1)S(1)}, bf16[2,352,256]{2,1,0:T(8,128)(2,1)S(1)}, u32[]{:S(2)}, u32[]{:S(2)}) collective-permute-start(bf16[2,352,256]{2,1,0:T(8,128)(2,1)S(1)} %get-tuple-element.78), channel_id=1, source_target_pairs={{0,8},{4,12},{8,0},{12,4},{16,24},{20,28},{24,16},{28,20},{1,9},{5... | collective-permute-start | bytes 1081352 | tf_op jit(solution)/shard_map/ppermute | solution.py:17
  44.5 8.6 %collective-permute-start.10 = (bf16[528,256]{1,0:T(8,128)(2,1)S(1)}, bf16[528,256]{1,0:T(8,128)(2,1)S(1)}, u32[]{:S(2)}, u32[]{:S(2)}) collective-permute-start(bf16[528,256]{1,0:T(8,128)(2,1)S(1)} %get-tuple-element.63), channel_id=1, source_target_pairs={{0,2},{1,3},{2,0},{3,1},{4,6},{5,7},{6,4},{7,5},{8,10},{9,11},{10,... | collective-permute-start | bytes 811016 | tf_op jit(solution)/shard_map/ppermute | solution.py:17
  46.1 9.2 %collective-permute-start.12 = (bf16[2,256,256]{2,1,0:T(8,128)(2,1)S(1)}, bf16[2,256,256]{2,1,0:T(8,128)(2,1)S(1)}, u32[]{:S(2)}, u32[]{:S(2)}) collective-permute-start(bf16[2,256,256]{2,1,0:T(8,128)(2,1)S(1)} %get-tuple-element.66), channel_id=1, source_target_pairs={{0,4},{4,0},{8,12},{12,8},{16,20},{20,16},{24,28},{28,24},{1,5},{5... | collective-permute-start | bytes 786440 | tf_op jit(solution)/shard_map/ppermute | solution.py:17
  49.2 9.9 %collective-permute-start.14 = (bf16[1,352,256]{2,1,0:T(8,128)(2,1)S(1)}, bf16[1,352,256]{2,1,0:T(8,128)(2,1)S(1)}, u32[]{:S(2)}, u32[]{:S(2)}) collective-permute-start(bf16[1,352,256]{2,1,0:T(8,128)(2,1)S(1)} %add_convert_fusion.1), channel_id=1, source_target_pairs={{0,4},{4,0},{8,12},{12,8},{16,20},{20,16},{24,28},{28,24},{1,5},{5... | collective-permute-start | bytes 540680 | tf_op jit(solution)/shard_map/ppermute | solution.py:17
  53.1 9.0 %collective-permute-start.11 = (bf16[272,256]{1,0:T(8,128)(2,1)S(1)}, bf16[272,256]{1,0:T(8,128)(2,1)S(1)}, u32[]{:S(2)}, u32[]{:S(2)}) collective-permute-start(bf16[272,256]{1,0:T(8,128)(2,1)S(1)} %get-tuple-element.65), channel_id=1, source_target_pairs={{0,4},{4,0},{8,12},{12,8},{16,20},{20,16},{24,28},{28,24},{1,5},{5... | collective-permute-start | bytes 417800 | tf_op jit(solution)/shard_map/ppermute | solution.py:17
  55.3 5.0 %collective-permute-start.15 = (bf16[256,256]{1,0:T(8,128)(2,1)S(1)}, bf16[256,256]{1,0:T(8,128)(2,1)S(1)}, u32[]{:S(2)}, u32[]{:S(2)}) collective-permute-start(bf16[256,256]{1,0:T(8,128)(2,1)S(1)} %get-tuple-element.74), channel_id=1, source_target_pairs={{0,2},{1,3},{2,0},{3,1},{4,6},{5,7},{6,4},{7,5},{8,10},{9,11},{10,... | collective-permute-start | bytes 393224 | tf_op jit(solution)/shard_map/ppermute | solution.py:17
  55.9 15.8 %collective-permute-start.19 = (bf16[3,352,256]{2,1,0:T(8,128)(2,1)S(1)}, bf16[3,352,256]{2,1,0:T(8,128)(2,1)S(1)}, u32[]{:S(2)}, u32[]{:S(2)}) collective-permute-start(bf16[3,352,256]{2,1,0:T(8,128)(2,1)S(1)} %get-tuple-element.90), channel_id=1, source_target_pairs={{0,8},{4,12},{8,0},{12,4},{16,24},{20,28},{24,16},{28,20},{1,9},{5... | collective-permute-start | bytes 1622024 | tf_op jit(solution)/shard_map/ppermute | solution.py:17
  57.5 11.2 %collective-permute-start.17 = (bf16[2,352,256]{2,1,0:T(8,128)(2,1)S(1)}, bf16[2,352,256]{2,1,0:T(8,128)(2,1)S(1)}, u32[]{:S(2)}, u32[]{:S(2)}) collective-permute-start(bf16[2,352,256]{2,1,0:T(8,128)(2,1)S(1)} %add_convert_fusion), channel_id=1, source_target_pairs={{0,4},{4,0},{8,12},{12,8},{16,20},{20,16},{24,28},{28,24},{1,5},{5... | collective-permute-start | bytes 1081352 | tf_op jit(solution)/shard_map/ppermute | solution.py:17
  62.1 8.8 %copy-start = (f32[128]{0:T(128)S(1)}, f32[128]{0:T(128)}, u32[]{:S(2)}) copy-start(f32[128]{0:T(128)} %param.10) | copy-start | bytes 1540
  62.2 8.7 %collective-permute-start.18 = (bf16[272,256]{1,0:T(8,128)(2,1)S(1)}, bf16[272,256]{1,0:T(8,128)(2,1)S(1)}, u32[]{:S(2)}, u32[]{:S(2)}) collective-permute-start(bf16[272,256]{1,0:T(8,128)(2,1)S(1)} %get-tuple-element.82), channel_id=1, source_target_pairs={{0,16},{4,20},{8,24},{12,28},{16,0},{20,4},{24,8},{28,12},{1,17},{... | collective-permute-start | bytes 417800 | tf_op jit(solution)/shard_map/ppermute | solution.py:17

commit v13 on v12

--- a/solution.py
+++ b/solution.py
@@ -122,7 +122,7 @@
         in_specs=[VMEM] * len(parts),
         out_specs=VMEM,
         compiler_params=PARAMS,
-        cost_estimate=pl.CostEstimate(flops=2 * 10**9, bytes_accessed=0, transcendentals=0),
+        cost_estimate=pl.CostEstimate(flops=1 * 10**9, bytes_accessed=0, transcendentals=0),
     )(*parts)
 
 
@@ -564,11 +564,9 @@
             routed, "wide", split_axis=0, concat_axis=0, axis_index_groups=groups, tiled=True
         )
 
-    from_x, from_z = lax.optimization_barrier(
-        (partner(give, "wide", 1), partner(keep, "wide", 2))
-    )
+    from_x, from_z = partner(give, "wide", 1), partner(keep, "wide", 2)
     from_d = partner(from_x, "wide", 2)
-    across = partner(mine, "narrow", 2)
+    across, from_z = lax.optimization_barrier((partner(mine, "narrow", 2), from_z))
     pieces = (mine, partner(mine, "narrow", 1), across, partner(across, "narrow", 1))
     x_all, s_all, w_part, part = gather_parts(own, pieces, (keep, from_x, from_z))
     units, kept, sent, grad_d, grad_d_down = outer(x_all, s_all, w_part, part, from_d)

time: 74.1 us -> 73.4 us (level)
  transfers between devices with their start and end apart: 20 -> 20, of which waited for: 16 -> 14; matrix products, arithmetic and copies ran while one was open for 0% -> 0% of each run, Pallas kernels for 6% -> 6%
where the time goes in v13:
time: 73.4 us; the launch traced here: 72 us
  waiting for transfers between devices  37.4 us (51%)
  starting transfers between devices  24.1 us (33%)
  Pallas kernels  9.72 us (13%)
    ppermute x20, waiting for transfers between devices, partner(): lax.ppermute(x, axis, [(i, i ^ mask) for i in range(lax.axis_size(axis))])  37.4 us
    ppermute x20, starting transfers between devices, partner(): lax.ppermute(x, axis, [(i, i ^ mask) for i in range(lax.axis_size(axis))])  24.1 us
    pallas_call x1, Pallas kernels, outer(): pl.pallas_call(outer_kernel, out_shape=(jax.ShapeDtypeStruct((3, half, to...  2.75 us
    pallas_call x2, Pallas kernels, write_half(): pl.pallas_call(kernel, out_shape=(jax.ShapeDtypeStruct((2 * shape[1], sha...  2.05 us
    pallas_call x1, Pallas kernels, prologue(): pl.pallas_call(functools.partial(prologue_kernel, bool(token_args)), out_...  1.47 us
  transfers between devices with their start and end apart: 20, of which 14 were waited for; matrix products, arithmetic and copies ran while one was open for 0% of the time, Pallas kernels for 6%

profile of v13, /device:TPU:0, one launch (start us, length us, event | category | flops | bytes accessed | tf_op | source)
XLA Modules:
  0.0 72.0 jit_solution(817734723672324802)
XLA Ops:
  0.6 1.5 %shard_map.118 = (bf16[3,352,256]{2,1,0:T(8,128)(2,1)S(1)}, bf16[3,352,256]{2,1,0:T(8,128)(2,1)S(1)}, bf16[2,128,1024]{2,1,0:T(8,128)(2,1)S(1)}, bf16[2,128,256]...) custom-call(bf16[704,256]{1,0:T(8,128)(2,1)} %bitcast.14, bf16[704,256]{1,0:T(8,128)(2,1)} %bitcast.15, ...), custom_call_target="tpu_custom_call" | custom-call | tf_op jit(solution)/shard_map/pallas_call | solution.py:103
  2.1 3.0 %collective-permute-start.7 = (bf16[3,352,256]{2,1,0:T(8,128)(2,1)S(1)}, bf16[3,352,256]{2,1,0:T(8,128)(2,1)S(1)}, u32[]{:S(2)}, u32[]{:S(2)}) collective-permute-start(bf16[3,352,256]{2,1,0:T(8,128)(2,1)S(1)} %get-tuple-element.55), channel_id=1, source_target_pairs={{0,4},{4,0},{8,12},{12,8},{16,20},{20,16},{24,28},{28,24},{1,5},{5... | collective-permute-start | bytes 1622024 | tf_op jit(solution)/shard_map/ppermute | solution.py:17
  5.2 4.0 %collective-permute-start.2 = (bf16[2,128,256]{2,1,0:T(8,128)(2,1)S(1)}, bf16[2,128,256]{2,1,0:T(8,128)(2,1)S(1)}, u32[]{:S(2)}, u32[]{:S(2)}) collective-permute-start(bf16[2,128,256]{2,1,0:T(8,128)(2,1)S(1)} %get-tuple-element.52), channel_id=1, source_target_pairs={{0,20},{4,16},{8,28},{12,24},{16,4},{20,0},{24,12},{28,8},{1,21},{... | collective-permute-start | bytes 393224 | tf_op jit(solution)/shard_map/ppermute | solution.py:17
  9.5 1.6 %collective-permute-start.5 = (bf16[3,352,256]{2,1,0:T(8,128)(2,1)S(1)}, bf16[3,352,256]{2,1,0:T(8,128)(2,1)S(1)}, u32[]{:S(2)}, u32[]{:S(2)}) collective-permute-start(bf16[3,352,256]{2,1,0:T(8,128)(2,1)S(1)} %get-tuple-element.53.refs_5_), channel_id=1, source_target_pairs={{0,8},{4,12},{8,0},{12,4},{16,24},{20,28},{24,16},{28,20},{1,9},{5... | collective-permute-start | bytes 1622024 | tf_op jit(solution)/shard_map/ppermute | solution.py:17
  11.1 11.9 %collective-permute-done.refs_0_ = bf16[2,128,256]{2,1,0:T(8,128)(2,1)S(1)} collective-permute-done((bf16[2,128,256]{2,1,0:T(8,128)(2,1)S(1)}, bf16[2,128,256]{2,1,0:T(8,128)(2,1)S(1)}, u32[]{:S(2)}, u32[]{:S(2)}) %collective-permute-start) | collective-permute-done | bytes 131104 | tf_op jit(solution)/shard_map/ppermute | solution.py:17
  23.1 1.8 %collective-permute-start.4 = (bf16[3,2,128,256]{3,2,1,0:T(8,128)(2,1)S(1)}, bf16[3,2,128,256]{3,2,1,0:T(8,128)(2,1)S(1)}, u32[]{:S(2)}, u32[]{:S(2)}) collective-permute-start(bf16[3,2,128,256]{3,2,1,0:T(8,128)(2,1)S(1)} %shard_map.119.refs_1_), channel_id=1, source_target_pairs={{0,2},{1,3},{2,0},{3,1},{4,6},{5,7},{6,4},{7,5},{8,10},{9,11},{10,... | collective-permute-start | bytes 1179656 | tf_op jit(solution)/shard_map/ppermute | solution.py:17
  24.9 1.6 %collective-permute-start.8 = (bf16[3,352,256]{2,1,0:T(8,128)(2,1)S(1)}, bf16[3,352,256]{2,1,0:T(8,128)(2,1)S(1)}, u32[]{:S(2)}, u32[]{:S(2)}) collective-permute-start(bf16[3,352,256]{2,1,0:T(8,128)(2,1)S(1)} %collective-permute-done.7.refs_6_), channel_id=1, source_target_pairs={{0,8},{4,12},{8,0},{12,4},{16,24},{20,28},{24,16},{28,20},{1,9},{5... | collective-permute-start | bytes 1622024 | tf_op jit(solution)/shard_map/ppermute | solution.py:17
  26.5 6.9 %collective-permute-done.4.refs_3_ = bf16[3,2,128,256]{3,2,1,0:T(8,128)(2,1)S(1)} collective-permute-done((bf16[3,2,128,256]{3,2,1,0:T(8,128)(2,1)S(1)}, bf16[3,2,128,256]{3,2,1,0:T(8,128)(2,1)S(1)}, u32[]{:S(2)}, u32[]{:S(2)}) %collective-permute-start.4) | collective-permute-done | bytes 393248 | tf_op jit(solution)/shard_map/ppermute | solution.py:17
  33.4 1.7 %collective-permute-done.6.refs_4_ = bf16[3,2,128,256]{3,2,1,0:T(8,128)(2,1)S(1)} collective-permute-done((bf16[3,2,128,256]{3,2,1,0:T(8,128)(2,1)S(1)}, bf16[3,2,128,256]{3,2,1,0:T(8,128)(2,1)S(1)}, u32[]{:S(2)}, u32[]{:S(2)}) %collective-permute-start.6) | collective-permute-done | bytes 393248 | tf_op jit(solution)/shard_map/ppermute | solution.py:17
  35.1 1.3 %shard_map.120 = (bf16[512,1024]{1,0:T(8,128)(2,1)S(1)}, bf16[512,1024]{1,0:T(8,128)(2,1)S(1)}, bf16[3,352,768]{2,1,0:T(8,128)(2,1)S(1)}, f32[3,352,512]{2,1,0:T(8,128)S(1)}) custom-call(bf16[2,128,1024]{2,1,0:T(8,128)(2,1)S(1)} %get-tuple-element.50.refs_0_, bf16[3,2,128,256]{3,2,1,0:T(8,128)(2,1)S(1)} %shard_map.119.refs_1_, ...), custom_call_target="tpu_custom_call" | custom-call | flops 1 | bytes 1 | tf_op jit(solution)/shard_map/pallas_call | solution.py:168
  36.4 2.1 %collective-permute-done.8.last = bf16[3,352,256]{2,1,0:T(8,128)(2,1)S(1)} collective-permute-done((bf16[3,352,256]{2,1,0:T(8,128)(2,1)S(1)}, bf16[3,352,256]{2,1,0:T(8,128)(2,1)S(1)}, u32[]{:S(2)}, u32[]{:S(2)}) %collective-permute-start.8) | collective-permute-done | bytes 540704 | tf_op jit(solution)/shard_map/ppermute | solution.py:17
  38.5 2.8 %shard_map.121 = (bf16[3,352,512]{2,1,0:T(8,128)(2,1)S(1)}, f32[2,1040,256]{2,1,0:T(8,128)S(1)}, bf16[2,1040,256]{2,1,0:T(8,128)(2,1)S(1)}, bf16[2,352,256]{2,1,0:T(8,128)(2,1)S(1)}, bf16[1,352,256]{2,1,0:T(8,128)(2,1)S(1)}) custom-call(bf16[512,1024]{1,0:T(8,128)(2,1)S(1)} %get-tuple-element.57.x_all, bf16[512,1024]{1,0:T(8,128)(2,1)S(1)} %get-tuple-element.58.s_all, ...), custom_call_target="tpu_custom_call" | custom-call | flops 1476395008 | tf_op jit(solution)/shard_map/pallas_call | solution.py:245
  41.3 1.4 %collective-permute-start.13 = (bf16[1,352,256]{2,1,0:T(8,128)(2,1)S(1)}, bf16[1,352,256]{2,1,0:T(8,128)(2,1)S(1)}, u32[]{:S(2)}, u32[]{:S(2)}) collective-permute-start(bf16[1,352,256]{2,1,0:T(8,128)(2,1)S(1)} %get-tuple-element.72), channel_id=1, source_target_pairs={{0,8},{4,12},{8,0},{12,4},{16,24},{20,28},{24,16},{28,20},{1,9},{5... | collective-permute-start | bytes 540680 | tf_op jit(solution)/shard_map/ppermute | solution.py:17
  44.1 1.6 %collective-permute-start.10 = (bf16[528,256]{1,0:T(8,128)(2,1)S(1)}, bf16[528,256]{1,0:T(8,128)(2,1)S(1)}, u32[]{:S(2)}, u32[]{:S(2)}) collective-permute-start(bf16[528,256]{1,0:T(8,128)(2,1)S(1)} %get-tuple-element.63), channel_id=1, source_target_pairs={{0,2},{1,3},{2,0},{3,1},{4,6},{5,7},{6,4},{7,5},{8,10},{9,11},{10,... | collective-permute-start | bytes 811016 | tf_op jit(solution)/shard_map/ppermute | solution.py:17
  47.2 1.5 %collective-permute-done.13 = bf16[1,352,256]{2,1,0:T(8,128)(2,1)S(1)} collective-permute-done((bf16[1,352,256]{2,1,0:T(8,128)(2,1)S(1)}, bf16[1,352,256]{2,1,0:T(8,128)(2,1)S(1)}, u32[]{:S(2)}, u32[]{:S(2)}) %collective-permute-start.13) | collective-permute-done | bytes 180256 | tf_op jit(solution)/shard_map/ppermute | solution.py:17
  49.6 3.1 %collective-permute-done.10.from_y = bf16[528,256]{1,0:T(8,128)(2,1)S(1)} collective-permute-done((bf16[528,256]{1,0:T(8,128)(2,1)S(1)}, bf16[528,256]{1,0:T(8,128)(2,1)S(1)}, u32[]{:S(2)}, u32[]{:S(2)}) %collective-permute-start.10) | collective-permute-done | bytes 270368 | tf_op jit(solution)/shard_map/ppermute | solution.py:17
  53.6 1.3 %collective-permute-done.12.from_x = bf16[2,256,256]{2,1,0:T(8,128)(2,1)S(1)} collective-permute-done((bf16[2,256,256]{2,1,0:T(8,128)(2,1)S(1)}, bf16[2,256,256]{2,1,0:T(8,128)(2,1)S(1)}, u32[]{:S(2)}, u32[]{:S(2)}) %collective-permute-start.12) | collective-permute-done | bytes 262176 | tf_op jit(solution)/shard_map/ppermute | solution.py:17
  55.5 1.4 %collective-permute-start.19 = (bf16[3,352,256]{2,1,0:T(8,128)(2,1)S(1)}, bf16[3,352,256]{2,1,0:T(8,128)(2,1)S(1)}, u32[]{:S(2)}, u32[]{:S(2)}) collective-permute-start(bf16[3,352,256]{2,1,0:T(8,128)(2,1)S(1)} %get-tuple-element.90), channel_id=1, source_target_pairs={{0,8},{4,12},{8,0},{12,4},{16,24},{20,28},{24,16},{28,20},{1,9},{5... | collective-permute-start | bytes 1622024 | tf_op jit(solution)/shard_map/ppermute | solution.py:17
  57.0 1.1 %collective-permute-start.17 = (bf16[2,352,256]{2,1,0:T(8,128)(2,1)S(1)}, bf16[2,352,256]{2,1,0:T(8,128)(2,1)S(1)}, u32[]{:S(2)}, u32[]{:S(2)}) collective-permute-start(bf16[2,352,256]{2,1,0:T(8,128)(2,1)S(1)} %add_convert_fusion), channel_id=1, source_target_pairs={{0,4},{4,0},{8,12},{12,8},{16,20},{20,16},{24,28},{28,24},{1,5},{5... | collective-permute-start | bytes 1081352 | tf_op jit(solution)/shard_map/ppermute | solution.py:17
  58.7 1.3 %collective-permute-done.15.from_y = bf16[256,256]{1,0:T(8,128)(2,1)S(1)} collective-permute-done((bf16[256,256]{1,0:T(8,128)(2,1)S(1)}, bf16[256,256]{1,0:T(8,128)(2,1)S(1)}, u32[]{:S(2)}, u32[]{:S(2)}) %collective-permute-start.15) | collective-permute-done | bytes 131104 | tf_op jit(solution)/shard_map/ppermute | solution.py:17
  60.0 1.7 %collective-permute-done.11.from_x = bf16[272,256]{1,0:T(8,128)(2,1)S(1)} collective-permute-done((bf16[272,256]{1,0:T(8,128)(2,1)S(1)}, bf16[272,256]{1,0:T(8,128)(2,1)S(1)}, u32[]{:S(2)}, u32[]{:S(2)}) %collective-permute-start.11) | collective-permute-done | bytes 139296 | tf_op jit(solution)/shard_map/ppermute | solution.py:17
  61.8 2.8 %collective-permute-start.18 = (bf16[272,256]{1,0:T(8,128)(2,1)S(1)}, bf16[272,256]{1,0:T(8,128)(2,1)S(1)}, u32[]{:S(2)}, u32[]{:S(2)}) collective-permute-start(bf16[272,256]{1,0:T(8,128)(2,1)S(1)} %get-tuple-element.82), channel_id=1, source_target_pairs={{0,16},{4,20},{8,24},{12,28},{16,0},{20,4},{24,8},{28,12},{1,17},{... | collective-permute-start | bytes 417800 | tf_op jit(solution)/shard_map/ppermute | solution.py:17
  64.6 3.8 %collective-permute-done.17.got = bf16[2,352,256]{2,1,0:T(8,128)(2,1)S(1)} collective-permute-done((bf16[2,352,256]{2,1,0:T(8,128)(2,1)S(1)}, bf16[2,352,256]{2,1,0:T(8,128)(2,1)S(1)}, u32[]{:S(2)}, u32[]{:S(2)}) %collective-permute-start.17) | collective-permute-done | bytes 360480 | tf_op jit(solution)/shard_map/ppermute | solution.py:17
  71.0 1.0 %shard_map.129 = (f32[704,256]{1,0:T(8,128)}, f32[704,256]{1,0:T(8,128)}, f32[704,256]{1,0:T(8,128)}) custom-call(f32[704,256]{1,0:T(8,128)} %get-tuple-element.80.in_0, f32[704,256]{1,0:T(8,128)} %get-tuple-element.86.in_1, f32[704,256]{1,0:T(8,128)} %get-tuple-element.87.in_2, ...), custom_call_target="tpu_custom_call", output_to_operand_aliasing={{0}: (0, {}), {1}: (1, {}), {2}: (2, {})} | custom-call | flops 1 | tf_op jit(solution)/shard_map/pallas_call | solution.py:318
  (32 shorter events, 9.3 us)
Async XLA Ops:
  2.1 22.8 %collective-permute-start.7 = (bf16[3,352,256]{2,1,0:T(8,128)(2,1)S(1)}, bf16[3,352,256]{2,1,0:T(8,128)(2,1)S(1)}, u32[]{:S(2)}, u32[]{:S(2)}) collective-permute-start(bf16[3,352,256]{2,1,0:T(8,128)(2,1)S(1)} %get-tuple-element.55), channel_id=1, source_target_pairs={{0,4},{4,0},{8,12},{12,8},{16,20},{20,16},{24,28},{28,24},{1,5},{5... | collective-permute-start | bytes 1622024 | tf_op jit(solution)/shard_map/ppermute | solution.py:17
  5.1 17.9 %collective-permute-start = (bf16[2,128,256]{2,1,0:T(8,128)(2,1)S(1)}, bf16[2,128,256]{2,1,0:T(8,128)(2,1)S(1)}, u32[]{:S(2)}, u32[]{:S(2)}) collective-permute-start(bf16[2,128,256]{2,1,0:T(8,128)(2,1)S(1)} %get-tuple-element.51), channel_id=1, source_target_pairs={{0,4},{4,0},{8,12},{12,8},{16,20},{20,16},{24,28},{28,24},{1,5},{5... | collective-permute-start | bytes 393224 | tf_op jit(solution)/shard_map/ppermute | solution.py:17
  5.2 17.8 %collective-permute-start.2 = (bf16[2,128,256]{2,1,0:T(8,128)(2,1)S(1)}, bf16[2,128,256]{2,1,0:T(8,128)(2,1)S(1)}, u32[]{:S(2)}, u32[]{:S(2)}) collective-permute-start(bf16[2,128,256]{2,1,0:T(8,128)(2,1)S(1)} %get-tuple-element.52), channel_id=1, source_target_pairs={{0,20},{4,16},{8,28},{12,24},{16,4},{20,0},{24,12},{28,8},{1,21},{... | collective-permute-start | bytes 393224 | tf_op jit(solution)/shard_map/ppermute | solution.py:17
  9.2 13.8 %collective-permute-start.1 = (bf16[2,128,256]{2,1,0:T(8,128)(2,1)S(1)}, bf16[2,128,256]{2,1,0:T(8,128)(2,1)S(1)}, u32[]{:S(2)}, u32[]{:S(2)}) collective-permute-start(bf16[2,128,256]{2,1,0:T(8,128)(2,1)S(1)} %get-tuple-element.52), channel_id=1, source_target_pairs={{0,16},{4,20},{8,24},{12,28},{16,0},{20,4},{24,8},{28,12},{1,17},{... | collective-permute-start | bytes 393224 | tf_op jit(solution)/shard_map/ppermute | solution.py:17
  9.5 23.9 %collective-permute-start.5 = (bf16[3,352,256]{2,1,0:T(8,128)(2,1)S(1)}, bf16[3,352,256]{2,1,0:T(8,128)(2,1)S(1)}, u32[]{:S(2)}, u32[]{:S(2)}) collective-permute-start(bf16[3,352,256]{2,1,0:T(8,128)(2,1)S(1)} %get-tuple-element.53.refs_5_), channel_id=1, source_target_pairs={{0,8},{4,12},{8,0},{12,4},{16,24},{20,28},{24,16},{28,20},{1,9},{5... | collective-permute-start | bytes 1622024 | tf_op jit(solution)/shard_map/ppermute | solution.py:17
  23.1 10.4 %collective-permute-start.4 = (bf16[3,2,128,256]{3,2,1,0:T(8,128)(2,1)S(1)}, bf16[3,2,128,256]{3,2,1,0:T(8,128)(2,1)S(1)}, u32[]{:S(2)}, u32[]{:S(2)}) collective-permute-start(bf16[3,2,128,256]{3,2,1,0:T(8,128)(2,1)S(1)} %shard_map.119.refs_1_), channel_id=1, source_target_pairs={{0,2},{1,3},{2,0},{3,1},{4,6},{5,7},{6,4},{7,5},{8,10},{9,11},{10,... | collective-permute-start | bytes 1179656 | tf_op jit(solution)/shard_map/ppermute | solution.py:17
  24.9 13.6 %collective-permute-start.8 = (bf16[3,352,256]{2,1,0:T(8,128)(2,1)S(1)}, bf16[3,352,256]{2,1,0:T(8,128)(2,1)S(1)}, u32[]{:S(2)}, u32[]{:S(2)}) collective-permute-start(bf16[3,352,256]{2,1,0:T(8,128)(2,1)S(1)} %collective-permute-done.7.refs_6_), channel_id=1, source_target_pairs={{0,8},{4,12},{8,0},{12,4},{16,24},{20,28},{24,16},{28,20},{1,9},{5... | collective-permute-start | bytes 1622024 | tf_op jit(solution)/shard_map/ppermute | solution.py:17
  26.5 7.0 %collective-permute-start.3 = (bf16[3,2,128,256]{3,2,1,0:T(8,128)(2,1)S(1)}, bf16[3,2,128,256]{3,2,1,0:T(8,128)(2,1)S(1)}, u32[]{:S(2)}, u32[]{:S(2)}) collective-permute-start(bf16[3,2,128,256]{3,2,1,0:T(8,128)(2,1)S(1)} %shard_map.119.refs_1_), channel_id=1, source_target_pairs={{0,1},{1,0},{2,3},{3,2},{4,5},{5,4},{6,7},{7,6},{8,9},{9,8},{10,11... | collective-permute-start | bytes 1179656 | tf_op jit(solution)/shard_map/ppermute | solution.py:17
  33.4 1.7 %collective-permute-start.6 = (bf16[3,2,128,256]{3,2,1,0:T(8,128)(2,1)S(1)}, bf16[3,2,128,256]{3,2,1,0:T(8,128)(2,1)S(1)}, u32[]{:S(2)}, u32[]{:S(2)}) collective-permute-start(bf16[3,2,128,256]{3,2,1,0:T(8,128)(2,1)S(1)} %collective-permute-done.4.refs_3_), channel_id=1, source_target_pairs={{0,1},{1,0},{2,3},{3,2},{4,5},{5,4},{6,7},{7,6},{8,9},{9,8},{10,11... | collective-permute-start | bytes 1179656 | tf_op jit(solution)/shard_map/ppermute | solution.py:17
  41.3 2.7 %collective-permute-start.9 = (bf16[2,1040,256]{2,1,0:T(8,128)(2,1)S(1)}, bf16[2,1040,256]{2,1,0:T(8,128)(2,1)S(1)}, u32[]{:S(2)}, u32[]{:S(2)}) collective-permute-start(bf16[2,1040,256]{2,1,0:T(8,128)(2,1)S(1)} %get-tuple-element.62), channel_id=1, source_target_pairs={{0,1},{1,0},{2,3},{3,2},{4,5},{5,4},{6,7},{7,6},{8,9},{9,8},{10,11... | collective-permute-start | bytes 3194888 | tf_op jit(solution)/shard_map/ppermute | solution.py:17
  41.3 7.4 %collective-permute-start.13 = (bf16[1,352,256]{2,1,0:T(8,128)(2,1)S(1)}, bf16[1,352,256]{2,1,0:T(8,128)(2,1)S(1)}, u32[]{:S(2)}, u32[]{:S(2)}) collective-permute-start(bf16[1,352,256]{2,1,0:T(8,128)(2,1)S(1)} %get-tuple-element.72), channel_id=1, source_target_pairs={{0,8},{4,12},{8,0},{12,4},{16,24},{20,28},{24,16},{28,20},{1,9},{5... | collective-permute-start | bytes 540680 | tf_op jit(solution)/shard_map/ppermute | solution.py:17
  42.8 14.1 %collective-permute-start.16 = (bf16[2,352,256]{2,1,0:T(8,128)(2,1)S(1)}, bf16[2,352,256]{2,1,0:T(8,128)(2,1)S(1)}, u32[]{:S(2)}, u32[]{:S(2)}) collective-permute-start(bf16[2,352,256]{2,1,0:T(8,128)(2,1)S(1)} %get-tuple-element.78), channel_id=1, source_target_pairs={{0,8},{4,12},{8,0},{12,4},{16,24},{20,28},{24,16},{28,20},{1,9},{5... | collective-permute-start | bytes 1081352 | tf_op jit(solution)/shard_map/ppermute | solution.py:17
  44.1 8.6 %collective-permute-start.10 = (bf16[528,256]{1,0:T(8,128)(2,1)S(1)}, bf16[528,256]{1,0:T(8,128)(2,1)S(1)}, u32[]{:S(2)}, u32[]{:S(2)}) collective-permute-start(bf16[528,256]{1,0:T(8,128)(2,1)S(1)} %get-tuple-element.63), channel_id=1, source_target_pairs={{0,2},{1,3},{2,0},{3,1},{4,6},{5,7},{6,4},{7,5},{8,10},{9,11},{10,... | collective-permute-start | bytes 811016 | tf_op jit(solution)/shard_map/ppermute | solution.py:17
  45.7 9.2 %collective-permute-start.12 = (bf16[2,256,256]{2,1,0:T(8,128)(2,1)S(1)}, bf16[2,256,256]{2,1,0:T(8,128)(2,1)S(1)}, u32[]{:S(2)}, u32[]{:S(2)}) collective-permute-start(bf16[2,256,256]{2,1,0:T(8,128)(2,1)S(1)} %get-tuple-element.66), channel_id=1, source_target_pairs={{0,4},{4,0},{8,12},{12,8},{16,20},{20,16},{24,28},{28,24},{1,5},{5... | collective-permute-start | bytes 786440 | tf_op jit(solution)/shard_map/ppermute | solution.py:17
  48.8 9.9 %collective-permute-start.14 = (bf16[1,352,256]{2,1,0:T(8,128)(2,1)S(1)}, bf16[1,352,256]{2,1,0:T(8,128)(2,1)S(1)}, u32[]{:S(2)}, u32[]{:S(2)}) collective-permute-start(bf16[1,352,256]{2,1,0:T(8,128)(2,1)S(1)} %add_convert_fusion.1), channel_id=1, source_target_pairs={{0,4},{4,0},{8,12},{12,8},{16,20},{20,16},{24,28},{28,24},{1,5},{5... | collective-permute-start | bytes 540680 | tf_op jit(solution)/shard_map/ppermute | solution.py:17
  52.8 8.9 %collective-permute-start.11 = (bf16[272,256]{1,0:T(8,128)(2,1)S(1)}, bf16[272,256]{1,0:T(8,128)(2,1)S(1)}, u32[]{:S(2)}, u32[]{:S(2)}) collective-permute-start(bf16[272,256]{1,0:T(8,128)(2,1)S(1)} %get-tuple-element.65), channel_id=1, source_target_pairs={{0,4},{4,0},{8,12},{12,8},{16,20},{20,16},{24,28},{28,24},{1,5},{5... | collective-permute-start | bytes 417800 | tf_op jit(solution)/shard_map/ppermute | solution.py:17
  55.0 5.0 %collective-permute-start.15 = (bf16[256,256]{1,0:T(8,128)(2,1)S(1)}, bf16[256,256]{1,0:T(8,128)(2,1)S(1)}, u32[]{:S(2)}, u32[]{:S(2)}) collective-permute-start(bf16[256,256]{1,0:T(8,128)(2,1)S(1)} %get-tuple-element.74), channel_id=1, source_target_pairs={{0,2},{1,3},{2,0},{3,1},{4,6},{5,7},{6,4},{7,5},{8,10},{9,11},{10,... | collective-permute-start | bytes 393224 | tf_op jit(solution)/shard_map/ppermute | solution.py:17
  55.5 15.4 %collective-permute-start.19 = (bf16[3,352,256]{2,1,0:T(8,128)(2,1)S(1)}, bf16[3,352,256]{2,1,0:T(8,128)(2,1)S(1)}, u32[]{:S(2)}, u32[]{:S(2)}) collective-permute-start(bf16[3,352,256]{2,1,0:T(8,128)(2,1)S(1)} %get-tuple-element.90), channel_id=1, source_target_pairs={{0,8},{4,12},{8,0},{12,4},{16,24},{20,28},{24,16},{28,20},{1,9},{5... | collective-permute-start | bytes 1622024 | tf_op jit(solution)/shard_map/ppermute | solution.py:17
  57.0 11.3 %collective-permute-start.17 = (bf16[2,352,256]{2,1,0:T(8,128)(2,1)S(1)}, bf16[2,352,256]{2,1,0:T(8,128)(2,1)S(1)}, u32[]{:S(2)}, u32[]{:S(2)}) collective-permute-start(bf16[2,352,256]{2,1,0:T(8,128)(2,1)S(1)} %add_convert_fusion), channel_id=1, source_target_pairs={{0,4},{4,0},{8,12},{12,8},{16,20},{20,16},{24,28},{28,24},{1,5},{5... | collective-permute-start | bytes 1081352 | tf_op jit(solution)/shard_map/ppermute | solution.py:17
  61.7 8.2 %copy-start = (f32[128]{0:T(128)S(1)}, f32[128]{0:T(128)}, u32[]{:S(2)}) copy-start(f32[128]{0:T(128)} %param.10) | copy-start | bytes 1540
  61.8 8.1 %collective-permute-start.18 = (bf16[272,256]{1,0:T(8,128)(2,1)S(1)}, bf16[272,256]{1,0:T(8,128)(2,1)S(1)}, u32[]{:S(2)}, u32[]{:S(2)}) collective-permute-start(bf16[272,256]{1,0:T(8,128)(2,1)S(1)} %get-tuple-element.82), channel_id=1, source_target_pairs={{0,16},{4,20},{8,24},{12,28},{16,0},{20,4},{24,8},{28,12},{1,17},{... | collective-permute-start | bytes 417800 | tf_op jit(solution)/shard_map/ppermute | solution.py:17

commit v14 on v13

--- a/solution.py
+++ b/solution.py
@@ -122,7 +122,7 @@
         in_specs=[VMEM] * len(parts),
         out_specs=VMEM,
         compiler_params=PARAMS,
-        cost_estimate=pl.CostEstimate(flops=1 * 10**9, bytes_accessed=0, transcendentals=0),
+        cost_estimate=pl.CostEstimate(flops=2 * 10**9, bytes_accessed=0, transcendentals=0),
     )(*parts)
 
 

time: 73.4 us -> 73.4 us (level)
  starting transfers between devices: 24.1 us -> 23 us
  waiting for transfers between devices: 37.4 us -> 38.4 us
    ppermute x20, waiting for transfers between devices: 37.4 us -> 38.4 us  [partner(): lax.ppermute(x, axis, [(i, i ^ mask) for i in range(lax.axis_size(axis))])]
    ppermute x20, starting transfers between devices: 24.1 us -> 23 us  [partner(): lax.ppermute(x, axis, [(i, i ^ mask) for i in range(lax.axis_size(axis))])]
  transfers between devices with their start and end apart: 20 -> 20, of which waited for: 14 -> 16; matrix products, arithmetic and copies ran while one was open for 0% -> 0% of each run, Pallas kernels for 6% -> 6%
where the time goes in v14:
time: 73.4 us; the launch traced here: 72 us
  waiting for transfers between devices  38.4 us (52%)
  starting transfers between devices  23 us (31%)
  Pallas kernels  9.71 us (13%)
    ppermute x20, waiting for transfers between devices, partner(): lax.ppermute(x, axis, [(i, i ^ mask) for i in range(lax.axis_size(axis))])  38.4 us
    ppermute x20, starting transfers between devices, partner(): lax.ppermute(x, axis, [(i, i ^ mask) for i in range(lax.axis_size(axis))])  23 us
    pallas_call x1, Pallas kernels, outer(): pl.pallas_call(outer_kernel, out_shape=(jax.ShapeDtypeStruct((3, half, to...  2.75 us
    pallas_call x2, Pallas kernels, write_half(): pl.pallas_call(kernel, out_shape=(jax.ShapeDtypeStruct((2 * shape[1], sha...  2.05 us
    pallas_call x1, Pallas kernels, prologue(): pl.pallas_call(functools.partial(prologue_kernel, bool(token_args)), out_...  1.47 us
  transfers between devices with their start and end apart: 20, of which 16 were waited for; matrix products, arithmetic and copies ran while one was open for 0% of the time, Pallas kernels for 6%

profile of v14, /device:TPU:0, one launch (start us, length us, event | category | flops | bytes accessed | tf_op | source)
XLA Modules:
  0.0 72.0 jit_solution(552063938711435397)
XLA Ops:
  0.6 1.5 %shard_map.118 = (bf16[3,352,256]{2,1,0:T(8,128)(2,1)S(1)}, bf16[3,352,256]{2,1,0:T(8,128)(2,1)S(1)}, bf16[2,128,1024]{2,1,0:T(8,128)(2,1)S(1)}, bf16[2,128,256]...) custom-call(bf16[704,256]{1,0:T(8,128)(2,1)} %bitcast.14, bf16[704,256]{1,0:T(8,128)(2,1)} %bitcast.15, ...), custom_call_target="tpu_custom_call" | custom-call | tf_op jit(solution)/shard_map/pallas_call | solution.py:103
  2.1 3.0 %collective-permute-start = (bf16[2,128,256]{2,1,0:T(8,128)(2,1)S(1)}, bf16[2,128,256]{2,1,0:T(8,128)(2,1)S(1)}, u32[]{:S(2)}, u32[]{:S(2)}) collective-permute-start(bf16[2,128,256]{2,1,0:T(8,128)(2,1)S(1)} %get-tuple-element.51), channel_id=1, source_target_pairs={{0,4},{4,0},{8,12},{12,8},{16,20},{20,16},{24,28},{28,24},{1,5},{5... | collective-permute-start | bytes 393224 | tf_op jit(solution)/shard_map/ppermute | solution.py:17
  5.1 2.6 %collective-permute-start.2 = (bf16[2,128,256]{2,1,0:T(8,128)(2,1)S(1)}, bf16[2,128,256]{2,1,0:T(8,128)(2,1)S(1)}, u32[]{:S(2)}, u32[]{:S(2)}) collective-permute-start(bf16[2,128,256]{2,1,0:T(8,128)(2,1)S(1)} %get-tuple-element.52), channel_id=1, source_target_pairs={{0,20},{4,16},{8,28},{12,24},{16,4},{20,0},{24,12},{28,8},{1,21},{... | collective-permute-start | bytes 393224 | tf_op jit(solution)/shard_map/ppermute | solution.py:17
  7.7 1.8 %collective-permute-start.7 = (bf16[3,352,256]{2,1,0:T(8,128)(2,1)S(1)}, bf16[3,352,256]{2,1,0:T(8,128)(2,1)S(1)}, u32[]{:S(2)}, u32[]{:S(2)}) collective-permute-start(bf16[3,352,256]{2,1,0:T(8,128)(2,1)S(1)} %get-tuple-element.55), channel_id=1, source_target_pairs={{0,4},{4,0},{8,12},{12,8},{16,20},{20,16},{24,28},{28,24},{1,5},{5... | collective-permute-start | bytes 1622024 | tf_op jit(solution)/shard_map/ppermute | solution.py:17
  9.5 1.6 %collective-permute-start.5 = (bf16[3,352,256]{2,1,0:T(8,128)(2,1)S(1)}, bf16[3,352,256]{2,1,0:T(8,128)(2,1)S(1)}, u32[]{:S(2)}, u32[]{:S(2)}) collective-permute-start(bf16[3,352,256]{2,1,0:T(8,128)(2,1)S(1)} %get-tuple-element.53.refs_5_), channel_id=1, source_target_pairs={{0,8},{4,12},{8,0},{12,4},{16,24},{20,28},{24,16},{28,20},{1,9},{5... | collective-permute-start | bytes 1622024 | tf_op jit(solution)/shard_map/ppermute | solution.py:17
  11.1 7.7 %collective-permute-done.2.refs_2_ = bf16[2,128,256]{2,1,0:T(8,128)(2,1)S(1)} collective-permute-done((bf16[2,128,256]{2,1,0:T(8,128)(2,1)S(1)}, bf16[2,128,256]{2,1,0:T(8,128)(2,1)S(1)}, u32[]{:S(2)}, u32[]{:S(2)}) %collective-permute-start.2) | collective-permute-done | bytes 131104 | tf_op jit(solution)/shard_map/ppermute | solution.py:17
  19.5 1.6 %collective-permute-start.4 = (bf16[3,2,128,256]{3,2,1,0:T(8,128)(2,1)S(1)}, bf16[3,2,128,256]{3,2,1,0:T(8,128)(2,1)S(1)}, u32[]{:S(2)}, u32[]{:S(2)}) collective-permute-start(bf16[3,2,128,256]{3,2,1,0:T(8,128)(2,1)S(1)} %shard_map.119.refs_1_), channel_id=1, source_target_pairs={{0,2},{1,3},{2,0},{3,1},{4,6},{5,7},{6,4},{7,5},{8,10},{9,11},{10,... | collective-permute-start | bytes 1179656 | tf_op jit(solution)/shard_map/ppermute | solution.py:17
  21.1 2.4 %collective-permute-done.7.refs_6_ = bf16[3,352,256]{2,1,0:T(8,128)(2,1)S(1)} collective-permute-done((bf16[3,352,256]{2,1,0:T(8,128)(2,1)S(1)}, bf16[3,352,256]{2,1,0:T(8,128)(2,1)S(1)}, u32[]{:S(2)}, u32[]{:S(2)}) %collective-permute-start.7) | collective-permute-done | bytes 540704 | tf_op jit(solution)/shard_map/ppermute | solution.py:17
  23.5 1.7 %collective-permute-start.8 = (bf16[3,352,256]{2,1,0:T(8,128)(2,1)S(1)}, bf16[3,352,256]{2,1,0:T(8,128)(2,1)S(1)}, u32[]{:S(2)}, u32[]{:S(2)}) collective-permute-start(bf16[3,352,256]{2,1,0:T(8,128)(2,1)S(1)} %collective-permute-done.7.refs_6_), channel_id=1, source_target_pairs={{0,8},{4,12},{8,0},{12,4},{16,24},{20,28},{24,16},{28,20},{1,9},{5... | collective-permute-start | bytes 1622024 | tf_op jit(solution)/shard_map/ppermute | solution.py:17
  25.1 4.3 %collective-permute-done.4.refs_3_ = bf16[3,2,128,256]{3,2,1,0:T(8,128)(2,1)S(1)} collective-permute-done((bf16[3,2,128,256]{3,2,1,0:T(8,128)(2,1)S(1)}, bf16[3,2,128,256]{3,2,1,0:T(8,128)(2,1)S(1)}, u32[]{:S(2)}, u32[]{:S(2)}) %collective-permute-start.4) | collective-permute-done | bytes 393248 | tf_op jit(solution)/shard_map/ppermute | solution.py:17
  29.5 1.7 %collective-permute-done.6.refs_4_ = bf16[3,2,128,256]{3,2,1,0:T(8,128)(2,1)S(1)} collective-permute-done((bf16[3,2,128,256]{3,2,1,0:T(8,128)(2,1)S(1)}, bf16[3,2,128,256]{3,2,1,0:T(8,128)(2,1)S(1)}, u32[]{:S(2)}, u32[]{:S(2)}) %collective-permute-start.6) | collective-permute-done | bytes 393248 | tf_op jit(solution)/shard_map/ppermute | solution.py:17
  31.2 1.3 %shard_map.120 = (bf16[512,1024]{1,0:T(8,128)(2,1)S(1)}, bf16[512,1024]{1,0:T(8,128)(2,1)S(1)}, bf16[3,352,768]{2,1,0:T(8,128)(2,1)S(1)}, f32[3,352,512]{2,1,0:T(8,128)S(1)}) custom-call(bf16[2,128,1024]{2,1,0:T(8,128)(2,1)S(1)} %get-tuple-element.50.refs_0_, bf16[3,2,128,256]{3,2,1,0:T(8,128)(2,1)S(1)} %shard_map.119.refs_1_, ...), custom_call_target="tpu_custom_call" | custom-call | flops 1 | bytes 1 | tf_op jit(solution)/shard_map/pallas_call | solution.py:168
  32.5 6.0 %collective-permute-done.8.last = bf16[3,352,256]{2,1,0:T(8,128)(2,1)S(1)} collective-permute-done((bf16[3,352,256]{2,1,0:T(8,128)(2,1)S(1)}, bf16[3,352,256]{2,1,0:T(8,128)(2,1)S(1)}, u32[]{:S(2)}, u32[]{:S(2)}) %collective-permute-start.8) | collective-permute-done | bytes 540704 | tf_op jit(solution)/shard_map/ppermute | solution.py:17
  38.5 2.7 %shard_map.121 = (bf16[3,352,512]{2,1,0:T(8,128)(2,1)S(1)}, f32[2,1040,256]{2,1,0:T(8,128)S(1)}, bf16[2,1040,256]{2,1,0:T(8,128)(2,1)S(1)}, bf16[2,352,256]{2,1,0:T(8,128)(2,1)S(1)}, bf16[1,352,256]{2,1,0:T(8,128)(2,1)S(1)}) custom-call(bf16[512,1024]{1,0:T(8,128)(2,1)S(1)} %get-tuple-element.57.x_all, bf16[512,1024]{1,0:T(8,128)(2,1)S(1)} %get-tuple-element.58.s_all, ...), custom_call_target="tpu_custom_call" | custom-call | flops 1476395008 | tf_op jit(solution)/shard_map/pallas_call | solution.py:245
  42.2 1.2 %collective-permute-start.16 = (bf16[2,352,256]{2,1,0:T(8,128)(2,1)S(1)}, bf16[2,352,256]{2,1,0:T(8,128)(2,1)S(1)}, u32[]{:S(2)}, u32[]{:S(2)}) collective-permute-start(bf16[2,352,256]{2,1,0:T(8,128)(2,1)S(1)} %get-tuple-element.78), channel_id=1, source_target_pairs={{0,8},{4,12},{8,0},{12,4},{16,24},{20,28},{24,16},{28,20},{1,9},{5... | collective-permute-start | bytes 1081352 | tf_op jit(solution)/shard_map/ppermute | solution.py:17
  44.1 1.6 %collective-permute-start.10 = (bf16[528,256]{1,0:T(8,128)(2,1)S(1)}, bf16[528,256]{1,0:T(8,128)(2,1)S(1)}, u32[]{:S(2)}, u32[]{:S(2)}) collective-permute-start(bf16[528,256]{1,0:T(8,128)(2,1)S(1)} %get-tuple-element.63), channel_id=1, source_target_pairs={{0,2},{1,3},{2,0},{3,1},{4,6},{5,7},{6,4},{7,5},{8,10},{9,11},{10,... | collective-permute-start | bytes 811016 | tf_op jit(solution)/shard_map/ppermute | solution.py:17
  47.2 1.5 %collective-permute-done.13 = bf16[1,352,256]{2,1,0:T(8,128)(2,1)S(1)} collective-permute-done((bf16[1,352,256]{2,1,0:T(8,128)(2,1)S(1)}, bf16[1,352,256]{2,1,0:T(8,128)(2,1)S(1)}, u32[]{:S(2)}, u32[]{:S(2)}) %collective-permute-start.13) | collective-permute-done | bytes 180256 | tf_op jit(solution)/shard_map/ppermute | solution.py:17
  49.4 3.3 %collective-permute-done.10.from_y = bf16[528,256]{1,0:T(8,128)(2,1)S(1)} collective-permute-done((bf16[528,256]{1,0:T(8,128)(2,1)S(1)}, bf16[528,256]{1,0:T(8,128)(2,1)S(1)}, u32[]{:S(2)}, u32[]{:S(2)}) %collective-permute-start.10) | collective-permute-done | bytes 270368 | tf_op jit(solution)/shard_map/ppermute | solution.py:17
  53.3 1.5 %collective-permute-done.12.from_x = bf16[2,256,256]{2,1,0:T(8,128)(2,1)S(1)} collective-permute-done((bf16[2,256,256]{2,1,0:T(8,128)(2,1)S(1)}, bf16[2,256,256]{2,1,0:T(8,128)(2,1)S(1)}, u32[]{:S(2)}, u32[]{:S(2)}) %collective-permute-start.12) | collective-permute-done | bytes 262176 | tf_op jit(solution)/shard_map/ppermute | solution.py:17
  57.5 1.2 %collective-permute-done.14.got_down = bf16[1,352,256]{2,1,0:T(8,128)(2,1)S(1)} collective-permute-done((bf16[1,352,256]{2,1,0:T(8,128)(2,1)S(1)}, bf16[1,352,256]{2,1,0:T(8,128)(2,1)S(1)}, u32[]{:S(2)}, u32[]{:S(2)}) %collective-permute-start.14) | collective-permute-done | bytes 180256 | tf_op jit(solution)/shard_map/ppermute | solution.py:17
  58.7 1.3 %collective-permute-done.15.from_y = bf16[256,256]{1,0:T(8,128)(2,1)S(1)} collective-permute-done((bf16[256,256]{1,0:T(8,128)(2,1)S(1)}, bf16[256,256]{1,0:T(8,128)(2,1)S(1)}, u32[]{:S(2)}, u32[]{:S(2)}) %collective-permute-start.15) | collective-permute-done | bytes 131104 | tf_op jit(solution)/shard_map/ppermute | solution.py:17
  60.0 1.7 %collective-permute-done.11.from_x = bf16[272,256]{1,0:T(8,128)(2,1)S(1)} collective-permute-done((bf16[272,256]{1,0:T(8,128)(2,1)S(1)}, bf16[272,256]{1,0:T(8,128)(2,1)S(1)}, u32[]{:S(2)}, u32[]{:S(2)}) %collective-permute-start.11) | collective-permute-done | bytes 139296 | tf_op jit(solution)/shard_map/ppermute | solution.py:17
  61.8 2.8 %collective-permute-start.18 = (bf16[272,256]{1,0:T(8,128)(2,1)S(1)}, bf16[272,256]{1,0:T(8,128)(2,1)S(1)}, u32[]{:S(2)}, u32[]{:S(2)}) collective-permute-start(bf16[272,256]{1,0:T(8,128)(2,1)S(1)} %get-tuple-element.82), channel_id=1, source_target_pairs={{0,16},{4,20},{8,24},{12,28},{16,0},{20,4},{24,8},{28,12},{1,17},{... | collective-permute-start | bytes 417800 | tf_op jit(solution)/shard_map/ppermute | solution.py:17
  64.6 3.7 %collective-permute-done.17.got = bf16[2,352,256]{2,1,0:T(8,128)(2,1)S(1)} collective-permute-done((bf16[2,352,256]{2,1,0:T(8,128)(2,1)S(1)}, bf16[2,352,256]{2,1,0:T(8,128)(2,1)S(1)}, u32[]{:S(2)}, u32[]{:S(2)}) %collective-permute-start.17) | collective-permute-done | bytes 360480 | tf_op jit(solution)/shard_map/ppermute | solution.py:17
  (32 shorter events, 11.7 us)
Async XLA Ops:
  2.1 9.0 %collective-permute-start = (bf16[2,128,256]{2,1,0:T(8,128)(2,1)S(1)}, bf16[2,128,256]{2,1,0:T(8,128)(2,1)S(1)}, u32[]{:S(2)}, u32[]{:S(2)}) collective-permute-start(bf16[2,128,256]{2,1,0:T(8,128)(2,1)S(1)} %get-tuple-element.51), channel_id=1, source_target_pairs={{0,4},{4,0},{8,12},{12,8},{16,20},{20,16},{24,28},{28,24},{1,5},{5... | collective-permute-start | bytes 393224 | tf_op jit(solution)/shard_map/ppermute | solution.py:17
  5.1 13.6 %collective-permute-start.2 = (bf16[2,128,256]{2,1,0:T(8,128)(2,1)S(1)}, bf16[2,128,256]{2,1,0:T(8,128)(2,1)S(1)}, u32[]{:S(2)}, u32[]{:S(2)}) collective-permute-start(bf16[2,128,256]{2,1,0:T(8,128)(2,1)S(1)} %get-tuple-element.52), channel_id=1, source_target_pairs={{0,20},{4,16},{8,28},{12,24},{16,4},{20,0},{24,12},{28,8},{1,21},{... | collective-permute-start | bytes 393224 | tf_op jit(solution)/shard_map/ppermute | solution.py:17
  7.7 11.8 %collective-permute-start.1 = (bf16[2,128,256]{2,1,0:T(8,128)(2,1)S(1)}, bf16[2,128,256]{2,1,0:T(8,128)(2,1)S(1)}, u32[]{:S(2)}, u32[]{:S(2)}) collective-permute-start(bf16[2,128,256]{2,1,0:T(8,128)(2,1)S(1)} %get-tuple-element.52), channel_id=1, source_target_pairs={{0,16},{4,20},{8,24},{12,28},{16,0},{20,4},{24,8},{28,12},{1,17},{... | collective-permute-start | bytes 393224 | tf_op jit(solution)/shard_map/ppermute | solution.py:17
  7.7 15.7 %collective-permute-start.7 = (bf16[3,352,256]{2,1,0:T(8,128)(2,1)S(1)}, bf16[3,352,256]{2,1,0:T(8,128)(2,1)S(1)}, u32[]{:S(2)}, u32[]{:S(2)}) collective-permute-start(bf16[3,352,256]{2,1,0:T(8,128)(2,1)S(1)} %get-tuple-element.55), channel_id=1, source_target_pairs={{0,4},{4,0},{8,12},{12,8},{16,20},{20,16},{24,28},{28,24},{1,5},{5... | collective-permute-start | bytes 1622024 | tf_op jit(solution)/shard_map/ppermute | solution.py:17
  9.5 20.0 %collective-permute-start.5 = (bf16[3,352,256]{2,1,0:T(8,128)(2,1)S(1)}, bf16[3,352,256]{2,1,0:T(8,128)(2,1)S(1)}, u32[]{:S(2)}, u32[]{:S(2)}) collective-permute-start(bf16[3,352,256]{2,1,0:T(8,128)(2,1)S(1)} %get-tuple-element.53.refs_5_), channel_id=1, source_target_pairs={{0,8},{4,12},{8,0},{12,4},{16,24},{20,28},{24,16},{28,20},{1,9},{5... | collective-permute-start | bytes 1622024 | tf_op jit(solution)/shard_map/ppermute | solution.py:17
  19.5 10.0 %collective-permute-start.4 = (bf16[3,2,128,256]{3,2,1,0:T(8,128)(2,1)S(1)}, bf16[3,2,128,256]{3,2,1,0:T(8,128)(2,1)S(1)}, u32[]{:S(2)}, u32[]{:S(2)}) collective-permute-start(bf16[3,2,128,256]{3,2,1,0:T(8,128)(2,1)S(1)} %shard_map.119.refs_1_), channel_id=1, source_target_pairs={{0,2},{1,3},{2,0},{3,1},{4,6},{5,7},{6,4},{7,5},{8,10},{9,11},{10,... | collective-permute-start | bytes 1179656 | tf_op jit(solution)/shard_map/ppermute | solution.py:17
  23.5 15.0 %collective-permute-start.8 = (bf16[3,352,256]{2,1,0:T(8,128)(2,1)S(1)}, bf16[3,352,256]{2,1,0:T(8,128)(2,1)S(1)}, u32[]{:S(2)}, u32[]{:S(2)}) collective-permute-start(bf16[3,352,256]{2,1,0:T(8,128)(2,1)S(1)} %collective-permute-done.7.refs_6_), channel_id=1, source_target_pairs={{0,8},{4,12},{8,0},{12,4},{16,24},{20,28},{24,16},{28,20},{1,9},{5... | collective-permute-start | bytes 1622024 | tf_op jit(solution)/shard_map/ppermute | solution.py:17
  25.1 4.4 %collective-permute-start.3 = (bf16[3,2,128,256]{3,2,1,0:T(8,128)(2,1)S(1)}, bf16[3,2,128,256]{3,2,1,0:T(8,128)(2,1)S(1)}, u32[]{:S(2)}, u32[]{:S(2)}) collective-permute-start(bf16[3,2,128,256]{3,2,1,0:T(8,128)(2,1)S(1)} %shard_map.119.refs_1_), channel_id=1, source_target_pairs={{0,1},{1,0},{2,3},{3,2},{4,5},{5,4},{6,7},{7,6},{8,9},{9,8},{10,11... | collective-permute-start | bytes 1179656 | tf_op jit(solution)/shard_map/ppermute | solution.py:17
  29.5 1.7 %collective-permute-start.6 = (bf16[3,2,128,256]{3,2,1,0:T(8,128)(2,1)S(1)}, bf16[3,2,128,256]{3,2,1,0:T(8,128)(2,1)S(1)}, u32[]{:S(2)}, u32[]{:S(2)}) collective-permute-start(bf16[3,2,128,256]{3,2,1,0:T(8,128)(2,1)S(1)} %collective-permute-done.4.refs_3_), channel_id=1, source_target_pairs={{0,1},{1,0},{2,3},{3,2},{4,5},{5,4},{6,7},{7,6},{8,9},{9,8},{10,11... | collective-permute-start | bytes 1179656 | tf_op jit(solution)/shard_map/ppermute | solution.py:17
  41.2 2.7 %collective-permute-start.9 = (bf16[2,1040,256]{2,1,0:T(8,128)(2,1)S(1)}, bf16[2,1040,256]{2,1,0:T(8,128)(2,1)S(1)}, u32[]{:S(2)}, u32[]{:S(2)}) collective-permute-start(bf16[2,1040,256]{2,1,0:T(8,128)(2,1)S(1)} %get-tuple-element.62), channel_id=1, source_target_pairs={{0,1},{1,0},{2,3},{3,2},{4,5},{5,4},{6,7},{7,6},{8,9},{9,8},{10,11... | collective-permute-start | bytes 3194888 | tf_op jit(solution)/shard_map/ppermute | solution.py:17
  41.3 7.4 %collective-permute-start.13 = (bf16[1,352,256]{2,1,0:T(8,128)(2,1)S(1)}, bf16[1,352,256]{2,1,0:T(8,128)(2,1)S(1)}, u32[]{:S(2)}, u32[]{:S(2)}) collective-permute-start(bf16[1,352,256]{2,1,0:T(8,128)(2,1)S(1)} %get-tuple-element.72), channel_id=1, source_target_pairs={{0,8},{4,12},{8,0},{12,4},{16,24},{20,28},{24,16},{28,20},{1,9},{5... | collective-permute-start | bytes 540680 | tf_op jit(solution)/shard_map/ppermute | solution.py:17
  42.2 14.1 %collective-permute-start.16 = (bf16[2,352,256]{2,1,0:T(8,128)(2,1)S(1)}, bf16[2,352,256]{2,1,0:T(8,128)(2,1)S(1)}, u32[]{:S(2)}, u32[]{:S(2)}) collective-permute-start(bf16[2,352,256]{2,1,0:T(8,128)(2,1)S(1)} %get-tuple-element.78), channel_id=1, source_target_pairs={{0,8},{4,12},{8,0},{12,4},{16,24},{20,28},{24,16},{28,20},{1,9},{5... | collective-permute-start | bytes 1081352 | tf_op jit(solution)/shard_map/ppermute | solution.py:17
  44.1 8.6 %collective-permute-start.10 = (bf16[528,256]{1,0:T(8,128)(2,1)S(1)}, bf16[528,256]{1,0:T(8,128)(2,1)S(1)}, u32[]{:S(2)}, u32[]{:S(2)}) collective-permute-start(bf16[528,256]{1,0:T(8,128)(2,1)S(1)} %get-tuple-element.63), channel_id=1, source_target_pairs={{0,2},{1,3},{2,0},{3,1},{4,6},{5,7},{6,4},{7,5},{8,10},{9,11},{10,... | collective-permute-start | bytes 811016 | tf_op jit(solution)/shard_map/ppermute | solution.py:17
  45.7 9.2 %collective-permute-start.12 = (bf16[2,256,256]{2,1,0:T(8,128)(2,1)S(1)}, bf16[2,256,256]{2,1,0:T(8,128)(2,1)S(1)}, u32[]{:S(2)}, u32[]{:S(2)}) collective-permute-start(bf16[2,256,256]{2,1,0:T(8,128)(2,1)S(1)} %get-tuple-element.66), channel_id=1, source_target_pairs={{0,4},{4,0},{8,12},{12,8},{16,20},{20,16},{24,28},{28,24},{1,5},{5... | collective-permute-start | bytes 786440 | tf_op jit(solution)/shard_map/ppermute | solution.py:17
  48.8 9.9 %collective-permute-start.14 = (bf16[1,352,256]{2,1,0:T(8,128)(2,1)S(1)}, bf16[1,352,256]{2,1,0:T(8,128)(2,1)S(1)}, u32[]{:S(2)}, u32[]{:S(2)}) collective-permute-start(bf16[1,352,256]{2,1,0:T(8,128)(2,1)S(1)} %add_convert_fusion.1), channel_id=1, source_target_pairs={{0,4},{4,0},{8,12},{12,8},{16,20},{20,16},{24,28},{28,24},{1,5},{5... | collective-permute-start | bytes 540680 | tf_op jit(solution)/shard_map/ppermute | solution.py:17
  52.7 9.0 %collective-permute-start.11 = (bf16[272,256]{1,0:T(8,128)(2,1)S(1)}, bf16[272,256]{1,0:T(8,128)(2,1)S(1)}, u32[]{:S(2)}, u32[]{:S(2)}) collective-permute-start(bf16[272,256]{1,0:T(8,128)(2,1)S(1)} %get-tuple-element.65), channel_id=1, source_target_pairs={{0,4},{4,0},{8,12},{12,8},{16,20},{20,16},{24,28},{28,24},{1,5},{5... | collective-permute-start | bytes 417800 | tf_op jit(solution)/shard_map/ppermute | solution.py:17
  55.0 5.0 %collective-permute-start.15 = (bf16[256,256]{1,0:T(8,128)(2,1)S(1)}, bf16[256,256]{1,0:T(8,128)(2,1)S(1)}, u32[]{:S(2)}, u32[]{:S(2)}) collective-permute-start(bf16[256,256]{1,0:T(8,128)(2,1)S(1)} %get-tuple-element.74), channel_id=1, source_target_pairs={{0,2},{1,3},{2,0},{3,1},{4,6},{5,7},{6,4},{7,5},{8,10},{9,11},{10,... | collective-permute-start | bytes 393224 | tf_op jit(solution)/shard_map/ppermute | solution.py:17
  55.5 15.4 %collective-permute-start.19 = (bf16[3,352,256]{2,1,0:T(8,128)(2,1)S(1)}, bf16[3,352,256]{2,1,0:T(8,128)(2,1)S(1)}, u32[]{:S(2)}, u32[]{:S(2)}) collective-permute-start(bf16[3,352,256]{2,1,0:T(8,128)(2,1)S(1)} %get-tuple-element.90), channel_id=1, source_target_pairs={{0,8},{4,12},{8,0},{12,4},{16,24},{20,28},{24,16},{28,20},{1,9},{5... | collective-permute-start | bytes 1622024 | tf_op jit(solution)/shard_map/ppermute | solution.py:17
  56.5 11.8 %collective-permute-start.17 = (bf16[2,352,256]{2,1,0:T(8,128)(2,1)S(1)}, bf16[2,352,256]{2,1,0:T(8,128)(2,1)S(1)}, u32[]{:S(2)}, u32[]{:S(2)}) collective-permute-start(bf16[2,352,256]{2,1,0:T(8,128)(2,1)S(1)} %add_convert_fusion), channel_id=1, source_target_pairs={{0,4},{4,0},{8,12},{12,8},{16,20},{20,16},{24,28},{28,24},{1,5},{5... | collective-permute-start | bytes 1081352 | tf_op jit(solution)/shard_map/ppermute | solution.py:17
  61.7 8.0 %copy-start = (f32[128]{0:T(128)S(1)}, f32[128]{0:T(128)}, u32[]{:S(2)}) copy-start(f32[128]{0:T(128)} %param.10) | copy-start | bytes 1540
  61.8 7.9 %collective-permute-start.18 = (bf16[272,256]{1,0:T(8,128)(2,1)S(1)}, bf16[272,256]{1,0:T(8,128)(2,1)S(1)}, u32[]{:S(2)}, u32[]{:S(2)}) collective-permute-start(bf16[272,256]{1,0:T(8,128)(2,1)S(1)} %get-tuple-element.82), channel_id=1, source_target_pairs={{0,16},{4,20},{8,24},{12,28},{16,0},{20,4},{24,8},{28,12},{1,17},{... | collective-permute-start | bytes 417800 | tf_op jit(solution)/shard_map/ppermute | solution.py:17
